TPU v7x, 512 devices: a whole 4x4x16 slice. The times are simulated.
512 devices in a mesh: dp: 64 (over z_hi, x, y), seq: 8 (over z_lo, core).
Axes of the slice: x: 4, y: 4, z: 16 (z_hi: 4, z_lo: 4; z = z_hi * 4 + z_lo), core: 2. Of those that a mesh axis runs over, the one named last changes fastest.
Arguments:
- tokens: bfloat16 [32768, 2048], P(('dp', 'seq')), may hold values from -24 to 24
- proj_weight: bfloat16 [2048, 2048], P('dp', 'seq'), may hold values from -0.125 to 0.125
- cotangent: bfloat16 [32768, 2048], P('dp', 'seq'), may hold values from -0.75 to 0.75
- filters: float32 [7, 2048], P(None, 'seq'), may hold values from -6 to 6
Outputs:
- input_grad: bfloat16 [32768, 2048], P(('dp', 'seq'))
- weight_grad: bfloat16 [2048, 2048], P('dp', 'seq')
- filter_grad: float32 [7, 2048], P(None, 'seq')
All inputs are finite; a program needn't handle non-finite values.
Results may differ from a plain program's by a relative error of at most 0.017.
Values may be sent and summed in bfloat16 or wider, within the bound.
No kernel may reach another device: no remote copies, remote signals or barrier semaphores. Data moves between devices by JAX's collectives and lax.ppermute only.
A program may use at most 64 MiB of HBM per device.

v0:
```python
import jax
import jax.numpy as jnp
from jax import lax
from jax.sharding import PartitionSpec as P

TAPS = 7


def from_behind(value, axis, steps):
    count = lax.axis_size(axis)
    first, last = (max(0, -steps), min(count, count - steps))
    return lax.ppermute(value, axis, [(source, source + steps) for source in range(first, last)])


def body(tokens, proj_weight, cotangent, filters):
    full_rows = lax.all_gather(tokens, "seq", axis=0, tiled=True)
    slab_len = full_rows.shape[0]
    weight_cols = lax.all_gather(proj_weight, "dp", axis=0, tiled=True)
    featured = jnp.dot(full_rows, weight_cols, preferred_element_type=jnp.float32)
    feat_bf = featured.astype(jnp.bfloat16)
    feat_float = lax.optimization_barrier(feat_bf).astype(jnp.float32)
    head_rows = cotangent[: TAPS - 1]
    following = from_behind(head_rows, "dp", -1)
    extended = jnp.concatenate([cotangent, following], 0).astype(jnp.float32)
    grad_feat = jnp.zeros((slab_len, cotangent.shape[1]), jnp.float32)
    filter_rows = []
    for tap_index in range(TAPS):
        window = extended[tap_index : tap_index + slab_len]
        grad_feat = grad_feat + filters[tap_index] * window
        filter_rows.append(jnp.sum(feat_float * window, axis=0))
    filter_local = jnp.stack(filter_rows)
    grad_bf = grad_feat.astype(jnp.bfloat16)
    filter_grad = lax.psum(filter_local, "dp")
    summed = lax.psum_scatter(
        lax.dot_general(
            grad_bf, weight_cols, (((1,), (1,)), ((), ())), preferred_element_type=jnp.float32
        ).astype(jnp.bfloat16),
        "seq",
        scatter_dimension=0,
        tiled=True,
    ).astype(jnp.float32)
    input_grad = summed.astype(jnp.bfloat16)
    summed = lax.psum_scatter(
        lax.dot_general(
            full_rows, grad_bf, (((0,), (0,)), ((), ())), preferred_element_type=jnp.float32
        ),
        "dp",
        scatter_dimension=0,
        tiled=True,
    )
    weight_grad = summed.astype(jnp.bfloat16)
    return (input_grad, weight_grad, filter_grad)


def solution(mesh):
    in_specs = (P(("dp", "seq"), None), P("dp", "seq"), P("dp", "seq"), P(None, "seq"))
    out_specs = (P(("dp", "seq"), None), P("dp", "seq"), P(None, "seq"))
    return jax.shard_map(body, mesh=mesh, in_specs=in_specs, out_specs=out_specs, check_vma=False)
```

profile of v0, /device:TPU:1, one launch (start us, length us, event | category | flops | bytes accessed | tf_op | source)
XLA Modules:
  0.0 662.4 jit_solution(9652204220833844286)
XLA Ops:
  7.2 0.0 all-gather.5.cloned.1.call-start
  7.2 0.7 all-gather.5.cloned.1.call-update
  7.9 0.0 all-gather.3.cloned.1.call-start
  7.9 0.7 all-gather.3.cloned.1.call-update
  8.6 0.0 reduce-scatter.7.cloned.1.call-start
  8.7 0.7 slice.46
  9.4 1.3 collective-permute-start
  10.7 1.0 fusion.7
  11.6 2.8 collective-permute-done
  14.4 1.0 maximum_convert_fusion
  15.4 0.4 add_convert_fusion
  15.8 42.3 %all-gather.5.cloned.1.call-done = bf16[512,2048]{1,0:T(8,128)(2,1)} async-done(((bf16[64,2048]{1,0:T(8,128)(2,1)}), bf16[512,2048]{1,0:T(8,128)(2,1)}) %all-gather.5.cloned.1.call-update) | async-done | bytes 2097168 | tf_op jit(solution)/shard_map/all_gather | solution.py:16
  58.1 2.3 convolution_bitcast_fusion
  60.5 1.9 copy.9
  62.3 0.0 reduce-scatter.5.cloned.1.call-start
  62.4 104.0 %all-gather.3.cloned.1.call-done = bf16[2048,256]{1,0:T(8,128)(2,1)} async-done(((bf16[32,256]{1,0:T(8,128)(2,1)}), bf16[2048,256]{1,0:T(8,128)(2,1)}) %all-gather.3.cloned.1.call-update) | async-done | bytes 1048592 | tf_op jit(solution)/shard_map/all_gather | solution.py:18
  166.4 3.3 convolution_convert_fusion
  169.7 1.9 convolution_convert_fusion.1
  171.6 0.5 fusion.6
  172.2 200.6 %psum.7 = f32[7,256]{1,0:T(8,128)} all-reduce(f32[7,256]{1,0:T(8,128)S(1)} %stack.31), channel_id=1, replica_groups=mesh['dp'=64,'seq'=8] {'dp'}, use_global_device_ids=true, to_apply=%region_9.0 | all-reduce | flops 1792 | bytes 14336 | tf_op jit(solution)/shard_map/psum | solution.py:33
  372.8 191.8 %reduce-scatter.7.cloned.1.call-done = f32[32,256]{1,0:T(8,128)} async-done(((f32[2048,256]{1,0:T(8,128)}), f32[32,256]{1,0:T(8,128)}) %reduce-scatter.7.cloned.1.call-update) | async-done | bytes 32784
  564.6 0.9 copy.10
  565.5 0.7 copy.8
  566.1 89.8 %reduce-scatter.5.cloned.1.call-done = bf16[64,2048]{1,0:T(8,128)(2,1)} async-done(((bf16[512,2048]{1,0:T(8,128)(2,1)}), bf16[64,2048]{1,0:T(8,128)(2,1)}) %reduce-scatter.5.cloned.1.call-update) | async-done | bytes 262160 | tf_op jit(solution)/shard_map/reduce_scatter | solution.py:34
  (5 shorter events, 0.1 us)
Async XLA Ops:
  7.2 51.0 %all-gather.5.cloned.1.call-start = ((), (), s32[]{:S(2)}) async-start(), calls=%async_computation.4 | async-start | bytes 2359296 | tf_op jit(solution)/shard_map/all_gather | solution.py:16
  7.9 158.5 %all-gather.3.cloned.1.call-start = ((), (), s32[]{:S(2)}) async-start(), calls=%async_computation.2 | async-start | bytes 1064960 | tf_op jit(solution)/shard_map/all_gather | solution.py:18
  8.6 555.9 %reduce-scatter.7.cloned.1.call-start = ((), (), s32[]{:S(2)}) async-start(), calls=%async_computation.5 | async-start | bytes 2129920
  9.4 5.0 collective-permute-start
  62.3 107.3 %copy-start = (bf16[512,2048]{1,0:T(8,128)(2,1)S(1)}, bf16[512,2048]{1,0:T(8,128)(2,1)}, u32[]{:S(2)}) copy-start(bf16[512,2048]{1,0:T(8,128)(2,1)} %all-gather.5.cloned.1.call-done) | copy-start | bytes 6291460
  62.3 593.6 %reduce-scatter.5.cloned.1.call-start = ((), (), s32[]{:S(2)}) async-start(), calls=%async_computation.3 | async-start | bytes 2359296 | tf_op jit(solution)/shard_map/reduce_scatter | solution.py:34
Sparse Core Ops, SparseCore 0:
  10.1 48.0 all-gather.4
  62.3 104.0 all-gather.2
  169.2 395.3 reduce-scatter.6
  568.1 87.7 reduce-scatter.4
where the time goes:
time: 664 us; the launch traced here: 662 us
  waiting for transfers between devices  432 us (65%)
  blocking collectives  201 us (30%)
  between operations  13.8 us (2%)
  matrix products  7.53 us (1%)
    psum x1, blocking collectives, body(): filter_grad = lax.psum(filter_local, 'dp')  201 us
    unnamed x5, waiting for transfers between devices  193 us
    all_gather x1, waiting for transfers between devices, body(): weight_cols = lax.all_gather(proj_weight, 'dp', axis=0, tiled=True)  104 us
    reduce_scatter x1, waiting for transfers between devices, body(): lax.psum_scatter(lax.dot_general(grad_bf, weight_cols, (((1,), (1,)), (()...  89.8 us
    all_gather x1, waiting for transfers between devices, body(): full_rows = lax.all_gather(tokens, 'seq', axis=0, tiled=True)  42.3 us
  transfers between devices with their start and end apart: 5, of which 5 were waited for; matrix products, arithmetic and copies ran while one was open for 2% of the time, Pallas kernels for 0%

commit v1 on v0

v1 whole, which is shorter than its diff:
```python
import jax
import jax.numpy as jnp
from jax import lax
from jax.sharding import Mesh, PartitionSpec as P

TAPS = 7
BF = jnp.bfloat16
F32 = jnp.float32
ZH, X, Y, ZL, C = "zh", "x", "y", "zl", "c"


def weight_columns(proj_weight):
    rows, cols = proj_weight.shape
    nz = lax.axis_size(ZH)
    nxy = lax.axis_size((X, Y))
    mine = lax.axis_index(ZH) == jnp.arange(nz)
    padded = jnp.where(mine[:, None, None], proj_weight[None], jnp.zeros((), BF))
    column = lax.psum(padded, ZH)
    repeated = jnp.broadcast_to(column[None], (nxy, nz, rows, cols))
    gathered = lax.all_to_all(repeated, (X, Y), split_axis=0, concat_axis=0, tiled=True)
    return gathered.transpose(1, 0, 2, 3).reshape(nz * nxy * rows, cols)


def body(tokens, proj_weight, cotangent, filters):
    nz = lax.axis_size(ZH)
    nxy = lax.axis_size((X, Y))
    nzl = lax.axis_size(ZL)
    ndp = nz * nxy
    rows, cols = proj_weight.shape
    own_tokens, depth = tokens.shape

    slab = lax.all_gather(tokens, (ZL, C), axis=0, tiled=True)
    slab_len = slab.shape[0]
    following = lax.ppermute(
        cotangent[: TAPS - 1], (ZH, X, Y), [(source, source - 1) for source in range(1, ndp)]
    )
    extended = jnp.concatenate([cotangent, following], 0).astype(F32)
    grad_feat = jnp.zeros((slab_len, cols), F32)
    for tap in range(TAPS):
        grad_feat = grad_feat + filters[tap] * extended[tap : tap + slab_len]
    grad_bf = grad_feat.astype(BF)

    weight = weight_columns(proj_weight)

    core = lax.axis_index(C)
    by_core = grad_bf.reshape(nzl, 2, own_tokens, cols)
    theirs = lax.dynamic_index_in_dim(by_core, 1 - core, 1, keepdims=False).reshape(-1, cols)
    ours = lax.dynamic_index_in_dim(by_core, core, 1, keepdims=False).reshape(-1, cols)
    contract_cols = (((1,), (1,)), ((), ()))
    for_other = lax.dot_general(theirs, weight, contract_cols, preferred_element_type=F32).astype(BF)
    from_other = lax.ppermute(for_other, C, [(0, 1), (1, 0)])
    here = lax.dot_general(ours, weight, contract_cols, preferred_element_type=F32)
    chip_sum = (here + from_other.astype(F32)).astype(BF)
    input_grad = lax.psum_scatter(chip_sum, ZL, scatter_dimension=0, tiled=True)

    partial = lax.dot_general(
        slab, grad_bf, (((0,), (0,)), ((), ())), preferred_element_type=F32
    ).astype(BF)
    partial = partial.reshape(nz, nxy, rows, cols).transpose(1, 0, 2, 3).reshape(nxy, nz * rows, cols)
    featured = jnp.dot(slab, weight, preferred_element_type=F32).astype(BF).astype(F32)
    taps = jnp.stack(
        [jnp.sum(featured * extended[tap : tap + slab_len], axis=0) for tap in range(TAPS)]
        + [jnp.zeros((cols,), F32)]
    )
    high = taps.astype(BF)
    low = (taps - high.astype(F32)).astype(BF)
    tail = jnp.broadcast_to(jnp.concatenate([high, low], 0)[None], (nxy, 16, cols))
    packed = jnp.concatenate([partial, tail], 1)
    arrived = lax.all_to_all(packed, (X, Y), split_axis=0, concat_axis=0, tiled=True)
    column_sum = jnp.sum(arrived.astype(F32), axis=0)
    body_rows = column_sum[: nz * rows]
    tap_rows = column_sum[nz * rows : nz * rows + 8] + column_sum[nz * rows + 8 :]
    total = lax.psum(jnp.concatenate([body_rows, tap_rows], 0), ZH)
    weight_grad = lax.dynamic_slice_in_dim(total, lax.axis_index(ZH) * rows, rows, 0).astype(BF)
    filter_grad = total[nz * rows : nz * rows + TAPS]
    return input_grad, weight_grad, filter_grad


def solution(mesh):
    fine = Mesh(mesh.devices.reshape(4, 4, 4, 4, 2), (ZH, X, Y, ZL, C))
    dp, seq = (ZH, X, Y), (ZL, C)
    in_specs = (P(dp + seq, None), P(dp, seq), P(dp, seq), P(None, seq))
    out_specs = (P(dp + seq, None), P(dp, seq), P(None, seq))
    return jax.shard_map(body, mesh=fine, in_specs=in_specs, out_specs=out_specs, check_vma=False)
```

time: 664 us -> 248 us (0.37)
  waiting for transfers between devices: 432 us -> 190 us
  blocking collectives: 201 us -> 0 us
  starting transfers between devices: 1.44 us -> 21.9 us
    psum x1 -> x0, blocking collectives: 201 us -> none  [body(): filter_grad = lax.psum(filter_local, 'dp')]
    unnamed x5 -> x4, waiting for transfers between devices: 193 us -> 0.57 us
    all_gather x2 -> x1, waiting for transfers between devices: 146 us -> 0.03 us  [body(): slab = lax.all_gather(tokens, (ZL, C), axis=0, tiled=True)]
    psum x0 -> x2, waiting for transfers between devices: none -> 136 us  [the longest x1 74.1 us: weight_columns(): column = lax.psum(padded, ZH)]
    reduce_scatter x1, waiting for transfers between devices: 89.8 us -> 36.5 us  [body(): input_grad = lax.psum_scatter(chip_sum, ZL, scatter_dimension=0, tiled=True)]
    all_to_all x0 -> x2, starting transfers between devices: none -> 14.2 us  [the longest x1 7.72 us: body(): lax.all_to_all(packed, (X, Y), split_axis=0, concat_axis=0, tiled=True)]
    all_to_all x0 -> x2, waiting for transfers between devices: none -> 12.5 us  [the longest x1 7.89 us: weight_columns(): lax.all_to_all(repeated, (X, Y), split_axis=0, concat_axis=0, tiled=True)]
  transfers between devices with their start and end apart: 5 -> 8, of which waited for: 5 -> 6; matrix products, arithmetic and copies ran while one was open for 2% -> 5% of each run, Pallas kernels for 0% -> 0%
where the time goes in v1:
time: 248 us
  waiting for transfers between devices  190 us (77%)
  starting transfers between devices  21.9 us (9%)
  between operations  15.4 us (6%)
  matrix products  9.7 us (4%)
  local copies, waits for them, and re-layouts  6.47 us (3%)
  other arithmetic  4.58 us (2%)
    psum x1, waiting for transfers between devices, weight_columns(): column = lax.psum(padded, ZH)  74.1 us
    psum x1, waiting for transfers between devices, body(): total = lax.psum(jnp.concatenate([body_rows, tap_rows], 0), ZH)  62.3 us
    reduce_scatter x1, waiting for transfers between devices, body(): input_grad = lax.psum_scatter(chip_sum, ZL, scatter_dimension=0, tiled=True)  36.5 us
    all_to_all x1, waiting for transfers between devices, weight_columns(): lax.all_to_all(repeated, (X, Y), split_axis=0, concat_axis=0, tiled=True)  7.89 us
    all_to_all x1, starting transfers between devices, body(): lax.all_to_all(packed, (X, Y), split_axis=0, concat_axis=0, tiled=True)  7.72 us
    all_to_all x1, starting transfers between devices, weight_columns(): lax.all_to_all(repeated, (X, Y), split_axis=0, concat_axis=0, tiled=True)  6.53 us
    ppermute x1, starting transfers between devices, body(): from_other = lax.ppermute(for_other, C, [(0, 1), (1, 0)])  6.19 us
  transfers between devices with their start and end apart: 8, of which 6 were waited for; matrix products, arithmetic and copies ran while one was open for 5% of the time, Pallas kernels for 0%

profile of v1, /device:TPU:1, one launch (start us, length us, event | category | flops | bytes accessed | tf_op | source)
XLA Modules:
  0.0 247.6 jit_solution(1912240180520042028)
XLA Ops:
  8.1 1.4 broadcast_select_fusion
  9.6 0.5 all-gather.2.cloned.1.call-update
  10.1 74.1 %all-reduce.3.cloned.1.call-done = bf16[4,32,256]{2,1,0:T(8,128)(2,1)} async-done(((bf16[4,32,256]{2,1,0:T(8,128)(2,1)}), bf16[4,32,256]{2,1,0:T(8,128)(2,1)}) %all-reduce.3.cloned.1.call-update) | async-done | bytes 65552 | tf_op jit(solution)/shard_map/psum | solution.py:18
  84.2 1.9 broadcast_in_dim.37
  86.2 6.5 %all-to-all-start = ((bf16[16,4,32,256]{3,2,1,0:T(8,128)(2,1)}), bf16[16,4,32,256]{3,2,1,0:T(8,128)(2,1)S(1)}, u32[]{:S(2)}, u32[]{:S(2)}) async-start(bf16[16,4,32,256]{3,2,1,0:T(8,128)(2,1)} %broadcast_in_dim.37), calls=%async_computation | async-start | bytes 2097152 | tf_op jit(solution)/shard_map/all_to_all | solution.py:20
  92.9 1.3 collective-permute-start
  94.4 3.5 %collective-permute-done = bf16[6,256]{0,1:T(8,128)(2,1)S(1)} collective-permute-done((bf16[6,256]{0,1:T(8,128)(2,1)S(1)}, bf16[6,256]{0,1:T(8,128)(2,1)S(1)}, u32[]{:S(2)}, u32[]{:S(2)}) %collective-permute-start) | collective-permute-done | bytes 3104 | tf_op jit(solution)/shard_map/ppermute | solution.py:34
  97.9 1.2 add_convert_fusion.1
  99.1 7.9 %all-to-all-done = bf16[16,4,32,256]{3,2,1,0:T(8,128)(2,1)S(1)} async-done(((bf16[16,4,32,256]{3,2,1,0:T(8,128)(2,1)}), bf16[16,4,32,256]{3,2,1,0:T(8,128)(2,1)S(1)}, u32[]{:S(2)}, u32[]{:S(2)}) %all-to-all-start) | async-done | bytes 1048608 | tf_op jit(solution)/shard_map/all_to_all | solution.py:20
  107.1 3.5 %multiply_reduce_fusion = (f32[256]{0:T(256)S(1)}, f32[256]{0:T(256)S(1)}, f32[256]{0:T(256)S(1)}, f32[256]{0:T(256)S(1)}, f32[256]{0:T(256)S(1)}, /*index=5*/f32[256]{0:T(256)S(1)}, f32[256]{0:T(256)S(1)}) fusion(f32[518,256]{0,1:T(8,128)S(1)} %maximum_convert_fusion, bf16[2048,256]{1,0:T(8,128)(2,1)S(1)} %bitcast.36, ...), kind=kOutput, calls=%fused_computation.9 | convolution fusion | flops 538966272 | bytes 6822912 | tf_op jit(solution)/shard_map/dot_general | solution.py:60
  110.7 2.3 fusion
  113.0 0.5 copy.18
  113.7 1.1 pad_maximum_fusion
  114.8 7.7 %all-to-all-start.1 = ((bf16[16,144,256]{2,1,0:T(8,128)(2,1)}), bf16[16,144,256]{2,1,0:T(8,128)(2,1)S(1)}, u32[]{:S(2)}, u32[]{:S(2)}) async-start(bf16[16,144,256]{2,1,0:T(8,128)(2,1)} %pad_maximum_fusion), calls=%async_computation.2 | async-start | bytes 2359296 | tf_op jit(solution)/shard_map/all_to_all | solution.py:69
  122.7 0.7 constant_dynamic-slice_fusion
  123.4 1.5 convolution_convert_fusion.1
  124.9 6.2 %collective-permute-start.1 = (bf16[256,2048]{1,0:T(8,128)(2,1)}, bf16[256,2048]{1,0:T(8,128)(2,1)S(1)}, u32[]{:S(2)}, u32[]{:S(2)}) collective-permute-start(bf16[256,2048]{1,0:T(8,128)(2,1)} %convolution_convert_fusion.1), channel_id=1, source_target_pairs={{0,1},{1,0},{2,3},{3,2},{4,5},{5,4},{6,7},{7,6},{8,9},{9,8},{10,11... | collective-permute-start | bytes 3145736 | tf_op jit(solution)/shard_map/ppermute | solution.py:51
  131.1 4.6 %all-to-all-done.1 = bf16[16,144,256]{2,1,0:T(8,128)(2,1)S(1)} async-done(((bf16[16,144,256]{2,1,0:T(8,128)(2,1)}), bf16[16,144,256]{2,1,0:T(8,128)(2,1)S(1)}, u32[]{:S(2)}, u32[]{:S(2)}) %all-to-all-start.1) | async-done | bytes 1179680 | tf_op jit(solution)/shard_map/all_to_all | solution.py:69
  135.9 0.7 pad_maximum_fusion.1
  136.7 2.4 add_convert_fusion
  139.0 62.3 %all-reduce.5.cloned.1.call-done = f32[136,256]{1,0:T(8,128)} async-done(((f32[136,256]{1,0:T(8,128)}), f32[136,256]{1,0:T(8,128)}) %all-reduce.5.cloned.1.call-update) | async-done | bytes 139280 | tf_op jit(solution)/shard_map/psum | solution.py:73
  201.3 1.3 slice.93
  202.6 1.4 dynamic-slice_convert_fusion
  204.0 36.5 %reduce-scatter.2.cloned.1.call-done = bf16[64,2048]{1,0:T(8,128)(2,1)} async-done(((bf16[256,2048]{1,0:T(8,128)(2,1)}), bf16[64,2048]{1,0:T(8,128)(2,1)}) %reduce-scatter.2.cloned.1.call-update) | async-done | bytes 262160 | tf_op jit(solution)/shard_map/reduce_scatter | solution.py:54
  (31 shorter events, 1.1 us)
Async XLA Ops:
  8.0 84.7 %slice-start = ((bf16[512,256]{1,0:T(8,128)(2,1)}), bf16[6,256]{1,0:T(8,128)(2,1)S(1)}, s32[]{:S(2)}) async-start(bf16[512,256]{1,0:T(8,128)(2,1)} %param.6), calls=%async_computation.7 | async-start | bytes 8192 | tf_op jit(solution)/shard_map/slice | solution.py:35
  8.0 86.2 %copy-start = (bf16[512,256]{1,0:T(8,128)(2,1)S(1)}, bf16[512,256]{1,0:T(8,128)(2,1)}, u32[]{:S(2)}) copy-start(bf16[512,256]{1,0:T(8,128)(2,1)} %param.6) | copy-start | bytes 786436
  8.0 86.2 %copy-start.1 = (f32[7,256]{1,0:T(8,128)S(1)}, f32[7,256]{1,0:T(8,128)}, u32[]{:S(2)}) copy-start(f32[7,256]{1,0:T(8,128)} %param.7) | copy-start | bytes 21508
  8.0 76.2 %all-reduce.3.cloned.1.call-start = ((), (), s32[]{:S(2)}) async-start(), calls=%async_computation.3 | async-start | bytes 131072 | tf_op jit(solution)/shard_map/psum | solution.py:18
  9.5 97.6 %all-gather.2.cloned.1.call-start = ((), (), s32[]{:S(2)}) async-start(), calls=%async_computation.5 | async-start | bytes 2359296 | tf_op jit(solution)/shard_map/all_gather | solution.py:32
  86.2 20.8 %all-to-all-start = ((bf16[16,4,32,256]{3,2,1,0:T(8,128)(2,1)}), bf16[16,4,32,256]{3,2,1,0:T(8,128)(2,1)S(1)}, u32[]{:S(2)}, u32[]{:S(2)}) async-start(bf16[16,4,32,256]{3,2,1,0:T(8,128)(2,1)} %broadcast_in_dim.37), calls=%async_computation | async-start | bytes 2097152 | tf_op jit(solution)/shard_map/all_to_all | solution.py:20
  92.9 5.0 %collective-permute-start = (bf16[6,256]{0,1:T(8,128)(2,1)S(1)}, bf16[6,256]{0,1:T(8,128)(2,1)S(1)}, u32[]{:S(2)}, u32[]{:S(2)}) collective-permute-start(bf16[6,256]{0,1:T(8,128)(2,1)S(1)} %copy.14), channel_id=1, source_target_pairs={{8,0},{16,8},{24,16},{32,24},{40,32},{48,40},{56,48},{64,56},{72,6... | collective-permute-start | bytes 9224 | tf_op jit(solution)/shard_map/ppermute | solution.py:34
  114.8 20.9 %all-to-all-start.1 = ((bf16[16,144,256]{2,1,0:T(8,128)(2,1)}), bf16[16,144,256]{2,1,0:T(8,128)(2,1)S(1)}, u32[]{:S(2)}, u32[]{:S(2)}) async-start(bf16[16,144,256]{2,1,0:T(8,128)(2,1)} %pad_maximum_fusion), calls=%async_computation.2 | async-start | bytes 2359296 | tf_op jit(solution)/shard_map/all_to_all | solution.py:69
  122.5 78.8 %all-reduce.5.cloned.1.call-start = ((), (), s32[]{:S(2)}) async-start(), calls=%async_computation.6 | async-start | bytes 278528 | tf_op jit(solution)/shard_map/psum | solution.py:73
  124.9 11.8 %collective-permute-start.1 = (bf16[256,2048]{1,0:T(8,128)(2,1)}, bf16[256,2048]{1,0:T(8,128)(2,1)S(1)}, u32[]{:S(2)}, u32[]{:S(2)}) collective-permute-start(bf16[256,2048]{1,0:T(8,128)(2,1)} %convolution_convert_fusion.1), channel_id=1, source_target_pairs={{0,1},{1,0},{2,3},{3,2},{4,5},{5,4},{6,7},{7,6},{8,9},{9,8},{10,11... | collective-permute-start | bytes 3145736 | tf_op jit(solution)/shard_map/ppermute | solution.py:51
  136.6 103.9 %reduce-scatter.2.cloned.1.call-start = ((), (), s32[]{:S(2)}) async-start(), calls=%async_computation.4 | async-start | bytes 1310720 | tf_op jit(solution)/shard_map/reduce_scatter | solution.py:54
Sparse Core Ops, SparseCore 0:
  12.3 71.8 all-reduce.2
  136.7 64.5 all-reduce.4
  204.8 35.6 reduce-scatter.1
Sparse Core Ops, SparseCore 1:
  12.3 48.9 all-gather.1

commit v2 on v1

--- a/solution.py
+++ b/solution.py
@@ -9,13 +9,21 @@
 ZH, X, Y, ZL, C = "zh", "x", "y", "zl", "c"
 
 
+def split_rows(value):
+    high = value.astype(BF)
+    return jnp.concatenate([high, (value - high.astype(F32)).astype(BF)], 0)
+
+
+def joined_rows(value):
+    half = value.shape[0] // 2
+    return value[:half] + value[half:]
+
+
 def weight_columns(proj_weight):
     rows, cols = proj_weight.shape
     nz = lax.axis_size(ZH)
     nxy = lax.axis_size((X, Y))
-    mine = lax.axis_index(ZH) == jnp.arange(nz)
-    padded = jnp.where(mine[:, None, None], proj_weight[None], jnp.zeros((), BF))
-    column = lax.psum(padded, ZH)
+    column = lax.all_gather(proj_weight, ZH)
     repeated = jnp.broadcast_to(column[None], (nxy, nz, rows, cols))
     gathered = lax.all_to_all(repeated, (X, Y), split_axis=0, concat_axis=0, tiled=True)
     return gathered.transpose(1, 0, 2, 3).reshape(nz * nxy * rows, cols)
@@ -62,17 +70,17 @@
         [jnp.sum(featured * extended[tap : tap + slab_len], axis=0) for tap in range(TAPS)]
         + [jnp.zeros((cols,), F32)]
     )
-    high = taps.astype(BF)
-    low = (taps - high.astype(F32)).astype(BF)
-    tail = jnp.broadcast_to(jnp.concatenate([high, low], 0)[None], (nxy, 16, cols))
+    tail = jnp.broadcast_to(split_rows(taps)[None], (nxy, 16, cols))
     packed = jnp.concatenate([partial, tail], 1)
     arrived = lax.all_to_all(packed, (X, Y), split_axis=0, concat_axis=0, tiled=True)
     column_sum = jnp.sum(arrived.astype(F32), axis=0)
-    body_rows = column_sum[: nz * rows]
-    tap_rows = column_sum[nz * rows : nz * rows + 8] + column_sum[nz * rows + 8 :]
-    total = lax.psum(jnp.concatenate([body_rows, tap_rows], 0), ZH)
-    weight_grad = lax.dynamic_slice_in_dim(total, lax.axis_index(ZH) * rows, rows, 0).astype(BF)
-    filter_grad = total[nz * rows : nz * rows + TAPS]
+    blocks = column_sum[: nz * rows].astype(BF).reshape(nz, rows, cols)
+    tail = jnp.broadcast_to(split_rows(joined_rows(column_sum[nz * rows :]))[None], (nz, 16, cols))
+    packed = jnp.concatenate([blocks, tail], 1)
+    arrived = lax.all_to_all(packed, ZH, split_axis=0, concat_axis=0, tiled=True)
+    total = jnp.sum(arrived.astype(F32), axis=0)
+    weight_grad = total[:rows].astype(BF)
+    filter_grad = joined_rows(total[rows:])[:TAPS]
     return input_grad, weight_grad, filter_grad
 
 

time: 248 us -> 128 us (0.52)
  waiting for transfers between devices: 190 us -> 33.6 us
  blocking collectives: 0 us -> 41.2 us
    psum x2 -> x0, waiting for transfers between devices: 136 us -> none  [the longest x1 74.1 us: weight_columns(): column = lax.psum(padded, ZH)]
    reduce_scatter x1, waiting for transfers between devices: 36.5 us -> 6.53 us  [body(): input_grad = lax.psum_scatter(chip_sum, ZL, scatter_dimension=0, tiled=True)]
    all_gather x0 -> x1, blocking collectives: none -> 23.9 us  [weight_columns(): column = lax.all_gather(proj_weight, ZH)]
    all_to_all x0 -> x1, blocking collectives: none -> 17.4 us  [body(): lax.all_to_all(packed, ZH, split_axis=0, concat_axis=0, tiled=True)]
    all_to_all x1, waiting for transfers between devices: 4.64 us -> 15.9 us  [body(): lax.all_to_all(packed, (X, Y), split_axis=0, concat_axis=0, tiled=True)]
    dot_general x1, matrix products: 3.53 us -> 1.03 us  [body(): jnp.dot(slab, weight, preferred_element_type=F32).astype(BF).astype(F32)]
  transfers between devices with their start and end apart: 8 -> 6, of which waited for: 6 -> 4; matrix products, arithmetic and copies ran while one was open for 5% -> 11% of each run, Pallas kernels for 0% -> 0%
where the time goes in v2:
time: 128 us
  blocking collectives  41.2 us (32%)
  waiting for transfers between devices  33.6 us (26%)
  starting transfers between devices  22.3 us (17%)
  between operations  15.7 us (12%)
  matrix products  7.5 us (6%)
  local copies, waits for them, and re-layouts  5.14 us (4%)
  other arithmetic  2.37 us (2%)
    all_gather x1, blocking collectives, weight_columns(): column = lax.all_gather(proj_weight, ZH)  23.9 us
    all_to_all x1, blocking collectives, body(): lax.all_to_all(packed, ZH, split_axis=0, concat_axis=0, tiled=True)  17.4 us
    all_to_all x1, waiting for transfers between devices, body(): lax.all_to_all(packed, (X, Y), split_axis=0, concat_axis=0, tiled=True)  15.9 us
    ppermute x1, starting transfers between devices, body(): from_other = lax.ppermute(for_other, C, [(0, 1), (1, 0)])  7.65 us
    all_to_all x1, waiting for transfers between devices, weight_columns(): lax.all_to_all(repeated, (X, Y), split_axis=0, concat_axis=0, tiled=True)  7.02 us
    all_to_all x1, starting transfers between devices, weight_columns(): lax.all_to_all(repeated, (X, Y), split_axis=0, concat_axis=0, tiled=True)  6.75 us
    reduce_scatter x1, waiting for transfers between devices, body(): input_grad = lax.psum_scatter(chip_sum, ZL, scatter_dimension=0, tiled=True)  6.53 us
    all_to_all x1, starting transfers between devices, body(): lax.all_to_all(packed, (X, Y), split_axis=0, concat_axis=0, tiled=True)  6.5 us
  transfers between devices with their start and end apart: 6, of which 4 were waited for; matrix products, arithmetic and copies ran while one was open for 11% of the time, Pallas kernels for 0%

profile of v2, /device:TPU:1, one launch (start us, length us, event | category | flops | bytes accessed | tf_op | source)
XLA Modules:
  0.0 127.8 jit_solution(16946467029009056463)
XLA Ops:
  8.1 0.7 all-gather.3.cloned.1.call-update
  8.8 23.9 %all-gather = bf16[128,256]{1,0:T(8,128)(2,1)S(1)} all-gather(bf16[32,256]{1,0:T(8,128)(2,1)} %param.5), channel_id=2, replica_groups=mesh['zh'=4,'x'=4,'y'=4,'zl'=4,'c'=2] {'zh'}, dimensions={0}, use_global_device_ids=true | all-gather | bytes 81920 | tf_op jit(solution)/shard_map/all_gather | solution.py:26
  32.6 1.1 broadcast_in_dim.6
  33.7 6.8 %all-to-all-start = ((bf16[16,4,32,256]{3,2,1,0:T(8,128)(2,1)}), bf16[16,4,32,256]{3,2,1,0:T(8,128)(2,1)S(1)}, u32[]{:S(2)}, u32[]{:S(2)}) async-start(bf16[16,4,32,256]{3,2,1,0:T(8,128)(2,1)} %broadcast_in_dim.6), calls=%async_computation | async-start | bytes 2097152 | tf_op jit(solution)/shard_map/all_to_all | solution.py:28
  40.5 1.3 %collective-permute-start = (bf16[6,256]{1,0:T(8,128)(2,1)S(1)}, bf16[6,256]{1,0:T(8,128)(2,1)S(1)}, u32[]{:S(2)}, u32[]{:S(2)}) collective-permute-start(bf16[6,256]{1,0:T(8,128)(2,1)S(1)} %slice.82), channel_id=1, source_target_pairs={{8,0},{16,8},{24,16},{32,24},{40,32},{48,40},{56,48},{64,56},{72,6... | collective-permute-start | bytes 9224 | tf_op jit(solution)/shard_map/ppermute | solution.py:42
  41.8 3.4 %collective-permute-done = bf16[6,256]{1,0:T(8,128)(2,1)S(1)} collective-permute-done((bf16[6,256]{1,0:T(8,128)(2,1)S(1)}, bf16[6,256]{1,0:T(8,128)(2,1)S(1)}, u32[]{:S(2)}, u32[]{:S(2)}) %collective-permute-start) | collective-permute-done | bytes 3104 | tf_op jit(solution)/shard_map/ppermute | solution.py:42
  45.3 0.4 add_convert_fusion.1
  45.8 7.0 %all-to-all-done = bf16[16,4,32,256]{3,2,1,0:T(8,128)(2,1)S(1)} async-done(((bf16[16,4,32,256]{3,2,1,0:T(8,128)(2,1)}), bf16[16,4,32,256]{3,2,1,0:T(8,128)(2,1)S(1)}, u32[]{:S(2)}, u32[]{:S(2)}) %all-to-all-start) | async-done | bytes 1048608 | tf_op jit(solution)/shard_map/all_to_all | solution.py:28
  52.9 1.5 %convolution_convert_fusion.1 = bf16[256,2048]{1,0:T(8,128)(2,1)} fusion(bf16[256,256]{1,0:T(8,128)(2,1)S(1)} %bitcast.43, bf16[2048,256]{1,0:T(8,128)(2,1)S(1)} %bitcast.36), kind=kOutput, calls=%fused_computation.1 | convolution fusion | flops 268959744 | bytes 2228224 | tf_op jit(solution)/shard_map/dot_general | solution.py:58
  54.4 7.6 %collective-permute-start.1 = (bf16[256,2048]{1,0:T(8,128)(2,1)}, bf16[256,2048]{1,0:T(8,128)(2,1)}, u32[]{:S(2)}, u32[]{:S(2)}) collective-permute-start(bf16[256,2048]{1,0:T(8,128)(2,1)} %convolution_convert_fusion.1), channel_id=1, source_target_pairs={{0,1},{1,0},{2,3},{3,2},{4,5},{5,4},{6,7},{7,6},{8,9},{9,8},{10,11... | collective-permute-start | bytes 3145736 | tf_op jit(solution)/shard_map/ppermute | solution.py:59
  62.0 2.3 %fusion = bf16[2048,256]{0,1:T(8,128)(2,1)S(1)} fusion(bf16[512,256]{1,0:T(8,128)(2,1)S(1)} %add_convert_fusion.1, bf16[512,2048]{1,0:T(8,128)(2,1)} %all-gather.3.cloned.1.call-done), kind=kOutput, calls=%fused_computation.2 | convolution fusion | flops 537395200 | bytes 3407872 | tf_op jit(solution)/shard_map/dot_general | solution.py:64
  64.4 1.3 %copy.13 = bf16[2048,256]{1,0:T(8,128)(2,1)} copy(bf16[2048,256]{0,1:T(8,128)(2,1)S(1)} %fusion) | data formatting | bytes 2097152 | tf_op jit(solution)/shard_map/convert_element_type | solution.py:66
  65.7 1.5 %copy.14 = bf16[16,4,32,256]{3,2,1,0:T(8,128)(2,1)S(1)} copy(bf16[16,4,32,256]{3,2,0,1:T(8,128)(2,1)} %bitcast.40) | data formatting | bytes 2097152 | tf_op jit(solution)/shard_map/transpose | solution.py:67
  67.2 0.4 copy-done
  67.6 1.0 fusion.7
  68.7 1.1 pad_maximum_fusion
  69.8 6.5 %all-to-all-start.1 = ((bf16[16,144,256]{2,1,0:T(8,128)(2,1)}), bf16[16,144,256]{2,1,0:T(8,128)(2,1)S(1)}, u32[]{:S(2)}, u32[]{:S(2)}) async-start(bf16[16,144,256]{2,1,0:T(8,128)(2,1)} %pad_maximum_fusion), calls=%async_computation.2 | async-start | bytes 2359296 | tf_op jit(solution)/shard_map/all_to_all | solution.py:75
  76.4 2.7 %add_convert_fusion = bf16[256,2048]{1,0:T(8,128)(2,1)} fusion(bf16[256,2048]{1,0:T(8,128)(2,1)} %collective-permute-done.1, bf16[256,256]{1,0:T(8,128)(2,1)S(1)} %bitcast.42, bf16[2048,256]{1,0:T(8,128)(2,1)S(1)} %bitcast.38), kind=kOutput, calls=%fused_computation.4 | convolution fusion | flops 270008320 | bytes 3276800 | tf_op jit(solution)/shard_map/dot_general | solution.py:60
  79.1 15.9 %all-to-all-done.1 = bf16[16,144,256]{2,1,0:T(8,128)(2,1)S(1)} async-done(((bf16[16,144,256]{2,1,0:T(8,128)(2,1)}), bf16[16,144,256]{2,1,0:T(8,128)(2,1)S(1)}, u32[]{:S(2)}, u32[]{:S(2)}) %all-to-all-start.1) | async-done | bytes 1179680 | tf_op jit(solution)/shard_map/all_to_all | solution.py:75
  95.0 0.2 convert_reduce_fusion
  95.3 17.4 %all_to_all.15 = bf16[4,48,256]{2,1,0:T(8,128)(2,1)S(1)} all-to-all(bf16[4,48,256]{2,1,0:T(8,128)(2,1)S(1)} %pad_maximum_fusion.1), channel_id=1, replica_groups=mesh['zh'=4,'x'=4,'y'=4,'zl'=4,'c'=2] {'zh'}, dimensions={0} | all-to-all | bytes 196608 | tf_op jit(solution)/shard_map/all_to_all | solution.py:80
  112.6 0.6 slice.147
  113.3 0.6 slice_add_fusion
  113.9 6.5 %reduce-scatter.2.cloned.1.call-done = bf16[64,2048]{1,0:T(8,128)(2,1)} async-done(((bf16[256,2048]{1,0:T(8,128)(2,1)}), bf16[64,2048]{1,0:T(8,128)(2,1)}) %reduce-scatter.2.cloned.1.call-update) | async-done | bytes 262160 | tf_op jit(solution)/shard_map/reduce_scatter | solution.py:62
  (27 shorter events, 0.4 us)
Async XLA Ops:
  8.0 32.5 %copy-start.1 = (bf16[512,256]{1,0:T(8,128)(2,1)S(1)}, bf16[512,256]{1,0:T(8,128)(2,1)}, u32[]{:S(2)}) copy-start(bf16[512,256]{1,0:T(8,128)(2,1)} %param.6) | copy-start | bytes 786436
  8.0 33.8 %copy-start.2 = (f32[7,256]{1,0:T(8,128)S(1)}, f32[7,256]{1,0:T(8,128)}, u32[]{:S(2)}) copy-start(f32[7,256]{1,0:T(8,128)} %param.7) | copy-start | bytes 21508
  8.0 54.0 %all-gather.3.cloned.1.call-start = ((), (), s32[]{:S(2)}) async-start(), calls=%async_computation.5 | async-start | bytes 2359296 | tf_op jit(solution)/shard_map/all_gather | solution.py:40
  33.7 19.1 %all-to-all-start = ((bf16[16,4,32,256]{3,2,1,0:T(8,128)(2,1)}), bf16[16,4,32,256]{3,2,1,0:T(8,128)(2,1)S(1)}, u32[]{:S(2)}, u32[]{:S(2)}) async-start(bf16[16,4,32,256]{3,2,1,0:T(8,128)(2,1)} %broadcast_in_dim.6), calls=%async_computation | async-start | bytes 2097152 | tf_op jit(solution)/shard_map/all_to_all | solution.py:28
  40.5 4.8 %collective-permute-start = (bf16[6,256]{1,0:T(8,128)(2,1)S(1)}, bf16[6,256]{1,0:T(8,128)(2,1)S(1)}, u32[]{:S(2)}, u32[]{:S(2)}) collective-permute-start(bf16[6,256]{1,0:T(8,128)(2,1)S(1)} %slice.82), channel_id=1, source_target_pairs={{8,0},{16,8},{24,16},{32,24},{40,32},{48,40},{56,48},{64,56},{72,6... | collective-permute-start | bytes 9224 | tf_op jit(solution)/shard_map/ppermute | solution.py:42
  54.4 22.0 %collective-permute-start.1 = (bf16[256,2048]{1,0:T(8,128)(2,1)}, bf16[256,2048]{1,0:T(8,128)(2,1)}, u32[]{:S(2)}, u32[]{:S(2)}) collective-permute-start(bf16[256,2048]{1,0:T(8,128)(2,1)} %convolution_convert_fusion.1), channel_id=1, source_target_pairs={{0,1},{1,0},{2,3},{3,2},{4,5},{5,4},{6,7},{7,6},{8,9},{9,8},{10,11... | collective-permute-start | bytes 3145736 | tf_op jit(solution)/shard_map/ppermute | solution.py:59
  65.7 1.9 %copy-start = (bf16[512,2048]{1,0:T(8,128)(2,1)S(1)}, bf16[512,2048]{1,0:T(8,128)(2,1)}, u32[]{:S(2)}) copy-start(bf16[512,2048]{1,0:T(8,128)(2,1)} %all-gather.3.cloned.1.call-done) | copy-start | bytes 6291460
  69.8 25.2 %all-to-all-start.1 = ((bf16[16,144,256]{2,1,0:T(8,128)(2,1)}), bf16[16,144,256]{2,1,0:T(8,128)(2,1)S(1)}, u32[]{:S(2)}, u32[]{:S(2)}) async-start(bf16[16,144,256]{2,1,0:T(8,128)(2,1)} %pad_maximum_fusion), calls=%async_computation.2 | async-start | bytes 2359296 | tf_op jit(solution)/shard_map/all_to_all | solution.py:75
  76.3 44.1 %reduce-scatter.2.cloned.1.call-start = ((), (), s32[]{:S(2)}) async-start(), calls=%async_computation.4 | async-start | bytes 1310720 | tf_op jit(solution)/shard_map/reduce_scatter | solution.py:62
Sparse Core Ops, SparseCore 0:
  11.1 48.1 all-gather.2
Sparse Core Ops, SparseCore 1:
  80.2 40.1 reduce-scatter.1

commit v3 on v2

v3 whole, which is shorter than its diff:
```python
import jax
import jax.numpy as jnp
from jax import lax
from jax.sharding import Mesh, PartitionSpec as P

TAPS = 7
BF = jnp.bfloat16
F32 = jnp.float32
ZH, X, Y, ZL, C = "zh", "x", "y", "zl", "c"


def split_rows(value):
    high = value.astype(BF)
    return jnp.concatenate([high, (value - high.astype(F32)).astype(BF)], 0)


def joined_rows(value):
    half = value.shape[0] // 2
    return value[:half] + value[half:]


def exchange(value, axes):
    return lax.all_to_all(value, axes, split_axis=0, concat_axis=0, tiled=True)


def spread(value, axes):
    count = lax.axis_size(axes)
    return exchange(jnp.broadcast_to(value[None], (count,) + value.shape), axes)


def from_ahead(value, axis, steps):
    count = lax.axis_size(axis)
    return lax.ppermute(value, axis, [(source, (source - steps) % count) for source in range(count)])


def swap(value):
    return lax.ppermute(value, C, [(0, 1), (1, 0)])


def rolled(value, start):
    return lax.dynamic_slice_in_dim(jnp.concatenate([value, value], 0), start, value.shape[0], 0)


def body(tokens, proj_weight, cotangent, filters):
    nz = lax.axis_size(ZH)
    nxy = lax.axis_size((X, Y))
    nzl = lax.axis_size(ZL)
    ndp = nz * nxy
    rows, cols = proj_weight.shape
    own_tokens, depth = tokens.shape
    slab_len = cotangent.shape[0]
    core, chip = lax.axis_index(C), lax.axis_index(ZL)
    chip_tokens = 2 * own_tokens

    direct = [tokens] + [None] * (nzl - 1)
    for steps in (2, 1, 3):
        direct[steps] = from_ahead(tokens, ZL, steps)
    column = spread(proj_weight, ZH)
    following = lax.ppermute(
        cotangent[: TAPS - 1], (ZH, X, Y), [(source, source - 1) for source in range(1, ndp)]
    )
    crossed = [swap(value) for value in direct]
    parts = []
    for mine, other in zip(direct, crossed):
        parts += [jnp.where(core == 0, mine, other), jnp.where(core == 0, other, mine)]
    slab = jnp.concatenate(parts, 0)

    extended = jnp.concatenate([cotangent, following], 0).astype(F32)
    grad_feat = jnp.zeros((slab_len, cols), F32)
    for tap in range(TAPS):
        grad_feat = grad_feat + filters[tap] * extended[tap : tap + slab_len]
    grad_bf = grad_feat.astype(BF)

    gathered = spread(column.reshape(nz * rows, cols), (X, Y))
    weight = gathered.reshape(nxy, nz, rows, cols).transpose(1, 0, 2, 3).reshape(depth, cols)

    partial = lax.dot_general(
        slab, rolled(grad_bf, chip * chip_tokens), (((0,), (0,)), ((), ())), preferred_element_type=F32
    ).astype(BF)
    partial = partial.reshape(nz, nxy, rows, cols).transpose(1, 0, 2, 3).reshape(nxy, nz * rows, cols)
    arrived = exchange(partial, (X, Y))
    blocks = jnp.sum(arrived.astype(F32), axis=0).astype(BF).reshape(nz, rows, cols)

    by_core = grad_bf.reshape(nzl, 2, own_tokens, cols)
    theirs = lax.dynamic_index_in_dim(by_core, 1 - core, 1, keepdims=False).reshape(-1, cols)
    ours = lax.dynamic_index_in_dim(by_core, core, 1, keepdims=False).reshape(-1, cols)
    contract_cols = (((1,), (1,)), ((), ()))
    for_other = lax.dot_general(theirs, weight, contract_cols, preferred_element_type=F32).astype(BF)
    from_other = swap(for_other)
    here = lax.dot_general(ours, weight, contract_cols, preferred_element_type=F32)
    chip_sum = (here + from_other.astype(F32)).astype(BF).reshape(nzl, own_tokens, depth)
    total = lax.dynamic_index_in_dim(chip_sum, chip, 0, keepdims=False).astype(F32)
    for steps in (2, 1, 3):
        outgoing = lax.dynamic_index_in_dim(chip_sum, (chip - steps) % nzl, 0, keepdims=False)
        total = total + from_ahead(outgoing, ZL, steps).astype(F32)
    input_grad = total.astype(BF)

    featured = jnp.dot(slab, weight, preferred_element_type=F32).astype(BF)
    featured = rolled(featured, (nzl - chip) * chip_tokens).astype(F32)
    taps = jnp.stack(
        [jnp.sum(featured * extended[tap : tap + slab_len], axis=0) for tap in range(TAPS)]
        + [jnp.zeros((cols,), F32)]
    )
    taps = joined_rows(jnp.sum(spread(split_rows(taps), (X, Y)).reshape(nxy, 16, cols).astype(F32), axis=0))

    tail = jnp.broadcast_to(split_rows(taps)[None], (nz, 16, cols))
    arrived = exchange(jnp.concatenate([blocks, tail], 1), ZH)
    summed = jnp.sum(arrived.astype(F32), axis=0)
    weight_grad = summed[:rows].astype(BF)
    filter_grad = joined_rows(summed[rows:])[:TAPS]
    return input_grad, weight_grad, filter_grad


def solution(mesh):
    fine = Mesh(mesh.devices.reshape(4, 4, 4, 4, 2), (ZH, X, Y, ZL, C))
    dp, seq = (ZH, X, Y), (ZL, C)
    in_specs = (P(dp + seq, None), P(dp, seq), P(dp, seq), P(None, seq))
    out_specs = (P(dp + seq, None), P(dp, seq), P(None, seq))
    return jax.shard_map(body, mesh=fine, in_specs=in_specs, out_specs=out_specs, check_vma=False)
```

time: 128 us -> 157 us (1.23)
  the two profiles are of different devices: /device:TPU:1 before, /device:TPU:32 now
where the time goes in v3:
time: 157 us; the launch traced here: 155 us
  starting transfers between devices  70.2 us (45%)
  waiting for transfers between devices  58.6 us (37%)
  other arithmetic  10.7 us (7%)
  matrix products  8.22 us (5%)
  local copies, waits for them, and re-layouts  6.67 us (4%)
    all_to_all x5, waiting for transfers between devices, exchange(): return lax.all_to_all(value, axes, split_axis=0, concat_axis=0, tiled=True)  43 us
    all_to_all x5, starting transfers between devices, exchange(): return lax.all_to_all(value, axes, split_axis=0, concat_axis=0, tiled=True)  36.9 us
    ppermute x6, starting transfers between devices, from_ahead(): lax.ppermute(value, axis, [(source, (source - steps) % count) for source...  22 us
    ppermute x6, waiting for transfers between devices, from_ahead(): lax.ppermute(value, axis, [(source, (source - steps) % count) for source...  12.3 us
    ppermute x5, starting transfers between devices, swap(): return lax.ppermute(value, C, [(0, 1), (1, 0)])  10.1 us
    unnamed x7, other arithmetic  5.38 us
    ppermute x1, waiting for transfers between devices, body(): lax.ppermute(cotangent[:TAPS - 1], (ZH, X, Y), [(source, source - 1) for...  3.22 us
  transfers between devices with their start and end apart: 17, of which 8 were waited for; matrix products, arithmetic and copies ran while one was open for 12% of the time, Pallas kernels for 0%

profile of v3, /device:TPU:32, one launch (start us, length us, event | category | flops | bytes accessed | tf_op | source)
XLA Modules:
  0.0 155.4 jit_solution(3354862517025109735)
XLA Ops:
  0.6 1.9 %collective-permute-start.5 = (bf16[64,2048]{1,0:T(8,128)(2,1)}, bf16[64,2048]{1,0:T(8,128)(2,1)S(1)}, u32[]{:S(2)}, u32[]{:S(2)}) collective-permute-start(bf16[64,2048]{1,0:T(8,128)(2,1)} %param.4), channel_id=1, source_target_pairs={{0,1},{1,0},{2,3},{3,2},{4,5},{5,4},{6,7},{7,6},{8,9},{9,8},{10,11... | collective-permute-start | bytes 786440 | tf_op jit(solution)/shard_map/ppermute | solution.py:37
  2.6 7.4 %collective-permute-start.6 = (bf16[64,2048]{1,0:T(8,128)(2,1)}, bf16[64,2048]{1,0:T(8,128)(2,1)S(1)}, u32[]{:S(2)}, u32[]{:S(2)}) collective-permute-start(bf16[64,2048]{1,0:T(8,128)(2,1)} %param.4), channel_id=1, source_target_pairs={{0,6},{2,0},{4,2},{6,4},{1,7},{3,1},{5,3},{7,5},{8,14},{10,8},{12,... | collective-permute-start | bytes 786440 | tf_op jit(solution)/shard_map/ppermute | solution.py:33
  10.0 1.9 %collective-permute-start.8 = (bf16[64,2048]{1,0:T(8,128)(2,1)}, bf16[64,2048]{1,0:T(8,128)(2,1)S(1)}, u32[]{:S(2)}, u32[]{:S(2)}) collective-permute-start(bf16[64,2048]{1,0:T(8,128)(2,1)} %param.4), channel_id=1, source_target_pairs={{0,4},{2,6},{4,0},{6,2},{1,5},{3,7},{5,1},{7,3},{8,12},{10,14},{12... | collective-permute-start | bytes 786440 | tf_op jit(solution)/shard_map/ppermute | solution.py:33
  11.9 3.4 %collective-permute-start.10 = (bf16[64,2048]{1,0:T(8,128)(2,1)}, bf16[64,2048]{1,0:T(8,128)(2,1)S(1)}, u32[]{:S(2)}, u32[]{:S(2)}) collective-permute-start(bf16[64,2048]{1,0:T(8,128)(2,1)} %param.4), channel_id=1, source_target_pairs={{0,2},{2,4},{4,6},{6,0},{1,3},{3,5},{5,7},{7,1},{8,10},{10,12},{12... | collective-permute-start | bytes 786440 | tf_op jit(solution)/shard_map/ppermute | solution.py:33
  16.6 11.6 %all-to-all-start = ((bf16[4,32,256]{2,1,0:T(8,128)(2,1)}), bf16[4,32,256]{2,1,0:T(8,128)(2,1)S(1)}, u32[]{:S(2)}, u32[]{:S(2)}) async-start(bf16[4,32,256]{2,1,0:T(8,128)(2,1)} %broadcast_in_dim.10), calls=%async_computation | async-start | bytes 131072 | tf_op jit(solution)/shard_map/all_to_all | solution.py:23
  31.2 3.2 %collective-permute-done = bf16[6,256]{1,0:T(8,128)(2,1)S(1)} collective-permute-done((bf16[6,256]{1,0:T(8,128)(2,1)S(1)}, bf16[6,256]{1,0:T(8,128)(2,1)S(1)}, u32[]{:S(2)}, u32[]{:S(2)}) %collective-permute-start) | collective-permute-done | bytes 3104 | tf_op jit(solution)/shard_map/ppermute | solution.py:59
  35.9 9.2 %all-to-all-done = bf16[4,32,256]{2,1,0:T(8,128)(2,1)S(1)} async-done(((bf16[4,32,256]{2,1,0:T(8,128)(2,1)}), bf16[4,32,256]{2,1,0:T(8,128)(2,1)S(1)}, u32[]{:S(2)}, u32[]{:S(2)}) %all-to-all-start) | async-done | bytes 65568 | tf_op jit(solution)/shard_map/all_to_all | solution.py:23
  46.2 7.0 %all-to-all-start.1 = ((bf16[16,128,256]{2,1,0:T(8,128)(2,1)}), bf16[16,128,256]{2,1,0:T(8,128)(2,1)S(1)}, u32[]{:S(2)}, u32[]{:S(2)}) async-start(bf16[16,128,256]{2,1,0:T(8,128)(2,1)} %broadcast_in_dim.12), calls=%async_computation.1 | async-start | bytes 2097152 | tf_op jit(solution)/shard_map/all_to_all | solution.py:23
  53.2 1.9 %collective-permute-start.7 = (bf16[64,2048]{1,0:T(8,128)(2,1)S(1)}, bf16[64,2048]{1,0:T(8,128)(2,1)S(1)}, u32[]{:S(2)}, u32[]{:S(2)}) collective-permute-start(bf16[64,2048]{1,0:T(8,128)(2,1)S(1)} %collective-permute-done.6), channel_id=1, source_target_pairs={{0,1},{1,0},{2,3},{3,2},{4,5},{5,4},{6,7},{7,6},{8,9},{9,8},{10,11... | collective-permute-start | bytes 786440 | tf_op jit(solution)/shard_map/ppermute | solution.py:37
  55.2 2.4 %collective-permute-start.9 = (bf16[64,2048]{1,0:T(8,128)(2,1)S(1)}, bf16[64,2048]{1,0:T(8,128)(2,1)S(1)}, u32[]{:S(2)}, u32[]{:S(2)}) collective-permute-start(bf16[64,2048]{1,0:T(8,128)(2,1)S(1)} %collective-permute-done.8), channel_id=1, source_target_pairs={{0,1},{1,0},{2,3},{3,2},{4,5},{5,4},{6,7},{7,6},{8,9},{9,8},{10,11... | collective-permute-start | bytes 786440 | tf_op jit(solution)/shard_map/ppermute | solution.py:37
  65.7 3.1 %all-to-all-done.1 = bf16[16,128,256]{2,1,0:T(8,128)(2,1)S(1)} async-done(((bf16[16,128,256]{2,1,0:T(8,128)(2,1)}), bf16[16,128,256]{2,1,0:T(8,128)(2,1)S(1)}, u32[]{:S(2)}, u32[]{:S(2)}) %all-to-all-start.1) | async-done | bytes 1048608 | tf_op jit(solution)/shard_map/all_to_all | solution.py:23
  68.9 2.3 %convolution_convert_fusion.2 = bf16[512,256]{1,0:T(8,128)(2,1)S(1)} fusion(bf16[512,2048]{1,0:T(8,128)(2,1)} %select_dynamic-update-slice_fusion, bf16[2048,256]{1,0:T(8,128)(2,1)S(1)} %bitcast.44), kind=kOutput, calls=%fused_computation.10 | convolution fusion | flops 537001984 | bytes 3407872 | tf_op jit(solution)/shard_map/dot_general | solution.py:98
  72.8 4.1 %all-to-all-start.3 = ((bf16[16,16,256]{2,1,0:T(8,128)(2,1)}), bf16[16,16,256]{2,1,0:T(8,128)(2,1)S(1)}, u32[]{:S(2)}, u32[]{:S(2)}) async-start(bf16[16,16,256]{2,1,0:T(8,128)(2,1)} %broadcast_in_dim.13), calls=%async_computation.3 | async-start | bytes 262144 | tf_op jit(solution)/shard_map/all_to_all | solution.py:23
  76.9 2.7 %convolution_convert_fusion = bf16[2048,256]{1,0:T(8,128)(2,1)S(1)} fusion(bf16[512,2048]{1,0:T(8,128)(2,1)} %select_dynamic-update-slice_fusion, s32[]{:T(128)S(6)} %select_n.95, bf16[512,256]{1,0:T(8,128)(2,1)S(1)} %add_convert_fusion.1), kind=kOutput, calls=%fused_computation | convolution fusion | flops 537919488 | bytes 3407876 | tf_op jit(solution)/shard_map/dot_general | solution.py:77
  80.8 4.2 %all-to-all-done.3 = bf16[16,16,256]{2,1,0:T(8,128)(2,1)S(1)} async-done(((bf16[16,16,256]{2,1,0:T(8,128)(2,1)}), bf16[16,16,256]{2,1,0:T(8,128)(2,1)S(1)}, u32[]{:S(2)}, u32[]{:S(2)}) %all-to-all-start.3) | async-done | bytes 131104 | tf_op jit(solution)/shard_map/all_to_all | solution.py:23
  84.9 3.7 %all-to-all-start.2 = ((bf16[16,128,256]{2,1,0:T(8,128)(2,1)}), bf16[16,128,256]{2,1,0:T(8,128)(2,1)S(1)}, u32[]{:S(2)}, u32[]{:S(2)}) async-start(bf16[16,128,256]{2,1,0:T(8,128)(2,1)} %bitcast.21), calls=%async_computation.2 | async-start | bytes 2097152 | tf_op jit(solution)/shard_map/all_to_all | solution.py:23
  92.0 13.5 %all-to-all-done.2 = bf16[16,128,256]{2,1,0:T(8,128)(2,1)S(1)} async-done(((bf16[16,128,256]{2,1,0:T(8,128)(2,1)}), bf16[16,128,256]{2,1,0:T(8,128)(2,1)S(1)}, u32[]{:S(2)}, u32[]{:S(2)}) %all-to-all-start.2) | async-done | bytes 1048608 | tf_op jit(solution)/shard_map/all_to_all | solution.py:23
  106.4 10.5 %all-to-all-start.4 = ((bf16[4,48,256]{2,1,0:T(8,128)(2,1)}), bf16[4,48,256]{2,1,0:T(8,128)(2,1)S(1)}, u32[]{:S(2)}, u32[]{:S(2)}) async-start(bf16[4,48,256]{2,1,0:T(8,128)(2,1)} %pad_maximum_fusion), calls=%async_computation.4 | async-start | bytes 196608 | tf_op jit(solution)/shard_map/all_to_all | solution.py:23
  116.9 13.0 %all-to-all-done.4 = bf16[4,48,256]{2,1,0:T(8,128)(2,1)S(1)} async-done(((bf16[4,48,256]{2,1,0:T(8,128)(2,1)}), bf16[4,48,256]{2,1,0:T(8,128)(2,1)S(1)}, u32[]{:S(2)}, u32[]{:S(2)}) %all-to-all-start.4) | async-done | bytes 98336 | tf_op jit(solution)/shard_map/all_to_all | solution.py:23
  131.7 3.4 %collective-permute-start.2 = (bf16[64,2048]{1,0:T(8,128)(2,1)S(1)}, bf16[64,2048]{1,0:T(8,128)(2,1)S(1)}, u32[]{:S(2)}, u32[]{:S(2)}) collective-permute-start(bf16[64,2048]{1,0:T(8,128)(2,1)S(1)} %get-tuple-element.14), channel_id=1, source_target_pairs={{0,4},{2,6},{4,0},{6,2},{1,5},{3,7},{5,1},{7,3},{8,12},{10,14},{12... | collective-permute-start | bytes 786440 | tf_op jit(solution)/shard_map/ppermute | solution.py:33
  135.2 2.0 %collective-permute-start.3 = (bf16[64,2048]{1,0:T(8,128)(2,1)S(1)}, bf16[64,2048]{1,0:T(8,128)(2,1)S(1)}, u32[]{:S(2)}, u32[]{:S(2)}) collective-permute-start(bf16[64,2048]{1,0:T(8,128)(2,1)S(1)} %get-tuple-element.16), channel_id=1, source_target_pairs={{0,6},{2,0},{4,2},{6,4},{1,7},{3,1},{5,3},{7,5},{8,14},{10,8},{12,... | collective-permute-start | bytes 786440 | tf_op jit(solution)/shard_map/ppermute | solution.py:33
  137.1 3.9 %collective-permute-start.4 = (bf16[64,2048]{1,0:T(8,128)(2,1)S(1)}, bf16[64,2048]{1,0:T(8,128)(2,1)S(1)}, u32[]{:S(2)}, u32[]{:S(2)}) collective-permute-start(bf16[64,2048]{1,0:T(8,128)(2,1)S(1)} %get-tuple-element.15), channel_id=1, source_target_pairs={{0,2},{2,4},{4,6},{6,0},{1,3},{3,5},{5,7},{7,1},{8,10},{10,12},{12... | collective-permute-start | bytes 786440 | tf_op jit(solution)/shard_map/ppermute | solution.py:33
  142.2 7.1 %collective-permute-done.2 = bf16[64,2048]{1,0:T(8,128)(2,1)S(1)} collective-permute-done((bf16[64,2048]{1,0:T(8,128)(2,1)S(1)}, bf16[64,2048]{1,0:T(8,128)(2,1)S(1)}, u32[]{:S(2)}, u32[]{:S(2)}) %collective-permute-start.2) | collective-permute-done | bytes 262176 | tf_op jit(solution)/shard_map/ppermute | solution.py:33
  149.3 5.2 %collective-permute-done.3 = bf16[64,2048]{1,0:T(8,128)(2,1)S(1)} collective-permute-done((bf16[64,2048]{1,0:T(8,128)(2,1)S(1)}, bf16[64,2048]{1,0:T(8,128)(2,1)S(1)}, u32[]{:S(2)}, u32[]{:S(2)}) %collective-permute-start.3) | collective-permute-done | bytes 262176 | tf_op jit(solution)/shard_map/ppermute | solution.py:33
  (51 shorter events, 25.7 us)
Async XLA Ops:
  0.6 58.9 %collective-permute-start.5 = (bf16[64,2048]{1,0:T(8,128)(2,1)}, bf16[64,2048]{1,0:T(8,128)(2,1)S(1)}, u32[]{:S(2)}, u32[]{:S(2)}) collective-permute-start(bf16[64,2048]{1,0:T(8,128)(2,1)} %param.4), channel_id=1, source_target_pairs={{0,1},{1,0},{2,3},{3,2},{4,5},{5,4},{6,7},{7,6},{8,9},{9,8},{10,11... | collective-permute-start | bytes 786440 | tf_op jit(solution)/shard_map/ppermute | solution.py:37
  2.6 50.7 %collective-permute-start.6 = (bf16[64,2048]{1,0:T(8,128)(2,1)}, bf16[64,2048]{1,0:T(8,128)(2,1)S(1)}, u32[]{:S(2)}, u32[]{:S(2)}) collective-permute-start(bf16[64,2048]{1,0:T(8,128)(2,1)} %param.4), channel_id=1, source_target_pairs={{0,6},{2,0},{4,2},{6,4},{1,7},{3,1},{5,3},{7,5},{8,14},{10,8},{12,... | collective-permute-start | bytes 786440 | tf_op jit(solution)/shard_map/ppermute | solution.py:33
  10.0 45.2 %collective-permute-start.8 = (bf16[64,2048]{1,0:T(8,128)(2,1)}, bf16[64,2048]{1,0:T(8,128)(2,1)S(1)}, u32[]{:S(2)}, u32[]{:S(2)}) collective-permute-start(bf16[64,2048]{1,0:T(8,128)(2,1)} %param.4), channel_id=1, source_target_pairs={{0,4},{2,6},{4,0},{6,2},{1,5},{3,7},{5,1},{7,3},{8,12},{10,14},{12... | collective-permute-start | bytes 786440 | tf_op jit(solution)/shard_map/ppermute | solution.py:33
  11.9 45.7 %collective-permute-start.10 = (bf16[64,2048]{1,0:T(8,128)(2,1)}, bf16[64,2048]{1,0:T(8,128)(2,1)S(1)}, u32[]{:S(2)}, u32[]{:S(2)}) collective-permute-start(bf16[64,2048]{1,0:T(8,128)(2,1)} %param.4), channel_id=1, source_target_pairs={{0,2},{2,4},{4,6},{6,0},{1,3},{3,5},{5,7},{7,1},{8,10},{10,12},{12... | collective-permute-start | bytes 786440 | tf_op jit(solution)/shard_map/ppermute | solution.py:33
  16.6 28.5 %all-to-all-start = ((bf16[4,32,256]{2,1,0:T(8,128)(2,1)}), bf16[4,32,256]{2,1,0:T(8,128)(2,1)S(1)}, u32[]{:S(2)}, u32[]{:S(2)}) async-start(bf16[4,32,256]{2,1,0:T(8,128)(2,1)} %broadcast_in_dim.10), calls=%async_computation | async-start | bytes 131072 | tf_op jit(solution)/shard_map/all_to_all | solution.py:23
  28.9 5.5 %collective-permute-start = (bf16[6,256]{1,0:T(8,128)(2,1)S(1)}, bf16[6,256]{1,0:T(8,128)(2,1)S(1)}, u32[]{:S(2)}, u32[]{:S(2)}) collective-permute-start(bf16[6,256]{1,0:T(8,128)(2,1)S(1)} %slice.75), channel_id=1, source_target_pairs={{8,0},{16,8},{24,16},{32,24},{40,32},{48,40},{56,48},{64,56},{72,6... | collective-permute-start | bytes 9224 | tf_op jit(solution)/shard_map/ppermute | solution.py:59
  35.9 23.7 %copy-start = (bf16[64,2048]{1,0:T(8,128)(2,1)S(1)}, bf16[64,2048]{1,0:T(8,128)(2,1)}, u32[]{:S(2)}) copy-start(bf16[64,2048]{1,0:T(8,128)(2,1)} %param.4) | copy-start | bytes 786436
  46.2 22.6 %all-to-all-start.1 = ((bf16[16,128,256]{2,1,0:T(8,128)(2,1)}), bf16[16,128,256]{2,1,0:T(8,128)(2,1)S(1)}, u32[]{:S(2)}, u32[]{:S(2)}) async-start(bf16[16,128,256]{2,1,0:T(8,128)(2,1)} %broadcast_in_dim.12), calls=%async_computation.1 | async-start | bytes 2097152 | tf_op jit(solution)/shard_map/all_to_all | solution.py:23
  53.2 7.8 %collective-permute-start.7 = (bf16[64,2048]{1,0:T(8,128)(2,1)S(1)}, bf16[64,2048]{1,0:T(8,128)(2,1)S(1)}, u32[]{:S(2)}, u32[]{:S(2)}) collective-permute-start(bf16[64,2048]{1,0:T(8,128)(2,1)S(1)} %collective-permute-done.6), channel_id=1, source_target_pairs={{0,1},{1,0},{2,3},{3,2},{4,5},{5,4},{6,7},{7,6},{8,9},{9,8},{10,11... | collective-permute-start | bytes 786440 | tf_op jit(solution)/shard_map/ppermute | solution.py:37
  55.2 7.4 %collective-permute-start.9 = (bf16[64,2048]{1,0:T(8,128)(2,1)S(1)}, bf16[64,2048]{1,0:T(8,128)(2,1)S(1)}, u32[]{:S(2)}, u32[]{:S(2)}) collective-permute-start(bf16[64,2048]{1,0:T(8,128)(2,1)S(1)} %collective-permute-done.8), channel_id=1, source_target_pairs={{0,1},{1,0},{2,3},{3,2},{4,5},{5,4},{6,7},{7,6},{8,9},{9,8},{10,11... | collective-permute-start | bytes 786440 | tf_op jit(solution)/shard_map/ppermute | solution.py:37
  57.6 6.6 %collective-permute-start.11 = (bf16[64,2048]{1,0:T(8,128)(2,1)S(1)}, bf16[64,2048]{1,0:T(8,128)(2,1)S(1)}, u32[]{:S(2)}, u32[]{:S(2)}) collective-permute-start(bf16[64,2048]{1,0:T(8,128)(2,1)S(1)} %collective-permute-done.10), channel_id=1, source_target_pairs={{0,1},{1,0},{2,3},{3,2},{4,5},{5,4},{6,7},{7,6},{8,9},{9,8},{10,11... | collective-permute-start | bytes 786440 | tf_op jit(solution)/shard_map/ppermute | solution.py:37
  72.8 12.1 %all-to-all-start.3 = ((bf16[16,16,256]{2,1,0:T(8,128)(2,1)}), bf16[16,16,256]{2,1,0:T(8,128)(2,1)S(1)}, u32[]{:S(2)}, u32[]{:S(2)}) async-start(bf16[16,16,256]{2,1,0:T(8,128)(2,1)} %broadcast_in_dim.13), calls=%async_computation.3 | async-start | bytes 262144 | tf_op jit(solution)/shard_map/all_to_all | solution.py:23
  84.9 20.7 %all-to-all-start.2 = ((bf16[16,128,256]{2,1,0:T(8,128)(2,1)}), bf16[16,128,256]{2,1,0:T(8,128)(2,1)S(1)}, u32[]{:S(2)}, u32[]{:S(2)}) async-start(bf16[16,128,256]{2,1,0:T(8,128)(2,1)} %bitcast.21), calls=%async_computation.2 | async-start | bytes 2097152 | tf_op jit(solution)/shard_map/all_to_all | solution.py:23
  90.1 39.8 %collective-permute-start.1 = (bf16[256,2048]{1,0:T(8,128)(2,1)}, bf16[256,2048]{1,0:T(8,128)(2,1)}, u32[]{:S(2)}, u32[]{:S(2)}) collective-permute-start(bf16[256,2048]{1,0:T(8,128)(2,1)} %convolution_convert_fusion.1), channel_id=1, source_target_pairs={{0,1},{1,0},{2,3},{3,2},{4,5},{5,4},{6,7},{7,6},{8,9},{9,8},{10,11... | collective-permute-start | bytes 3145736 | tf_op jit(solution)/shard_map/ppermute | solution.py:37
  106.4 23.5 %all-to-all-start.4 = ((bf16[4,48,256]{2,1,0:T(8,128)(2,1)}), bf16[4,48,256]{2,1,0:T(8,128)(2,1)S(1)}, u32[]{:S(2)}, u32[]{:S(2)}) async-start(bf16[4,48,256]{2,1,0:T(8,128)(2,1)} %pad_maximum_fusion), calls=%async_computation.4 | async-start | bytes 196608 | tf_op jit(solution)/shard_map/all_to_all | solution.py:23
  131.7 17.6 %collective-permute-start.2 = (bf16[64,2048]{1,0:T(8,128)(2,1)S(1)}, bf16[64,2048]{1,0:T(8,128)(2,1)S(1)}, u32[]{:S(2)}, u32[]{:S(2)}) collective-permute-start(bf16[64,2048]{1,0:T(8,128)(2,1)S(1)} %get-tuple-element.14), channel_id=1, source_target_pairs={{0,4},{2,6},{4,0},{6,2},{1,5},{3,7},{5,1},{7,3},{8,12},{10,14},{12... | collective-permute-start | bytes 786440 | tf_op jit(solution)/shard_map/ppermute | solution.py:33
  135.2 19.4 %collective-permute-start.3 = (bf16[64,2048]{1,0:T(8,128)(2,1)S(1)}, bf16[64,2048]{1,0:T(8,128)(2,1)S(1)}, u32[]{:S(2)}, u32[]{:S(2)}) collective-permute-start(bf16[64,2048]{1,0:T(8,128)(2,1)S(1)} %get-tuple-element.16), channel_id=1, source_target_pairs={{0,6},{2,0},{4,2},{6,4},{1,7},{3,1},{5,3},{7,5},{8,14},{10,8},{12,... | collective-permute-start | bytes 786440 | tf_op jit(solution)/shard_map/ppermute | solution.py:33
  137.1 17.4 %collective-permute-start.4 = (bf16[64,2048]{1,0:T(8,128)(2,1)S(1)}, bf16[64,2048]{1,0:T(8,128)(2,1)S(1)}, u32[]{:S(2)}, u32[]{:S(2)}) collective-permute-start(bf16[64,2048]{1,0:T(8,128)(2,1)S(1)} %get-tuple-element.15), channel_id=1, source_target_pairs={{0,2},{2,4},{4,6},{6,0},{1,3},{3,5},{5,7},{7,1},{8,10},{10,12},{12... | collective-permute-start | bytes 786440 | tf_op jit(solution)/shard_map/ppermute | solution.py:33

commit v4 on v2

--- a/solution.py
+++ b/solution.py
@@ -59,10 +59,11 @@
     from_other = lax.ppermute(for_other, C, [(0, 1), (1, 0)])
     here = lax.dot_general(ours, weight, contract_cols, preferred_element_type=F32)
     chip_sum = (here + from_other.astype(F32)).astype(BF)
+
+    chip_sum, grad_late = lax.optimization_barrier((chip_sum, grad_bf))
     input_grad = lax.psum_scatter(chip_sum, ZL, scatter_dimension=0, tiled=True)
-
     partial = lax.dot_general(
-        slab, grad_bf, (((0,), (0,)), ((), ())), preferred_element_type=F32
+        slab, grad_late, (((0,), (0,)), ((), ())), preferred_element_type=F32
     ).astype(BF)
     partial = partial.reshape(nz, nxy, rows, cols).transpose(1, 0, 2, 3).reshape(nxy, nz * rows, cols)
     featured = jnp.dot(slab, weight, preferred_element_type=F32).astype(BF).astype(F32)
@@ -74,13 +75,12 @@
     packed = jnp.concatenate([partial, tail], 1)
     arrived = lax.all_to_all(packed, (X, Y), split_axis=0, concat_axis=0, tiled=True)
     column_sum = jnp.sum(arrived.astype(F32), axis=0)
-    blocks = column_sum[: nz * rows].astype(BF).reshape(nz, rows, cols)
-    tail = jnp.broadcast_to(split_rows(joined_rows(column_sum[nz * rows :]))[None], (nz, 16, cols))
-    packed = jnp.concatenate([blocks, tail], 1)
-    arrived = lax.all_to_all(packed, ZH, split_axis=0, concat_axis=0, tiled=True)
-    total = jnp.sum(arrived.astype(F32), axis=0)
-    weight_grad = total[:rows].astype(BF)
-    filter_grad = joined_rows(total[rows:])[:TAPS]
+    blocks = column_sum[: nz * rows].astype(BF)
+    tail = split_rows(joined_rows(column_sum[nz * rows :]))
+    arrived = lax.all_gather(jnp.concatenate([blocks, tail], 0), ZH).astype(F32)
+    total = jnp.sum(arrived, axis=0)
+    weight_grad = lax.dynamic_slice_in_dim(total, lax.axis_index(ZH) * rows, rows, 0).astype(BF)
+    filter_grad = joined_rows(total[nz * rows :])[:TAPS]
     return input_grad, weight_grad, filter_grad
 
 

time: 128 us -> 133 us (1.039)
  waiting for transfers between devices: 33.6 us -> 41.4 us
  local copies, waits for them, and re-layouts: 5.14 us -> 2.51 us
    all_gather x0 -> x1, blocking collectives: none -> 17.5 us  [body(): arrived = lax.all_gather(jnp.concatenate([blocks, tail], 0), ZH).astype(F32)]
    all_to_all x1 -> x0, blocking collectives: 17.4 us -> none  [body(): lax.all_to_all(packed, ZH, split_axis=0, concat_axis=0, tiled=True)]
    reduce_scatter x1, waiting for transfers between devices: 6.53 us -> 11.1 us  [body(): input_grad = lax.psum_scatter(chip_sum, ZL, scatter_dimension=0, tiled=True)]
    ppermute x1, waiting for transfers between devices: 0.01 us -> 2.26 us  [body(): from_other = lax.ppermute(for_other, C, [(0, 1), (1, 0)])]
    dot_general x1, matrix products: 1.03 us -> 2.63 us  [body(): jnp.dot(slab, weight, preferred_element_type=F32).astype(BF).astype(F32)]
    transpose x1, local copies, waits for them, and re-layouts: 1.46 us -> 0.08 us  [body(): partial.reshape(nz, nxy, rows, cols).transpose(1, 0, 2, 3)]
  transfers between devices with their start and end apart: 6 -> 6, of which waited for: 4 -> 5; matrix products, arithmetic and copies ran while one was open for 11% -> 4% of each run, Pallas kernels for 0% -> 0%
where the time goes in v4:
time: 133 us
  waiting for transfers between devices  41.4 us (31%)
  blocking collectives  41.3 us (31%)
  starting transfers between devices  22.3 us (17%)
  between operations  15.7 us (12%)
  matrix products  6.88 us (5%)
  local copies, waits for them, and re-layouts  2.51 us (2%)
  other arithmetic  2.39 us (2%)
    all_gather x1, blocking collectives, weight_columns(): column = lax.all_gather(proj_weight, ZH)  23.9 us
    all_gather x1, blocking collectives, body(): arrived = lax.all_gather(jnp.concatenate([blocks, tail], 0), ZH).astype(F32)  17.5 us
    all_to_all x1, waiting for transfers between devices, body(): lax.all_to_all(packed, (X, Y), split_axis=0, concat_axis=0, tiled=True)  16.5 us
    reduce_scatter x1, waiting for transfers between devices, body(): input_grad = lax.psum_scatter(chip_sum, ZL, scatter_dimension=0, tiled=True)  11.1 us
    ppermute x1, starting transfers between devices, body(): from_other = lax.ppermute(for_other, C, [(0, 1), (1, 0)])  7.66 us
    all_to_all x1, waiting for transfers between devices, weight_columns(): lax.all_to_all(repeated, (X, Y), split_axis=0, concat_axis=0, tiled=True)  7.02 us
    all_to_all x1, starting transfers between devices, weight_columns(): lax.all_to_all(repeated, (X, Y), split_axis=0, concat_axis=0, tiled=True)  6.75 us
    all_to_all x1, starting transfers between devices, body(): lax.all_to_all(packed, (X, Y), split_axis=0, concat_axis=0, tiled=True)  6.51 us
  transfers between devices with their start and end apart: 6, of which 5 were waited for; matrix products, arithmetic and copies ran while one was open for 4% of the time, Pallas kernels for 0%

profile of v4, /device:TPU:1, one launch (start us, length us, event | category | flops | bytes accessed | tf_op | source)
XLA Modules:
  0.0 132.5 jit_solution(693972377917715287)
XLA Ops:
  8.1 0.7 all-gather.4.cloned.1.call-update
  8.8 23.9 %all-gather = bf16[128,256]{1,0:T(8,128)(2,1)S(1)} all-gather(bf16[32,256]{1,0:T(8,128)(2,1)} %param.5), channel_id=2, replica_groups=mesh['zh'=4,'x'=4,'y'=4,'zl'=4,'c'=2] {'zh'}, dimensions={0}, use_global_device_ids=true | all-gather | bytes 81920 | tf_op jit(solution)/shard_map/all_gather | solution.py:26
  32.6 1.1 broadcast_in_dim.4
  33.7 6.8 %all-to-all-start = ((bf16[16,4,32,256]{3,2,1,0:T(8,128)(2,1)}), bf16[16,4,32,256]{3,2,1,0:T(8,128)(2,1)S(1)}, u32[]{:S(2)}, u32[]{:S(2)}) async-start(bf16[16,4,32,256]{3,2,1,0:T(8,128)(2,1)} %broadcast_in_dim.4), calls=%async_computation | async-start | bytes 2097152 | tf_op jit(solution)/shard_map/all_to_all | solution.py:28
  40.5 1.3 collective-permute-start
  41.8 3.4 %collective-permute-done = bf16[6,256]{1,0:T(8,128)(2,1)S(1)} collective-permute-done((bf16[6,256]{1,0:T(8,128)(2,1)S(1)}, bf16[6,256]{1,0:T(8,128)(2,1)S(1)}, u32[]{:S(2)}, u32[]{:S(2)}) %collective-permute-start) | collective-permute-done | bytes 3104 | tf_op jit(solution)/shard_map/ppermute | solution.py:42
  45.3 0.4 add_convert_fusion.1
  45.8 7.0 %all-to-all-done = bf16[16,4,32,256]{3,2,1,0:T(8,128)(2,1)S(1)} async-done(((bf16[16,4,32,256]{3,2,1,0:T(8,128)(2,1)}), bf16[16,4,32,256]{3,2,1,0:T(8,128)(2,1)S(1)}, u32[]{:S(2)}, u32[]{:S(2)}) %all-to-all-start) | async-done | bytes 1048608 | tf_op jit(solution)/shard_map/all_to_all | solution.py:28
  52.9 0.5 convolution_convert_fusion.1
  53.4 7.7 %collective-permute-start.1 = (bf16[256,2048]{1,0:T(8,128)(2,1)S(1)}, bf16[256,2048]{1,0:T(8,128)(2,1)S(1)}, u32[]{:S(2)}, u32[]{:S(2)}) collective-permute-start(bf16[256,2048]{1,0:T(8,128)(2,1)S(1)} %convolution_convert_fusion.1), channel_id=1, source_target_pairs={{0,1},{1,0},{2,3},{3,2},{4,5},{5,4},{6,7},{7,6},{8,9},{9,8},{10,11... | collective-permute-start | bytes 3145736 | tf_op jit(solution)/shard_map/ppermute | solution.py:59
  61.0 2.3 %collective-permute-done.1 = bf16[256,2048]{1,0:T(8,128)(2,1)S(1)} collective-permute-done((bf16[256,2048]{1,0:T(8,128)(2,1)S(1)}, bf16[256,2048]{1,0:T(8,128)(2,1)S(1)}, u32[]{:S(2)}, u32[]{:S(2)}) %collective-permute-start.1) | collective-permute-done | bytes 1048608 | tf_op jit(solution)/shard_map/ppermute | solution.py:59
  63.3 1.5 %add_convert_fusion = bf16[256,2048]{1,0:T(8,128)(2,1)} fusion(bf16[256,2048]{1,0:T(8,128)(2,1)S(1)} %collective-permute-done.1, bf16[256,256]{1,0:T(8,128)(2,1)S(1)} %bitcast.44, bf16[2048,256]{1,0:T(8,128)(2,1)S(1)} %bitcast.38), kind=kOutput, calls=%fused_computation.4 | convolution fusion | flops 270008320 | bytes 3276800 | tf_op jit(solution)/shard_map/dot_general | solution.py:60
  64.8 2.6 %fusion.7 = (f32[256]{0:T(256)S(1)}, f32[256]{0:T(256)S(1)}, f32[256]{0:T(256)S(1)}, f32[256]{0:T(256)S(1)}, f32[256]{0:T(256)S(1)}, /*index=5*/f32[256]{0:T(256)S(1)}, f32[256]{0:T(256)S(1)}) fusion(f32[518,256]{1,0:T(8,128)S(1)} %maximum_convert_fusion, bf16[512,2048]{1,0:T(8,128)(2,1)} %all-gather.4.cloned.1.call-done, bf16[2048,256]{1,0:T(8,128)(2,1)S(1)} %bitcast.39), kind=kOutput, calls=%fused_computation.21 | convolution fusion | flops 538966272 | bytes 6822912 | tf_op jit(solution)/shard_map/dot_general | solution.py:69
  67.4 2.3 %fusion = bf16[2048,256]{0,1:T(8,128)(2,1)S(1)} fusion(bf16[512,256]{1,0:T(8,128)(2,1)S(1)} %add_convert_fusion.1, bf16[512,2048]{1,0:T(8,128)(2,1)} %all-gather.4.cloned.1.call-done), kind=kOutput, calls=%fused_computation.2 | convolution fusion | flops 537395200 | bytes 3407872 | tf_op jit(solution)/shard_map/dot_general | solution.py:65
  69.8 0.5 copy.13
  70.4 1.1 pad_maximum_fusion
  71.5 6.5 %all-to-all-start.1 = ((bf16[16,144,256]{2,1,0:T(8,128)(2,1)}), bf16[16,144,256]{2,1,0:T(8,128)(2,1)S(1)}, u32[]{:S(2)}, u32[]{:S(2)}) async-start(bf16[16,144,256]{2,1,0:T(8,128)(2,1)} %pad_maximum_fusion), calls=%async_computation.2 | async-start | bytes 2359296 | tf_op jit(solution)/shard_map/all_to_all | solution.py:76
  78.1 0.5 reduce-scatter.2.cloned.1.call-update
  78.6 16.5 %all-to-all-done.1 = bf16[16,144,256]{2,1,0:T(8,128)(2,1)S(1)} async-done(((bf16[16,144,256]{2,1,0:T(8,128)(2,1)}), bf16[16,144,256]{2,1,0:T(8,128)(2,1)S(1)}, u32[]{:S(2)}, u32[]{:S(2)}) %all-to-all-start.1) | async-done | bytes 1179680 | tf_op jit(solution)/shard_map/all_to_all | solution.py:76
  95.1 0.2 convert_reduce_fusion
  95.3 17.5 %all-gather.1 = bf16[576,256]{1,0:T(8,128)(2,1)S(1)} all-gather(bf16[144,256]{1,0:T(8,128)(2,1)S(1)} %pad_maximum_fusion.1), channel_id=3, replica_groups=mesh['zh'=4,'x'=4,'y'=4,'zl'=4,'c'=2] {'zh'}, dimensions={0}, use_global_device_ids=true | all-gather | bytes 368640 | tf_op jit(solution)/shard_map/all_gather | solution.py:80
  112.8 0.6 dynamic-slice_convert_fusion
  113.4 0.6 slice_add_fusion
  114.0 11.1 %reduce-scatter.2.cloned.1.call-done = bf16[64,2048]{1,0:T(8,128)(2,1)} async-done(((bf16[256,2048]{1,0:T(8,128)(2,1)}), bf16[64,2048]{1,0:T(8,128)(2,1)}) %reduce-scatter.2.cloned.1.call-update) | async-done | bytes 262160 | tf_op jit(solution)/shard_map/reduce_scatter | solution.py:64
  (23 shorter events, 0.4 us)
Async XLA Ops:
  8.0 32.5 %copy-start = (bf16[512,256]{1,0:T(8,128)(2,1)S(1)}, bf16[512,256]{1,0:T(8,128)(2,1)}, u32[]{:S(2)}) copy-start(bf16[512,256]{1,0:T(8,128)(2,1)} %param.6) | copy-start | bytes 786436
  8.0 33.8 %copy-start.1 = (f32[7,256]{1,0:T(8,128)S(1)}, f32[7,256]{1,0:T(8,128)}, u32[]{:S(2)}) copy-start(f32[7,256]{1,0:T(8,128)} %param.7) | copy-start | bytes 21508
  8.0 56.7 %all-gather.4.cloned.1.call-start = ((), (), s32[]{:S(2)}) async-start(), calls=%async_computation.4 | async-start | bytes 2359296 | tf_op jit(solution)/shard_map/all_gather | solution.py:40
  33.7 19.1 %all-to-all-start = ((bf16[16,4,32,256]{3,2,1,0:T(8,128)(2,1)}), bf16[16,4,32,256]{3,2,1,0:T(8,128)(2,1)S(1)}, u32[]{:S(2)}, u32[]{:S(2)}) async-start(bf16[16,4,32,256]{3,2,1,0:T(8,128)(2,1)} %broadcast_in_dim.4), calls=%async_computation | async-start | bytes 2097152 | tf_op jit(solution)/shard_map/all_to_all | solution.py:28
  40.5 4.8 %collective-permute-start = (bf16[6,256]{1,0:T(8,128)(2,1)S(1)}, bf16[6,256]{1,0:T(8,128)(2,1)S(1)}, u32[]{:S(2)}, u32[]{:S(2)}) collective-permute-start(bf16[6,256]{1,0:T(8,128)(2,1)S(1)} %slice.78), channel_id=1, source_target_pairs={{8,0},{16,8},{24,16},{32,24},{40,32},{48,40},{56,48},{64,56},{72,6... | collective-permute-start | bytes 9224 | tf_op jit(solution)/shard_map/ppermute | solution.py:42
  53.4 9.9 %collective-permute-start.1 = (bf16[256,2048]{1,0:T(8,128)(2,1)S(1)}, bf16[256,2048]{1,0:T(8,128)(2,1)S(1)}, u32[]{:S(2)}, u32[]{:S(2)}) collective-permute-start(bf16[256,2048]{1,0:T(8,128)(2,1)S(1)} %convolution_convert_fusion.1), channel_id=1, source_target_pairs={{0,1},{1,0},{2,3},{3,2},{4,5},{5,4},{6,7},{7,6},{8,9},{9,8},{10,11... | collective-permute-start | bytes 3145736 | tf_op jit(solution)/shard_map/ppermute | solution.py:59
  71.5 23.6 %all-to-all-start.1 = ((bf16[16,144,256]{2,1,0:T(8,128)(2,1)}), bf16[16,144,256]{2,1,0:T(8,128)(2,1)S(1)}, u32[]{:S(2)}, u32[]{:S(2)}) async-start(bf16[16,144,256]{2,1,0:T(8,128)(2,1)} %pad_maximum_fusion), calls=%async_computation.2 | async-start | bytes 2359296 | tf_op jit(solution)/shard_map/all_to_all | solution.py:76
  78.0 47.0 %reduce-scatter.2.cloned.1.call-start = ((), (), s32[]{:S(2)}) async-start(), calls=%async_computation.3 | async-start | bytes 1310720 | tf_op jit(solution)/shard_map/reduce_scatter | solution.py:64
Sparse Core Ops, SparseCore 0:
  11.1 48.1 all-gather.3
Sparse Core Ops, SparseCore 1:
  81.9 43.1 reduce-scatter.1

commit v5 on v0

v5 whole, which is shorter than its diff:
```python
import jax
import jax.numpy as jnp
from jax import lax
from jax.sharding import Mesh, PartitionSpec as P

TAPS = 7
BF = jnp.bfloat16
F32 = jnp.float32
ZH, X, Y, ZP, ZQ, C = "zh", "x", "y", "zp", "zq", "c"
DP, SEQ, XY, PAIR, COLUMN = (ZH, X, Y), (ZP, ZQ, C), (X, Y), (ZQ, C), (ZH, ZQ, C)


def split_rows(value, parts):
    pieces = []
    for _ in range(parts):
        piece = value.astype(BF)
        pieces.append(piece)
        value = value - piece.astype(F32)
    return pieces


def exchange(value, axes):
    return lax.all_to_all(value, axes, split_axis=0, concat_axis=0, tiled=True)


def spread(value, axes):
    return exchange(jnp.broadcast_to(value[None], (lax.axis_size(axes),) + value.shape), axes)


def body(tokens, proj_weight, cotangent, filters):
    nz, nxy, nseq, npair = (lax.axis_size(a) for a in (ZH, XY, SEQ, PAIR))
    ndp = nz * nxy
    rows, cols = proj_weight.shape
    own_tokens, depth = tokens.shape
    slab_len = cotangent.shape[0]
    quarter, half = depth // npair, cols * npair
    zh, mine = lax.axis_index(ZH), lax.axis_index(PAIR)

    head = cotangent[: TAPS + 1]
    following = lax.ppermute(head, DP, [(source, source - 1) for source in range(1, ndp)])
    taps3 = [jnp.pad(piece, ((0, 1), (0, 0))) for piece in split_rows(filters, 3)]
    block = lax.all_gather(jnp.concatenate([cotangent, following] + taps3, 0), PAIR)
    block = block.transpose(1, 0, 2).reshape(-1, half).astype(F32)
    extended = block[: slab_len + TAPS + 1]
    taps = block[slab_len + TAPS + 1 :].reshape(3, TAPS + 1, half)
    taps = taps[0] + taps[1] + taps[2]

    column = spread(proj_weight, COLUMN).reshape(nz, npair, rows, cols)
    column = lax.dynamic_index_in_dim(column, mine, 0, keepdims=False)
    column = column.transpose(1, 0, 2).reshape(rows, half)
    weight = spread(column, XY).reshape(quarter, half)

    pieces = tokens.reshape(own_tokens, npair, quarter).transpose(1, 0, 2)
    pieces = jnp.broadcast_to(pieces[None], (nseq // npair,) + pieces.shape)
    slab = exchange(pieces.reshape(nseq, own_tokens, quarter), SEQ).reshape(slab_len, quarter)

    grad_feat = jnp.zeros((slab_len, half), F32)
    for tap in range(TAPS):
        grad_feat = grad_feat + taps[tap] * extended[tap : tap + slab_len]
    grad_bf = grad_feat.astype(BF)

    partial = lax.dot_general(grad_bf, weight, (((1,), (1,)), ((), ())), preferred_element_type=F32)
    arrived = exchange(partial.astype(BF).reshape(nseq, own_tokens, quarter), SEQ)
    arrived = arrived.reshape(nseq // npair, npair, own_tokens, quarter).astype(F32)
    input_grad = jnp.sum(arrived, axis=0).transpose(1, 0, 2).reshape(own_tokens, depth).astype(BF)

    products = lax.dot_general(slab, grad_bf, (((0,), (0,)), ((), ())), preferred_element_type=F32)
    featured = jnp.dot(slab, weight, preferred_element_type=F32)
    tap_sums = jnp.stack(
        [jnp.sum(featured * extended[tap : tap + slab_len], axis=0) for tap in range(TAPS)]
        + [jnp.zeros((half,), F32)]
    )
    tail = jnp.broadcast_to(jnp.concatenate(split_rows(tap_sums, 2), 0)[None], (nxy, 16, half))
    arrived = exchange(jnp.concatenate([products.astype(BF).reshape(nxy, rows, half), tail], 1), XY)
    summed = jnp.sum(arrived.astype(F32), axis=0)

    tap_sums = summed[rows : rows + 8] + summed[rows + 8 :]
    packed = jnp.concatenate([summed[:rows].astype(BF)] + split_rows(tap_sums, 2), 0)
    packed = packed.reshape(-1, npair, cols).transpose(1, 0, 2)
    packed = jnp.broadcast_to(packed[None], (nz,) + packed.shape).reshape(nz * npair, -1, cols)
    arrived = exchange(packed, COLUMN).reshape(nz, npair, -1, cols)
    blocks = lax.dynamic_index_in_dim(arrived, zh, 1, keepdims=False)[:, :rows]
    weight_grad = jnp.sum(blocks.astype(F32), axis=0).astype(BF)
    tails = jnp.sum(arrived[:, :, rows:].astype(F32), axis=(0, 1))
    filter_grad = tails[:TAPS] + tails[8 : 8 + TAPS]
    return input_grad, weight_grad, filter_grad


def solution(mesh):
    fine = Mesh(mesh.devices.reshape(4, 4, 4, 2, 2, 2), (ZH, X, Y, ZP, ZQ, C))
    in_specs = (P(DP + SEQ, None), P(DP, SEQ), P(DP, SEQ), P(None, SEQ))
    out_specs = (P(DP + SEQ, None), P(DP, SEQ), P(None, SEQ))
    return jax.shard_map(body, mesh=fine, in_specs=in_specs, out_specs=out_specs, check_vma=False)
```

time: 664 us -> 210 us (0.32)
  waiting for transfers between devices: 432 us -> 98.2 us
  blocking collectives: 201 us -> 0 us
  starting transfers between devices: 1.44 us -> 55.7 us
  local copies, waits for them, and re-layouts: 5.12 us -> 24.8 us
    psum x1 -> x0, blocking collectives: 201 us -> none  [body(): filter_grad = lax.psum(filter_local, 'dp')]
    unnamed x5 -> x1, waiting for transfers between devices: 193 us -> 0.02 us
    all_gather x2 -> x1, waiting for transfers between devices: 146 us -> 26.3 us  [body(): lax.all_gather(jnp.concatenate([cotangent, following] + taps3, 0), PAIR)]
    reduce_scatter x1 -> x0, waiting for transfers between devices: 89.8 us -> none  [body(): lax.psum_scatter(lax.dot_general(grad_bf, weight_cols, (((1,), (1,)), (()...]
    all_to_all x0 -> x6, waiting for transfers between devices: none -> 71.4 us  [exchange(): return lax.all_to_all(value, axes, split_axis=0, concat_axis=0, tiled=True)]
    all_to_all x0 -> x6, starting transfers between devices: none -> 54.4 us  [exchange(): return lax.all_to_all(value, axes, split_axis=0, concat_axis=0, tiled=True)]
    unnamed x5 -> x24, local copies, waits for them, and re-layouts: 3.44 us -> 13 us
  transfers between devices with their start and end apart: 5 -> 8, of which waited for: 5 -> 7; matrix products, arithmetic and copies ran while one was open for 2% -> 11% of each run, Pallas kernels for 0% -> 0%
where the time goes in v5:
time: 210 us; the launch traced here: 209 us
  waiting for transfers between devices  98.2 us (47%)
  starting transfers between devices  55.7 us (27%)
  local copies, waits for them, and re-layouts  24.8 us (12%)
  between operations  14.3 us (7%)
  matrix products  12.4 us (6%)
  other arithmetic  3.72 us (2%)
    all_to_all x6, waiting for transfers between devices, exchange(): return lax.all_to_all(value, axes, split_axis=0, concat_axis=0, tiled=True)  71.4 us
    all_to_all x6, starting transfers between devices, exchange(): return lax.all_to_all(value, axes, split_axis=0, concat_axis=0, tiled=True)  54.4 us
    all_gather x1, waiting for transfers between devices, body(): lax.all_gather(jnp.concatenate([cotangent, following] + taps3, 0), PAIR)  26.3 us
    unnamed x24, local copies, waits for them, and re-layouts  13 us
    dot_general x1, matrix products, body(): featured = jnp.dot(slab, weight, preferred_element_type=F32)  7.49 us
  transfers between devices with their start and end apart: 8, of which 7 were waited for; matrix products, arithmetic and copies ran while one was open for 11% of the time, Pallas kernels for 0%

profile of v5, /device:TPU:1, one launch (start us, length us, event | category | flops | bytes accessed | tf_op | source)
XLA Modules:
  0.0 209.1 jit_solution(8428616281736316362)
XLA Ops:
  7.2 1.4 broadcast_in_dim.12
  8.6 16.6 %all-to-all-start = ((bf16[16,32,256]{2,1,0:T(8,128)(2,1)}), bf16[16,32,256]{2,1,0:T(8,128)(2,1)S(1)}, u32[]{:S(2)}, u32[]{:S(2)}) async-start(bf16[16,32,256]{2,1,0:T(8,128)(2,1)} %broadcast_in_dim.12), calls=%async_computation | async-start | bytes 524288 | tf_op jit(solution)/shard_map/all_to_all | solution.py:23
  30.6 13.3 %all-to-all-done = bf16[16,32,256]{2,1,0:T(8,128)(2,1)S(1)} async-done(((bf16[16,32,256]{2,1,0:T(8,128)(2,1)}), bf16[16,32,256]{2,1,0:T(8,128)(2,1)S(1)}, u32[]{:S(2)}, u32[]{:S(2)}) %all-to-all-start) | async-done | bytes 262176 | tf_op jit(solution)/shard_map/all_to_all | solution.py:23
  44.8 6.3 %all-to-all-start.3 = ((bf16[8,64,512]{2,1,0:T(8,128)(2,1)}), bf16[8,64,512]{2,1,0:T(8,128)(2,1)S(1)}, u32[]{:S(2)}, u32[]{:S(2)}) async-start(bf16[8,64,512]{2,1,0:T(8,128)(2,1)} %bitcast.10), calls=%async_computation.3 | async-start | bytes 1048576 | tf_op jit(solution)/shard_map/all_to_all | solution.py:23
  51.8 26.3 %all-gather.3.cloned.1.call-done = bf16[2176,256]{1,0:T(8,128)(2,1)} async-done(((bf16[544,256]{1,0:T(8,128)(2,1)}), bf16[2176,256]{1,0:T(8,128)(2,1)}) %all-gather.3.cloned.1.call-update) | async-done | bytes 1114128 | tf_op jit(solution)/shard_map/all_gather | solution.py:42
  78.1 2.1 %copy.55 = f32[4,544,256]{2,0,1:T(4,128)S(1)} copy(bf16[4,544,256]{2,1,0:T(8,128)(2,1)} %bitcast.120) | data formatting | bytes 3342336 | tf_op jit(solution)/shard_map/convert_element_type | solution.py:43
  81.5 6.5 %all-to-all-start.1 = ((bf16[16,32,1024]{2,1,0:T(8,128)(2,1)}), bf16[16,32,1024]{2,1,0:T(8,128)(2,1)S(1)}, u32[]{:S(2)}, u32[]{:S(2)}) async-start(bf16[16,32,1024]{2,1,0:T(8,128)(2,1)} %broadcast_in_dim.14), calls=%async_computation.1 | async-start | bytes 2097152 | tf_op jit(solution)/shard_map/all_to_all | solution.py:23
  88.1 2.7 %fusion.10 = (f32[512,4,256]{2,1,0:T(4,128)S(1)}, f32[512,4,256]{2,1,0:T(4,128)S(1)}, f32[512,4,256]{2,1,0:T(4,128)S(1)}, f32[512,4,256]{2,1,0:T(4,128)S(1)}, f3...) fusion(f32[544,4,256]{2,1,0:T(4,128)S(1)} %bitcast.100), kind=kLoop, calls=%fused_computation.49 | loop fusion | bytes 29360128 | tf_op jit(solution)/shard_map/slice | solution.py:59
  91.3 1.9 copy.49
  93.1 1.8 copy.47
  94.9 1.8 copy.45
  96.7 1.8 copy.43
  98.5 1.8 copy.53
  100.3 1.8 copy.51
  102.1 1.8 all-to-all-done.1
  103.8 7.5 %fusion.6 = (f32[1024]{0:T(1024)S(1)}, f32[1024]{0:T(1024)S(1)}, f32[1024]{0:T(1024)S(1)}, f32[1024]{0:T(1024)S(1)}, f32[1024]{0:T(1024)S(1)}, /*index=5*/f32[10...) fusion(f32[512,1024]{1,0:T(8,128)} %bitcast.113, f32[512,1024]{1,0:T(8,128)} %bitcast.112, ...), kind=kOutput, calls=%fused_computation.15 | convolution fusion | flops 551543808 | bytes 17358848 | tf_op jit(solution)/shard_map/dot_general | solution.py:68
  111.4 2.1 %convolution_convert_fusion = bf16[1024,512]{0,1:T(8,128)(2,1)S(1)} fusion(bf16[512,1024]{1,0:T(8,128)(2,1)} %get-tuple-element.14, bf16[512,512]{1,0:T(8,128)(2,1)} %bitcast.118), kind=kOutput, calls=%fused_computation.18 | convolution fusion | flops 537395200 | bytes 2621440 | tf_op jit(solution)/shard_map/dot_general | solution.py:67
  114.9 4.9 %all-to-all-start.4 = ((bf16[16,48,1024]{2,1,0:T(8,128)(2,1)}), bf16[16,48,1024]{2,1,0:T(8,128)(2,1)S(1)}, u32[]{:S(2)}, u32[]{:S(2)}) async-start(bf16[16,48,1024]{2,1,0:T(8,128)(2,1)} %pad_maximum_fusion), calls=%async_computation.4 | async-start | bytes 3145728 | tf_op jit(solution)/shard_map/all_to_all | solution.py:23
  119.8 2.8 %convolution_convert_fusion.1 = bf16[512,512]{1,0:T(8,128)(2,1)} fusion(bf16[512,1024]{1,0:T(8,128)(2,1)} %get-tuple-element.14, bf16[512,1024]{1,0:T(8,128)(2,1)S(1)} %bitcast.116), kind=kOutput, calls=%fused_computation.19 | convolution fusion | flops 537133056 | bytes 2621440 | tf_op jit(solution)/shard_map/dot_general | solution.py:62
  122.5 17.7 %all-to-all-done.4 = bf16[16,48,1024]{2,1,0:T(8,128)(2,1)S(1)} async-done(((bf16[16,48,1024]{2,1,0:T(8,128)(2,1)}), bf16[16,48,1024]{2,1,0:T(8,128)(2,1)S(1)}, u32[]{:S(2)}, u32[]{:S(2)}) %all-to-all-start.4) | async-done | bytes 1572896 | tf_op jit(solution)/shard_map/all_to_all | solution.py:23
  140.2 8.4 %all-to-all-start.2 = ((bf16[8,64,512]{2,1,0:T(8,128)(2,1)}), bf16[8,64,512]{2,1,0:T(8,128)(2,1)S(1)}, u32[]{:S(2)}, u32[]{:S(2)}) async-start(bf16[8,64,512]{2,1,0:T(8,128)(2,1)} %bitcast.126), calls=%async_computation.2 | async-start | bytes 1048576 | tf_op jit(solution)/shard_map/all_to_all | solution.py:23
  149.0 14.1 %all-to-all-done.2 = bf16[8,64,512]{2,1,0:T(8,128)(2,1)S(1)} async-done(((bf16[8,64,512]{2,1,0:T(8,128)(2,1)}), bf16[8,64,512]{2,1,0:T(8,128)(2,1)S(1)}, u32[]{:S(2)}, u32[]{:S(2)}) %all-to-all-start.2) | async-done | bytes 524320 | tf_op jit(solution)/shard_map/all_to_all | solution.py:23
  163.9 11.7 %all-to-all-start.5 = ((bf16[16,48,256]{2,1,0:T(8,128)(2,1)}), bf16[16,48,256]{2,1,0:T(8,128)(2,1)S(1)}, u32[]{:S(2)}, u32[]{:S(2)}) async-start(bf16[16,48,256]{2,1,0:T(8,128)(2,1)} %bitcast.23), calls=%async_computation.5 | async-start | bytes 786432 | tf_op jit(solution)/shard_map/all_to_all | solution.py:23
  176.4 24.6 %all-to-all-done.5 = bf16[16,48,256]{2,1,0:T(8,128)(2,1)S(1)} async-done(((bf16[16,48,256]{2,1,0:T(8,128)(2,1)}), bf16[16,48,256]{2,1,0:T(8,128)(2,1)S(1)}, u32[]{:S(2)}, u32[]{:S(2)}) %all-to-all-start.5) | async-done | bytes 393248 | tf_op jit(solution)/shard_map/all_to_all | solution.py:23
  (51 shorter events, 13.3 us)
Async XLA Ops:
  8.6 35.3 %all-to-all-start = ((bf16[16,32,256]{2,1,0:T(8,128)(2,1)}), bf16[16,32,256]{2,1,0:T(8,128)(2,1)S(1)}, u32[]{:S(2)}, u32[]{:S(2)}) async-start(bf16[16,32,256]{2,1,0:T(8,128)(2,1)} %broadcast_in_dim.12), calls=%async_computation | async-start | bytes 524288 | tf_op jit(solution)/shard_map/all_to_all | solution.py:23
  25.9 4.7 %collective-permute-start = (bf16[8,256]{1,0:T(8,128)(2,1)S(1)}, bf16[8,256]{1,0:T(8,128)(2,1)S(1)}, u32[]{:S(2)}, u32[]{:S(2)}) collective-permute-start(bf16[8,256]{1,0:T(8,128)(2,1)S(1)} %slice.129), channel_id=1, source_target_pairs={{8,0},{16,8},{24,16},{32,24},{40,32},{48,40},{56,48},{64,56},{72,6... | collective-permute-start | bytes 12296 | tf_op jit(solution)/shard_map/ppermute | solution.py:40
  44.8 35.5 %all-to-all-start.3 = ((bf16[8,64,512]{2,1,0:T(8,128)(2,1)}), bf16[8,64,512]{2,1,0:T(8,128)(2,1)S(1)}, u32[]{:S(2)}, u32[]{:S(2)}) async-start(bf16[8,64,512]{2,1,0:T(8,128)(2,1)} %bitcast.10), calls=%async_computation.3 | async-start | bytes 1048576 | tf_op jit(solution)/shard_map/all_to_all | solution.py:23
  51.0 27.1 %all-gather.3.cloned.1.call-start = ((), (), s32[]{:S(2)}) async-start(), calls=%async_computation.6 | async-start | bytes 1392640 | tf_op jit(solution)/shard_map/all_gather | solution.py:42
  51.0 0.7 copy-start.1
  80.2 1.2 copy-start
  81.5 22.4 %all-to-all-start.1 = ((bf16[16,32,1024]{2,1,0:T(8,128)(2,1)}), bf16[16,32,1024]{2,1,0:T(8,128)(2,1)S(1)}, u32[]{:S(2)}, u32[]{:S(2)}) async-start(bf16[16,32,1024]{2,1,0:T(8,128)(2,1)} %broadcast_in_dim.14), calls=%async_computation.1 | async-start | bytes 2097152 | tf_op jit(solution)/shard_map/all_to_all | solution.py:23
  114.9 25.3 %all-to-all-start.4 = ((bf16[16,48,1024]{2,1,0:T(8,128)(2,1)}), bf16[16,48,1024]{2,1,0:T(8,128)(2,1)S(1)}, u32[]{:S(2)}, u32[]{:S(2)}) async-start(bf16[16,48,1024]{2,1,0:T(8,128)(2,1)} %pad_maximum_fusion), calls=%async_computation.4 | async-start | bytes 3145728 | tf_op jit(solution)/shard_map/all_to_all | solution.py:23
  140.2 22.9 %all-to-all-start.2 = ((bf16[8,64,512]{2,1,0:T(8,128)(2,1)}), bf16[8,64,512]{2,1,0:T(8,128)(2,1)S(1)}, u32[]{:S(2)}, u32[]{:S(2)}) async-start(bf16[8,64,512]{2,1,0:T(8,128)(2,1)} %bitcast.126), calls=%async_computation.2 | async-start | bytes 1048576 | tf_op jit(solution)/shard_map/all_to_all | solution.py:23
  163.9 37.1 %all-to-all-start.5 = ((bf16[16,48,256]{2,1,0:T(8,128)(2,1)}), bf16[16,48,256]{2,1,0:T(8,128)(2,1)S(1)}, u32[]{:S(2)}, u32[]{:S(2)}) async-start(bf16[16,48,256]{2,1,0:T(8,128)(2,1)} %bitcast.23), calls=%async_computation.5 | async-start | bytes 786432 | tf_op jit(solution)/shard_map/all_to_all | solution.py:23
Sparse Core Ops, SparseCore 0:
  53.9 24.1 all-gather.2

commit v6 on v2

v6 whole, which is shorter than its diff:
```python
import jax
import jax.numpy as jnp
from jax import lax
from jax.experimental import pallas as pl
from jax.experimental.pallas import tpu as pltpu
from jax.sharding import Mesh, PartitionSpec as P

TAPS = 7
BF = jnp.bfloat16
F32 = jnp.float32
ZH, X, Y, ZL, C = "zh", "x", "y", "zl", "c"


def split_rows(value):
    high = value.astype(BF)
    return jnp.concatenate([high, (value - high.astype(F32)).astype(BF)], 0)


def joined_rows(value):
    half = value.shape[0] // 2
    return value[:half] + value[half:]


def exchange(value, axes):
    return lax.all_to_all(value, axes, split_axis=0, concat_axis=0, tiled=True)


def from_ahead(value, axis, steps):
    count = lax.axis_size(axis)
    return lax.ppermute(value, axis, [(source, (source - steps) % count) for source in range(count)])


def products_kernel(slab_ref, weight_ref, grad_ref, extended_ref, out_ref, featured_ref):
    step = pl.program_id(0)
    slab_len, cols = grad_ref.shape
    nxy = out_ref.shape[0]
    rows = slab_ref.shape[1] // nxy
    products = lax.dot_general(
        slab_ref[...], grad_ref[...], (((0,), (0,)), ((), ())), preferred_element_type=F32
    )
    here = pl.ds(pl.multiple_of(step * rows, rows), rows)
    out_ref[:, here, :] = products.astype(BF).reshape(nxy, rows, cols)
    term = jnp.dot(slab_ref[...], weight_ref[...], preferred_element_type=F32)

    @pl.when(step == 0)
    def _():
        featured_ref[...] = term

    @pl.when(step > 0)
    def _():
        featured_ref[...] += term

    @pl.when(step == pl.num_programs(0) - 1)
    def _():
        featured = featured_ref[...].astype(BF).astype(F32)
        sums = [
            jnp.sum(featured * extended_ref[tap : tap + slab_len, :], axis=0, keepdims=True)
            for tap in range(TAPS)
        ]
        tail = split_rows(jnp.concatenate(sums + [jnp.zeros((1, cols), F32)], 0))
        out_ref[:, pl.num_programs(0) * rows :, :] = jnp.broadcast_to(tail[None], (nxy, 16, cols))


def local_products(slab, weight, grad_bf, extended, nxy, rows):
    slab_len, depth = slab.shape
    cols = weight.shape[1]
    nz = depth // (nxy * rows)
    part = nxy * rows
    return pl.pallas_call(
        products_kernel,
        grid=(nz,),
        in_specs=[
            pl.BlockSpec((slab_len, part), lambda i: (0, i)),
            pl.BlockSpec((part, cols), lambda i: (i, 0)),
            pl.BlockSpec((slab_len, cols), lambda i: (0, 0)),
            pl.BlockSpec(extended.shape, lambda i: (0, 0)),
        ],
        out_specs=pl.BlockSpec((nxy, nz * rows + 16, cols), lambda i: (0, 0, 0)),
        out_shape=jax.ShapeDtypeStruct((nxy, nz * rows + 16, cols), BF),
        scratch_shapes=[pltpu.VMEM((slab_len, cols), F32)],
        compiler_params=pltpu.CompilerParams(vmem_limit_bytes=32 * 1024 * 1024),
        cost_estimate=pl.CostEstimate(
            flops=4 * slab_len * depth * cols, bytes_accessed=4 * slab_len * depth, transcendentals=0
        ),
    )(slab, weight, grad_bf, extended)


def weight_columns(proj_weight):
    rows, cols = proj_weight.shape
    nz = lax.axis_size(ZH)
    nxy = lax.axis_size((X, Y))
    column = lax.all_gather(proj_weight, ZH)
    repeated = jnp.broadcast_to(column[None], (nxy, nz, rows, cols))
    gathered = lax.all_to_all(repeated, (X, Y), split_axis=0, concat_axis=0, tiled=True)
    return gathered.transpose(1, 0, 2, 3).reshape(nz * nxy * rows, cols)


def body(tokens, proj_weight, cotangent, filters):
    nz = lax.axis_size(ZH)
    nxy = lax.axis_size((X, Y))
    nzl = lax.axis_size(ZL)
    ndp = nz * nxy
    rows, cols = proj_weight.shape
    own_tokens, depth = tokens.shape

    slab = lax.all_gather(tokens, (ZL, C), axis=0, tiled=True)
    slab_len = slab.shape[0]
    following = lax.ppermute(
        cotangent[: TAPS - 1], (ZH, X, Y), [(source, source - 1) for source in range(1, ndp)]
    )
    nothing = jnp.zeros((2, cols), BF)
    extended = jnp.concatenate([cotangent, following, nothing], 0).astype(F32)
    grad_feat = jnp.zeros((slab_len, cols), F32)
    for tap in range(TAPS):
        grad_feat = grad_feat + filters[tap] * extended[tap : tap + slab_len]
    grad_bf = grad_feat.astype(BF)

    weight = weight_columns(proj_weight)

    core, chip = lax.axis_index(C), lax.axis_index(ZL)
    by_core = grad_bf.reshape(nzl, 2, own_tokens, cols)
    theirs = lax.dynamic_index_in_dim(by_core, 1 - core, 1, keepdims=False).reshape(-1, cols)
    ours = lax.dynamic_index_in_dim(by_core, core, 1, keepdims=False).reshape(-1, cols)
    contract_cols = (((1,), (1,)), ((), ()))
    for_other = lax.dot_general(theirs, weight, contract_cols, preferred_element_type=F32).astype(BF)
    for_other, grad_late = lax.optimization_barrier((for_other, grad_bf))
    from_other = lax.ppermute(for_other, C, [(0, 1), (1, 0)])

    packed = local_products(slab, weight, grad_late, extended, nxy, rows)
    packed, ours = lax.optimization_barrier((packed, ours))
    arrived = exchange(packed, (X, Y))
    total = jnp.sum(arrived.astype(F32), axis=0)

    here = lax.dot_general(ours, weight, contract_cols, preferred_element_type=F32)
    chip_sum = (here + from_other.astype(F32)).astype(BF)
    chip_sum = chip_sum.reshape(nzl, own_tokens, depth)
    summed = lax.dynamic_index_in_dim(chip_sum, chip, 0, keepdims=False).astype(F32)
    for steps in (2, 1, 3):
        outgoing = lax.dynamic_index_in_dim(chip_sum, (chip - steps) % nzl, 0, keepdims=False)
        summed = summed + from_ahead(outgoing, ZL, steps).astype(F32)
    input_grad = summed.astype(BF)

    blocks = total[: nz * rows].astype(BF).reshape(nz, rows, cols)
    tail = split_rows(joined_rows(total[nz * rows :]))
    packed = jnp.concatenate([blocks, jnp.broadcast_to(tail[None], (nz, 16, cols))], 1)
    arrived = exchange(packed, ZH)
    arrived, input_grad = lax.optimization_barrier((arrived, input_grad))
    total = jnp.sum(arrived.astype(F32), axis=0)
    weight_grad = total[:rows].astype(BF)
    filter_grad = joined_rows(total[rows:])[:TAPS]
    return input_grad, weight_grad, filter_grad


def solution(mesh):
    fine = Mesh(mesh.devices.reshape(4, 4, 4, 4, 2), (ZH, X, Y, ZL, C))
    dp, seq = (ZH, X, Y), (ZL, C)
    in_specs = (P(dp + seq, None), P(dp, seq), P(dp, seq), P(None, seq))
    out_specs = (P(dp + seq, None), P(dp, seq), P(None, seq))
    return jax.shard_map(body, mesh=fine, in_specs=in_specs, out_specs=out_specs, check_vma=False)
```

time: 128 us -> 121 us (0.945)
  the two profiles are of different devices: /device:TPU:1 before, /device:TPU:40 now
where the time goes in v6:
time: 121 us
  starting transfers between devices  35.3 us (29%)
  waiting for transfers between devices  31.9 us (26%)
  blocking collectives  25.1 us (21%)
  between operations  14.2 us (12%)
  other arithmetic  3.8 us (3%)
  Pallas kernels  3.77 us (3%)
  local copies, waits for them, and re-layouts  3.57 us (3%)
  matrix products  3.14 us (3%)
    all_gather x1, blocking collectives, weight_columns(): column = lax.all_gather(proj_weight, ZH)  25.1 us
    all_to_all x2, waiting for transfers between devices, exchange(): return lax.all_to_all(value, axes, split_axis=0, concat_axis=0, tiled=True)  15.9 us
    all_to_all x2, starting transfers between devices, exchange(): return lax.all_to_all(value, axes, split_axis=0, concat_axis=0, tiled=True)  14.7 us
    ppermute x3, starting transfers between devices, from_ahead(): lax.ppermute(value, axis, [(source, (source - steps) % count) for source...  9.26 us
    all_to_all x1, starting transfers between devices, weight_columns(): lax.all_to_all(repeated, (X, Y), split_axis=0, concat_axis=0, tiled=True)  7.39 us
    ppermute x3, waiting for transfers between devices, from_ahead(): lax.ppermute(value, axis, [(source, (source - steps) % count) for source...  5.28 us
    ppermute x1, waiting for transfers between devices, body(): lax.ppermute(cotangent[:TAPS - 1], (ZH, X, Y), [(source, source - 1) for...  5 us
    all_to_all x1, waiting for transfers between devices, weight_columns(): lax.all_to_all(repeated, (X, Y), split_axis=0, concat_axis=0, tiled=True)  4.99 us
  transfers between devices with their start and end apart: 9, of which 5 were waited for; matrix products, arithmetic and copies ran while one was open for 6% of the time, Pallas kernels for 3%

profile of v6, /device:TPU:40, one launch (start us, length us, event | category | flops | bytes accessed | tf_op | source)
XLA Modules:
  0.0 120.8 jit_solution(2125980125162230878)
XLA Ops:
  7.2 0.7 all-gather.3.cloned.1.call-update
  7.9 25.1 %all-gather = bf16[128,256]{1,0:T(8,128)(2,1)S(1)} all-gather(bf16[32,256]{1,0:T(8,128)(2,1)} %param.5), channel_id=2, replica_groups=mesh['zh'=4,'x'=4,'y'=4,'zl'=4,'c'=2] {'zh'}, dimensions={0}, use_global_device_ids=true | all-gather | bytes 81920 | tf_op jit(solution)/shard_map/all_gather | solution.py:92
  33.0 1.1 broadcast_in_dim.6
  34.1 7.4 %all-to-all-start = ((bf16[16,4,32,256]{3,2,1,0:T(8,128)(2,1)}), bf16[16,4,32,256]{3,2,1,0:T(8,128)(2,1)S(1)}, u32[]{:S(2)}, u32[]{:S(2)}) async-start(bf16[16,4,32,256]{3,2,1,0:T(8,128)(2,1)} %broadcast_in_dim.6), calls=%async_computation | async-start | bytes 2097152 | tf_op jit(solution)/shard_map/all_to_all | solution.py:94
  41.5 2.0 %collective-permute-start = (bf16[6,256]{1,0:T(8,128)(2,1)S(1)}, bf16[6,256]{1,0:T(8,128)(2,1)S(1)}, u32[]{:S(2)}, u32[]{:S(2)}) collective-permute-start(bf16[6,256]{1,0:T(8,128)(2,1)S(1)} %slice.75), channel_id=1, source_target_pairs={{8,0},{16,8},{24,16},{32,24},{40,32},{48,40},{56,48},{64,56},{72,6... | collective-permute-start | bytes 9224 | tf_op jit(solution)/shard_map/ppermute | solution.py:108
  43.7 5.0 %collective-permute-done = bf16[6,256]{1,0:T(8,128)(2,1)S(1)} collective-permute-done((bf16[6,256]{1,0:T(8,128)(2,1)S(1)}, bf16[6,256]{1,0:T(8,128)(2,1)S(1)}, u32[]{:S(2)}, u32[]{:S(2)}) %collective-permute-start) | collective-permute-done | bytes 3104 | tf_op jit(solution)/shard_map/ppermute | solution.py:108
  49.3 5.0 %all-to-all-done = bf16[16,4,32,256]{3,2,1,0:T(8,128)(2,1)S(1)} async-done(((bf16[16,4,32,256]{3,2,1,0:T(8,128)(2,1)}), bf16[16,4,32,256]{3,2,1,0:T(8,128)(2,1)S(1)}, u32[]{:S(2)}, u32[]{:S(2)}) %all-to-all-start) | async-done | bytes 1048608 | tf_op jit(solution)/shard_map/all_to_all | solution.py:94
  54.4 1.4 %convolution_convert_fusion = bf16[256,2048]{1,0:T(8,128)(2,1)} fusion(bf16[256,256]{1,0:T(8,128)(2,1)S(1)} %bitcast.36, bf16[2048,256]{1,0:T(8,128)(2,1)S(1)} %bitcast.28), kind=kOutput, calls=%fused_computation | convolution fusion | flops 268959744 | bytes 2228224 | tf_op jit(solution)/shard_map/dot_general | solution.py:125
  55.8 1.9 %collective-permute-start.1 = (bf16[256,2048]{1,0:T(8,128)(2,1)}, bf16[256,2048]{1,0:T(8,128)(2,1)}, u32[]{:S(2)}, u32[]{:S(2)}) collective-permute-start(bf16[256,2048]{1,0:T(8,128)(2,1)} %convolution_convert_fusion), channel_id=1, source_target_pairs={{0,1},{1,0},{2,3},{3,2},{4,5},{5,4},{6,7},{7,6},{8,9},{9,8},{10,11... | collective-permute-start | bytes 3145736 | tf_op jit(solution)/shard_map/ppermute | solution.py:127
  57.8 1.6 %copy-done = bf16[512,2048]{1,0:T(8,128)(2,1)S(1)} copy-done((bf16[512,2048]{1,0:T(8,128)(2,1)S(1)}, bf16[512,2048]{1,0:T(8,128)(2,1)}, u32[]{:S(2)}) %copy-start) | copy-done | bytes 2097176
  59.4 3.8 %shard_map.67 = bf16[16,144,256]{2,1,0:T(8,128)(2,1)} custom-call(bf16[512,2048]{1,0:T(8,128)(2,1)S(1)} %copy-done, bf16[2048,256]{1,0:T(8,128)(2,1)S(1)} %bitcast.29, bf16[512,256]{1,0:T(8,128)(2,1)S(1)} %fusion.1.grad_ref, f32[520,256]{1,0:T(8,128)S(1)} %maximum_convert_fusion.extended_ref), custom_call_target="tpu_custom_call" | custom-call | flops 1073741824 | bytes 4194304 | tf_op jit(solution)/shard_map/pallas_call | solution.py:69
  63.1 8.1 %all-to-all-start.1 = ((bf16[16,144,256]{2,1,0:T(8,128)(2,1)}), bf16[16,144,256]{2,1,0:T(8,128)(2,1)S(1)}, u32[]{:S(2)}, u32[]{:S(2)}) async-start(bf16[16,144,256]{2,1,0:T(8,128)(2,1)} %shard_map.67), calls=%async_computation.1 | async-start | bytes 2359296 | tf_op jit(solution)/shard_map/all_to_all | solution.py:25
  71.3 1.7 %add_convert_fusion = bf16[256,2048]{1,0:T(8,128)(2,1)S(1)} fusion(bf16[256,2048]{1,0:T(8,128)(2,1)} %collective-permute-done.1, bf16[256,256]{1,0:T(8,128)(2,1)S(1)} %bitcast.35, bf16[2048,256]{1,0:T(8,128)(2,1)S(1)} %bitcast.30), kind=kOutput, calls=%fused_computation.2 | convolution fusion | flops 270008320 | bytes 3276800 | tf_op jit(solution)/shard_map/dot_general | solution.py:134
  73.1 3.4 %collective-permute-start.2 = (bf16[64,2048]{1,0:T(8,128)(2,1)S(1)}, bf16[64,2048]{1,0:T(8,128)(2,1)S(1)}, u32[]{:S(2)}, u32[]{:S(2)}) collective-permute-start(bf16[64,2048]{1,0:T(8,128)(2,1)S(1)} %get-tuple-element.17), channel_id=1, source_target_pairs={{0,4},{2,6},{4,0},{6,2},{1,5},{3,7},{5,1},{7,3},{8,12},{10,14},{12... | collective-permute-start | bytes 786440 | tf_op jit(solution)/shard_map/ppermute | solution.py:30
  76.5 3.1 %collective-permute-start.3 = (bf16[64,2048]{1,0:T(8,128)(2,1)S(1)}, bf16[64,2048]{1,0:T(8,128)(2,1)S(1)}, u32[]{:S(2)}, u32[]{:S(2)}) collective-permute-start(bf16[64,2048]{1,0:T(8,128)(2,1)S(1)} %get-tuple-element.19), channel_id=1, source_target_pairs={{0,6},{2,0},{4,2},{6,4},{1,7},{3,1},{5,3},{7,5},{8,14},{10,8},{12,... | collective-permute-start | bytes 786440 | tf_op jit(solution)/shard_map/ppermute | solution.py:30
  79.6 2.7 %collective-permute-start.4 = (bf16[64,2048]{1,0:T(8,128)(2,1)S(1)}, bf16[64,2048]{1,0:T(8,128)(2,1)S(1)}, u32[]{:S(2)}, u32[]{:S(2)}) collective-permute-start(bf16[64,2048]{1,0:T(8,128)(2,1)S(1)} %get-tuple-element.18), channel_id=1, source_target_pairs={{0,2},{2,4},{4,6},{6,0},{1,3},{3,5},{5,7},{7,1},{8,10},{10,12},{12... | collective-permute-start | bytes 786440 | tf_op jit(solution)/shard_map/ppermute | solution.py:30
  82.4 7.6 %all-to-all-done.1 = bf16[16,144,256]{2,1,0:T(8,128)(2,1)S(1)} async-done(((bf16[16,144,256]{2,1,0:T(8,128)(2,1)}), bf16[16,144,256]{2,1,0:T(8,128)(2,1)S(1)}, u32[]{:S(2)}, u32[]{:S(2)}) %all-to-all-start.1) | async-done | bytes 1179680 | tf_op jit(solution)/shard_map/all_to_all | solution.py:25
  90.2 0.7 pad_maximum_fusion
  90.8 6.5 %all-to-all-start.2 = ((bf16[4,48,256]{2,1,0:T(8,128)(2,1)}), bf16[4,48,256]{2,1,0:T(8,128)(2,1)S(1)}, u32[]{:S(2)}, u32[]{:S(2)}) async-start(bf16[4,48,256]{2,1,0:T(8,128)(2,1)} %pad_maximum_fusion), calls=%async_computation.2 | async-start | bytes 196608 | tf_op jit(solution)/shard_map/all_to_all | solution.py:25
  97.4 5.3 %collective-permute-done.3 = bf16[64,2048]{1,0:T(8,128)(2,1)S(1)} collective-permute-done((bf16[64,2048]{1,0:T(8,128)(2,1)S(1)}, bf16[64,2048]{1,0:T(8,128)(2,1)S(1)}, u32[]{:S(2)}, u32[]{:S(2)}) %collective-permute-start.3) | collective-permute-done | bytes 262176 | tf_op jit(solution)/shard_map/ppermute | solution.py:30
  102.7 1.8 %fusion.9 = bf16[64,2048]{1,0:T(8,128)(2,1)} fusion(bf16[64,2048]{1,0:T(8,128)(2,1)S(1)} %collective-permute-done.4, bf16[64,2048]{1,0:T(8,128)(2,1)S(1)} %collective-permute-done.3, bf16[64,2048]{1,0:T(8,128)(2,1)S(1)} %collective-permute-done.2, bf16[4,64,2048]{2,1,0:T(8,128)(2,1)} %bitcast.33, s32[]{:T(128)S(6)} %select_n.37), kind=kLoop, calls=%fused_computation.20 | loop fusion | flops 1048576 | bytes 1310724 | tf_op jit(solution)/shard_map/convert_element_type | solution.py:141
  104.4 8.3 %all-to-all-done.2 = bf16[4,48,256]{2,1,0:T(8,128)(2,1)S(1)} async-done(((bf16[4,48,256]{2,1,0:T(8,128)(2,1)}), bf16[4,48,256]{2,1,0:T(8,128)(2,1)S(1)}, u32[]{:S(2)}, u32[]{:S(2)}) %all-to-all-start.2) | async-done | bytes 98336 | tf_op jit(solution)/shard_map/all_to_all | solution.py:25
  112.8 0.6 slice.159
  113.4 0.6 slice_add_fusion
  (28 shorter events, 1.1 us)
Async XLA Ops:
  7.2 34.4 %copy-start.2 = (bf16[512,256]{1,0:T(8,128)(2,1)S(1)}, bf16[512,256]{1,0:T(8,128)(2,1)}, u32[]{:S(2)}) copy-start(bf16[512,256]{1,0:T(8,128)(2,1)} %param.6) | copy-start | bytes 786436
  7.2 36.4 %copy-start.3 = (f32[7,256]{1,0:T(8,128)S(1)}, f32[7,256]{1,0:T(8,128)}, u32[]{:S(2)}) copy-start(f32[7,256]{1,0:T(8,128)} %param.7) | copy-start | bytes 21508
  7.2 50.6 %all-gather.3.cloned.1.call-start = ((), (), s32[]{:S(2)}) async-start(), calls=%async_computation.3 | async-start | bytes 2359296 | tf_op jit(solution)/shard_map/all_gather | solution.py:106
  34.1 20.2 %all-to-all-start = ((bf16[16,4,32,256]{3,2,1,0:T(8,128)(2,1)}), bf16[16,4,32,256]{3,2,1,0:T(8,128)(2,1)S(1)}, u32[]{:S(2)}, u32[]{:S(2)}) async-start(bf16[16,4,32,256]{3,2,1,0:T(8,128)(2,1)} %broadcast_in_dim.6), calls=%async_computation | async-start | bytes 2097152 | tf_op jit(solution)/shard_map/all_to_all | solution.py:94
  41.5 7.1 %collective-permute-start = (bf16[6,256]{1,0:T(8,128)(2,1)S(1)}, bf16[6,256]{1,0:T(8,128)(2,1)S(1)}, u32[]{:S(2)}, u32[]{:S(2)}) collective-permute-start(bf16[6,256]{1,0:T(8,128)(2,1)S(1)} %slice.75), channel_id=1, source_target_pairs={{8,0},{16,8},{24,16},{32,24},{40,32},{48,40},{56,48},{64,56},{72,6... | collective-permute-start | bytes 9224 | tf_op jit(solution)/shard_map/ppermute | solution.py:108
  55.8 15.5 %collective-permute-start.1 = (bf16[256,2048]{1,0:T(8,128)(2,1)}, bf16[256,2048]{1,0:T(8,128)(2,1)}, u32[]{:S(2)}, u32[]{:S(2)}) collective-permute-start(bf16[256,2048]{1,0:T(8,128)(2,1)} %convolution_convert_fusion), channel_id=1, source_target_pairs={{0,1},{1,0},{2,3},{3,2},{4,5},{5,4},{6,7},{7,6},{8,9},{9,8},{10,11... | collective-permute-start | bytes 3145736 | tf_op jit(solution)/shard_map/ppermute | solution.py:127
  57.8 1.6 %copy-start = (bf16[512,2048]{1,0:T(8,128)(2,1)S(1)}, bf16[512,2048]{1,0:T(8,128)(2,1)}, u32[]{:S(2)}) copy-start(bf16[512,2048]{1,0:T(8,128)(2,1)} %all-gather.3.cloned.1.call-done.slab_ref) | copy-start | bytes 6291460
  63.1 26.8 %all-to-all-start.1 = ((bf16[16,144,256]{2,1,0:T(8,128)(2,1)}), bf16[16,144,256]{2,1,0:T(8,128)(2,1)S(1)}, u32[]{:S(2)}, u32[]{:S(2)}) async-start(bf16[16,144,256]{2,1,0:T(8,128)(2,1)} %shard_map.67), calls=%async_computation.1 | async-start | bytes 2359296 | tf_op jit(solution)/shard_map/all_to_all | solution.py:25
  73.0 6.6 %copy-start.1 = (bf16[256,2048]{1,0:T(8,128)(2,1)}, bf16[256,2048]{1,0:T(8,128)(2,1)S(1)}, u32[]{:S(2)}) copy-start(bf16[256,2048]{1,0:T(8,128)(2,1)S(1)} %add_convert_fusion) | copy-start | bytes 3145732
  73.1 24.3 %collective-permute-start.2 = (bf16[64,2048]{1,0:T(8,128)(2,1)S(1)}, bf16[64,2048]{1,0:T(8,128)(2,1)S(1)}, u32[]{:S(2)}, u32[]{:S(2)}) collective-permute-start(bf16[64,2048]{1,0:T(8,128)(2,1)S(1)} %get-tuple-element.17), channel_id=1, source_target_pairs={{0,4},{2,6},{4,0},{6,2},{1,5},{3,7},{5,1},{7,3},{8,12},{10,14},{12... | collective-permute-start | bytes 786440 | tf_op jit(solution)/shard_map/ppermute | solution.py:30
  76.5 26.2 %collective-permute-start.3 = (bf16[64,2048]{1,0:T(8,128)(2,1)S(1)}, bf16[64,2048]{1,0:T(8,128)(2,1)S(1)}, u32[]{:S(2)}, u32[]{:S(2)}) collective-permute-start(bf16[64,2048]{1,0:T(8,128)(2,1)S(1)} %get-tuple-element.19), channel_id=1, source_target_pairs={{0,6},{2,0},{4,2},{6,4},{1,7},{3,1},{5,3},{7,5},{8,14},{10,8},{12,... | collective-permute-start | bytes 786440 | tf_op jit(solution)/shard_map/ppermute | solution.py:30
  79.6 23.0 %collective-permute-start.4 = (bf16[64,2048]{1,0:T(8,128)(2,1)S(1)}, bf16[64,2048]{1,0:T(8,128)(2,1)S(1)}, u32[]{:S(2)}, u32[]{:S(2)}) collective-permute-start(bf16[64,2048]{1,0:T(8,128)(2,1)S(1)} %get-tuple-element.18), channel_id=1, source_target_pairs={{0,2},{2,4},{4,6},{6,0},{1,3},{3,5},{5,7},{7,1},{8,10},{10,12},{12... | collective-permute-start | bytes 786440 | tf_op jit(solution)/shard_map/ppermute | solution.py:30
  90.8 21.9 %all-to-all-start.2 = ((bf16[4,48,256]{2,1,0:T(8,128)(2,1)}), bf16[4,48,256]{2,1,0:T(8,128)(2,1)S(1)}, u32[]{:S(2)}, u32[]{:S(2)}) async-start(bf16[4,48,256]{2,1,0:T(8,128)(2,1)} %pad_maximum_fusion), calls=%async_computation.2 | async-start | bytes 196608 | tf_op jit(solution)/shard_map/all_to_all | solution.py:25
Sparse Core Ops, SparseCore 0:
  10.1 45.4 all-gather.2

commit v7 on v6

v7 whole, which is shorter than its diff:
```python
import jax
import jax.numpy as jnp
from jax import lax
from jax.experimental import pallas as pl
from jax.experimental.pallas import tpu as pltpu
from jax.sharding import Mesh, PartitionSpec as P

TAPS = 7
VMEM_BYTES = 12 * 1024 * 1024
BF = jnp.bfloat16
F32 = jnp.float32
ZH, X, Y, ZL, C = "zh", "x", "y", "zl", "c"


def split_rows(value):
    high = value.astype(BF)
    return jnp.concatenate([high, (value - high.astype(F32)).astype(BF)], 0)


def joined_rows(value):
    half = value.shape[0] // 2
    return value[:half] + value[half:]


def exchange(value, axes):
    return lax.all_to_all(value, axes, split_axis=0, concat_axis=0, tiled=True)


def from_ahead(value, axis, steps):
    count = lax.axis_size(axis)
    return lax.ppermute(value, axis, [(source, (source - steps) % count) for source in range(count)])


def in_order(place_ref, chunks, block_ref):
    count = chunks[0].shape[0]
    for index, chunk in enumerate(chunks):
        block_ref[pl.ds(pl.multiple_of(place_ref[index] * count, count), count), :] = chunk[...]


def products_kernel(place_ref, *refs):
    chunks, (grad_ref, out_ref, block_ref) = refs[:-3], refs[-3:]
    nxy, cols = out_ref.shape[0], grad_ref.shape[1]
    rows = chunks[0].shape[1] // nxy
    in_order(place_ref, chunks, block_ref)
    products = lax.dot_general(
        block_ref[...], grad_ref[...], (((0,), (0,)), ((), ())), preferred_element_type=F32
    )
    here = pl.ds(pl.multiple_of(pl.program_id(0) * rows, rows), rows)
    out_ref[:, here, :] = products.astype(BF).reshape(nxy, rows, cols)

    @pl.when(pl.program_id(0) == 0)
    def _():
        out_ref[:, pl.num_programs(0) * rows :, :] = jnp.zeros((nxy, 16, cols), BF)


def weight_products(places, chunks, grad_bf, nxy, rows):
    slab_len, cols = grad_bf.shape
    step_rows, depth = chunks[0].shape
    part = nxy * rows
    nz = depth // part
    return pl.pallas_call(
        products_kernel,
        grid_spec=pltpu.PrefetchScalarGridSpec(
            num_scalar_prefetch=1,
            grid=(nz,),
            in_specs=[pl.BlockSpec((step_rows, part), lambda i, _: (0, i)) for _ in chunks]
            + [pl.BlockSpec((slab_len, cols), lambda i, _: (0, 0))],
            out_specs=pl.BlockSpec((nxy, nz * rows + 16, cols), lambda i, _: (0, 0, 0)),
            scratch_shapes=[pltpu.VMEM((slab_len, part), BF)],
        ),
        out_shape=jax.ShapeDtypeStruct((nxy, nz * rows + 16, cols), BF),
        compiler_params=pltpu.CompilerParams(vmem_limit_bytes=VMEM_BYTES),
        cost_estimate=pl.CostEstimate(
            flops=2 * slab_len * depth * cols, bytes_accessed=6 * slab_len * depth, transcendentals=0
        ),
    )(places, *chunks, grad_bf)


def taps_kernel(place_ref, *refs):
    chunks, (weight_ref, extended_ref, _, out_ref, block_ref, featured_ref) = refs[:-6], refs[-6:]
    step = pl.program_id(0)
    slab_len, cols = featured_ref.shape
    in_order(place_ref, chunks, block_ref)
    term = jnp.dot(block_ref[...], weight_ref[...], preferred_element_type=F32)

    @pl.when(step == 0)
    def _():
        featured_ref[...] = term

    @pl.when(step > 0)
    def _():
        featured_ref[...] += term

    @pl.when(step == pl.num_programs(0) - 1)
    def _():
        featured = featured_ref[...].astype(BF).astype(F32)
        sums = [
            jnp.sum(featured * extended_ref[tap : tap + slab_len, :], axis=0, keepdims=True)
            for tap in range(TAPS)
        ]
        tail = split_rows(jnp.concatenate(sums + [jnp.zeros((1, cols), F32)], 0))
        out_ref[...] = jnp.broadcast_to(tail[None], out_ref.shape)


def with_tap_sums(packed, places, chunks, weight, extended):
    step_rows, depth = chunks[0].shape
    slab_len, cols = step_rows * len(chunks), weight.shape[1]
    steps = 4
    part = depth // steps
    nxy, packed_rows, _ = packed.shape
    last = packed_rows // 16 - 1
    return pl.pallas_call(
        taps_kernel,
        grid_spec=pltpu.PrefetchScalarGridSpec(
            num_scalar_prefetch=1,
            grid=(steps,),
            in_specs=[pl.BlockSpec((step_rows, part), lambda i, _: (0, i)) for _ in chunks]
            + [
                pl.BlockSpec((part, cols), lambda i, _: (i, 0)),
                pl.BlockSpec(extended.shape, lambda i, _: (0, 0)),
                pl.BlockSpec((1, 16, cols), lambda i, _: (0, last, 0)),
            ],
            out_specs=pl.BlockSpec((nxy, 16, cols), lambda i, _: (0, last, 0)),
            scratch_shapes=[pltpu.VMEM((slab_len, part), BF), pltpu.VMEM((slab_len, cols), F32)],
        ),
        out_shape=jax.ShapeDtypeStruct(packed.shape, BF),
        input_output_aliases={len(chunks) + 3: 0},
        compiler_params=pltpu.CompilerParams(vmem_limit_bytes=VMEM_BYTES),
        cost_estimate=pl.CostEstimate(
            flops=2 * slab_len * depth * cols, bytes_accessed=3 * slab_len * depth, transcendentals=0
        ),
    )(places, *chunks, weight, extended, packed)


def spread(value, axes):
    return exchange(jnp.broadcast_to(value[None], (lax.axis_size(axes),) + value.shape), axes)


def swap(value):
    return lax.ppermute(value, C, [(0, 1), (1, 0)])


def weight_columns(proj_weight):
    rows, cols = proj_weight.shape
    nz, nxy = lax.axis_size(ZH), lax.axis_size((X, Y))
    gathered = spread(spread(proj_weight, ZH).reshape(nz * rows, cols), (X, Y))
    return gathered.reshape(nxy, nz, rows, cols).transpose(1, 0, 2, 3).reshape(nz * nxy * rows, cols)


def body(tokens, proj_weight, cotangent, filters):
    nz = lax.axis_size(ZH)
    nxy = lax.axis_size((X, Y))
    nzl = lax.axis_size(ZL)
    ndp = nz * nxy
    rows, cols = proj_weight.shape
    own_tokens, depth = tokens.shape

    slab_len = cotangent.shape[0]
    core, chip = lax.axis_index(C), lax.axis_index(ZL)
    direct = [tokens] + [None] * (nzl - 1)
    for steps in (2, 1, 3):
        direct[steps] = from_ahead(tokens, ZL, steps)
    sources = (chip + jnp.arange(nzl)) % nzl
    places = jnp.concatenate([2 * sources + core, 2 * sources + 1 - core]).astype(jnp.int32)
    following = lax.ppermute(
        cotangent[: TAPS - 1], (ZH, X, Y), [(source, source - 1) for source in range(1, ndp)]
    )
    nothing = jnp.zeros((2, cols), BF)
    extended = jnp.concatenate([cotangent, following, nothing], 0).astype(F32)
    grad_feat = jnp.zeros((slab_len, cols), F32)
    for tap in range(TAPS):
        grad_feat = grad_feat + filters[tap] * extended[tap : tap + slab_len]
    grad_bf = grad_feat.astype(BF)

    weight = weight_columns(proj_weight)
    chunks = direct + [swap(value) for value in direct]
    packed = weight_products(places, chunks, grad_bf, nxy, rows)
    packed = with_tap_sums(packed, places, chunks, weight, extended)
    packed, grad_late = lax.optimization_barrier((packed, grad_bf))
    total = jnp.sum(exchange(packed, (X, Y)).astype(F32), axis=0)

    by_core = grad_late.reshape(nzl, 2, own_tokens, cols)
    theirs = lax.dynamic_index_in_dim(by_core, 1 - core, 1, keepdims=False).reshape(-1, cols)
    ours = lax.dynamic_index_in_dim(by_core, core, 1, keepdims=False).reshape(-1, cols)
    contract_cols = (((1,), (1,)), ((), ()))
    for_other = lax.dot_general(theirs, weight, contract_cols, preferred_element_type=F32).astype(BF)
    from_other = swap(for_other)
    here = lax.dot_general(ours, weight, contract_cols, preferred_element_type=F32)
    chip_sum = (here + from_other.astype(F32)).astype(BF)
    chip_sum = chip_sum.reshape(nzl, own_tokens, depth)
    summed = lax.dynamic_index_in_dim(chip_sum, chip, 0, keepdims=False).astype(F32)
    for steps in (2, 1, 3):
        outgoing = lax.dynamic_index_in_dim(chip_sum, (chip - steps) % nzl, 0, keepdims=False)
        summed = summed + from_ahead(outgoing, ZL, steps).astype(F32)
    input_grad = summed.astype(BF)

    blocks = total[: nz * rows].astype(BF).reshape(nz, rows, cols)
    tail = split_rows(joined_rows(total[nz * rows :]))
    packed = jnp.concatenate([blocks, jnp.broadcast_to(tail[None], (nz, 16, cols))], 1)
    arrived = exchange(packed, ZH)
    arrived, input_grad = lax.optimization_barrier((arrived, input_grad))
    total = jnp.sum(arrived.astype(F32), axis=0)
    weight_grad = total[:rows].astype(BF)
    filter_grad = joined_rows(total[rows:])[:TAPS]
    return input_grad, weight_grad, filter_grad


def solution(mesh):
    fine = Mesh(mesh.devices.reshape(4, 4, 4, 4, 2), (ZH, X, Y, ZL, C))
    dp, seq = (ZH, X, Y), (ZL, C)
    in_specs = (P(dp + seq, None), P(dp, seq), P(dp, seq), P(None, seq))
    out_specs = (P(dp + seq, None), P(dp, seq), P(None, seq))
    return jax.shard_map(body, mesh=fine, in_specs=in_specs, out_specs=out_specs, check_vma=False)
```

time: 121 us -> 123 us (1.017)
  the two profiles are of different devices: /device:TPU:40 before, /device:TPU:1 now
where the time goes in v7:
time: 123 us; the launch traced here: 120 us
  starting transfers between devices  78.5 us (64%)
  waiting for transfers between devices  20.9 us (17%)
  Pallas kernels  7.54 us (6%)
  local copies, waits for them, and re-layouts  5.31 us (4%)
  other arithmetic  3.9 us (3%)
  matrix products  3.13 us (3%)
    all_to_all x4, starting transfers between devices, exchange(): return lax.all_to_all(value, axes, split_axis=0, concat_axis=0, tiled=True)  43.6 us
    all_to_all x4, waiting for transfers between devices, exchange(): return lax.all_to_all(value, axes, split_axis=0, concat_axis=0, tiled=True)  17.5 us
    ppermute x6, starting transfers between devices, from_ahead(): lax.ppermute(value, axis, [(source, (source - steps) % count) for source...  16.9 us
    ppermute x5, starting transfers between devices, swap(): return lax.ppermute(value, C, [(0, 1), (1, 0)])  16.6 us
    pallas_call x1, Pallas kernels, with_tap_sums(): pl.pallas_call(taps_kernel, grid_spec=pltpu.PrefetchScalarGridSpec(num_sc...  4.13 us
    pallas_call x1, Pallas kernels, weight_products(): pl.pallas_call(products_kernel, grid_spec=pltpu.PrefetchScalarGridSpec(nu...  3.41 us
    ppermute x6, waiting for transfers between devices, from_ahead(): lax.ppermute(value, axis, [(source, (source - steps) % count) for source...  2.57 us
  transfers between devices with their start and end apart: 16, of which 4 were waited for; matrix products, arithmetic and copies ran while one was open for 6% of the time, Pallas kernels for 3%

profile of v7, /device:TPU:1, one launch (start us, length us, event | category | flops | bytes accessed | tf_op | source)
XLA Modules:
  0.0 120.3 jit_solution(4012344812048373499)
XLA Ops:
  2.0 15.6 %all-to-all-start = ((bf16[4,32,256]{2,1,0:T(8,128)(2,1)}), bf16[4,32,256]{2,1,0:T(8,128)(2,1)S(1)}, u32[]{:S(2)}, u32[]{:S(2)}) async-start(bf16[4,32,256]{2,1,0:T(8,128)(2,1)} %broadcast_in_dim.10), calls=%async_computation | async-start | bytes 131072 | tf_op jit(solution)/shard_map/all_to_all | solution.py:26
  17.6 3.5 %collective-permute-start = (bf16[64,2048]{1,0:T(8,128)(2,1)}, bf16[64,2048]{1,0:T(8,128)(2,1)S(1)}, u32[]{:S(2)}, u32[]{:S(2)}) collective-permute-start(bf16[64,2048]{1,0:T(8,128)(2,1)} %refs_0_.3), channel_id=1, source_target_pairs={{0,6},{2,0},{4,2},{6,4},{1,7},{3,1},{5,3},{7,5},{8,14},{10,8},{12,... | collective-permute-start | bytes 786440 | tf_op jit(solution)/shard_map/ppermute | solution.py:31
  21.2 2.2 %collective-permute-start.1 = (bf16[64,2048]{1,0:T(8,128)(2,1)}, bf16[64,2048]{1,0:T(8,128)(2,1)S(1)}, u32[]{:S(2)}, u32[]{:S(2)}) collective-permute-start(bf16[64,2048]{1,0:T(8,128)(2,1)} %refs_0_.3), channel_id=1, source_target_pairs={{0,4},{2,6},{4,0},{6,2},{1,5},{3,7},{5,1},{7,3},{8,12},{10,14},{12... | collective-permute-start | bytes 786440 | tf_op jit(solution)/shard_map/ppermute | solution.py:31
  23.4 2.6 %collective-permute-start.2 = (bf16[64,2048]{1,0:T(8,128)(2,1)}, bf16[64,2048]{1,0:T(8,128)(2,1)S(1)}, u32[]{:S(2)}, u32[]{:S(2)}) collective-permute-start(bf16[64,2048]{1,0:T(8,128)(2,1)} %refs_0_.3), channel_id=1, source_target_pairs={{0,2},{2,4},{4,6},{6,0},{1,3},{3,5},{5,7},{7,1},{8,10},{10,12},{12... | collective-permute-start | bytes 786440 | tf_op jit(solution)/shard_map/ppermute | solution.py:31
  26.0 3.7 %collective-permute-start.3 = (bf16[64,2048]{1,0:T(8,128)(2,1)}, bf16[64,2048]{1,0:T(8,128)(2,1)S(1)}, u32[]{:S(2)}, u32[]{:S(2)}) collective-permute-start(bf16[64,2048]{1,0:T(8,128)(2,1)} %refs_0_.3), channel_id=1, source_target_pairs={{0,1},{1,0},{2,3},{3,2},{4,5},{5,4},{6,7},{7,6},{8,9},{9,8},{10,11... | collective-permute-start | bytes 786440 | tf_op jit(solution)/shard_map/ppermute | solution.py:140
  32.8 7.8 %all-to-all-start.1 = ((bf16[16,128,256]{2,1,0:T(8,128)(2,1)}), bf16[16,128,256]{2,1,0:T(8,128)(2,1)}, u32[]{:S(2)}, u32[]{:S(2)}) async-start(bf16[16,128,256]{2,1,0:T(8,128)(2,1)} %broadcast_in_dim.24), calls=%async_computation.1 | async-start | bytes 2097152 | tf_op jit(solution)/shard_map/all_to_all | solution.py:26
  40.9 2.5 %collective-permute-start.4 = (bf16[64,2048]{1,0:T(8,128)(2,1)S(1)}, bf16[64,2048]{1,0:T(8,128)(2,1)S(1)}, u32[]{:S(2)}, u32[]{:S(2)}) collective-permute-start(bf16[64,2048]{1,0:T(8,128)(2,1)S(1)} %collective-permute-done.refs_1_), channel_id=1, source_target_pairs={{0,1},{1,0},{2,3},{3,2},{4,5},{5,4},{6,7},{7,6},{8,9},{9,8},{10,11... | collective-permute-start | bytes 786440 | tf_op jit(solution)/shard_map/ppermute | solution.py:140
  43.3 2.6 %collective-permute-done.1.refs_2_ = bf16[64,2048]{1,0:T(8,128)(2,1)S(1)} collective-permute-done((bf16[64,2048]{1,0:T(8,128)(2,1)}, bf16[64,2048]{1,0:T(8,128)(2,1)S(1)}, u32[]{:S(2)}, u32[]{:S(2)}) %collective-permute-start.1) | collective-permute-done | bytes 262176 | tf_op jit(solution)/shard_map/ppermute | solution.py:31
  45.9 3.7 %collective-permute-start.5 = (bf16[64,2048]{1,0:T(8,128)(2,1)S(1)}, bf16[64,2048]{1,0:T(8,128)(2,1)S(1)}, u32[]{:S(2)}, u32[]{:S(2)}) collective-permute-start(bf16[64,2048]{1,0:T(8,128)(2,1)S(1)} %collective-permute-done.1.refs_2_), channel_id=1, source_target_pairs={{0,1},{1,0},{2,3},{3,2},{4,5},{5,4},{6,7},{7,6},{8,9},{9,8},{10,11... | collective-permute-start | bytes 786440 | tf_op jit(solution)/shard_map/ppermute | solution.py:140
  49.6 1.9 %collective-permute-start.6 = (bf16[64,2048]{1,0:T(8,128)(2,1)S(1)}, bf16[64,2048]{1,0:T(8,128)(2,1)S(1)}, u32[]{:S(2)}, u32[]{:S(2)}) collective-permute-start(bf16[64,2048]{1,0:T(8,128)(2,1)S(1)} %collective-permute-done.2.refs_3_), channel_id=1, source_target_pairs={{0,1},{1,0},{2,3},{3,2},{4,5},{5,4},{6,7},{7,6},{8,9},{9,8},{10,11... | collective-permute-start | bytes 786440 | tf_op jit(solution)/shard_map/ppermute | solution.py:140
  53.0 3.4 %shard_map.67.refs_10_ = bf16[16,144,256]{2,1,0:T(8,128)(2,1)} custom-call(s32[8]{0:T(128)S(1)} %pad_add_fusion.place_ref, bf16[64,2048]{1,0:T(8,128)(2,1)S(1)} %copy-done, bf16[64,2048]{1,0:T(8,128)(2,1)S(1)} %collective-permute-done.refs_1_, bf16[64,2048]{1,0:T(8,128)(2,1)S(1)} %collective-permute-done.1.refs_2_, ...), custom_call_target="tpu_custom_call" | custom-call | flops 536870912 | bytes 6291456 | tf_op jit(solution)/shard_map/pallas_call | solution.py:61
  56.5 1.4 %copy.9 = bf16[4,16,32,256]{3,2,1,0:T(8,128)(2,1)S(1)} copy(bf16[4,16,32,256]{3,2,0,1:T(8,128)(2,1)} %bitcast.2) | data formatting | bytes 2097152 | tf_op jit(solution)/shard_map/transpose | solution.py:147
  57.9 4.1 %shard_map.68 = bf16[16,144,256]{2,1,0:T(8,128)(2,1)} custom-call(s32[8]{0:T(128)S(1)} %pad_add_fusion.place_ref, bf16[64,2048]{1,0:T(8,128)(2,1)S(1)} %copy-done, bf16[64,2048]{1,0:T(8,128)(2,1)S(1)} %collective-permute-done.refs_1_, bf16[64,2048]{1,0:T(8,128)(2,1)S(1)} %collective-permute-done.1.refs_2_, ...), custom_call_target="tpu_custom_call", output_to_operand_aliasing={{}: (11, {})} | custom-call | flops 536870912 | bytes 3145728 | tf_op jit(solution)/shard_map/pallas_call | solution.py:112
  62.0 1.4 %convolution_convert_fusion = bf16[256,2048]{1,0:T(8,128)(2,1)} fusion(bf16[256,256]{1,0:T(8,128)(2,1)S(1)} %bitcast.37, bf16[2048,256]{1,0:T(8,128)(2,1)S(1)} %bitcast.31), kind=kOutput, calls=%fused_computation | convolution fusion | flops 268959744 | bytes 2228224 | tf_op jit(solution)/shard_map/dot_general | solution.py:186
  63.4 4.9 %collective-permute-start.8 = (bf16[256,2048]{1,0:T(8,128)(2,1)}, bf16[256,2048]{1,0:T(8,128)(2,1)}, u32[]{:S(2)}, u32[]{:S(2)}) collective-permute-start(bf16[256,2048]{1,0:T(8,128)(2,1)} %convolution_convert_fusion), channel_id=1, source_target_pairs={{0,1},{1,0},{2,3},{3,2},{4,5},{5,4},{6,7},{7,6},{8,9},{9,8},{10,11... | collective-permute-start | bytes 3145736 | tf_op jit(solution)/shard_map/ppermute | solution.py:140
  68.3 3.7 %all-to-all-start.2 = ((bf16[16,144,256]{2,1,0:T(8,128)(2,1)}), bf16[16,144,256]{2,1,0:T(8,128)(2,1)S(1)}, u32[]{:S(2)}, u32[]{:S(2)}) async-start(bf16[16,144,256]{2,1,0:T(8,128)(2,1)} %shard_map.68), calls=%async_computation.2 | async-start | bytes 2359296 | tf_op jit(solution)/shard_map/all_to_all | solution.py:26
  72.1 1.7 %add_convert_fusion = bf16[256,2048]{1,0:T(8,128)(2,1)S(1)} fusion(bf16[256,2048]{1,0:T(8,128)(2,1)} %collective-permute-done.8, bf16[256,256]{1,0:T(8,128)(2,1)S(1)} %bitcast.36, bf16[2048,256]{1,0:T(8,128)(2,1)S(1)} %bitcast.32), kind=kOutput, calls=%fused_computation.2 | convolution fusion | flops 270008320 | bytes 3276800 | tf_op jit(solution)/shard_map/dot_general | solution.py:188
  73.9 4.4 %collective-permute-start.10 = (bf16[64,2048]{1,0:T(8,128)(2,1)S(1)}, bf16[64,2048]{1,0:T(8,128)(2,1)S(1)}, u32[]{:S(2)}, u32[]{:S(2)}) collective-permute-start(bf16[64,2048]{1,0:T(8,128)(2,1)S(1)} %get-tuple-element.15), channel_id=1, source_target_pairs={{0,6},{2,0},{4,2},{6,4},{1,7},{3,1},{5,3},{7,5},{8,14},{10,8},{12,... | collective-permute-start | bytes 786440 | tf_op jit(solution)/shard_map/ppermute | solution.py:31
  78.4 1.9 %collective-permute-start.11 = (bf16[64,2048]{1,0:T(8,128)(2,1)S(1)}, bf16[64,2048]{1,0:T(8,128)(2,1)S(1)}, u32[]{:S(2)}, u32[]{:S(2)}) collective-permute-start(bf16[64,2048]{1,0:T(8,128)(2,1)S(1)} %get-tuple-element.14), channel_id=1, source_target_pairs={{0,2},{2,4},{4,6},{6,0},{1,3},{3,5},{5,7},{7,1},{8,10},{10,12},{12... | collective-permute-start | bytes 786440 | tf_op jit(solution)/shard_map/ppermute | solution.py:31
  80.3 2.2 %collective-permute-start.9 = (bf16[64,2048]{1,0:T(8,128)(2,1)S(1)}, bf16[64,2048]{1,0:T(8,128)(2,1)S(1)}, u32[]{:S(2)}, u32[]{:S(2)}) collective-permute-start(bf16[64,2048]{1,0:T(8,128)(2,1)S(1)} %get-tuple-element.13), channel_id=1, source_target_pairs={{0,4},{2,6},{4,0},{6,2},{1,5},{3,7},{5,1},{7,3},{8,12},{10,14},{12... | collective-permute-start | bytes 786440 | tf_op jit(solution)/shard_map/ppermute | solution.py:31
  82.5 6.6 %all-to-all-done.2 = bf16[16,144,256]{2,1,0:T(8,128)(2,1)S(1)} async-done(((bf16[16,144,256]{2,1,0:T(8,128)(2,1)}), bf16[16,144,256]{2,1,0:T(8,128)(2,1)S(1)}, u32[]{:S(2)}, u32[]{:S(2)}) %all-to-all-start.2) | async-done | bytes 1179680 | tf_op jit(solution)/shard_map/all_to_all | solution.py:26
  90.0 16.4 %all-to-all-start.3 = ((bf16[4,48,256]{2,1,0:T(8,128)(2,1)}), bf16[4,48,256]{2,1,0:T(8,128)(2,1)S(1)}, u32[]{:S(2)}, u32[]{:S(2)}) async-start(bf16[4,48,256]{2,1,0:T(8,128)(2,1)} %pad_maximum_fusion), calls=%async_computation.3 | async-start | bytes 196608 | tf_op jit(solution)/shard_map/all_to_all | solution.py:26
  106.4 1.8 %fusion.9 = bf16[64,2048]{1,0:T(8,128)(2,1)} fusion(bf16[64,2048]{1,0:T(8,128)(2,1)S(1)} %collective-permute-done.11, bf16[64,2048]{1,0:T(8,128)(2,1)S(1)} %collective-permute-done.10, bf16[64,2048]{1,0:T(8,128)(2,1)S(1)} %collective-permute-done.9, bf16[4,64,2048]{2,1,0:T(8,128)(2,1)} %bitcast.35, s32[]{:T(128)S(6)} %select_n.44), kind=kLoop, calls=%fused_computation.20 | loop fusion | flops 1048576 | bytes 1310724 | tf_op jit(solution)/shard_map/convert_element_type | solution.py:195
  108.2 10.8 %all-to-all-done.3 = bf16[4,48,256]{2,1,0:T(8,128)(2,1)S(1)} async-done(((bf16[4,48,256]{2,1,0:T(8,128)(2,1)}), bf16[4,48,256]{2,1,0:T(8,128)(2,1)S(1)}, u32[]{:S(2)}, u32[]{:S(2)}) %all-to-all-start.3) | async-done | bytes 98336 | tf_op jit(solution)/shard_map/all_to_all | solution.py:26
  (52 shorter events, 8.3 us)
Async XLA Ops:
  2.0 29.7 %all-to-all-start = ((bf16[4,32,256]{2,1,0:T(8,128)(2,1)}), bf16[4,32,256]{2,1,0:T(8,128)(2,1)S(1)}, u32[]{:S(2)}, u32[]{:S(2)}) async-start(bf16[4,32,256]{2,1,0:T(8,128)(2,1)} %broadcast_in_dim.10), calls=%async_computation | async-start | bytes 131072 | tf_op jit(solution)/shard_map/all_to_all | solution.py:26
  17.6 23.3 %collective-permute-start = (bf16[64,2048]{1,0:T(8,128)(2,1)}, bf16[64,2048]{1,0:T(8,128)(2,1)S(1)}, u32[]{:S(2)}, u32[]{:S(2)}) collective-permute-start(bf16[64,2048]{1,0:T(8,128)(2,1)} %refs_0_.3), channel_id=1, source_target_pairs={{0,6},{2,0},{4,2},{6,4},{1,7},{3,1},{5,3},{7,5},{8,14},{10,8},{12,... | collective-permute-start | bytes 786440 | tf_op jit(solution)/shard_map/ppermute | solution.py:31
  21.2 24.7 %collective-permute-start.1 = (bf16[64,2048]{1,0:T(8,128)(2,1)}, bf16[64,2048]{1,0:T(8,128)(2,1)S(1)}, u32[]{:S(2)}, u32[]{:S(2)}) collective-permute-start(bf16[64,2048]{1,0:T(8,128)(2,1)} %refs_0_.3), channel_id=1, source_target_pairs={{0,4},{2,6},{4,0},{6,2},{1,5},{3,7},{5,1},{7,3},{8,12},{10,14},{12... | collective-permute-start | bytes 786440 | tf_op jit(solution)/shard_map/ppermute | solution.py:31
  23.4 26.2 %collective-permute-start.2 = (bf16[64,2048]{1,0:T(8,128)(2,1)}, bf16[64,2048]{1,0:T(8,128)(2,1)S(1)}, u32[]{:S(2)}, u32[]{:S(2)}) collective-permute-start(bf16[64,2048]{1,0:T(8,128)(2,1)} %refs_0_.3), channel_id=1, source_target_pairs={{0,2},{2,4},{4,6},{6,0},{1,3},{3,5},{5,7},{7,1},{8,10},{10,12},{12... | collective-permute-start | bytes 786440 | tf_op jit(solution)/shard_map/ppermute | solution.py:31
  26.0 26.1 %collective-permute-start.3 = (bf16[64,2048]{1,0:T(8,128)(2,1)}, bf16[64,2048]{1,0:T(8,128)(2,1)S(1)}, u32[]{:S(2)}, u32[]{:S(2)}) collective-permute-start(bf16[64,2048]{1,0:T(8,128)(2,1)} %refs_0_.3), channel_id=1, source_target_pairs={{0,1},{1,0},{2,3},{3,2},{4,5},{5,4},{6,7},{7,6},{8,9},{9,8},{10,11... | collective-permute-start | bytes 786440 | tf_op jit(solution)/shard_map/ppermute | solution.py:140
  30.4 21.1 %collective-permute-start.7 = (bf16[6,256]{1,0:T(8,128)(2,1)S(1)}, bf16[6,256]{1,0:T(8,128)(2,1)S(1)}, u32[]{:S(2)}, u32[]{:S(2)}) collective-permute-start(bf16[6,256]{1,0:T(8,128)(2,1)S(1)} %slice.74), channel_id=1, source_target_pairs={{8,0},{16,8},{24,16},{32,24},{40,32},{48,40},{56,48},{64,56},{72,6... | collective-permute-start | bytes 9224 | tf_op jit(solution)/shard_map/ppermute | solution.py:165
  32.8 7.9 %copy-start.7 = (f32[7,256]{1,0:T(8,128)S(1)}, f32[7,256]{1,0:T(8,128)}, u32[]{:S(2)}) copy-start(f32[7,256]{1,0:T(8,128)} %param.7) | copy-start | bytes 21508
  32.8 18.7 %copy-start.6 = (bf16[512,256]{1,0:T(8,128)(2,1)S(1)}, bf16[512,256]{1,0:T(8,128)(2,1)}, u32[]{:S(2)}) copy-start(bf16[512,256]{1,0:T(8,128)(2,1)} %param.6) | copy-start | bytes 786436
  32.8 23.7 %all-to-all-start.1 = ((bf16[16,128,256]{2,1,0:T(8,128)(2,1)}), bf16[16,128,256]{2,1,0:T(8,128)(2,1)}, u32[]{:S(2)}, u32[]{:S(2)}) async-start(bf16[16,128,256]{2,1,0:T(8,128)(2,1)} %broadcast_in_dim.24), calls=%async_computation.1 | async-start | bytes 2097152 | tf_op jit(solution)/shard_map/all_to_all | solution.py:26
  40.9 11.3 %collective-permute-start.4 = (bf16[64,2048]{1,0:T(8,128)(2,1)S(1)}, bf16[64,2048]{1,0:T(8,128)(2,1)S(1)}, u32[]{:S(2)}, u32[]{:S(2)}) collective-permute-start(bf16[64,2048]{1,0:T(8,128)(2,1)S(1)} %collective-permute-done.refs_1_), channel_id=1, source_target_pairs={{0,1},{1,0},{2,3},{3,2},{4,5},{5,4},{6,7},{7,6},{8,9},{9,8},{10,11... | collective-permute-start | bytes 786440 | tf_op jit(solution)/shard_map/ppermute | solution.py:140
  45.9 6.3 %collective-permute-start.5 = (bf16[64,2048]{1,0:T(8,128)(2,1)S(1)}, bf16[64,2048]{1,0:T(8,128)(2,1)S(1)}, u32[]{:S(2)}, u32[]{:S(2)}) collective-permute-start(bf16[64,2048]{1,0:T(8,128)(2,1)S(1)} %collective-permute-done.1.refs_2_), channel_id=1, source_target_pairs={{0,1},{1,0},{2,3},{3,2},{4,5},{5,4},{6,7},{7,6},{8,9},{9,8},{10,11... | collective-permute-start | bytes 786440 | tf_op jit(solution)/shard_map/ppermute | solution.py:140
  49.6 3.4 %collective-permute-start.6 = (bf16[64,2048]{1,0:T(8,128)(2,1)S(1)}, bf16[64,2048]{1,0:T(8,128)(2,1)S(1)}, u32[]{:S(2)}, u32[]{:S(2)}) collective-permute-start(bf16[64,2048]{1,0:T(8,128)(2,1)S(1)} %collective-permute-done.2.refs_3_), channel_id=1, source_target_pairs={{0,1},{1,0},{2,3},{3,2},{4,5},{5,4},{6,7},{7,6},{8,9},{9,8},{10,11... | collective-permute-start | bytes 786440 | tf_op jit(solution)/shard_map/ppermute | solution.py:140
  51.7 1.3 %copy-start = (bf16[64,2048]{1,0:T(8,128)(2,1)S(1)}, bf16[64,2048]{1,0:T(8,128)(2,1)}, u32[]{:S(2)}) copy-start(bf16[64,2048]{1,0:T(8,128)(2,1)} %refs_0_.3) | copy-start | bytes 786436
  52.2 4.3 %copy-start.1 = (bf16[64,2048]{1,0:T(8,128)(2,1)}, bf16[64,2048]{1,0:T(8,128)(2,1)S(1)}, u32[]{:S(2)}) copy-start(bf16[64,2048]{1,0:T(8,128)(2,1)S(1)} %collective-permute-done.5.refs_6_) | copy-start | bytes 786436
  53.0 3.4 %copy-start.3 = (bf16[64,2048]{1,0:T(8,128)(2,1)}, bf16[64,2048]{1,0:T(8,128)(2,1)S(1)}, u32[]{:S(2)}) copy-start(bf16[64,2048]{1,0:T(8,128)(2,1)S(1)} %collective-permute-done.6.refs_7_) | copy-start | bytes 786436
  56.5 1.4 %copy-start.2 = (bf16[64,2048]{1,0:T(8,128)(2,1)S(1)}, bf16[64,2048]{1,0:T(8,128)(2,1)}, u32[]{:S(2)}) copy-start(bf16[64,2048]{1,0:T(8,128)(2,1)} %copy-done.1) | copy-start | bytes 786436
  56.5 1.4 %copy-start.4 = (bf16[64,2048]{1,0:T(8,128)(2,1)S(1)}, bf16[64,2048]{1,0:T(8,128)(2,1)}, u32[]{:S(2)}) copy-start(bf16[64,2048]{1,0:T(8,128)(2,1)} %copy-done.3) | copy-start | bytes 786436
  63.4 8.7 %collective-permute-start.8 = (bf16[256,2048]{1,0:T(8,128)(2,1)}, bf16[256,2048]{1,0:T(8,128)(2,1)}, u32[]{:S(2)}, u32[]{:S(2)}) collective-permute-start(bf16[256,2048]{1,0:T(8,128)(2,1)} %convolution_convert_fusion), channel_id=1, source_target_pairs={{0,1},{1,0},{2,3},{3,2},{4,5},{5,4},{6,7},{7,6},{8,9},{9,8},{10,11... | collective-permute-start | bytes 3145736 | tf_op jit(solution)/shard_map/ppermute | solution.py:140
  68.3 20.8 %all-to-all-start.2 = ((bf16[16,144,256]{2,1,0:T(8,128)(2,1)}), bf16[16,144,256]{2,1,0:T(8,128)(2,1)S(1)}, u32[]{:S(2)}, u32[]{:S(2)}) async-start(bf16[16,144,256]{2,1,0:T(8,128)(2,1)} %shard_map.68), calls=%async_computation.2 | async-start | bytes 2359296 | tf_op jit(solution)/shard_map/all_to_all | solution.py:26
  73.9 6.4 %copy-start.5 = (bf16[256,2048]{1,0:T(8,128)(2,1)}, bf16[256,2048]{1,0:T(8,128)(2,1)S(1)}, u32[]{:S(2)}) copy-start(bf16[256,2048]{1,0:T(8,128)(2,1)S(1)} %add_convert_fusion) | copy-start | bytes 3145732
  73.9 32.5 %collective-permute-start.10 = (bf16[64,2048]{1,0:T(8,128)(2,1)S(1)}, bf16[64,2048]{1,0:T(8,128)(2,1)S(1)}, u32[]{:S(2)}, u32[]{:S(2)}) collective-permute-start(bf16[64,2048]{1,0:T(8,128)(2,1)S(1)} %get-tuple-element.15), channel_id=1, source_target_pairs={{0,6},{2,0},{4,2},{6,4},{1,7},{3,1},{5,3},{7,5},{8,14},{10,8},{12,... | collective-permute-start | bytes 786440 | tf_op jit(solution)/shard_map/ppermute | solution.py:31
  78.4 28.1 %collective-permute-start.11 = (bf16[64,2048]{1,0:T(8,128)(2,1)S(1)}, bf16[64,2048]{1,0:T(8,128)(2,1)S(1)}, u32[]{:S(2)}, u32[]{:S(2)}) collective-permute-start(bf16[64,2048]{1,0:T(8,128)(2,1)S(1)} %get-tuple-element.14), channel_id=1, source_target_pairs={{0,2},{2,4},{4,6},{6,0},{1,3},{3,5},{5,7},{7,1},{8,10},{10,12},{12... | collective-permute-start | bytes 786440 | tf_op jit(solution)/shard_map/ppermute | solution.py:31
  80.3 26.1 %collective-permute-start.9 = (bf16[64,2048]{1,0:T(8,128)(2,1)S(1)}, bf16[64,2048]{1,0:T(8,128)(2,1)S(1)}, u32[]{:S(2)}, u32[]{:S(2)}) collective-permute-start(bf16[64,2048]{1,0:T(8,128)(2,1)S(1)} %get-tuple-element.13), channel_id=1, source_target_pairs={{0,4},{2,6},{4,0},{6,2},{1,5},{3,7},{5,1},{7,3},{8,12},{10,14},{12... | collective-permute-start | bytes 786440 | tf_op jit(solution)/shard_map/ppermute | solution.py:31
  90.0 29.1 %all-to-all-start.3 = ((bf16[4,48,256]{2,1,0:T(8,128)(2,1)}), bf16[4,48,256]{2,1,0:T(8,128)(2,1)S(1)}, u32[]{:S(2)}, u32[]{:S(2)}) async-start(bf16[4,48,256]{2,1,0:T(8,128)(2,1)} %pad_maximum_fusion), calls=%async_computation.3 | async-start | bytes 196608 | tf_op jit(solution)/shard_map/all_to_all | solution.py:26

commit v8 on v7

--- a/solution.py
+++ b/solution.py
@@ -38,12 +38,12 @@
 
 
 def products_kernel(place_ref, *refs):
-    chunks, (grad_ref, out_ref, block_ref) = refs[:-3], refs[-3:]
+    chunks, (grad_ref, out_ref, slab_ref) = refs[:-3], refs[-3:]
     nxy, cols = out_ref.shape[0], grad_ref.shape[1]
     rows = chunks[0].shape[1] // nxy
-    in_order(place_ref, chunks, block_ref)
+    in_order(place_ref, chunks, slab_ref)
     products = lax.dot_general(
-        block_ref[...], grad_ref[...], (((0,), (0,)), ((), ())), preferred_element_type=F32
+        slab_ref[...], grad_ref[...], (((0,), (0,)), ((), ())), preferred_element_type=F32
     )
     here = pl.ds(pl.multiple_of(pl.program_id(0) * rows, rows), rows)
     out_ref[:, here, :] = products.astype(BF).reshape(nxy, rows, cols)
@@ -65,10 +65,15 @@
             grid=(nz,),
             in_specs=[pl.BlockSpec((step_rows, part), lambda i, _: (0, i)) for _ in chunks]
             + [pl.BlockSpec((slab_len, cols), lambda i, _: (0, 0))],
-            out_specs=pl.BlockSpec((nxy, nz * rows + 16, cols), lambda i, _: (0, 0, 0)),
-            scratch_shapes=[pltpu.VMEM((slab_len, part), BF)],
+            out_specs=[
+                pl.BlockSpec((nxy, nz * rows + 16, cols), lambda i, _: (0, 0, 0)),
+                pl.BlockSpec((slab_len, part), lambda i, _: (0, i)),
+            ],
         ),
-        out_shape=jax.ShapeDtypeStruct((nxy, nz * rows + 16, cols), BF),
+        out_shape=[
+            jax.ShapeDtypeStruct((nxy, nz * rows + 16, cols), BF),
+            jax.ShapeDtypeStruct((slab_len, depth), BF),
+        ],
         compiler_params=pltpu.CompilerParams(vmem_limit_bytes=VMEM_BYTES),
         cost_estimate=pl.CostEstimate(
             flops=2 * slab_len * depth * cols, bytes_accessed=6 * slab_len * depth, transcendentals=0
@@ -76,12 +81,11 @@
     )(places, *chunks, grad_bf)
 
 
-def taps_kernel(place_ref, *refs):
-    chunks, (weight_ref, extended_ref, _, out_ref, block_ref, featured_ref) = refs[:-6], refs[-6:]
+def taps_kernel(slab_ref, weight_ref, extended_ref, _, out_ref, featured_ref):
     step = pl.program_id(0)
     slab_len, cols = featured_ref.shape
-    in_order(place_ref, chunks, block_ref)
-    term = jnp.dot(block_ref[...], weight_ref[...], preferred_element_type=F32)
+    weight = weight_ref[...].reshape(-1, cols)
+    term = jnp.dot(slab_ref[...], weight, preferred_element_type=F32)
 
     @pl.when(step == 0)
     def _():
@@ -102,34 +106,29 @@
         out_ref[...] = jnp.broadcast_to(tail[None], out_ref.shape)
 
 
-def with_tap_sums(packed, places, chunks, weight, extended):
-    step_rows, depth = chunks[0].shape
-    slab_len, cols = step_rows * len(chunks), weight.shape[1]
-    steps = 4
-    part = depth // steps
-    nxy, packed_rows, _ = packed.shape
-    last = packed_rows // 16 - 1
+def with_tap_sums(packed, slab, gathered, extended):
+    slab_len, depth = slab.shape
+    nxy, nz, rows, cols = gathered.shape
+    part = depth // nz
+    last = packed.shape[1] // 16 - 1
     return pl.pallas_call(
         taps_kernel,
-        grid_spec=pltpu.PrefetchScalarGridSpec(
-            num_scalar_prefetch=1,
-            grid=(steps,),
-            in_specs=[pl.BlockSpec((step_rows, part), lambda i, _: (0, i)) for _ in chunks]
-            + [
-                pl.BlockSpec((part, cols), lambda i, _: (i, 0)),
-                pl.BlockSpec(extended.shape, lambda i, _: (0, 0)),
-                pl.BlockSpec((1, 16, cols), lambda i, _: (0, last, 0)),
-            ],
-            out_specs=pl.BlockSpec((nxy, 16, cols), lambda i, _: (0, last, 0)),
-            scratch_shapes=[pltpu.VMEM((slab_len, part), BF), pltpu.VMEM((slab_len, cols), F32)],
-        ),
+        grid=(nz,),
+        in_specs=[
+            pl.BlockSpec((slab_len, part), lambda i: (0, i)),
+            pl.BlockSpec((nxy, 1, rows, cols), lambda i: (0, i, 0, 0)),
+            pl.BlockSpec(extended.shape, lambda i: (0, 0)),
+            pl.BlockSpec((1, 16, cols), lambda i: (0, last, 0)),
+        ],
+        out_specs=pl.BlockSpec((nxy, 16, cols), lambda i: (0, last, 0)),
+        scratch_shapes=[pltpu.VMEM((slab_len, cols), F32)],
         out_shape=jax.ShapeDtypeStruct(packed.shape, BF),
-        input_output_aliases={len(chunks) + 3: 0},
-        compiler_params=pltpu.CompilerParams(vmem_limit_bytes=VMEM_BYTES),
+        input_output_aliases={3: 0},
+        compiler_params=pltpu.CompilerParams(vmem_limit_bytes=52 * 1024 * 1024),
         cost_estimate=pl.CostEstimate(
             flops=2 * slab_len * depth * cols, bytes_accessed=3 * slab_len * depth, transcendentals=0
         ),
-    )(places, *chunks, weight, extended, packed)
+    )(slab, gathered, extended, packed)
 
 
 def spread(value, axes):
@@ -138,13 +137,6 @@
 
 def swap(value):
     return lax.ppermute(value, C, [(0, 1), (1, 0)])
-
-
-def weight_columns(proj_weight):
-    rows, cols = proj_weight.shape
-    nz, nxy = lax.axis_size(ZH), lax.axis_size((X, Y))
-    gathered = spread(spread(proj_weight, ZH).reshape(nz * rows, cols), (X, Y))
-    return gathered.reshape(nxy, nz, rows, cols).transpose(1, 0, 2, 3).reshape(nz * nxy * rows, cols)
 
 
 def body(tokens, proj_weight, cotangent, filters):
@@ -162,8 +154,11 @@
         direct[steps] = from_ahead(tokens, ZL, steps)
     sources = (chip + jnp.arange(nzl)) % nzl
     places = jnp.concatenate([2 * sources + core, 2 * sources + 1 - core]).astype(jnp.int32)
+    column = spread(proj_weight, ZH).reshape(nz * rows, cols)
+    column, head = lax.optimization_barrier((column, cotangent[: TAPS - 1]))
+    gathered = spread(column, (X, Y)).reshape(nxy, nz, rows, cols)
     following = lax.ppermute(
-        cotangent[: TAPS - 1], (ZH, X, Y), [(source, source - 1) for source in range(1, ndp)]
+        head, (ZH, X, Y), [(source, source - 1) for source in range(1, ndp)]
     )
     nothing = jnp.zeros((2, cols), BF)
     extended = jnp.concatenate([cotangent, following, nothing], 0).astype(F32)
@@ -172,13 +167,13 @@
         grad_feat = grad_feat + filters[tap] * extended[tap : tap + slab_len]
     grad_bf = grad_feat.astype(BF)
 
-    weight = weight_columns(proj_weight)
     chunks = direct + [swap(value) for value in direct]
-    packed = weight_products(places, chunks, grad_bf, nxy, rows)
-    packed = with_tap_sums(packed, places, chunks, weight, extended)
-    packed, grad_late = lax.optimization_barrier((packed, grad_bf))
+    packed, slab = weight_products(places, chunks, grad_bf, nxy, rows)
+    packed = with_tap_sums(packed, slab, gathered, extended)
+    packed, grad_late, gathered = lax.optimization_barrier((packed, grad_bf, gathered))
     total = jnp.sum(exchange(packed, (X, Y)).astype(F32), axis=0)
 
+    weight = gathered.transpose(1, 0, 2, 3).reshape(depth, cols)
     by_core = grad_late.reshape(nzl, 2, own_tokens, cols)
     theirs = lax.dynamic_index_in_dim(by_core, 1 - core, 1, keepdims=False).reshape(-1, cols)
     ours = lax.dynamic_index_in_dim(by_core, core, 1, keepdims=False).reshape(-1, cols)

time: 123 us -> 122 us (level)
  starting transfers between devices: 78.5 us -> 76.2 us
  waiting for transfers between devices: 20.9 us -> 22.4 us
    ppermute x5, starting transfers between devices: 16.6 us -> 14.9 us  [swap(): return lax.ppermute(value, C, [(0, 1), (1, 0)])]
    all_to_all x4, waiting for transfers between devices: 17.5 us -> 19.1 us  [exchange(): return lax.all_to_all(value, axes, split_axis=0, concat_axis=0, tiled=True)]
    all_to_all x4, starting transfers between devices: 43.6 us -> 42.3 us  [exchange(): return lax.all_to_all(value, axes, split_axis=0, concat_axis=0, tiled=True)]
    unnamed x16 -> x12, local copies, waits for them, and re-layouts: 0.04 us -> 1.35 us
    transpose x1, local copies, waits for them, and re-layouts: 1.35 us -> 0.08 us  [body(): weight = gathered.transpose(1, 0, 2, 3).reshape(depth, cols)]
    dot_general x1, matrix products: 1.71 us -> 0.47 us  [body(): lax.dot_general(ours, weight, contract_cols, preferred_element_type=F32)]
  transfers between devices with their start and end apart: 16 -> 16, of which waited for: 4 -> 4; matrix products, arithmetic and copies ran while one was open for 6% -> 5% of each run, Pallas kernels for 3% -> 3%
where the time goes in v8:
time: 122 us; the launch traced here: 119 us
  starting transfers between devices  76.2 us (62%)
  waiting for transfers between devices  22.4 us (18%)
  Pallas kernels  8 us (7%)
  local copies, waits for them, and re-layouts  6.07 us (5%)
  other arithmetic  3.88 us (3%)
  matrix products  1.95 us (2%)
    all_to_all x4, starting transfers between devices, exchange(): return lax.all_to_all(value, axes, split_axis=0, concat_axis=0, tiled=True)  42.3 us
    all_to_all x4, waiting for transfers between devices, exchange(): return lax.all_to_all(value, axes, split_axis=0, concat_axis=0, tiled=True)  19.1 us
    ppermute x6, starting transfers between devices, from_ahead(): lax.ppermute(value, axis, [(source, (source - steps) % count) for source...  17.8 us
    ppermute x5, starting transfers between devices, swap(): return lax.ppermute(value, C, [(0, 1), (1, 0)])  14.9 us
    pallas_call x1, Pallas kernels, with_tap_sums(): pl.pallas_call(taps_kernel, grid=(nz,), in_specs=[pl.BlockSpec((slab_len,...  4.49 us
    pallas_call x1, Pallas kernels, weight_products(): pl.pallas_call(products_kernel, grid_spec=pltpu.PrefetchScalarGridSpec(nu...  3.51 us
    broadcast_in_dim x2, local copies, waits for them, and re-layouts, spread(): jnp.broadcast_to(value[None], (lax.axis_size(axes),) + value.shape)  2.48 us
  transfers between devices with their start and end apart: 16, of which 4 were waited for; matrix products, arithmetic and copies ran while one was open for 5% of the time, Pallas kernels for 3%

profile of v8, /device:TPU:1, one launch (start us, length us, event | category | flops | bytes accessed | tf_op | source)
XLA Modules:
  0.0 119.5 jit_solution(204206362452795144)
XLA Ops:
  0.7 1.4 %broadcast_in_dim.8 = bf16[4,32,256]{2,1,0:T(8,128)(2,1)} broadcast(bf16[32,256]{1,0:T(8,128)(2,1)} %param.5), dimensions={1,2} | broadcast | bytes 81920 | tf_op jit(solution)/shard_map/broadcast_in_dim | solution.py:135
  2.1 15.6 %all-to-all-start = ((bf16[4,32,256]{2,1,0:T(8,128)(2,1)}), bf16[4,32,256]{2,1,0:T(8,128)(2,1)S(1)}, u32[]{:S(2)}, u32[]{:S(2)}) async-start(bf16[4,32,256]{2,1,0:T(8,128)(2,1)} %broadcast_in_dim.8), calls=%async_computation | async-start | bytes 131072 | tf_op jit(solution)/shard_map/all_to_all | solution.py:26
  17.7 3.5 %collective-permute-start = (bf16[64,2048]{1,0:T(8,128)(2,1)}, bf16[64,2048]{1,0:T(8,128)(2,1)S(1)}, u32[]{:S(2)}, u32[]{:S(2)}) collective-permute-start(bf16[64,2048]{1,0:T(8,128)(2,1)} %refs_0_.1), channel_id=1, source_target_pairs={{0,6},{2,0},{4,2},{6,4},{1,7},{3,1},{5,3},{7,5},{8,14},{10,8},{12,... | collective-permute-start | bytes 786440 | tf_op jit(solution)/shard_map/ppermute | solution.py:31
  21.2 2.2 %collective-permute-start.1 = (bf16[64,2048]{1,0:T(8,128)(2,1)}, bf16[64,2048]{1,0:T(8,128)(2,1)S(1)}, u32[]{:S(2)}, u32[]{:S(2)}) collective-permute-start(bf16[64,2048]{1,0:T(8,128)(2,1)} %refs_0_.1), channel_id=1, source_target_pairs={{0,4},{2,6},{4,0},{6,2},{1,5},{3,7},{5,1},{7,3},{8,12},{10,14},{12... | collective-permute-start | bytes 786440 | tf_op jit(solution)/shard_map/ppermute | solution.py:31
  23.4 2.6 %collective-permute-start.2 = (bf16[64,2048]{1,0:T(8,128)(2,1)}, bf16[64,2048]{1,0:T(8,128)(2,1)S(1)}, u32[]{:S(2)}, u32[]{:S(2)}) collective-permute-start(bf16[64,2048]{1,0:T(8,128)(2,1)} %refs_0_.1), channel_id=1, source_target_pairs={{0,2},{2,4},{4,6},{6,0},{1,3},{3,5},{5,7},{7,1},{8,10},{10,12},{12... | collective-permute-start | bytes 786440 | tf_op jit(solution)/shard_map/ppermute | solution.py:31
  26.1 3.7 %collective-permute-start.3 = (bf16[64,2048]{1,0:T(8,128)(2,1)}, bf16[64,2048]{1,0:T(8,128)(2,1)S(1)}, u32[]{:S(2)}, u32[]{:S(2)}) collective-permute-start(bf16[64,2048]{1,0:T(8,128)(2,1)} %refs_0_.1), channel_id=1, source_target_pairs={{0,1},{1,0},{2,3},{3,2},{4,5},{5,4},{6,7},{7,6},{8,9},{9,8},{10,11... | collective-permute-start | bytes 786440 | tf_op jit(solution)/shard_map/ppermute | solution.py:139
  31.6 6.8 %all-to-all-start.1 = ((bf16[16,128,256]{2,1,0:T(8,128)(2,1)}), bf16[16,128,256]{2,1,0:T(8,128)(2,1)S(1)}, u32[]{:S(2)}, u32[]{:S(2)}) async-start(bf16[16,128,256]{2,1,0:T(8,128)(2,1)} %broadcast_in_dim.10), calls=%async_computation.1 | async-start | bytes 2097152 | tf_op jit(solution)/shard_map/all_to_all | solution.py:26
  39.8 3.5 %collective-permute-start.4 = (bf16[64,2048]{1,0:T(8,128)(2,1)S(1)}, bf16[64,2048]{1,0:T(8,128)(2,1)S(1)}, u32[]{:S(2)}, u32[]{:S(2)}) collective-permute-start(bf16[64,2048]{1,0:T(8,128)(2,1)S(1)} %collective-permute-done.refs_1_), channel_id=1, source_target_pairs={{0,1},{1,0},{2,3},{3,2},{4,5},{5,4},{6,7},{7,6},{8,9},{9,8},{10,11... | collective-permute-start | bytes 786440 | tf_op jit(solution)/shard_map/ppermute | solution.py:139
  43.3 2.4 %collective-permute-done.1.refs_2_ = bf16[64,2048]{1,0:T(8,128)(2,1)S(1)} collective-permute-done((bf16[64,2048]{1,0:T(8,128)(2,1)}, bf16[64,2048]{1,0:T(8,128)(2,1)S(1)}, u32[]{:S(2)}, u32[]{:S(2)}) %collective-permute-start.1) | collective-permute-done | bytes 262176 | tf_op jit(solution)/shard_map/ppermute | solution.py:31
  45.7 3.8 %collective-permute-start.5 = (bf16[64,2048]{1,0:T(8,128)(2,1)S(1)}, bf16[64,2048]{1,0:T(8,128)(2,1)S(1)}, u32[]{:S(2)}, u32[]{:S(2)}) collective-permute-start(bf16[64,2048]{1,0:T(8,128)(2,1)S(1)} %collective-permute-done.1.refs_2_), channel_id=1, source_target_pairs={{0,1},{1,0},{2,3},{3,2},{4,5},{5,4},{6,7},{7,6},{8,9},{9,8},{10,11... | collective-permute-start | bytes 786440 | tf_op jit(solution)/shard_map/ppermute | solution.py:139
  49.5 1.9 %collective-permute-start.6 = (bf16[64,2048]{1,0:T(8,128)(2,1)S(1)}, bf16[64,2048]{1,0:T(8,128)(2,1)S(1)}, u32[]{:S(2)}, u32[]{:S(2)}) collective-permute-start(bf16[64,2048]{1,0:T(8,128)(2,1)S(1)} %collective-permute-done.2.refs_3_), channel_id=1, source_target_pairs={{0,1},{1,0},{2,3},{3,2},{4,5},{5,4},{6,7},{7,6},{8,9},{9,8},{10,11... | collective-permute-start | bytes 786440 | tf_op jit(solution)/shard_map/ppermute | solution.py:139
  52.9 3.5 %shard_map.67 = (bf16[16,144,256]{2,1,0:T(8,128)(2,1)}, bf16[512,2048]{1,0:T(8,128)(2,1)S(1)}) custom-call(s32[8]{0:T(128)S(1)} %pad_add_fusion.place_ref, bf16[64,2048]{1,0:T(8,128)(2,1)S(1)} %copy-done.1, bf16[64,2048]{1,0:T(8,128)(2,1)S(1)} %collective-permute-done.refs_1_, bf16[64,2048]{1,0:T(8,128)(2,1)S(1)} %collective-permute-done.1.refs_2_, ...), custom_call_target="tpu_custom_call" | custom-call | flops 536870912 | bytes 6291456 | tf_op jit(solution)/shard_map/pallas_call | solution.py:61
  56.4 1.3 %copy-done = bf16[512,2048]{1,0:T(8,128)(2,1)} copy-done((bf16[512,2048]{1,0:T(8,128)(2,1)}, bf16[512,2048]{1,0:T(8,128)(2,1)S(1)}, u32[]{:S(2)}) %copy-start) | copy-done | bytes 2097176
  57.8 4.5 %shard_map.68 = bf16[16,144,256]{2,1,0:T(8,128)(2,1)} custom-call(bf16[512,2048]{1,0:T(8,128)(2,1)} %copy-done, bf16[16,4,32,256]{3,2,1,0:T(8,128)(2,1)S(1)} %bitcast.29, f32[520,256]{1,0:T(8,128)S(1)} %maximum_convert_fusion.extended_ref, bf16[16,144,256]{2,1,0:T(8,128)(2,1)} %get-tuple-element.15._), custom_call_target="tpu_custom_call", output_to_operand_aliasing={{}: (3, {})} | custom-call | flops 536870912 | bytes 3145728 | tf_op jit(solution)/shard_map/pallas_call | solution.py:114
  63.0 1.5 %convolution_convert_fusion = bf16[256,2048]{1,0:T(8,128)(2,1)} fusion(bf16[256,256]{1,0:T(8,128)(2,1)S(1)} %bitcast.37, bf16[2048,256]{1,0:T(8,128)(2,1)S(1)} %bitcast.32), kind=kOutput, calls=%fused_computation | convolution fusion | flops 268959744 | bytes 2228224 | tf_op jit(solution)/shard_map/dot_general | solution.py:181
  64.5 2.0 %collective-permute-start.8 = (bf16[256,2048]{1,0:T(8,128)(2,1)}, bf16[256,2048]{1,0:T(8,128)(2,1)S(1)}, u32[]{:S(2)}, u32[]{:S(2)}) collective-permute-start(bf16[256,2048]{1,0:T(8,128)(2,1)} %convolution_convert_fusion), channel_id=1, source_target_pairs={{0,1},{1,0},{2,3},{3,2},{4,5},{5,4},{6,7},{7,6},{8,9},{9,8},{10,11... | collective-permute-start | bytes 3145736 | tf_op jit(solution)/shard_map/ppermute | solution.py:139
  66.5 8.0 %all-to-all-start.2 = ((bf16[16,144,256]{2,1,0:T(8,128)(2,1)}), bf16[16,144,256]{2,1,0:T(8,128)(2,1)S(1)}, u32[]{:S(2)}, u32[]{:S(2)}) async-start(bf16[16,144,256]{2,1,0:T(8,128)(2,1)} %shard_map.68), calls=%async_computation.2 | async-start | bytes 2359296 | tf_op jit(solution)/shard_map/all_to_all | solution.py:26
  75.2 3.8 %collective-permute-start.10 = (bf16[64,2048]{1,0:T(8,128)(2,1)S(1)}, bf16[64,2048]{1,0:T(8,128)(2,1)S(1)}, u32[]{:S(2)}, u32[]{:S(2)}) collective-permute-start(bf16[64,2048]{1,0:T(8,128)(2,1)S(1)} %get-tuple-element.25), channel_id=1, source_target_pairs={{0,6},{2,0},{4,2},{6,4},{1,7},{3,1},{5,3},{7,5},{8,14},{10,8},{12,... | collective-permute-start | bytes 786440 | tf_op jit(solution)/shard_map/ppermute | solution.py:31
  79.0 1.9 %collective-permute-start.11 = (bf16[64,2048]{1,0:T(8,128)(2,1)S(1)}, bf16[64,2048]{1,0:T(8,128)(2,1)S(1)}, u32[]{:S(2)}, u32[]{:S(2)}) collective-permute-start(bf16[64,2048]{1,0:T(8,128)(2,1)S(1)} %get-tuple-element.24), channel_id=1, source_target_pairs={{0,2},{2,4},{4,6},{6,0},{1,3},{3,5},{5,7},{7,1},{8,10},{10,12},{12... | collective-permute-start | bytes 786440 | tf_op jit(solution)/shard_map/ppermute | solution.py:31
  80.9 3.7 %collective-permute-start.9 = (bf16[64,2048]{1,0:T(8,128)(2,1)S(1)}, bf16[64,2048]{1,0:T(8,128)(2,1)S(1)}, u32[]{:S(2)}, u32[]{:S(2)}) collective-permute-start(bf16[64,2048]{1,0:T(8,128)(2,1)S(1)} %get-tuple-element.23), channel_id=1, source_target_pairs={{0,4},{2,6},{4,0},{6,2},{1,5},{3,7},{5,1},{7,3},{8,12},{10,14},{12... | collective-permute-start | bytes 786440 | tf_op jit(solution)/shard_map/ppermute | solution.py:31
  84.6 8.6 %all-to-all-done.2 = bf16[16,144,256]{2,1,0:T(8,128)(2,1)S(1)} async-done(((bf16[16,144,256]{2,1,0:T(8,128)(2,1)}), bf16[16,144,256]{2,1,0:T(8,128)(2,1)S(1)}, u32[]{:S(2)}, u32[]{:S(2)}) %all-to-all-start.2) | async-done | bytes 1179680 | tf_op jit(solution)/shard_map/all_to_all | solution.py:26
  94.1 11.9 %all-to-all-start.3 = ((bf16[4,48,256]{2,1,0:T(8,128)(2,1)}), bf16[4,48,256]{2,1,0:T(8,128)(2,1)S(1)}, u32[]{:S(2)}, u32[]{:S(2)}) async-start(bf16[4,48,256]{2,1,0:T(8,128)(2,1)} %pad_maximum_fusion), calls=%async_computation.3 | async-start | bytes 196608 | tf_op jit(solution)/shard_map/all_to_all | solution.py:26
  106.0 1.8 %fusion.9 = bf16[64,2048]{1,0:T(8,128)(2,1)} fusion(bf16[64,2048]{1,0:T(8,128)(2,1)S(1)} %collective-permute-done.11, bf16[64,2048]{1,0:T(8,128)(2,1)S(1)} %collective-permute-done.10, bf16[64,2048]{1,0:T(8,128)(2,1)S(1)} %collective-permute-done.9, bf16[4,64,2048]{2,1,0:T(8,128)(2,1)} %bitcast.35, s32[]{:T(128)S(6)} %select_n.44), kind=kLoop, calls=%fused_computation.20 | loop fusion | flops 1048576 | bytes 1310724 | tf_op jit(solution)/shard_map/convert_element_type | solution.py:190
  107.8 10.5 %all-to-all-done.3 = bf16[4,48,256]{2,1,0:T(8,128)(2,1)S(1)} async-done(((bf16[4,48,256]{2,1,0:T(8,128)(2,1)}), bf16[4,48,256]{2,1,0:T(8,128)(2,1)S(1)}, u32[]{:S(2)}, u32[]{:S(2)}) %all-to-all-start.3) | async-done | bytes 98336 | tf_op jit(solution)/shard_map/all_to_all | solution.py:26
  (48 shorter events, 8.1 us)
Async XLA Ops:
  0.6 50.8 %copy-start.4 = (bf16[512,256]{1,0:T(8,128)(2,1)S(1)}, bf16[512,256]{1,0:T(8,128)(2,1)}, u32[]{:S(2)}) copy-start(bf16[512,256]{1,0:T(8,128)(2,1)} %param.6) | copy-start | bytes 786436
  0.6 37.7 %copy-start.5 = (f32[7,256]{1,0:T(8,128)S(1)}, f32[7,256]{1,0:T(8,128)}, u32[]{:S(2)}) copy-start(f32[7,256]{1,0:T(8,128)} %param.7) | copy-start | bytes 21508
  2.1 28.4 %all-to-all-start = ((bf16[4,32,256]{2,1,0:T(8,128)(2,1)}), bf16[4,32,256]{2,1,0:T(8,128)(2,1)S(1)}, u32[]{:S(2)}, u32[]{:S(2)}) async-start(bf16[4,32,256]{2,1,0:T(8,128)(2,1)} %broadcast_in_dim.8), calls=%async_computation | async-start | bytes 131072 | tf_op jit(solution)/shard_map/all_to_all | solution.py:26
  17.7 22.2 %collective-permute-start = (bf16[64,2048]{1,0:T(8,128)(2,1)}, bf16[64,2048]{1,0:T(8,128)(2,1)S(1)}, u32[]{:S(2)}, u32[]{:S(2)}) collective-permute-start(bf16[64,2048]{1,0:T(8,128)(2,1)} %refs_0_.1), channel_id=1, source_target_pairs={{0,6},{2,0},{4,2},{6,4},{1,7},{3,1},{5,3},{7,5},{8,14},{10,8},{12,... | collective-permute-start | bytes 786440 | tf_op jit(solution)/shard_map/ppermute | solution.py:31
  21.2 24.5 %collective-permute-start.1 = (bf16[64,2048]{1,0:T(8,128)(2,1)}, bf16[64,2048]{1,0:T(8,128)(2,1)S(1)}, u32[]{:S(2)}, u32[]{:S(2)}) collective-permute-start(bf16[64,2048]{1,0:T(8,128)(2,1)} %refs_0_.1), channel_id=1, source_target_pairs={{0,4},{2,6},{4,0},{6,2},{1,5},{3,7},{5,1},{7,3},{8,12},{10,14},{12... | collective-permute-start | bytes 786440 | tf_op jit(solution)/shard_map/ppermute | solution.py:31
  23.4 26.0 %collective-permute-start.2 = (bf16[64,2048]{1,0:T(8,128)(2,1)}, bf16[64,2048]{1,0:T(8,128)(2,1)S(1)}, u32[]{:S(2)}, u32[]{:S(2)}) collective-permute-start(bf16[64,2048]{1,0:T(8,128)(2,1)} %refs_0_.1), channel_id=1, source_target_pairs={{0,2},{2,4},{4,6},{6,0},{1,3},{3,5},{5,7},{7,1},{8,10},{10,12},{12... | collective-permute-start | bytes 786440 | tf_op jit(solution)/shard_map/ppermute | solution.py:31
  26.1 25.9 %collective-permute-start.3 = (bf16[64,2048]{1,0:T(8,128)(2,1)}, bf16[64,2048]{1,0:T(8,128)(2,1)S(1)}, u32[]{:S(2)}, u32[]{:S(2)}) collective-permute-start(bf16[64,2048]{1,0:T(8,128)(2,1)} %refs_0_.1), channel_id=1, source_target_pairs={{0,1},{1,0},{2,3},{3,2},{4,5},{5,4},{6,7},{7,6},{8,9},{9,8},{10,11... | collective-permute-start | bytes 786440 | tf_op jit(solution)/shard_map/ppermute | solution.py:139
  31.6 26.2 %all-to-all-start.1 = ((bf16[16,128,256]{2,1,0:T(8,128)(2,1)}), bf16[16,128,256]{2,1,0:T(8,128)(2,1)S(1)}, u32[]{:S(2)}, u32[]{:S(2)}) async-start(bf16[16,128,256]{2,1,0:T(8,128)(2,1)} %broadcast_in_dim.10), calls=%async_computation.1 | async-start | bytes 2097152 | tf_op jit(solution)/shard_map/all_to_all | solution.py:26
  38.4 13.0 %collective-permute-start.7 = (bf16[6,256]{1,0:T(8,128)(2,1)S(1)}, bf16[6,256]{1,0:T(8,128)(2,1)S(1)}, u32[]{:S(2)}, u32[]{:S(2)}) collective-permute-start(bf16[6,256]{1,0:T(8,128)(2,1)S(1)} %slice.75), channel_id=1, source_target_pairs={{8,0},{16,8},{24,16},{32,24},{40,32},{48,40},{56,48},{64,56},{72,6... | collective-permute-start | bytes 9224 | tf_op jit(solution)/shard_map/ppermute | solution.py:160
  39.8 12.2 %collective-permute-start.4 = (bf16[64,2048]{1,0:T(8,128)(2,1)S(1)}, bf16[64,2048]{1,0:T(8,128)(2,1)S(1)}, u32[]{:S(2)}, u32[]{:S(2)}) collective-permute-start(bf16[64,2048]{1,0:T(8,128)(2,1)S(1)} %collective-permute-done.refs_1_), channel_id=1, source_target_pairs={{0,1},{1,0},{2,3},{3,2},{4,5},{5,4},{6,7},{7,6},{8,9},{9,8},{10,11... | collective-permute-start | bytes 786440 | tf_op jit(solution)/shard_map/ppermute | solution.py:139
  45.7 6.4 %collective-permute-start.5 = (bf16[64,2048]{1,0:T(8,128)(2,1)S(1)}, bf16[64,2048]{1,0:T(8,128)(2,1)S(1)}, u32[]{:S(2)}, u32[]{:S(2)}) collective-permute-start(bf16[64,2048]{1,0:T(8,128)(2,1)S(1)} %collective-permute-done.1.refs_2_), channel_id=1, source_target_pairs={{0,1},{1,0},{2,3},{3,2},{4,5},{5,4},{6,7},{7,6},{8,9},{9,8},{10,11... | collective-permute-start | bytes 786440 | tf_op jit(solution)/shard_map/ppermute | solution.py:139
  49.5 3.4 %collective-permute-start.6 = (bf16[64,2048]{1,0:T(8,128)(2,1)S(1)}, bf16[64,2048]{1,0:T(8,128)(2,1)S(1)}, u32[]{:S(2)}, u32[]{:S(2)}) collective-permute-start(bf16[64,2048]{1,0:T(8,128)(2,1)S(1)} %collective-permute-done.2.refs_3_), channel_id=1, source_target_pairs={{0,1},{1,0},{2,3},{3,2},{4,5},{5,4},{6,7},{7,6},{8,9},{9,8},{10,11... | collective-permute-start | bytes 786440 | tf_op jit(solution)/shard_map/ppermute | solution.py:139
  51.6 1.3 %copy-start.1 = (bf16[64,2048]{1,0:T(8,128)(2,1)S(1)}, bf16[64,2048]{1,0:T(8,128)(2,1)}, u32[]{:S(2)}) copy-start(bf16[64,2048]{1,0:T(8,128)(2,1)} %refs_0_.1) | copy-start | bytes 786436
  56.4 1.3 %copy-start = (bf16[512,2048]{1,0:T(8,128)(2,1)}, bf16[512,2048]{1,0:T(8,128)(2,1)S(1)}, u32[]{:S(2)}) copy-start(bf16[512,2048]{1,0:T(8,128)(2,1)S(1)} %get-tuple-element.13.slab_ref) | copy-start | bytes 6291460
  63.0 11.6 %copy-start.3 = (bf16[4,1,64,256]{3,2,1,0:T(8,128)(2,1)S(1)}, bf16[4,1,64,256]{3,2,1,0:T(8,128)(2,1)}, u32[]{:S(2)}) copy-start(bf16[4,1,64,256]{3,2,1,0:T(8,128)(2,1)} %get-tuple-element.27) | copy-start | bytes 393220
  64.5 10.1 %collective-permute-start.8 = (bf16[256,2048]{1,0:T(8,128)(2,1)}, bf16[256,2048]{1,0:T(8,128)(2,1)S(1)}, u32[]{:S(2)}, u32[]{:S(2)}) collective-permute-start(bf16[256,2048]{1,0:T(8,128)(2,1)} %convolution_convert_fusion), channel_id=1, source_target_pairs={{0,1},{1,0},{2,3},{3,2},{4,5},{5,4},{6,7},{7,6},{8,9},{9,8},{10,11... | collective-permute-start | bytes 3145736 | tf_op jit(solution)/shard_map/ppermute | solution.py:139
  66.5 26.7 %all-to-all-start.2 = ((bf16[16,144,256]{2,1,0:T(8,128)(2,1)}), bf16[16,144,256]{2,1,0:T(8,128)(2,1)S(1)}, u32[]{:S(2)}, u32[]{:S(2)}) async-start(bf16[16,144,256]{2,1,0:T(8,128)(2,1)} %shard_map.68), calls=%async_computation.2 | async-start | bytes 2359296 | tf_op jit(solution)/shard_map/all_to_all | solution.py:26
  75.1 5.8 %copy-start.2 = (bf16[256,2048]{1,0:T(8,128)(2,1)}, bf16[256,2048]{1,0:T(8,128)(2,1)S(1)}, u32[]{:S(2)}) copy-start(bf16[256,2048]{1,0:T(8,128)(2,1)S(1)} %add_convert_fusion) | copy-start | bytes 3145732
  75.2 30.8 %collective-permute-start.10 = (bf16[64,2048]{1,0:T(8,128)(2,1)S(1)}, bf16[64,2048]{1,0:T(8,128)(2,1)S(1)}, u32[]{:S(2)}, u32[]{:S(2)}) collective-permute-start(bf16[64,2048]{1,0:T(8,128)(2,1)S(1)} %get-tuple-element.25), channel_id=1, source_target_pairs={{0,6},{2,0},{4,2},{6,4},{1,7},{3,1},{5,3},{7,5},{8,14},{10,8},{12,... | collective-permute-start | bytes 786440 | tf_op jit(solution)/shard_map/ppermute | solution.py:31
  79.0 27.0 %collective-permute-start.11 = (bf16[64,2048]{1,0:T(8,128)(2,1)S(1)}, bf16[64,2048]{1,0:T(8,128)(2,1)S(1)}, u32[]{:S(2)}, u32[]{:S(2)}) collective-permute-start(bf16[64,2048]{1,0:T(8,128)(2,1)S(1)} %get-tuple-element.24), channel_id=1, source_target_pairs={{0,2},{2,4},{4,6},{6,0},{1,3},{3,5},{5,7},{7,1},{8,10},{10,12},{12... | collective-permute-start | bytes 786440 | tf_op jit(solution)/shard_map/ppermute | solution.py:31
  80.9 25.1 %collective-permute-start.9 = (bf16[64,2048]{1,0:T(8,128)(2,1)S(1)}, bf16[64,2048]{1,0:T(8,128)(2,1)S(1)}, u32[]{:S(2)}, u32[]{:S(2)}) collective-permute-start(bf16[64,2048]{1,0:T(8,128)(2,1)S(1)} %get-tuple-element.23), channel_id=1, source_target_pairs={{0,4},{2,6},{4,0},{6,2},{1,5},{3,7},{5,1},{7,3},{8,12},{10,14},{12... | collective-permute-start | bytes 786440 | tf_op jit(solution)/shard_map/ppermute | solution.py:31
  94.1 24.2 %all-to-all-start.3 = ((bf16[4,48,256]{2,1,0:T(8,128)(2,1)}), bf16[4,48,256]{2,1,0:T(8,128)(2,1)S(1)}, u32[]{:S(2)}, u32[]{:S(2)}) async-start(bf16[4,48,256]{2,1,0:T(8,128)(2,1)} %pad_maximum_fusion), calls=%async_computation.3 | async-start | bytes 196608 | tf_op jit(solution)/shard_map/all_to_all | solution.py:26

commit v9 on v6

--- a/solution.py
+++ b/solution.py
@@ -6,6 +6,7 @@
 from jax.sharding import Mesh, PartitionSpec as P
 
 TAPS = 7
+VMEM_BYTES = 12 * 1024 * 1024
 BF = jnp.bfloat16
 F32 = jnp.float32
 ZH, X, Y, ZL, C = "zh", "x", "y", "zl", "c"
@@ -30,17 +31,43 @@
     return lax.ppermute(value, axis, [(source, (source - steps) % count) for source in range(count)])
 
 
+def order_kernel(place_ref, *refs):
+    chunks, slab_ref = refs[:-1], refs[-1]
+    count = chunks[0].shape[0]
+    for index, chunk in enumerate(chunks):
+        slab_ref[pl.ds(pl.multiple_of(place_ref[index] * count, count), count), :] = chunk[...]
+
+
+def in_order(places, chunks):
+    count, depth = chunks[0].shape
+    part = depth // 4
+    return pl.pallas_call(
+        order_kernel,
+        grid_spec=pltpu.PrefetchScalarGridSpec(
+            num_scalar_prefetch=1,
+            grid=(depth // part,),
+            in_specs=[pl.BlockSpec((count, part), lambda i, _: (0, i)) for _ in chunks],
+            out_specs=pl.BlockSpec((len(chunks) * count, part), lambda i, _: (0, i)),
+        ),
+        out_shape=jax.ShapeDtypeStruct((len(chunks) * count, depth), BF),
+        compiler_params=pltpu.CompilerParams(vmem_limit_bytes=VMEM_BYTES),
+        cost_estimate=pl.CostEstimate(
+            flops=8 * 10**9, bytes_accessed=4 * len(chunks) * count * depth, transcendentals=0
+        ),
+    )(places, *chunks)
+
+
 def products_kernel(slab_ref, weight_ref, grad_ref, extended_ref, out_ref, featured_ref):
     step = pl.program_id(0)
     slab_len, cols = grad_ref.shape
-    nxy = out_ref.shape[0]
-    rows = slab_ref.shape[1] // nxy
+    nxy, rows, _ = weight_ref.shape
     products = lax.dot_general(
         slab_ref[...], grad_ref[...], (((0,), (0,)), ((), ())), preferred_element_type=F32
     )
     here = pl.ds(pl.multiple_of(step * rows, rows), rows)
     out_ref[:, here, :] = products.astype(BF).reshape(nxy, rows, cols)
-    term = jnp.dot(slab_ref[...], weight_ref[...], preferred_element_type=F32)
+    weight = weight_ref[...].reshape(nxy * rows, cols)
+    term = jnp.dot(slab_ref[...], weight, preferred_element_type=F32)
 
     @pl.when(step == 0)
     def _():
@@ -61,38 +88,35 @@
         out_ref[:, pl.num_programs(0) * rows :, :] = jnp.broadcast_to(tail[None], (nxy, 16, cols))
 
 
-def local_products(slab, weight, grad_bf, extended, nxy, rows):
+def local_products(slab, gathered, grad_bf, extended, nz, rows):
     slab_len, depth = slab.shape
-    cols = weight.shape[1]
-    nz = depth // (nxy * rows)
+    nxy, _, cols = gathered.shape
     part = nxy * rows
     return pl.pallas_call(
         products_kernel,
         grid=(nz,),
         in_specs=[
             pl.BlockSpec((slab_len, part), lambda i: (0, i)),
-            pl.BlockSpec((part, cols), lambda i: (i, 0)),
+            pl.BlockSpec((nxy, rows, cols), lambda i: (0, i, 0)),
             pl.BlockSpec((slab_len, cols), lambda i: (0, 0)),
             pl.BlockSpec(extended.shape, lambda i: (0, 0)),
         ],
         out_specs=pl.BlockSpec((nxy, nz * rows + 16, cols), lambda i: (0, 0, 0)),
         out_shape=jax.ShapeDtypeStruct((nxy, nz * rows + 16, cols), BF),
         scratch_shapes=[pltpu.VMEM((slab_len, cols), F32)],
-        compiler_params=pltpu.CompilerParams(vmem_limit_bytes=32 * 1024 * 1024),
+        compiler_params=pltpu.CompilerParams(vmem_limit_bytes=52 * 1024 * 1024),
         cost_estimate=pl.CostEstimate(
             flops=4 * slab_len * depth * cols, bytes_accessed=4 * slab_len * depth, transcendentals=0
         ),
-    )(slab, weight, grad_bf, extended)
+    )(slab, gathered, grad_bf, extended)
 
 
-def weight_columns(proj_weight):
-    rows, cols = proj_weight.shape
-    nz = lax.axis_size(ZH)
-    nxy = lax.axis_size((X, Y))
-    column = lax.all_gather(proj_weight, ZH)
-    repeated = jnp.broadcast_to(column[None], (nxy, nz, rows, cols))
-    gathered = lax.all_to_all(repeated, (X, Y), split_axis=0, concat_axis=0, tiled=True)
-    return gathered.transpose(1, 0, 2, 3).reshape(nz * nxy * rows, cols)
+def spread(value, axes):
+    return exchange(jnp.broadcast_to(value[None], (lax.axis_size(axes),) + value.shape), axes)
+
+
+def swap(value):
+    return lax.ppermute(value, C, [(0, 1), (1, 0)])
 
 
 def body(tokens, proj_weight, cotangent, filters):
@@ -103,34 +127,43 @@
     rows, cols = proj_weight.shape
     own_tokens, depth = tokens.shape
 
-    slab = lax.all_gather(tokens, (ZL, C), axis=0, tiled=True)
-    slab_len = slab.shape[0]
-    following = lax.ppermute(
-        cotangent[: TAPS - 1], (ZH, X, Y), [(source, source - 1) for source in range(1, ndp)]
-    )
-    nothing = jnp.zeros((2, cols), BF)
-    extended = jnp.concatenate([cotangent, following, nothing], 0).astype(F32)
+    slab_len = cotangent.shape[0]
+    core, chip = lax.axis_index(C), lax.axis_index(ZL)
+    direct = [tokens] + [None] * (nzl - 1)
+    for steps in (2, 1, 3):
+        direct[steps] = from_ahead(tokens, ZL, steps)
+    sources = (chip + jnp.arange(nzl)) % nzl
+    places = jnp.concatenate([2 * sources + core, 2 * sources + 1 - core]).astype(jnp.int32)
+
+    zh, xy = lax.axis_index(ZH), lax.axis_index((X, Y))
+    head = cotangent[:8]
+    column = spread(jnp.concatenate([proj_weight, head], 0), ZH)
+    ahead = lax.dynamic_index_in_dim(column, (zh + 1) % nz, 0, keepdims=False)[rows:]
+    column = column[:, :rows].reshape(nz * rows, cols)
+    gathered = spread(jnp.concatenate([column, head, ahead], 0), (X, Y))
+    heads = lax.dynamic_index_in_dim(gathered, (xy + 1) % nxy, 0, keepdims=False)[nz * rows :]
+    following = jnp.where(xy == nxy - 1, heads[8:], heads[:8])
+    following = jnp.where(zh * nxy + xy == ndp - 1, jnp.zeros((), BF), following)
+    extended = jnp.concatenate([cotangent, following], 0).astype(F32)
     grad_feat = jnp.zeros((slab_len, cols), F32)
     for tap in range(TAPS):
         grad_feat = grad_feat + filters[tap] * extended[tap : tap + slab_len]
     grad_bf = grad_feat.astype(BF)
 
-    weight = weight_columns(proj_weight)
+    chunks = direct + [swap(value) for value in direct]
+    slab = in_order(places, chunks)
+    packed = local_products(slab, gathered, grad_bf, extended, nz, rows)
+    packed, grad_late, gathered = lax.optimization_barrier((packed, grad_bf, gathered))
+    total = jnp.sum(exchange(packed, (X, Y)).astype(F32), axis=0)
 
-    core, chip = lax.axis_index(C), lax.axis_index(ZL)
-    by_core = grad_bf.reshape(nzl, 2, own_tokens, cols)
+    weight = gathered[:, : nz * rows].reshape(nxy, nz, rows, cols)
+    weight = weight.transpose(1, 0, 2, 3).reshape(depth, cols)
+    by_core = grad_late.reshape(nzl, 2, own_tokens, cols)
     theirs = lax.dynamic_index_in_dim(by_core, 1 - core, 1, keepdims=False).reshape(-1, cols)
     ours = lax.dynamic_index_in_dim(by_core, core, 1, keepdims=False).reshape(-1, cols)
     contract_cols = (((1,), (1,)), ((), ()))
     for_other = lax.dot_general(theirs, weight, contract_cols, preferred_element_type=F32).astype(BF)
-    for_other, grad_late = lax.optimization_barrier((for_other, grad_bf))
-    from_other = lax.ppermute(for_other, C, [(0, 1), (1, 0)])
-
-    packed = local_products(slab, weight, grad_late, extended, nxy, rows)
-    packed, ours = lax.optimization_barrier((packed, ours))
-    arrived = exchange(packed, (X, Y))
-    total = jnp.sum(arrived.astype(F32), axis=0)
-
+    from_other = swap(for_other)
     here = lax.dot_general(ours, weight, contract_cols, preferred_element_type=F32)
     chip_sum = (here + from_other.astype(F32)).astype(BF)
     chip_sum = chip_sum.reshape(nzl, own_tokens, depth)

time: 121 us -> 122 us (level)
  the two profiles are of different devices: /device:TPU:40 before, /device:TPU:1 now
where the time goes in v9:
time: 122 us; the launch traced here: 120 us
  starting transfers between devices  75.9 us (62%)
  waiting for transfers between devices  20.1 us (16%)
  local copies, waits for them, and re-layouts  8.06 us (7%)
  Pallas kernels  6.68 us (5%)
  other arithmetic  5.37 us (4%)
  matrix products  3.13 us (3%)
    all_to_all x4, starting transfers between devices, exchange(): return lax.all_to_all(value, axes, split_axis=0, concat_axis=0, tiled=True)  41 us
    ppermute x5, starting transfers between devices, swap(): return lax.ppermute(value, C, [(0, 1), (1, 0)])  17.5 us
    ppermute x6, starting transfers between devices, from_ahead(): lax.ppermute(value, axis, [(source, (source - steps) % count) for source...  17.4 us
    all_to_all x4, waiting for transfers between devices, exchange(): return lax.all_to_all(value, axes, split_axis=0, concat_axis=0, tiled=True)  14.4 us
    pallas_call x1, Pallas kernels, local_products(): pl.pallas_call(products_kernel, grid=(nz,), in_specs=[pl.BlockSpec((slab_...  5.49 us
    ppermute x6, waiting for transfers between devices, from_ahead(): lax.ppermute(value, axis, [(source, (source - steps) % count) for source...  4.86 us
  transfers between devices with their start and end apart: 15, of which 6 were waited for; matrix products, arithmetic and copies ran while one was open for 6% of the time, Pallas kernels for 1%

profile of v9, /device:TPU:1, one launch (start us, length us, event | category | flops | bytes accessed | tf_op | source)
XLA Modules:
  0.0 120.2 jit_solution(7103239200011429423)
XLA Ops:
  2.7 15.8 %all-to-all-start = ((bf16[4,40,256]{2,1,0:T(8,128)(2,1)}), bf16[4,40,256]{2,1,0:T(8,128)(2,1)S(1)}, u32[]{:S(2)}, u32[]{:S(2)}) async-start(bf16[4,40,256]{2,1,0:T(8,128)(2,1)} %broadcast_in_dim.10), calls=%async_computation | async-start | bytes 163840 | tf_op jit(solution)/shard_map/all_to_all | solution.py:26
  18.5 3.5 %collective-permute-start = (bf16[64,2048]{1,0:T(8,128)(2,1)}, bf16[64,2048]{1,0:T(8,128)(2,1)S(1)}, u32[]{:S(2)}, u32[]{:S(2)}) collective-permute-start(bf16[64,2048]{1,0:T(8,128)(2,1)} %refs_0_.1), channel_id=1, source_target_pairs={{0,6},{2,0},{4,2},{6,4},{1,7},{3,1},{5,3},{7,5},{8,14},{10,8},{12,... | collective-permute-start | bytes 786440 | tf_op jit(solution)/shard_map/ppermute | solution.py:31
  22.0 2.2 %collective-permute-start.1 = (bf16[64,2048]{1,0:T(8,128)(2,1)}, bf16[64,2048]{1,0:T(8,128)(2,1)S(1)}, u32[]{:S(2)}, u32[]{:S(2)}) collective-permute-start(bf16[64,2048]{1,0:T(8,128)(2,1)} %refs_0_.1), channel_id=1, source_target_pairs={{0,4},{2,6},{4,0},{6,2},{1,5},{3,7},{5,1},{7,3},{8,12},{10,14},{12... | collective-permute-start | bytes 786440 | tf_op jit(solution)/shard_map/ppermute | solution.py:31
  24.2 2.6 %collective-permute-start.2 = (bf16[64,2048]{1,0:T(8,128)(2,1)}, bf16[64,2048]{1,0:T(8,128)(2,1)S(1)}, u32[]{:S(2)}, u32[]{:S(2)}) collective-permute-start(bf16[64,2048]{1,0:T(8,128)(2,1)} %refs_0_.1), channel_id=1, source_target_pairs={{0,2},{2,4},{4,6},{6,0},{1,3},{3,5},{5,7},{7,1},{8,10},{10,12},{12... | collective-permute-start | bytes 786440 | tf_op jit(solution)/shard_map/ppermute | solution.py:31
  26.9 3.7 %collective-permute-start.3 = (bf16[64,2048]{1,0:T(8,128)(2,1)}, bf16[64,2048]{1,0:T(8,128)(2,1)S(1)}, u32[]{:S(2)}, u32[]{:S(2)}) collective-permute-start(bf16[64,2048]{1,0:T(8,128)(2,1)} %refs_0_.1), channel_id=1, source_target_pairs={{0,1},{1,0},{2,3},{3,2},{4,5},{5,4},{6,7},{7,6},{8,9},{9,8},{10,11... | collective-permute-start | bytes 786440 | tf_op jit(solution)/shard_map/ppermute | solution.py:119
  32.1 6.8 %all-to-all-start.1 = ((bf16[16,144,256]{2,1,0:T(8,128)(2,1)}), bf16[16,144,256]{2,1,0:T(8,128)(2,1)S(1)}, u32[]{:S(2)}, u32[]{:S(2)}) async-start(bf16[16,144,256]{2,1,0:T(8,128)(2,1)} %broadcast_in_dim.11), calls=%async_computation.1 | async-start | bytes 2359296 | tf_op jit(solution)/shard_map/all_to_all | solution.py:26
  38.9 4.4 %collective-permute-start.4 = (bf16[64,2048]{1,0:T(8,128)(2,1)S(1)}, bf16[64,2048]{1,0:T(8,128)(2,1)S(1)}, u32[]{:S(2)}, u32[]{:S(2)}) collective-permute-start(bf16[64,2048]{1,0:T(8,128)(2,1)S(1)} %collective-permute-done.refs_1_), channel_id=1, source_target_pairs={{0,1},{1,0},{2,3},{3,2},{4,5},{5,4},{6,7},{7,6},{8,9},{9,8},{10,11... | collective-permute-start | bytes 786440 | tf_op jit(solution)/shard_map/ppermute | solution.py:119
  43.4 3.5 %collective-permute-done.1.refs_2_ = bf16[64,2048]{1,0:T(8,128)(2,1)S(1)} collective-permute-done((bf16[64,2048]{1,0:T(8,128)(2,1)}, bf16[64,2048]{1,0:T(8,128)(2,1)S(1)}, u32[]{:S(2)}, u32[]{:S(2)}) %collective-permute-start.1) | collective-permute-done | bytes 262176 | tf_op jit(solution)/shard_map/ppermute | solution.py:31
  46.9 3.8 %collective-permute-start.5 = (bf16[64,2048]{1,0:T(8,128)(2,1)S(1)}, bf16[64,2048]{1,0:T(8,128)(2,1)S(1)}, u32[]{:S(2)}, u32[]{:S(2)}) collective-permute-start(bf16[64,2048]{1,0:T(8,128)(2,1)S(1)} %collective-permute-done.1.refs_2_), channel_id=1, source_target_pairs={{0,1},{1,0},{2,3},{3,2},{4,5},{5,4},{6,7},{7,6},{8,9},{9,8},{10,11... | collective-permute-start | bytes 786440 | tf_op jit(solution)/shard_map/ppermute | solution.py:119
  50.7 1.9 %collective-permute-start.6 = (bf16[64,2048]{1,0:T(8,128)(2,1)S(1)}, bf16[64,2048]{1,0:T(8,128)(2,1)S(1)}, u32[]{:S(2)}, u32[]{:S(2)}) collective-permute-start(bf16[64,2048]{1,0:T(8,128)(2,1)S(1)} %collective-permute-done.2.refs_3_), channel_id=1, source_target_pairs={{0,1},{1,0},{2,3},{3,2},{4,5},{5,4},{6,7},{7,6},{8,9},{9,8},{10,11... | collective-permute-start | bytes 786440 | tf_op jit(solution)/shard_map/ppermute | solution.py:119
  55.3 1.3 %copy-done = bf16[512,2048]{1,0:T(8,128)(2,1)} copy-done((bf16[512,2048]{1,0:T(8,128)(2,1)}, bf16[512,2048]{1,0:T(8,128)(2,1)S(1)}, u32[]{:S(2)}) %copy-start) | copy-done | bytes 2097176
  58.0 5.5 %shard_map.68 = bf16[16,144,256]{2,1,0:T(8,128)(2,1)} custom-call(bf16[512,2048]{1,0:T(8,128)(2,1)} %copy-done, bf16[16,144,256]{2,1,0:T(8,128)(2,1)} %copy-done.2, bf16[512,256]{1,0:T(8,128)(2,1)S(1)} %fusion.1.grad_ref, f32[520,256]{1,0:T(8,128)S(1)} %maximum_convert_fusion.extended_ref), custom_call_target="tpu_custom_call" | custom-call | flops 1073741824 | bytes 4194304 | tf_op jit(solution)/shard_map/pallas_call | solution.py:95
  64.8 1.4 %convolution_convert_fusion = bf16[256,2048]{1,0:T(8,128)(2,1)} fusion(bf16[256,256]{1,0:T(8,128)(2,1)S(1)} %bitcast.41, bf16[2048,256]{1,0:T(8,128)(2,1)S(1)} %bitcast.36), kind=kOutput, calls=%fused_computation | convolution fusion | flops 268959744 | bytes 2228224 | tf_op jit(solution)/shard_map/dot_general | solution.py:165
  66.3 3.7 %collective-permute-start.7 = (bf16[256,2048]{1,0:T(8,128)(2,1)}, bf16[256,2048]{1,0:T(8,128)(2,1)S(1)}, u32[]{:S(2)}, u32[]{:S(2)}) collective-permute-start(bf16[256,2048]{1,0:T(8,128)(2,1)} %convolution_convert_fusion), channel_id=1, source_target_pairs={{0,1},{1,0},{2,3},{3,2},{4,5},{5,4},{6,7},{7,6},{8,9},{9,8},{10,11... | collective-permute-start | bytes 3145736 | tf_op jit(solution)/shard_map/ppermute | solution.py:119
  69.9 5.2 %all-to-all-start.2 = ((bf16[16,144,256]{2,1,0:T(8,128)(2,1)}), bf16[16,144,256]{2,1,0:T(8,128)(2,1)S(1)}, u32[]{:S(2)}, u32[]{:S(2)}) async-start(bf16[16,144,256]{2,1,0:T(8,128)(2,1)} %shard_map.68), calls=%async_computation.2 | async-start | bytes 2359296 | tf_op jit(solution)/shard_map/all_to_all | solution.py:26
  76.1 1.7 %add_convert_fusion = bf16[256,2048]{1,0:T(8,128)(2,1)S(1)} fusion(bf16[256,2048]{1,0:T(8,128)(2,1)} %copy-done.3, bf16[256,256]{1,0:T(8,128)(2,1)S(1)} %bitcast.40, bf16[2048,256]{1,0:T(8,128)(2,1)S(1)} %bitcast.37), kind=kOutput, calls=%fused_computation.2 | convolution fusion | flops 270008320 | bytes 3276800 | tf_op jit(solution)/shard_map/dot_general | solution.py:167
  78.6 1.9 %collective-permute-start.10 = (bf16[64,2048]{1,0:T(8,128)(2,1)}, bf16[64,2048]{1,0:T(8,128)(2,1)S(1)}, u32[]{:S(2)}, u32[]{:S(2)}) collective-permute-start(bf16[64,2048]{1,0:T(8,128)(2,1)} %get-tuple-element.16), channel_id=1, source_target_pairs={{0,2},{2,4},{4,6},{6,0},{1,3},{3,5},{5,7},{7,1},{8,10},{10,12},{12... | collective-permute-start | bytes 786440 | tf_op jit(solution)/shard_map/ppermute | solution.py:31
  80.5 5.2 %collective-permute-start.9 = (bf16[64,2048]{1,0:T(8,128)(2,1)S(1)}, bf16[64,2048]{1,0:T(8,128)(2,1)S(1)}, u32[]{:S(2)}, u32[]{:S(2)}) collective-permute-start(bf16[64,2048]{1,0:T(8,128)(2,1)S(1)} %get-tuple-element.17), channel_id=1, source_target_pairs={{0,6},{2,0},{4,2},{6,4},{1,7},{3,1},{5,3},{7,5},{8,14},{10,8},{12,... | collective-permute-start | bytes 786440 | tf_op jit(solution)/shard_map/ppermute | solution.py:31
  85.7 1.9 %collective-permute-start.8 = (bf16[64,2048]{1,0:T(8,128)(2,1)S(1)}, bf16[64,2048]{1,0:T(8,128)(2,1)}, u32[]{:S(2)}, u32[]{:S(2)}) collective-permute-start(bf16[64,2048]{1,0:T(8,128)(2,1)S(1)} %get-tuple-element.15), channel_id=1, source_target_pairs={{0,4},{2,6},{4,0},{6,2},{1,5},{3,7},{5,1},{7,3},{8,12},{10,14},{12... | collective-permute-start | bytes 786440 | tf_op jit(solution)/shard_map/ppermute | solution.py:31
  87.6 4.5 %all-to-all-done.2 = bf16[16,144,256]{2,1,0:T(8,128)(2,1)S(1)} async-done(((bf16[16,144,256]{2,1,0:T(8,128)(2,1)}), bf16[16,144,256]{2,1,0:T(8,128)(2,1)S(1)}, u32[]{:S(2)}, u32[]{:S(2)}) %all-to-all-start.2) | async-done | bytes 1179680 | tf_op jit(solution)/shard_map/all_to_all | solution.py:26
  93.0 13.4 %all-to-all-start.3 = ((bf16[4,48,256]{2,1,0:T(8,128)(2,1)}), bf16[4,48,256]{2,1,0:T(8,128)(2,1)S(1)}, u32[]{:S(2)}, u32[]{:S(2)}) async-start(bf16[4,48,256]{2,1,0:T(8,128)(2,1)} %pad_maximum_fusion), calls=%async_computation.3 | async-start | bytes 196608 | tf_op jit(solution)/shard_map/all_to_all | solution.py:26
  106.4 1.3 %collective-permute-done.8 = bf16[64,2048]{1,0:T(8,128)(2,1)} collective-permute-done((bf16[64,2048]{1,0:T(8,128)(2,1)S(1)}, bf16[64,2048]{1,0:T(8,128)(2,1)}, u32[]{:S(2)}, u32[]{:S(2)}) %collective-permute-start.8) | collective-permute-done | bytes 262176 | tf_op jit(solution)/shard_map/ppermute | solution.py:31
  107.7 1.8 %fusion.9 = bf16[64,2048]{1,0:T(8,128)(2,1)} fusion(bf16[64,2048]{1,0:T(8,128)(2,1)S(1)} %collective-permute-done.10, bf16[64,2048]{1,0:T(8,128)(2,1)S(1)} %collective-permute-done.9, bf16[64,2048]{1,0:T(8,128)(2,1)} %collective-permute-done.8, bf16[4,64,2048]{2,1,0:T(8,128)(2,1)S(1)} %bitcast.39, s32[]{:T(128)S(6)} %select_n.89), kind=kLoop, calls=%fused_computation.20 | loop fusion | flops 1048576 | bytes 1310724 | tf_op jit(solution)/shard_map/convert_element_type | solution.py:174
  109.5 9.5 %all-to-all-done.3 = bf16[4,48,256]{2,1,0:T(8,128)(2,1)S(1)} async-done(((bf16[4,48,256]{2,1,0:T(8,128)(2,1)}), bf16[4,48,256]{2,1,0:T(8,128)(2,1)S(1)}, u32[]{:S(2)}, u32[]{:S(2)}) %all-to-all-start.3) | async-done | bytes 98336 | tf_op jit(solution)/shard_map/all_to_all | solution.py:26
  (51 shorter events, 12.8 us)
Async XLA Ops:
  2.7 50.0 %copy-start.5 = (f32[7,256]{1,0:T(8,128)S(1)}, f32[7,256]{1,0:T(8,128)}, u32[]{:S(2)}) copy-start(f32[7,256]{1,0:T(8,128)} %param.7) | copy-start | bytes 21508
  2.7 51.4 %copy-start.1 = (bf16[64,2048]{1,0:T(8,128)(2,1)S(1)}, bf16[64,2048]{1,0:T(8,128)(2,1)}, u32[]{:S(2)}) copy-start(bf16[64,2048]{1,0:T(8,128)(2,1)} %refs_0_.1) | copy-start | bytes 786436
  2.7 28.3 %all-to-all-start = ((bf16[4,40,256]{2,1,0:T(8,128)(2,1)}), bf16[4,40,256]{2,1,0:T(8,128)(2,1)S(1)}, u32[]{:S(2)}, u32[]{:S(2)}) async-start(bf16[4,40,256]{2,1,0:T(8,128)(2,1)} %broadcast_in_dim.10), calls=%async_computation | async-start | bytes 163840 | tf_op jit(solution)/shard_map/all_to_all | solution.py:26
  18.5 20.5 %collective-permute-start = (bf16[64,2048]{1,0:T(8,128)(2,1)}, bf16[64,2048]{1,0:T(8,128)(2,1)S(1)}, u32[]{:S(2)}, u32[]{:S(2)}) collective-permute-start(bf16[64,2048]{1,0:T(8,128)(2,1)} %refs_0_.1), channel_id=1, source_target_pairs={{0,6},{2,0},{4,2},{6,4},{1,7},{3,1},{5,3},{7,5},{8,14},{10,8},{12,... | collective-permute-start | bytes 786440 | tf_op jit(solution)/shard_map/ppermute | solution.py:31
  22.0 24.9 %collective-permute-start.1 = (bf16[64,2048]{1,0:T(8,128)(2,1)}, bf16[64,2048]{1,0:T(8,128)(2,1)S(1)}, u32[]{:S(2)}, u32[]{:S(2)}) collective-permute-start(bf16[64,2048]{1,0:T(8,128)(2,1)} %refs_0_.1), channel_id=1, source_target_pairs={{0,4},{2,6},{4,0},{6,2},{1,5},{3,7},{5,1},{7,3},{8,12},{10,14},{12... | collective-permute-start | bytes 786440 | tf_op jit(solution)/shard_map/ppermute | solution.py:31
  24.2 26.5 %collective-permute-start.2 = (bf16[64,2048]{1,0:T(8,128)(2,1)}, bf16[64,2048]{1,0:T(8,128)(2,1)S(1)}, u32[]{:S(2)}, u32[]{:S(2)}) collective-permute-start(bf16[64,2048]{1,0:T(8,128)(2,1)} %refs_0_.1), channel_id=1, source_target_pairs={{0,2},{2,4},{4,6},{6,0},{1,3},{3,5},{5,7},{7,1},{8,10},{10,12},{12... | collective-permute-start | bytes 786440 | tf_op jit(solution)/shard_map/ppermute | solution.py:31
  26.9 26.4 %collective-permute-start.3 = (bf16[64,2048]{1,0:T(8,128)(2,1)}, bf16[64,2048]{1,0:T(8,128)(2,1)S(1)}, u32[]{:S(2)}, u32[]{:S(2)}) collective-permute-start(bf16[64,2048]{1,0:T(8,128)(2,1)} %refs_0_.1), channel_id=1, source_target_pairs={{0,1},{1,0},{2,3},{3,2},{4,5},{5,4},{6,7},{7,6},{8,9},{9,8},{10,11... | collective-permute-start | bytes 786440 | tf_op jit(solution)/shard_map/ppermute | solution.py:119
  32.1 24.5 %all-to-all-start.1 = ((bf16[16,144,256]{2,1,0:T(8,128)(2,1)}), bf16[16,144,256]{2,1,0:T(8,128)(2,1)S(1)}, u32[]{:S(2)}, u32[]{:S(2)}) async-start(bf16[16,144,256]{2,1,0:T(8,128)(2,1)} %broadcast_in_dim.11), calls=%async_computation.1 | async-start | bytes 2359296 | tf_op jit(solution)/shard_map/all_to_all | solution.py:26
  38.9 14.4 %collective-permute-start.4 = (bf16[64,2048]{1,0:T(8,128)(2,1)S(1)}, bf16[64,2048]{1,0:T(8,128)(2,1)S(1)}, u32[]{:S(2)}, u32[]{:S(2)}) collective-permute-start(bf16[64,2048]{1,0:T(8,128)(2,1)S(1)} %collective-permute-done.refs_1_), channel_id=1, source_target_pairs={{0,1},{1,0},{2,3},{3,2},{4,5},{5,4},{6,7},{7,6},{8,9},{9,8},{10,11... | collective-permute-start | bytes 786440 | tf_op jit(solution)/shard_map/ppermute | solution.py:119
  46.9 6.4 %collective-permute-start.5 = (bf16[64,2048]{1,0:T(8,128)(2,1)S(1)}, bf16[64,2048]{1,0:T(8,128)(2,1)S(1)}, u32[]{:S(2)}, u32[]{:S(2)}) collective-permute-start(bf16[64,2048]{1,0:T(8,128)(2,1)S(1)} %collective-permute-done.1.refs_2_), channel_id=1, source_target_pairs={{0,1},{1,0},{2,3},{3,2},{4,5},{5,4},{6,7},{7,6},{8,9},{9,8},{10,11... | collective-permute-start | bytes 786440 | tf_op jit(solution)/shard_map/ppermute | solution.py:119
  50.7 3.4 %collective-permute-start.6 = (bf16[64,2048]{1,0:T(8,128)(2,1)S(1)}, bf16[64,2048]{1,0:T(8,128)(2,1)S(1)}, u32[]{:S(2)}, u32[]{:S(2)}) collective-permute-start(bf16[64,2048]{1,0:T(8,128)(2,1)S(1)} %collective-permute-done.2.refs_3_), channel_id=1, source_target_pairs={{0,1},{1,0},{2,3},{3,2},{4,5},{5,4},{6,7},{7,6},{8,9},{9,8},{10,11... | collective-permute-start | bytes 786440 | tf_op jit(solution)/shard_map/ppermute | solution.py:119
  53.3 3.3 %copy-start.4 = (bf16[512,256]{1,0:T(8,128)(2,1)S(1)}, bf16[512,256]{1,0:T(8,128)(2,1)}, u32[]{:S(2)}) copy-start(bf16[512,256]{1,0:T(8,128)(2,1)} %param.6) | copy-start | bytes 786436
  55.3 1.3 %copy-start = (bf16[512,2048]{1,0:T(8,128)(2,1)}, bf16[512,2048]{1,0:T(8,128)(2,1)S(1)}, u32[]{:S(2)}) copy-start(bf16[512,2048]{1,0:T(8,128)(2,1)S(1)} %shard_map.67.slab_ref) | copy-start | bytes 6291460
  56.6 1.4 %copy-start.2 = (bf16[16,144,256]{2,1,0:T(8,128)(2,1)}, bf16[16,144,256]{2,1,0:T(8,128)(2,1)S(1)}, u32[]{:S(2)}) copy-start(bf16[16,144,256]{2,1,0:T(8,128)(2,1)S(1)} %all-to-all-done.1.weight_ref) | copy-start | bytes 3538948
  63.5 1.2 %slice-start = ((bf16[16,144,256]{2,1,0:T(8,128)(2,1)}), bf16[16,128,256]{2,1,0:T(8,128)(2,1)S(1)}, s32[]{:S(2)}) async-start(bf16[16,144,256]{2,1,0:T(8,128)(2,1)} %copy-done.2), calls=%async_computation.4 | async-start | bytes 2097152 | tf_op jit(solution)/shard_map/slice | solution.py:159
  66.3 8.9 %collective-permute-start.7 = (bf16[256,2048]{1,0:T(8,128)(2,1)}, bf16[256,2048]{1,0:T(8,128)(2,1)S(1)}, u32[]{:S(2)}, u32[]{:S(2)}) collective-permute-start(bf16[256,2048]{1,0:T(8,128)(2,1)} %convolution_convert_fusion), channel_id=1, source_target_pairs={{0,1},{1,0},{2,3},{3,2},{4,5},{5,4},{6,7},{7,6},{8,9},{9,8},{10,11... | collective-permute-start | bytes 3145736 | tf_op jit(solution)/shard_map/ppermute | solution.py:119
  69.9 22.2 %all-to-all-start.2 = ((bf16[16,144,256]{2,1,0:T(8,128)(2,1)}), bf16[16,144,256]{2,1,0:T(8,128)(2,1)S(1)}, u32[]{:S(2)}, u32[]{:S(2)}) async-start(bf16[16,144,256]{2,1,0:T(8,128)(2,1)} %shard_map.68), calls=%async_computation.2 | async-start | bytes 2359296 | tf_op jit(solution)/shard_map/all_to_all | solution.py:26
  75.2 1.0 copy-start.3
  78.6 27.7 %collective-permute-start.10 = (bf16[64,2048]{1,0:T(8,128)(2,1)}, bf16[64,2048]{1,0:T(8,128)(2,1)S(1)}, u32[]{:S(2)}, u32[]{:S(2)}) collective-permute-start(bf16[64,2048]{1,0:T(8,128)(2,1)} %get-tuple-element.16), channel_id=1, source_target_pairs={{0,2},{2,4},{4,6},{6,0},{1,3},{3,5},{5,7},{7,1},{8,10},{10,12},{12... | collective-permute-start | bytes 786440 | tf_op jit(solution)/shard_map/ppermute | solution.py:31
  80.5 25.8 %collective-permute-start.9 = (bf16[64,2048]{1,0:T(8,128)(2,1)S(1)}, bf16[64,2048]{1,0:T(8,128)(2,1)S(1)}, u32[]{:S(2)}, u32[]{:S(2)}) collective-permute-start(bf16[64,2048]{1,0:T(8,128)(2,1)S(1)} %get-tuple-element.17), channel_id=1, source_target_pairs={{0,6},{2,0},{4,2},{6,4},{1,7},{3,1},{5,3},{7,5},{8,14},{10,8},{12,... | collective-permute-start | bytes 786440 | tf_op jit(solution)/shard_map/ppermute | solution.py:31
  85.7 22.0 %collective-permute-start.8 = (bf16[64,2048]{1,0:T(8,128)(2,1)S(1)}, bf16[64,2048]{1,0:T(8,128)(2,1)}, u32[]{:S(2)}, u32[]{:S(2)}) collective-permute-start(bf16[64,2048]{1,0:T(8,128)(2,1)S(1)} %get-tuple-element.15), channel_id=1, source_target_pairs={{0,4},{2,6},{4,0},{6,2},{1,5},{3,7},{5,1},{7,3},{8,12},{10,14},{12... | collective-permute-start | bytes 786440 | tf_op jit(solution)/shard_map/ppermute | solution.py:31
  93.0 26.0 %all-to-all-start.3 = ((bf16[4,48,256]{2,1,0:T(8,128)(2,1)}), bf16[4,48,256]{2,1,0:T(8,128)(2,1)S(1)}, u32[]{:S(2)}, u32[]{:S(2)}) async-start(bf16[4,48,256]{2,1,0:T(8,128)(2,1)} %pad_maximum_fusion), calls=%async_computation.3 | async-start | bytes 196608 | tf_op jit(solution)/shard_map/all_to_all | solution.py:26

commit v10 on v9

--- a/solution.py
+++ b/solution.py
@@ -7,6 +7,7 @@
 
 TAPS = 7
 VMEM_BYTES = 12 * 1024 * 1024
+PRODUCTS_VMEM = 49 * 1024 * 1024
 BF = jnp.bfloat16
 F32 = jnp.float32
 ZH, X, Y, ZL, C = "zh", "x", "y", "zl", "c"
@@ -57,16 +58,43 @@
     )(places, *chunks)
 
 
-def products_kernel(slab_ref, weight_ref, grad_ref, extended_ref, out_ref, featured_ref):
-    step = pl.program_id(0)
+def products_kernel(
+    core_ref, slab_ref, weight_ref, cotangent_ref, following_ref, filters_ref,
+    packed_ref, theirs_out, ours_out, extended_ref, grad_ref, theirs_ref, ours_ref, featured_ref,
+):
+    step, core = pl.program_id(0), core_ref[0]
     slab_len, cols = grad_ref.shape
     nxy, rows, _ = weight_ref.shape
+    half = theirs_ref.shape[0]
+    own = slab_len // 8
+
+    @pl.when(step == 0)
+    def _():
+        extended_ref[:slab_len, :] = cotangent_ref[...].astype(F32)
+        extended_ref[slab_len:, :] = following_ref[...]
+        grad_feat = filters_ref[0:1, :] * extended_ref[0:slab_len, :]
+        for tap in range(1, TAPS):
+            grad_feat = grad_feat + filters_ref[tap : tap + 1, :] * extended_ref[tap : tap + slab_len, :]
+        grad_ref[...] = grad_feat.astype(BF)
+        for index in range(half // own):
+            there = pl.ds(pl.multiple_of((2 * index + 1 - core) * own, own), own)
+            here = pl.ds(pl.multiple_of((2 * index + core) * own, own), own)
+            theirs_ref[index * own : (index + 1) * own, :] = grad_ref[there, :]
+            ours_ref[index * own : (index + 1) * own, :] = grad_ref[here, :]
+
+    weight = weight_ref[...].reshape(nxy * rows, cols)
+    contract_cols = (((1,), (1,)), ((), ()))
+    theirs_out[...] = lax.dot_general(
+        theirs_ref[...], weight, contract_cols, preferred_element_type=F32
+    ).astype(BF)
+    ours_out[...] = lax.dot_general(
+        ours_ref[...], weight, contract_cols, preferred_element_type=F32
+    ).astype(BF)
     products = lax.dot_general(
         slab_ref[...], grad_ref[...], (((0,), (0,)), ((), ())), preferred_element_type=F32
     )
-    here = pl.ds(pl.multiple_of(step * rows, rows), rows)
-    out_ref[:, here, :] = products.astype(BF).reshape(nxy, rows, cols)
-    weight = weight_ref[...].reshape(nxy * rows, cols)
+    place = pl.ds(pl.multiple_of(step * rows, rows), rows)
+    packed_ref[:, place, :] = products.astype(BF).reshape(nxy, rows, cols)
     term = jnp.dot(slab_ref[...], weight, preferred_element_type=F32)
 
     @pl.when(step == 0)
@@ -85,30 +113,49 @@
             for tap in range(TAPS)
         ]
         tail = split_rows(jnp.concatenate(sums + [jnp.zeros((1, cols), F32)], 0))
-        out_ref[:, pl.num_programs(0) * rows :, :] = jnp.broadcast_to(tail[None], (nxy, 16, cols))
-
-
-def local_products(slab, gathered, grad_bf, extended, nz, rows):
+        packed_ref[:, pl.num_programs(0) * rows :, :] = jnp.broadcast_to(tail[None], (nxy, 16, cols))
+
+
+def local_products(core, slab, gathered, cotangent, following, filters, nz, rows):
     slab_len, depth = slab.shape
     nxy, _, cols = gathered.shape
     part = nxy * rows
+    half = slab_len // 2
     return pl.pallas_call(
         products_kernel,
-        grid=(nz,),
-        in_specs=[
-            pl.BlockSpec((slab_len, part), lambda i: (0, i)),
-            pl.BlockSpec((nxy, rows, cols), lambda i: (0, i, 0)),
-            pl.BlockSpec((slab_len, cols), lambda i: (0, 0)),
-            pl.BlockSpec(extended.shape, lambda i: (0, 0)),
+        grid_spec=pltpu.PrefetchScalarGridSpec(
+            num_scalar_prefetch=1,
+            grid=(nz,),
+            in_specs=[
+                pl.BlockSpec((slab_len, part), lambda i, _: (0, i)),
+                pl.BlockSpec((nxy, rows, cols), lambda i, _: (0, i, 0)),
+                pl.BlockSpec((slab_len, cols), lambda i, _: (0, 0)),
+                pl.BlockSpec(following.shape, lambda i, _: (0, 0)),
+                pl.BlockSpec(filters.shape, lambda i, _: (0, 0)),
+            ],
+            out_specs=[
+                pl.BlockSpec((nxy, nz * rows + 16, cols), lambda i, _: (0, 0, 0)),
+                pl.BlockSpec((half, part), lambda i, _: (0, i)),
+                pl.BlockSpec((half, part), lambda i, _: (0, i)),
+            ],
+            scratch_shapes=[
+                pltpu.VMEM((slab_len + 8, cols), F32),
+                pltpu.VMEM((slab_len, cols), BF),
+                pltpu.VMEM((half, cols), BF),
+                pltpu.VMEM((half, cols), BF),
+                pltpu.VMEM((slab_len, cols), F32),
+            ],
+        ),
+        out_shape=[
+            jax.ShapeDtypeStruct((nxy, nz * rows + 16, cols), BF),
+            jax.ShapeDtypeStruct((half, depth), BF),
+            jax.ShapeDtypeStruct((half, depth), BF),
         ],
-        out_specs=pl.BlockSpec((nxy, nz * rows + 16, cols), lambda i: (0, 0, 0)),
-        out_shape=jax.ShapeDtypeStruct((nxy, nz * rows + 16, cols), BF),
-        scratch_shapes=[pltpu.VMEM((slab_len, cols), F32)],
-        compiler_params=pltpu.CompilerParams(vmem_limit_bytes=52 * 1024 * 1024),
+        compiler_params=pltpu.CompilerParams(vmem_limit_bytes=PRODUCTS_VMEM),
         cost_estimate=pl.CostEstimate(
-            flops=4 * slab_len * depth * cols, bytes_accessed=4 * slab_len * depth, transcendentals=0
-        ),
-    )(slab, gathered, grad_bf, extended)
+            flops=6 * slab_len * depth * cols, bytes_accessed=6 * slab_len * depth, transcendentals=0
+        ),
+    )(core.reshape(1).astype(jnp.int32), slab, gathered, cotangent, following, filters)
 
 
 def spread(value, axes):
@@ -143,29 +190,15 @@
     gathered = spread(jnp.concatenate([column, head, ahead], 0), (X, Y))
     heads = lax.dynamic_index_in_dim(gathered, (xy + 1) % nxy, 0, keepdims=False)[nz * rows :]
     following = jnp.where(xy == nxy - 1, heads[8:], heads[:8])
-    following = jnp.where(zh * nxy + xy == ndp - 1, jnp.zeros((), BF), following)
-    extended = jnp.concatenate([cotangent, following], 0).astype(F32)
-    grad_feat = jnp.zeros((slab_len, cols), F32)
-    for tap in range(TAPS):
-        grad_feat = grad_feat + filters[tap] * extended[tap : tap + slab_len]
-    grad_bf = grad_feat.astype(BF)
-
+    following = jnp.where(zh * nxy + xy == ndp - 1, jnp.zeros((), BF), following).astype(F32)
     chunks = direct + [swap(value) for value in direct]
     slab = in_order(places, chunks)
-    packed = local_products(slab, gathered, grad_bf, extended, nz, rows)
-    packed, grad_late, gathered = lax.optimization_barrier((packed, grad_bf, gathered))
+    packed, for_other, here = local_products(
+        core, slab, gathered, cotangent, following, filters, nz, rows
+    )
     total = jnp.sum(exchange(packed, (X, Y)).astype(F32), axis=0)
 
-    weight = gathered[:, : nz * rows].reshape(nxy, nz, rows, cols)
-    weight = weight.transpose(1, 0, 2, 3).reshape(depth, cols)
-    by_core = grad_late.reshape(nzl, 2, own_tokens, cols)
-    theirs = lax.dynamic_index_in_dim(by_core, 1 - core, 1, keepdims=False).reshape(-1, cols)
-    ours = lax.dynamic_index_in_dim(by_core, core, 1, keepdims=False).reshape(-1, cols)
-    contract_cols = (((1,), (1,)), ((), ()))
-    for_other = lax.dot_general(theirs, weight, contract_cols, preferred_element_type=F32).astype(BF)
-    from_other = swap(for_other)
-    here = lax.dot_general(ours, weight, contract_cols, preferred_element_type=F32)
-    chip_sum = (here + from_other.astype(F32)).astype(BF)
+    chip_sum = (here.astype(F32) + swap(for_other).astype(F32)).astype(BF)
     chip_sum = chip_sum.reshape(nzl, own_tokens, depth)
     summed = lax.dynamic_index_in_dim(chip_sum, chip, 0, keepdims=False).astype(F32)
     for steps in (2, 1, 3):

time: 122 us -> 116 us (0.951)
  the two profiles are of different devices: /device:TPU:1 before, /device:TPU:8 now
where the time goes in v10:
time: 116 us; the launch traced here: 115 us
  starting transfers between devices  69.1 us (60%)
  waiting for transfers between devices  26.6 us (23%)
  Pallas kernels  7.74 us (7%)
  other arithmetic  5.65 us (5%)
  local copies, waits for them, and re-layouts  5.16 us (4%)
    all_to_all x4, starting transfers between devices, exchange(): return lax.all_to_all(value, axes, split_axis=0, concat_axis=0, tiled=True)  39.7 us
    all_to_all x4, waiting for transfers between devices, exchange(): return lax.all_to_all(value, axes, split_axis=0, concat_axis=0, tiled=True)  23.1 us
    ppermute x6, starting transfers between devices, from_ahead(): lax.ppermute(value, axis, [(source, (source - steps) % count) for source...  18.8 us
    ppermute x5, starting transfers between devices, swap(): return lax.ppermute(value, C, [(0, 1), (1, 0)])  10.6 us
    pallas_call x1, Pallas kernels, local_products(): pl.pallas_call(products_kernel, grid_spec=pltpu.PrefetchScalarGridSpec(nu...  6.55 us
    ppermute x6, waiting for transfers between devices, from_ahead(): lax.ppermute(value, axis, [(source, (source - steps) % count) for source...  2.52 us
  transfers between devices with their start and end apart: 15, of which 6 were waited for; matrix products, arithmetic and copies ran while one was open for 5% of the time, Pallas kernels for 1%

profile of v10, /device:TPU:8, one launch (start us, length us, event | category | flops | bytes accessed | tf_op | source)
XLA Modules:
  0.0 115.1 jit_solution(1168365152130773632)
XLA Ops:
  2.7 15.1 %all-to-all-start = ((bf16[4,40,256]{2,1,0:T(8,128)(2,1)}), bf16[4,40,256]{2,1,0:T(8,128)(2,1)S(1)}, u32[]{:S(2)}, u32[]{:S(2)}) async-start(bf16[4,40,256]{2,1,0:T(8,128)(2,1)} %broadcast_in_dim.10), calls=%async_computation | async-start | bytes 163840 | tf_op jit(solution)/shard_map/all_to_all | solution.py:27
  17.8 3.8 %collective-permute-start = (bf16[64,2048]{1,0:T(8,128)(2,1)}, bf16[64,2048]{1,0:T(8,128)(2,1)S(1)}, u32[]{:S(2)}, u32[]{:S(2)}) collective-permute-start(bf16[64,2048]{1,0:T(8,128)(2,1)} %refs_0_.1), channel_id=1, source_target_pairs={{0,6},{2,0},{4,2},{6,4},{1,7},{3,1},{5,3},{7,5},{8,14},{10,8},{12,... | collective-permute-start | bytes 786440 | tf_op jit(solution)/shard_map/ppermute | solution.py:32
  21.6 2.5 %collective-permute-start.1 = (bf16[64,2048]{1,0:T(8,128)(2,1)}, bf16[64,2048]{1,0:T(8,128)(2,1)S(1)}, u32[]{:S(2)}, u32[]{:S(2)}) collective-permute-start(bf16[64,2048]{1,0:T(8,128)(2,1)} %refs_0_.1), channel_id=1, source_target_pairs={{0,4},{2,6},{4,0},{6,2},{1,5},{3,7},{5,1},{7,3},{8,12},{10,14},{12... | collective-permute-start | bytes 786440 | tf_op jit(solution)/shard_map/ppermute | solution.py:32
  24.1 2.9 %collective-permute-start.2 = (bf16[64,2048]{1,0:T(8,128)(2,1)}, bf16[64,2048]{1,0:T(8,128)(2,1)S(1)}, u32[]{:S(2)}, u32[]{:S(2)}) collective-permute-start(bf16[64,2048]{1,0:T(8,128)(2,1)} %refs_0_.1), channel_id=1, source_target_pairs={{0,2},{2,4},{4,6},{6,0},{1,3},{3,5},{5,7},{7,1},{8,10},{10,12},{12... | collective-permute-start | bytes 786440 | tf_op jit(solution)/shard_map/ppermute | solution.py:32
  27.0 4.6 %all-to-all-done = bf16[4,40,256]{2,1,0:T(8,128)(2,1)S(1)} async-done(((bf16[4,40,256]{2,1,0:T(8,128)(2,1)}), bf16[4,40,256]{2,1,0:T(8,128)(2,1)S(1)}, u32[]{:S(2)}, u32[]{:S(2)}) %all-to-all-start) | async-done | bytes 81952 | tf_op jit(solution)/shard_map/all_to_all | solution.py:27
  32.7 7.5 %all-to-all-start.1 = ((bf16[16,144,256]{2,1,0:T(8,128)(2,1)}), bf16[16,144,256]{2,1,0:T(8,128)(2,1)S(1)}, u32[]{:S(2)}, u32[]{:S(2)}) async-start(bf16[16,144,256]{2,1,0:T(8,128)(2,1)} %broadcast_in_dim.11), calls=%async_computation.1 | async-start | bytes 2359296 | tf_op jit(solution)/shard_map/all_to_all | solution.py:27
  40.3 1.9 %collective-permute-start.3 = (bf16[64,2048]{1,0:T(8,128)(2,1)S(1)}, bf16[64,2048]{1,0:T(8,128)(2,1)S(1)}, u32[]{:S(2)}, u32[]{:S(2)}) collective-permute-start(bf16[64,2048]{1,0:T(8,128)(2,1)S(1)} %copy-done.1), channel_id=1, source_target_pairs={{0,1},{1,0},{2,3},{3,2},{4,5},{5,4},{6,7},{7,6},{8,9},{9,8},{10,11... | collective-permute-start | bytes 786440 | tf_op jit(solution)/shard_map/ppermute | solution.py:166
  42.2 2.4 %collective-permute-start.4 = (bf16[64,2048]{1,0:T(8,128)(2,1)S(1)}, bf16[64,2048]{1,0:T(8,128)(2,1)S(1)}, u32[]{:S(2)}, u32[]{:S(2)}) collective-permute-start(bf16[64,2048]{1,0:T(8,128)(2,1)S(1)} %collective-permute-done.refs_1_), channel_id=1, source_target_pairs={{0,1},{1,0},{2,3},{3,2},{4,5},{5,4},{6,7},{7,6},{8,9},{9,8},{10,11... | collective-permute-start | bytes 786440 | tf_op jit(solution)/shard_map/ppermute | solution.py:166
  44.6 2.5 %collective-permute-done.1.refs_2_ = bf16[64,2048]{1,0:T(8,128)(2,1)S(1)} collective-permute-done((bf16[64,2048]{1,0:T(8,128)(2,1)}, bf16[64,2048]{1,0:T(8,128)(2,1)S(1)}, u32[]{:S(2)}, u32[]{:S(2)}) %collective-permute-start.1) | collective-permute-done | bytes 262176 | tf_op jit(solution)/shard_map/ppermute | solution.py:32
  47.1 1.9 %collective-permute-start.5 = (bf16[64,2048]{1,0:T(8,128)(2,1)S(1)}, bf16[64,2048]{1,0:T(8,128)(2,1)S(1)}, u32[]{:S(2)}, u32[]{:S(2)}) collective-permute-start(bf16[64,2048]{1,0:T(8,128)(2,1)S(1)} %collective-permute-done.1.refs_2_), channel_id=1, source_target_pairs={{0,1},{1,0},{2,3},{3,2},{4,5},{5,4},{6,7},{7,6},{8,9},{9,8},{10,11... | collective-permute-start | bytes 786440 | tf_op jit(solution)/shard_map/ppermute | solution.py:166
  49.1 2.4 %collective-permute-start.6 = (bf16[64,2048]{1,0:T(8,128)(2,1)S(1)}, bf16[64,2048]{1,0:T(8,128)(2,1)S(1)}, u32[]{:S(2)}, u32[]{:S(2)}) collective-permute-start(bf16[64,2048]{1,0:T(8,128)(2,1)S(1)} %collective-permute-done.2.refs_3_), channel_id=1, source_target_pairs={{0,1},{1,0},{2,3},{3,2},{4,5},{5,4},{6,7},{7,6},{8,9},{9,8},{10,11... | collective-permute-start | bytes 786440 | tf_op jit(solution)/shard_map/ppermute | solution.py:166
  52.6 1.2 %shard_map.67.slab_ref = bf16[512,2048]{1,0:T(8,128)(2,1)S(1)} custom-call(s32[8]{0:T(128)S(1)} %pad_add_fusion.place_ref, bf16[64,2048]{1,0:T(8,128)(2,1)S(1)} %copy-done.1, bf16[64,2048]{1,0:T(8,128)(2,1)S(1)} %collective-permute-done.refs_1_, bf16[64,2048]{1,0:T(8,128)(2,1)S(1)} %collective-permute-done.1.refs_2_, ...), custom_call_target="tpu_custom_call" | custom-call | flops 8000000000 | bytes 4194304 | tf_op jit(solution)/shard_map/pallas_call | solution.py:45
  53.8 1.3 %copy-done.3 = bf16[512,2048]{1,0:T(8,128)(2,1)} copy-done((bf16[512,2048]{1,0:T(8,128)(2,1)}, bf16[512,2048]{1,0:T(8,128)(2,1)S(1)}, u32[]{:S(2)}) %copy-start.3) | copy-done | bytes 2097176
  55.9 6.5 %shard_map.68 = (bf16[16,144,256]{2,1,0:T(8,128)(2,1)}, bf16[256,2048]{1,0:T(8,128)(2,1)S(1)}, bf16[256,2048]{1,0:T(8,128)(2,1)S(1)}) custom-call(s32[1]{0:T(128)} %bitcast.core_ref, bf16[512,2048]{1,0:T(8,128)(2,1)} %copy-done.3, bf16[16,144,256]{2,1,0:T(8,128)(2,1)S(1)} %all-to-all-done.1.weight_ref, bf16[512,256]{1,0:T(8,128)(2,1)S(1)} %copy-done, ...), custom_call_target="tpu_custom_call" | custom-call | flops 1610612736 | bytes 6291456 | tf_op jit(solution)/shard_map/pallas_call | solution.py:124
  62.5 1.9 %collective-permute-start.7 = (bf16[256,2048]{1,0:T(8,128)(2,1)S(1)}, bf16[256,2048]{1,0:T(8,128)(2,1)}, u32[]{:S(2)}, u32[]{:S(2)}) collective-permute-start(bf16[256,2048]{1,0:T(8,128)(2,1)S(1)} %get-tuple-element.10), channel_id=1, source_target_pairs={{0,1},{1,0},{2,3},{3,2},{4,5},{5,4},{6,7},{7,6},{8,9},{9,8},{10,11... | collective-permute-start | bytes 3145736 | tf_op jit(solution)/shard_map/ppermute | solution.py:166
  64.4 7.0 %all-to-all-start.2 = ((bf16[16,144,256]{2,1,0:T(8,128)(2,1)}), bf16[16,144,256]{2,1,0:T(8,128)(2,1)S(1)}, u32[]{:S(2)}, u32[]{:S(2)}) async-start(bf16[16,144,256]{2,1,0:T(8,128)(2,1)} %get-tuple-element.8), calls=%async_computation.2 | async-start | bytes 2359296 | tf_op jit(solution)/shard_map/all_to_all | solution.py:27
  71.4 1.6 %add_convert_fusion = bf16[256,2048]{1,0:T(8,128)(2,1)S(1)} fusion(bf16[256,2048]{1,0:T(8,128)(2,1)} %collective-permute-done.7, bf16[256,2048]{1,0:T(8,128)(2,1)S(1)} %get-tuple-element.9), kind=kLoop, calls=%fused_computation.1 | loop fusion | flops 2097152 | bytes 3145728 | tf_op jit(solution)/shard_map/convert_element_type | solution.py:201
  73.8 1.9 %collective-permute-start.10 = (bf16[64,2048]{1,0:T(8,128)(2,1)}, bf16[64,2048]{1,0:T(8,128)(2,1)S(1)}, u32[]{:S(2)}, u32[]{:S(2)}) collective-permute-start(bf16[64,2048]{1,0:T(8,128)(2,1)} %get-tuple-element.16), channel_id=1, source_target_pairs={{0,2},{2,4},{4,6},{6,0},{1,3},{3,5},{5,7},{7,1},{8,10},{10,12},{12... | collective-permute-start | bytes 786440 | tf_op jit(solution)/shard_map/ppermute | solution.py:32
  75.7 2.4 %collective-permute-start.8 = (bf16[64,2048]{1,0:T(8,128)(2,1)S(1)}, bf16[64,2048]{1,0:T(8,128)(2,1)S(1)}, u32[]{:S(2)}, u32[]{:S(2)}) collective-permute-start(bf16[64,2048]{1,0:T(8,128)(2,1)S(1)} %get-tuple-element.15), channel_id=1, source_target_pairs={{0,4},{2,6},{4,0},{6,2},{1,5},{3,7},{5,1},{7,3},{8,12},{10,14},{12... | collective-permute-start | bytes 786440 | tf_op jit(solution)/shard_map/ppermute | solution.py:32
  78.1 5.2 %collective-permute-start.9 = (bf16[64,2048]{1,0:T(8,128)(2,1)S(1)}, bf16[64,2048]{1,0:T(8,128)(2,1)}, u32[]{:S(2)}, u32[]{:S(2)}) collective-permute-start(bf16[64,2048]{1,0:T(8,128)(2,1)S(1)} %get-tuple-element.17), channel_id=1, source_target_pairs={{0,6},{2,0},{4,2},{6,4},{1,7},{3,1},{5,3},{7,5},{8,14},{10,8},{12,... | collective-permute-start | bytes 786440 | tf_op jit(solution)/shard_map/ppermute | solution.py:32
  83.4 6.3 %all-to-all-done.2 = bf16[16,144,256]{2,1,0:T(8,128)(2,1)S(1)} async-done(((bf16[16,144,256]{2,1,0:T(8,128)(2,1)}), bf16[16,144,256]{2,1,0:T(8,128)(2,1)S(1)}, u32[]{:S(2)}, u32[]{:S(2)}) %all-to-all-start.2) | async-done | bytes 1179680 | tf_op jit(solution)/shard_map/all_to_all | solution.py:27
  90.5 10.1 %all-to-all-start.3 = ((bf16[4,48,256]{2,1,0:T(8,128)(2,1)}), bf16[4,48,256]{2,1,0:T(8,128)(2,1)S(1)}, u32[]{:S(2)}, u32[]{:S(2)}) async-start(bf16[4,48,256]{2,1,0:T(8,128)(2,1)} %pad_maximum_fusion), calls=%async_computation.3 | async-start | bytes 196608 | tf_op jit(solution)/shard_map/all_to_all | solution.py:27
  100.6 1.8 %fusion.2 = bf16[64,2048]{1,0:T(8,128)(2,1)} fusion(bf16[64,2048]{1,0:T(8,128)(2,1)S(1)} %collective-permute-done.10, bf16[64,2048]{1,0:T(8,128)(2,1)} %collective-permute-done.9, bf16[64,2048]{1,0:T(8,128)(2,1)S(1)} %collective-permute-done.8, bf16[4,64,2048]{2,1,0:T(8,128)(2,1)S(1)} %bitcast.21, s32[]{:T(128)S(6)} %select_n.77), kind=kLoop, calls=%fused_computation.5 | loop fusion | flops 1048576 | bytes 1310724 | tf_op jit(solution)/shard_map/convert_element_type | solution.py:207
  102.4 11.5 %all-to-all-done.3 = bf16[4,48,256]{2,1,0:T(8,128)(2,1)S(1)} async-done(((bf16[4,48,256]{2,1,0:T(8,128)(2,1)}), bf16[4,48,256]{2,1,0:T(8,128)(2,1)S(1)}, u32[]{:S(2)}, u32[]{:S(2)}) %all-to-all-start.3) | async-done | bytes 98336 | tf_op jit(solution)/shard_map/all_to_all | solution.py:27
  (39 shorter events, 7.9 us)
Async XLA Ops:
  2.7 28.9 %all-to-all-start = ((bf16[4,40,256]{2,1,0:T(8,128)(2,1)}), bf16[4,40,256]{2,1,0:T(8,128)(2,1)S(1)}, u32[]{:S(2)}, u32[]{:S(2)}) async-start(bf16[4,40,256]{2,1,0:T(8,128)(2,1)} %broadcast_in_dim.10), calls=%async_computation | async-start | bytes 163840 | tf_op jit(solution)/shard_map/all_to_all | solution.py:27
  17.8 24.4 %collective-permute-start = (bf16[64,2048]{1,0:T(8,128)(2,1)}, bf16[64,2048]{1,0:T(8,128)(2,1)S(1)}, u32[]{:S(2)}, u32[]{:S(2)}) collective-permute-start(bf16[64,2048]{1,0:T(8,128)(2,1)} %refs_0_.1), channel_id=1, source_target_pairs={{0,6},{2,0},{4,2},{6,4},{1,7},{3,1},{5,3},{7,5},{8,14},{10,8},{12,... | collective-permute-start | bytes 786440 | tf_op jit(solution)/shard_map/ppermute | solution.py:32
  21.6 25.5 %collective-permute-start.1 = (bf16[64,2048]{1,0:T(8,128)(2,1)}, bf16[64,2048]{1,0:T(8,128)(2,1)S(1)}, u32[]{:S(2)}, u32[]{:S(2)}) collective-permute-start(bf16[64,2048]{1,0:T(8,128)(2,1)} %refs_0_.1), channel_id=1, source_target_pairs={{0,4},{2,6},{4,0},{6,2},{1,5},{3,7},{5,1},{7,3},{8,12},{10,14},{12... | collective-permute-start | bytes 786440 | tf_op jit(solution)/shard_map/ppermute | solution.py:32
  24.1 25.0 %collective-permute-start.2 = (bf16[64,2048]{1,0:T(8,128)(2,1)}, bf16[64,2048]{1,0:T(8,128)(2,1)S(1)}, u32[]{:S(2)}, u32[]{:S(2)}) collective-permute-start(bf16[64,2048]{1,0:T(8,128)(2,1)} %refs_0_.1), channel_id=1, source_target_pairs={{0,2},{2,4},{4,6},{6,0},{1,3},{3,5},{5,7},{7,1},{8,10},{10,12},{12... | collective-permute-start | bytes 786440 | tf_op jit(solution)/shard_map/ppermute | solution.py:32
  32.7 7.5 %copy-start.1 = (bf16[64,2048]{1,0:T(8,128)(2,1)S(1)}, bf16[64,2048]{1,0:T(8,128)(2,1)}, u32[]{:S(2)}) copy-start(bf16[64,2048]{1,0:T(8,128)(2,1)} %refs_0_.1) | copy-start | bytes 786436
  32.7 23.2 %all-to-all-start.1 = ((bf16[16,144,256]{2,1,0:T(8,128)(2,1)}), bf16[16,144,256]{2,1,0:T(8,128)(2,1)S(1)}, u32[]{:S(2)}, u32[]{:S(2)}) async-start(bf16[16,144,256]{2,1,0:T(8,128)(2,1)} %broadcast_in_dim.11), calls=%async_computation.1 | async-start | bytes 2359296 | tf_op jit(solution)/shard_map/all_to_all | solution.py:27
  40.3 11.3 %collective-permute-start.3 = (bf16[64,2048]{1,0:T(8,128)(2,1)S(1)}, bf16[64,2048]{1,0:T(8,128)(2,1)S(1)}, u32[]{:S(2)}, u32[]{:S(2)}) collective-permute-start(bf16[64,2048]{1,0:T(8,128)(2,1)S(1)} %copy-done.1), channel_id=1, source_target_pairs={{0,1},{1,0},{2,3},{3,2},{4,5},{5,4},{6,7},{7,6},{8,9},{9,8},{10,11... | collective-permute-start | bytes 786440 | tf_op jit(solution)/shard_map/ppermute | solution.py:166
  42.2 9.4 %collective-permute-start.4 = (bf16[64,2048]{1,0:T(8,128)(2,1)S(1)}, bf16[64,2048]{1,0:T(8,128)(2,1)S(1)}, u32[]{:S(2)}, u32[]{:S(2)}) collective-permute-start(bf16[64,2048]{1,0:T(8,128)(2,1)S(1)} %collective-permute-done.refs_1_), channel_id=1, source_target_pairs={{0,1},{1,0},{2,3},{3,2},{4,5},{5,4},{6,7},{7,6},{8,9},{9,8},{10,11... | collective-permute-start | bytes 786440 | tf_op jit(solution)/shard_map/ppermute | solution.py:166
  47.1 4.5 %collective-permute-start.5 = (bf16[64,2048]{1,0:T(8,128)(2,1)S(1)}, bf16[64,2048]{1,0:T(8,128)(2,1)S(1)}, u32[]{:S(2)}, u32[]{:S(2)}) collective-permute-start(bf16[64,2048]{1,0:T(8,128)(2,1)S(1)} %collective-permute-done.1.refs_2_), channel_id=1, source_target_pairs={{0,1},{1,0},{2,3},{3,2},{4,5},{5,4},{6,7},{7,6},{8,9},{9,8},{10,11... | collective-permute-start | bytes 786440 | tf_op jit(solution)/shard_map/ppermute | solution.py:166
  49.1 3.6 %collective-permute-start.6 = (bf16[64,2048]{1,0:T(8,128)(2,1)S(1)}, bf16[64,2048]{1,0:T(8,128)(2,1)S(1)}, u32[]{:S(2)}, u32[]{:S(2)}) collective-permute-start(bf16[64,2048]{1,0:T(8,128)(2,1)S(1)} %collective-permute-done.2.refs_3_), channel_id=1, source_target_pairs={{0,1},{1,0},{2,3},{3,2},{4,5},{5,4},{6,7},{7,6},{8,9},{9,8},{10,11... | collective-permute-start | bytes 786440 | tf_op jit(solution)/shard_map/ppermute | solution.py:166
  51.6 4.3 %copy-start = (bf16[512,256]{1,0:T(8,128)(2,1)S(1)}, bf16[512,256]{1,0:T(8,128)(2,1)}, u32[]{:S(2)}) copy-start(bf16[512,256]{1,0:T(8,128)(2,1)} %cotangent_ref.1) | copy-start | bytes 786436
  51.6 4.3 %copy-start.2 = (f32[7,256]{1,0:T(8,128)S(1)}, f32[7,256]{1,0:T(8,128)}, u32[]{:S(2)}) copy-start(f32[7,256]{1,0:T(8,128)} %filters_ref.1) | copy-start | bytes 21508
  53.8 1.3 %copy-start.3 = (bf16[512,2048]{1,0:T(8,128)(2,1)}, bf16[512,2048]{1,0:T(8,128)(2,1)S(1)}, u32[]{:S(2)}) copy-start(bf16[512,2048]{1,0:T(8,128)(2,1)S(1)} %shard_map.67.slab_ref) | copy-start | bytes 6291460
  62.5 8.9 %collective-permute-start.7 = (bf16[256,2048]{1,0:T(8,128)(2,1)S(1)}, bf16[256,2048]{1,0:T(8,128)(2,1)}, u32[]{:S(2)}, u32[]{:S(2)}) collective-permute-start(bf16[256,2048]{1,0:T(8,128)(2,1)S(1)} %get-tuple-element.10), channel_id=1, source_target_pairs={{0,1},{1,0},{2,3},{3,2},{4,5},{5,4},{6,7},{7,6},{8,9},{9,8},{10,11... | collective-permute-start | bytes 3145736 | tf_op jit(solution)/shard_map/ppermute | solution.py:166
  64.4 25.2 %all-to-all-start.2 = ((bf16[16,144,256]{2,1,0:T(8,128)(2,1)}), bf16[16,144,256]{2,1,0:T(8,128)(2,1)S(1)}, u32[]{:S(2)}, u32[]{:S(2)}) async-start(bf16[16,144,256]{2,1,0:T(8,128)(2,1)} %get-tuple-element.8), calls=%async_computation.2 | async-start | bytes 2359296 | tf_op jit(solution)/shard_map/all_to_all | solution.py:27
  73.8 26.8 %collective-permute-start.10 = (bf16[64,2048]{1,0:T(8,128)(2,1)}, bf16[64,2048]{1,0:T(8,128)(2,1)S(1)}, u32[]{:S(2)}, u32[]{:S(2)}) collective-permute-start(bf16[64,2048]{1,0:T(8,128)(2,1)} %get-tuple-element.16), channel_id=1, source_target_pairs={{0,2},{2,4},{4,6},{6,0},{1,3},{3,5},{5,7},{7,1},{8,10},{10,12},{12... | collective-permute-start | bytes 786440 | tf_op jit(solution)/shard_map/ppermute | solution.py:32
  75.7 24.9 %collective-permute-start.8 = (bf16[64,2048]{1,0:T(8,128)(2,1)S(1)}, bf16[64,2048]{1,0:T(8,128)(2,1)S(1)}, u32[]{:S(2)}, u32[]{:S(2)}) collective-permute-start(bf16[64,2048]{1,0:T(8,128)(2,1)S(1)} %get-tuple-element.15), channel_id=1, source_target_pairs={{0,4},{2,6},{4,0},{6,2},{1,5},{3,7},{5,1},{7,3},{8,12},{10,14},{12... | collective-permute-start | bytes 786440 | tf_op jit(solution)/shard_map/ppermute | solution.py:32
  78.1 22.5 %collective-permute-start.9 = (bf16[64,2048]{1,0:T(8,128)(2,1)S(1)}, bf16[64,2048]{1,0:T(8,128)(2,1)}, u32[]{:S(2)}, u32[]{:S(2)}) collective-permute-start(bf16[64,2048]{1,0:T(8,128)(2,1)S(1)} %get-tuple-element.17), channel_id=1, source_target_pairs={{0,6},{2,0},{4,2},{6,4},{1,7},{3,1},{5,3},{7,5},{8,14},{10,8},{12,... | collective-permute-start | bytes 786440 | tf_op jit(solution)/shard_map/ppermute | solution.py:32
  90.5 23.4 %all-to-all-start.3 = ((bf16[4,48,256]{2,1,0:T(8,128)(2,1)}), bf16[4,48,256]{2,1,0:T(8,128)(2,1)S(1)}, u32[]{:S(2)}, u32[]{:S(2)}) async-start(bf16[4,48,256]{2,1,0:T(8,128)(2,1)} %pad_maximum_fusion), calls=%async_computation.3 | async-start | bytes 196608 | tf_op jit(solution)/shard_map/all_to_all | solution.py:27

commit v11 on v10

--- a/solution.py
+++ b/solution.py
@@ -53,13 +53,13 @@
         out_shape=jax.ShapeDtypeStruct((len(chunks) * count, depth), BF),
         compiler_params=pltpu.CompilerParams(vmem_limit_bytes=VMEM_BYTES),
         cost_estimate=pl.CostEstimate(
-            flops=8 * 10**9, bytes_accessed=4 * len(chunks) * count * depth, transcendentals=0
+            flops=4 * 10**9, bytes_accessed=4 * len(chunks) * count * depth, transcendentals=0
         ),
     )(places, *chunks)
 
 
 def products_kernel(
-    core_ref, slab_ref, weight_ref, cotangent_ref, following_ref, filters_ref,
+    core_ref, slab_ref, weight_ref, cotangent_ref, early_ref, following_ref, filters_ref,
     packed_ref, theirs_out, ours_out, extended_ref, grad_ref, theirs_ref, ours_ref, featured_ref,
 ):
     step, core = pl.program_id(0), core_ref[0]
@@ -72,10 +72,12 @@
     def _():
         extended_ref[:slab_len, :] = cotangent_ref[...].astype(F32)
         extended_ref[slab_len:, :] = following_ref[...]
-        grad_feat = filters_ref[0:1, :] * extended_ref[0:slab_len, :]
+        last = slab_len - 16
+        grad_feat = filters_ref[0:1, :] * extended_ref[last:slab_len, :]
         for tap in range(1, TAPS):
-            grad_feat = grad_feat + filters_ref[tap : tap + 1, :] * extended_ref[tap : tap + slab_len, :]
-        grad_ref[...] = grad_feat.astype(BF)
+            grad_feat = grad_feat + filters_ref[tap : tap + 1, :] * extended_ref[last + tap : slab_len + tap, :]
+        grad_ref[:last, :] = early_ref[:last, :]
+        grad_ref[last:, :] = grad_feat.astype(BF)
         for index in range(half // own):
             there = pl.ds(pl.multiple_of((2 * index + 1 - core) * own, own), own)
             here = pl.ds(pl.multiple_of((2 * index + core) * own, own), own)
@@ -116,7 +118,7 @@
         packed_ref[:, pl.num_programs(0) * rows :, :] = jnp.broadcast_to(tail[None], (nxy, 16, cols))
 
 
-def local_products(core, slab, gathered, cotangent, following, filters, nz, rows):
+def local_products(core, slab, gathered, cotangent, early, following, filters, nz, rows):
     slab_len, depth = slab.shape
     nxy, _, cols = gathered.shape
     part = nxy * rows
@@ -129,6 +131,7 @@
             in_specs=[
                 pl.BlockSpec((slab_len, part), lambda i, _: (0, i)),
                 pl.BlockSpec((nxy, rows, cols), lambda i, _: (0, i, 0)),
+                pl.BlockSpec((slab_len, cols), lambda i, _: (0, 0)),
                 pl.BlockSpec((slab_len, cols), lambda i, _: (0, 0)),
                 pl.BlockSpec(following.shape, lambda i, _: (0, 0)),
                 pl.BlockSpec(filters.shape, lambda i, _: (0, 0)),
@@ -155,7 +158,7 @@
         cost_estimate=pl.CostEstimate(
             flops=6 * slab_len * depth * cols, bytes_accessed=6 * slab_len * depth, transcendentals=0
         ),
-    )(core.reshape(1).astype(jnp.int32), slab, gathered, cotangent, following, filters)
+    )(core.reshape(1).astype(jnp.int32), slab, gathered, cotangent, early, following, filters)
 
 
 def spread(value, axes):
@@ -181,6 +184,12 @@
         direct[steps] = from_ahead(tokens, ZL, steps)
     sources = (chip + jnp.arange(nzl)) % nzl
     places = jnp.concatenate([2 * sources + core, 2 * sources + 1 - core]).astype(jnp.int32)
+
+    extended = jnp.pad(cotangent, ((0, 8), (0, 0))).astype(F32)
+    early = filters[0] * extended[:slab_len]
+    for tap in range(1, TAPS):
+        early = early + filters[tap] * extended[tap : tap + slab_len]
+    early = early.astype(BF)
 
     zh, xy = lax.axis_index(ZH), lax.axis_index((X, Y))
     head = cotangent[:8]
@@ -194,7 +203,7 @@
     chunks = direct + [swap(value) for value in direct]
     slab = in_order(places, chunks)
     packed, for_other, here = local_products(
-        core, slab, gathered, cotangent, following, filters, nz, rows
+        core, slab, gathered, cotangent, early, following, filters, nz, rows
     )
     total = jnp.sum(exchange(packed, (X, Y)).astype(F32), axis=0)
 

time: 116 us -> 119 us (1.026)
  the two profiles are of different devices: /device:TPU:8 before, /device:TPU:1 now
where the time goes in v11:
time: 119 us; the launch traced here: 118 us
  starting transfers between devices  72.7 us (61%)
  waiting for transfers between devices  20.7 us (17%)
  other arithmetic  9.76 us (8%)
  Pallas kernels  8.71 us (7%)
  local copies, waits for them, and re-layouts  5.2 us (4%)
    all_to_all x4, starting transfers between devices, exchange(): return lax.all_to_all(value, axes, split_axis=0, concat_axis=0, tiled=True)  39.1 us
    all_to_all x4, waiting for transfers between devices, exchange(): return lax.all_to_all(value, axes, split_axis=0, concat_axis=0, tiled=True)  18.1 us
    ppermute x6, starting transfers between devices, from_ahead(): lax.ppermute(value, axis, [(source, (source - steps) % count) for source...  17.4 us
    ppermute x5, starting transfers between devices, swap(): return lax.ppermute(value, C, [(0, 1), (1, 0)])  16.2 us
    pallas_call x1, Pallas kernels, local_products(): pl.pallas_call(products_kernel, grid_spec=pltpu.PrefetchScalarGridSpec(nu...  6.01 us
    convert_element_type x1, other arithmetic, body(): early = early.astype(BF)  3.25 us
    pallas_call x1, Pallas kernels, in_order(): pl.pallas_call(order_kernel, grid_spec=pltpu.PrefetchScalarGridSpec(num_s...  2.69 us
    ppermute x6, waiting for transfers between devices, from_ahead(): lax.ppermute(value, axis, [(source, (source - steps) % count) for source...  2.52 us
  transfers between devices with their start and end apart: 15, of which 4 were waited for; matrix products, arithmetic and copies ran while one was open for 9% of the time, Pallas kernels for 2%

profile of v11, /device:TPU:1, one launch (start us, length us, event | category | flops | bytes accessed | tf_op | source)
XLA Modules:
  0.0 118.1 jit_solution(4842096491069424309)
XLA Ops:
  2.7 15.6 %all-to-all-start = ((bf16[4,40,256]{2,1,0:T(8,128)(2,1)}), bf16[4,40,256]{2,1,0:T(8,128)(2,1)S(1)}, u32[]{:S(2)}, u32[]{:S(2)}) async-start(bf16[4,40,256]{2,1,0:T(8,128)(2,1)} %broadcast_in_dim.10), calls=%async_computation | async-start | bytes 163840 | tf_op jit(solution)/shard_map/all_to_all | solution.py:27
  18.3 3.5 %collective-permute-start = (bf16[64,2048]{1,0:T(8,128)(2,1)}, bf16[64,2048]{1,0:T(8,128)(2,1)S(1)}, u32[]{:S(2)}, u32[]{:S(2)}) collective-permute-start(bf16[64,2048]{1,0:T(8,128)(2,1)} %refs_0_.1), channel_id=1, source_target_pairs={{0,6},{2,0},{4,2},{6,4},{1,7},{3,1},{5,3},{7,5},{8,14},{10,8},{12,... | collective-permute-start | bytes 786440 | tf_op jit(solution)/shard_map/ppermute | solution.py:32
  21.9 2.2 %collective-permute-start.1 = (bf16[64,2048]{1,0:T(8,128)(2,1)}, bf16[64,2048]{1,0:T(8,128)(2,1)S(1)}, u32[]{:S(2)}, u32[]{:S(2)}) collective-permute-start(bf16[64,2048]{1,0:T(8,128)(2,1)} %refs_0_.1), channel_id=1, source_target_pairs={{0,4},{2,6},{4,0},{6,2},{1,5},{3,7},{5,1},{7,3},{8,12},{10,14},{12... | collective-permute-start | bytes 786440 | tf_op jit(solution)/shard_map/ppermute | solution.py:32
  24.1 2.6 %collective-permute-start.2 = (bf16[64,2048]{1,0:T(8,128)(2,1)}, bf16[64,2048]{1,0:T(8,128)(2,1)S(1)}, u32[]{:S(2)}, u32[]{:S(2)}) collective-permute-start(bf16[64,2048]{1,0:T(8,128)(2,1)} %refs_0_.1), channel_id=1, source_target_pairs={{0,2},{2,4},{4,6},{6,0},{1,3},{3,5},{5,7},{7,1},{8,10},{10,12},{12... | collective-permute-start | bytes 786440 | tf_op jit(solution)/shard_map/ppermute | solution.py:32
  26.7 3.7 %collective-permute-start.3 = (bf16[64,2048]{1,0:T(8,128)(2,1)}, bf16[64,2048]{1,0:T(8,128)(2,1)S(1)}, u32[]{:S(2)}, u32[]{:S(2)}) collective-permute-start(bf16[64,2048]{1,0:T(8,128)(2,1)} %refs_0_.1), channel_id=1, source_target_pairs={{0,1},{1,0},{2,3},{3,2},{4,5},{5,4},{6,7},{7,6},{8,9},{9,8},{10,11... | collective-permute-start | bytes 786440 | tf_op jit(solution)/shard_map/ppermute | solution.py:169
  32.0 6.9 %all-to-all-start.1 = ((bf16[16,144,256]{2,1,0:T(8,128)(2,1)}), bf16[16,144,256]{2,1,0:T(8,128)(2,1)S(1)}, u32[]{:S(2)}, u32[]{:S(2)}) async-start(bf16[16,144,256]{2,1,0:T(8,128)(2,1)} %broadcast_in_dim.11), calls=%async_computation.1 | async-start | bytes 2359296 | tf_op jit(solution)/shard_map/all_to_all | solution.py:27
  39.8 4.4 %collective-permute-start.4 = (bf16[64,2048]{1,0:T(8,128)(2,1)S(1)}, bf16[64,2048]{1,0:T(8,128)(2,1)S(1)}, u32[]{:S(2)}, u32[]{:S(2)}) collective-permute-start(bf16[64,2048]{1,0:T(8,128)(2,1)S(1)} %collective-permute-done.refs_1_), channel_id=1, source_target_pairs={{0,1},{1,0},{2,3},{3,2},{4,5},{5,4},{6,7},{7,6},{8,9},{9,8},{10,11... | collective-permute-start | bytes 786440 | tf_op jit(solution)/shard_map/ppermute | solution.py:169
  44.3 2.5 %collective-permute-done.1.refs_2_ = bf16[64,2048]{1,0:T(8,128)(2,1)S(1)} collective-permute-done((bf16[64,2048]{1,0:T(8,128)(2,1)}, bf16[64,2048]{1,0:T(8,128)(2,1)S(1)}, u32[]{:S(2)}, u32[]{:S(2)}) %collective-permute-start.1) | collective-permute-done | bytes 262176 | tf_op jit(solution)/shard_map/ppermute | solution.py:32
  46.8 3.8 %collective-permute-start.5 = (bf16[64,2048]{1,0:T(8,128)(2,1)S(1)}, bf16[64,2048]{1,0:T(8,128)(2,1)S(1)}, u32[]{:S(2)}, u32[]{:S(2)}) collective-permute-start(bf16[64,2048]{1,0:T(8,128)(2,1)S(1)} %collective-permute-done.1.refs_2_), channel_id=1, source_target_pairs={{0,1},{1,0},{2,3},{3,2},{4,5},{5,4},{6,7},{7,6},{8,9},{9,8},{10,11... | collective-permute-start | bytes 786440 | tf_op jit(solution)/shard_map/ppermute | solution.py:169
  50.5 1.9 %collective-permute-start.6 = (bf16[64,2048]{1,0:T(8,128)(2,1)S(1)}, bf16[64,2048]{1,0:T(8,128)(2,1)}, u32[]{:S(2)}, u32[]{:S(2)}) collective-permute-start(bf16[64,2048]{1,0:T(8,128)(2,1)S(1)} %collective-permute-done.2.refs_3_), channel_id=1, source_target_pairs={{0,1},{1,0},{2,3},{3,2},{4,5},{5,4},{6,7},{7,6},{8,9},{9,8},{10,11... | collective-permute-start | bytes 786440 | tf_op jit(solution)/shard_map/ppermute | solution.py:169
  52.6 3.3 %fusion.1.early_ref = bf16[512,256]{1,0:T(8,128)(2,1)S(1)} fusion(f32[520,256]{1,0:T(8,128)} %pad_convert_fusion, f32[256]{0:T(256)S(1)} %bitcast.37, f32[256]{0:T(256)S(1)} %bitcast.32, f32[256]{0:T(256)S(1)} %bitcast.33, f32[256]{0:T(256)S(1)} %bitcast.34, f32[256]{0:T(256)S(1)} %bitcast.35, f32[256]{0:T(256)S(1)} %bitcast.36, f32[256]{0:T(256)S(1)} %bitcast.31), kind=kLoop, calls=%fused_computation.4 | loop fusion | flops 1835008 | bytes 3939328 | tf_op jit(solution)/shard_map/convert_element_type | solution.py:192
  55.9 2.7 %shard_map.67.slab_ref = bf16[512,2048]{1,0:T(8,128)(2,1)S(1)} custom-call(s32[8]{0:T(128)S(1)} %pad_add_fusion.place_ref, bf16[64,2048]{1,0:T(8,128)(2,1)S(1)} %copy-done.2, bf16[64,2048]{1,0:T(8,128)(2,1)S(1)} %collective-permute-done.refs_1_, bf16[64,2048]{1,0:T(8,128)(2,1)S(1)} %collective-permute-done.1.refs_2_, ...), custom_call_target="tpu_custom_call" | custom-call | flops 4000000000 | bytes 4194304 | tf_op jit(solution)/shard_map/pallas_call | solution.py:45
  58.6 1.3 %copy-done.3 = bf16[512,2048]{1,0:T(8,128)(2,1)} copy-done((bf16[512,2048]{1,0:T(8,128)(2,1)}, bf16[512,2048]{1,0:T(8,128)(2,1)S(1)}, u32[]{:S(2)}) %copy-start.3) | copy-done | bytes 2097176
  59.9 6.0 %shard_map.68 = (bf16[16,144,256]{2,1,0:T(8,128)(2,1)}, bf16[256,2048]{1,0:T(8,128)(2,1)}, bf16[256,2048]{1,0:T(8,128)(2,1)S(1)}) custom-call(s32[1]{0:T(128)} %bitcast.core_ref, bf16[512,2048]{1,0:T(8,128)(2,1)} %copy-done.3, bf16[16,144,256]{2,1,0:T(8,128)(2,1)S(1)} %all-to-all-done.1.weight_ref, bf16[512,256]{1,0:T(8,128)(2,1)S(1)} %copy-done, ...), custom_call_target="tpu_custom_call" | custom-call | flops 1610612736 | bytes 6291456 | tf_op jit(solution)/shard_map/pallas_call | solution.py:126
  65.9 2.4 %collective-permute-start.7 = (bf16[256,2048]{1,0:T(8,128)(2,1)}, bf16[256,2048]{1,0:T(8,128)(2,1)}, u32[]{:S(2)}, u32[]{:S(2)}) collective-permute-start(bf16[256,2048]{1,0:T(8,128)(2,1)} %get-tuple-element.10), channel_id=1, source_target_pairs={{0,1},{1,0},{2,3},{3,2},{4,5},{5,4},{6,7},{7,6},{8,9},{9,8},{10,11... | collective-permute-start | bytes 3145736 | tf_op jit(solution)/shard_map/ppermute | solution.py:169
  68.3 6.8 %all-to-all-start.2 = ((bf16[16,144,256]{2,1,0:T(8,128)(2,1)}), bf16[16,144,256]{2,1,0:T(8,128)(2,1)S(1)}, u32[]{:S(2)}, u32[]{:S(2)}) async-start(bf16[16,144,256]{2,1,0:T(8,128)(2,1)} %get-tuple-element.8), calls=%async_computation.2 | async-start | bytes 2359296 | tf_op jit(solution)/shard_map/all_to_all | solution.py:27
  75.2 1.6 %add_convert_fusion = bf16[256,2048]{1,0:T(8,128)(2,1)S(1)} fusion(bf16[256,2048]{1,0:T(8,128)(2,1)} %collective-permute-done.7, bf16[256,2048]{1,0:T(8,128)(2,1)S(1)} %get-tuple-element.9), kind=kLoop, calls=%fused_computation.1 | loop fusion | flops 2097152 | bytes 3145728 | tf_op jit(solution)/shard_map/convert_element_type | solution.py:210
  77.6 1.9 %collective-permute-start.10 = (bf16[64,2048]{1,0:T(8,128)(2,1)}, bf16[64,2048]{1,0:T(8,128)(2,1)S(1)}, u32[]{:S(2)}, u32[]{:S(2)}) collective-permute-start(bf16[64,2048]{1,0:T(8,128)(2,1)} %get-tuple-element.16), channel_id=1, source_target_pairs={{0,2},{2,4},{4,6},{6,0},{1,3},{3,5},{5,7},{7,1},{8,10},{10,12},{12... | collective-permute-start | bytes 786440 | tf_op jit(solution)/shard_map/ppermute | solution.py:32
  79.5 1.9 %collective-permute-start.8 = (bf16[64,2048]{1,0:T(8,128)(2,1)S(1)}, bf16[64,2048]{1,0:T(8,128)(2,1)S(1)}, u32[]{:S(2)}, u32[]{:S(2)}) collective-permute-start(bf16[64,2048]{1,0:T(8,128)(2,1)S(1)} %get-tuple-element.15), channel_id=1, source_target_pairs={{0,4},{2,6},{4,0},{6,2},{1,5},{3,7},{5,1},{7,3},{8,12},{10,14},{12... | collective-permute-start | bytes 786440 | tf_op jit(solution)/shard_map/ppermute | solution.py:32
  81.4 5.2 %collective-permute-start.9 = (bf16[64,2048]{1,0:T(8,128)(2,1)S(1)}, bf16[64,2048]{1,0:T(8,128)(2,1)}, u32[]{:S(2)}, u32[]{:S(2)}) collective-permute-start(bf16[64,2048]{1,0:T(8,128)(2,1)S(1)} %get-tuple-element.17), channel_id=1, source_target_pairs={{0,6},{2,0},{4,2},{6,4},{1,7},{3,1},{5,3},{7,5},{8,14},{10,8},{12,... | collective-permute-start | bytes 786440 | tf_op jit(solution)/shard_map/ppermute | solution.py:32
  86.6 7.2 %all-to-all-done.2 = bf16[16,144,256]{2,1,0:T(8,128)(2,1)S(1)} async-done(((bf16[16,144,256]{2,1,0:T(8,128)(2,1)}), bf16[16,144,256]{2,1,0:T(8,128)(2,1)S(1)}, u32[]{:S(2)}, u32[]{:S(2)}) %all-to-all-start.2) | async-done | bytes 1179680 | tf_op jit(solution)/shard_map/all_to_all | solution.py:27
  94.6 9.9 %all-to-all-start.3 = ((bf16[4,48,256]{2,1,0:T(8,128)(2,1)}), bf16[4,48,256]{2,1,0:T(8,128)(2,1)S(1)}, u32[]{:S(2)}, u32[]{:S(2)}) async-start(bf16[4,48,256]{2,1,0:T(8,128)(2,1)} %pad_maximum_fusion), calls=%async_computation.3 | async-start | bytes 196608 | tf_op jit(solution)/shard_map/all_to_all | solution.py:27
  104.5 1.8 %fusion.9 = bf16[64,2048]{1,0:T(8,128)(2,1)} fusion(bf16[64,2048]{1,0:T(8,128)(2,1)S(1)} %collective-permute-done.10, bf16[64,2048]{1,0:T(8,128)(2,1)} %collective-permute-done.9, bf16[64,2048]{1,0:T(8,128)(2,1)S(1)} %collective-permute-done.8, bf16[4,64,2048]{2,1,0:T(8,128)(2,1)S(1)} %bitcast.28, s32[]{:T(128)S(6)} %select_n.77), kind=kLoop, calls=%fused_computation.19 | loop fusion | flops 1048576 | bytes 1310724 | tf_op jit(solution)/shard_map/convert_element_type | solution.py:216
  106.3 10.5 %all-to-all-done.3 = bf16[4,48,256]{2,1,0:T(8,128)(2,1)S(1)} async-done(((bf16[4,48,256]{2,1,0:T(8,128)(2,1)}), bf16[4,48,256]{2,1,0:T(8,128)(2,1)S(1)}, u32[]{:S(2)}, u32[]{:S(2)}) %all-to-all-start.3) | async-done | bytes 98336 | tf_op jit(solution)/shard_map/all_to_all | solution.py:27
  (42 shorter events, 7.4 us)
Async XLA Ops:
  2.7 28.2 %all-to-all-start = ((bf16[4,40,256]{2,1,0:T(8,128)(2,1)}), bf16[4,40,256]{2,1,0:T(8,128)(2,1)S(1)}, u32[]{:S(2)}, u32[]{:S(2)}) async-start(bf16[4,40,256]{2,1,0:T(8,128)(2,1)} %broadcast_in_dim.10), calls=%async_computation | async-start | bytes 163840 | tf_op jit(solution)/shard_map/all_to_all | solution.py:27
  18.3 21.5 %collective-permute-start = (bf16[64,2048]{1,0:T(8,128)(2,1)}, bf16[64,2048]{1,0:T(8,128)(2,1)S(1)}, u32[]{:S(2)}, u32[]{:S(2)}) collective-permute-start(bf16[64,2048]{1,0:T(8,128)(2,1)} %refs_0_.1), channel_id=1, source_target_pairs={{0,6},{2,0},{4,2},{6,4},{1,7},{3,1},{5,3},{7,5},{8,14},{10,8},{12,... | collective-permute-start | bytes 786440 | tf_op jit(solution)/shard_map/ppermute | solution.py:32
  21.9 24.9 %collective-permute-start.1 = (bf16[64,2048]{1,0:T(8,128)(2,1)}, bf16[64,2048]{1,0:T(8,128)(2,1)S(1)}, u32[]{:S(2)}, u32[]{:S(2)}) collective-permute-start(bf16[64,2048]{1,0:T(8,128)(2,1)} %refs_0_.1), channel_id=1, source_target_pairs={{0,4},{2,6},{4,0},{6,2},{1,5},{3,7},{5,1},{7,3},{8,12},{10,14},{12... | collective-permute-start | bytes 786440 | tf_op jit(solution)/shard_map/ppermute | solution.py:32
  24.1 26.5 %collective-permute-start.2 = (bf16[64,2048]{1,0:T(8,128)(2,1)}, bf16[64,2048]{1,0:T(8,128)(2,1)S(1)}, u32[]{:S(2)}, u32[]{:S(2)}) collective-permute-start(bf16[64,2048]{1,0:T(8,128)(2,1)} %refs_0_.1), channel_id=1, source_target_pairs={{0,2},{2,4},{4,6},{6,0},{1,3},{3,5},{5,7},{7,1},{8,10},{10,12},{12... | collective-permute-start | bytes 786440 | tf_op jit(solution)/shard_map/ppermute | solution.py:32
  26.7 29.1 %collective-permute-start.3 = (bf16[64,2048]{1,0:T(8,128)(2,1)}, bf16[64,2048]{1,0:T(8,128)(2,1)S(1)}, u32[]{:S(2)}, u32[]{:S(2)}) collective-permute-start(bf16[64,2048]{1,0:T(8,128)(2,1)} %refs_0_.1), channel_id=1, source_target_pairs={{0,1},{1,0},{2,3},{3,2},{4,5},{5,4},{6,7},{7,6},{8,9},{9,8},{10,11... | collective-permute-start | bytes 786440 | tf_op jit(solution)/shard_map/ppermute | solution.py:169
  32.0 6.9 %copy-start = (bf16[512,256]{1,0:T(8,128)(2,1)S(1)}, bf16[512,256]{1,0:T(8,128)(2,1)}, u32[]{:S(2)}) copy-start(bf16[512,256]{1,0:T(8,128)(2,1)} %cotangent_ref.1) | copy-start | bytes 786436
  32.0 7.8 %copy-start.1 = (f32[7,256]{1,0:T(8,128)S(1)}, f32[7,256]{1,0:T(8,128)}, u32[]{:S(2)}) copy-start(f32[7,256]{1,0:T(8,128)} %filters_ref.1) | copy-start | bytes 21508
  32.0 27.9 %all-to-all-start.1 = ((bf16[16,144,256]{2,1,0:T(8,128)(2,1)}), bf16[16,144,256]{2,1,0:T(8,128)(2,1)S(1)}, u32[]{:S(2)}, u32[]{:S(2)}) async-start(bf16[16,144,256]{2,1,0:T(8,128)(2,1)} %broadcast_in_dim.11), calls=%async_computation.1 | async-start | bytes 2359296 | tf_op jit(solution)/shard_map/all_to_all | solution.py:27
  39.8 16.0 %collective-permute-start.4 = (bf16[64,2048]{1,0:T(8,128)(2,1)S(1)}, bf16[64,2048]{1,0:T(8,128)(2,1)S(1)}, u32[]{:S(2)}, u32[]{:S(2)}) collective-permute-start(bf16[64,2048]{1,0:T(8,128)(2,1)S(1)} %collective-permute-done.refs_1_), channel_id=1, source_target_pairs={{0,1},{1,0},{2,3},{3,2},{4,5},{5,4},{6,7},{7,6},{8,9},{9,8},{10,11... | collective-permute-start | bytes 786440 | tf_op jit(solution)/shard_map/ppermute | solution.py:169
  46.8 9.1 %collective-permute-start.5 = (bf16[64,2048]{1,0:T(8,128)(2,1)S(1)}, bf16[64,2048]{1,0:T(8,128)(2,1)S(1)}, u32[]{:S(2)}, u32[]{:S(2)}) collective-permute-start(bf16[64,2048]{1,0:T(8,128)(2,1)S(1)} %collective-permute-done.1.refs_2_), channel_id=1, source_target_pairs={{0,1},{1,0},{2,3},{3,2},{4,5},{5,4},{6,7},{7,6},{8,9},{9,8},{10,11... | collective-permute-start | bytes 786440 | tf_op jit(solution)/shard_map/ppermute | solution.py:169
  50.5 5.3 %collective-permute-start.6 = (bf16[64,2048]{1,0:T(8,128)(2,1)S(1)}, bf16[64,2048]{1,0:T(8,128)(2,1)}, u32[]{:S(2)}, u32[]{:S(2)}) collective-permute-start(bf16[64,2048]{1,0:T(8,128)(2,1)S(1)} %collective-permute-done.2.refs_3_), channel_id=1, source_target_pairs={{0,1},{1,0},{2,3},{3,2},{4,5},{5,4},{6,7},{7,6},{8,9},{9,8},{10,11... | collective-permute-start | bytes 786440 | tf_op jit(solution)/shard_map/ppermute | solution.py:169
  52.6 3.3 %copy-start.2 = (bf16[64,2048]{1,0:T(8,128)(2,1)S(1)}, bf16[64,2048]{1,0:T(8,128)(2,1)}, u32[]{:S(2)}) copy-start(bf16[64,2048]{1,0:T(8,128)(2,1)} %refs_0_.1) | copy-start | bytes 786436
  58.6 1.3 %copy-start.3 = (bf16[512,2048]{1,0:T(8,128)(2,1)}, bf16[512,2048]{1,0:T(8,128)(2,1)S(1)}, u32[]{:S(2)}) copy-start(bf16[512,2048]{1,0:T(8,128)(2,1)S(1)} %shard_map.67.slab_ref) | copy-start | bytes 6291460
  65.9 9.2 %collective-permute-start.7 = (bf16[256,2048]{1,0:T(8,128)(2,1)}, bf16[256,2048]{1,0:T(8,128)(2,1)}, u32[]{:S(2)}, u32[]{:S(2)}) collective-permute-start(bf16[256,2048]{1,0:T(8,128)(2,1)} %get-tuple-element.10), channel_id=1, source_target_pairs={{0,1},{1,0},{2,3},{3,2},{4,5},{5,4},{6,7},{7,6},{8,9},{9,8},{10,11... | collective-permute-start | bytes 3145736 | tf_op jit(solution)/shard_map/ppermute | solution.py:169
  68.3 25.5 %all-to-all-start.2 = ((bf16[16,144,256]{2,1,0:T(8,128)(2,1)}), bf16[16,144,256]{2,1,0:T(8,128)(2,1)S(1)}, u32[]{:S(2)}, u32[]{:S(2)}) async-start(bf16[16,144,256]{2,1,0:T(8,128)(2,1)} %get-tuple-element.8), calls=%async_computation.2 | async-start | bytes 2359296 | tf_op jit(solution)/shard_map/all_to_all | solution.py:27
  77.6 26.9 %collective-permute-start.10 = (bf16[64,2048]{1,0:T(8,128)(2,1)}, bf16[64,2048]{1,0:T(8,128)(2,1)S(1)}, u32[]{:S(2)}, u32[]{:S(2)}) collective-permute-start(bf16[64,2048]{1,0:T(8,128)(2,1)} %get-tuple-element.16), channel_id=1, source_target_pairs={{0,2},{2,4},{4,6},{6,0},{1,3},{3,5},{5,7},{7,1},{8,10},{10,12},{12... | collective-permute-start | bytes 786440 | tf_op jit(solution)/shard_map/ppermute | solution.py:32
  79.5 25.0 %collective-permute-start.8 = (bf16[64,2048]{1,0:T(8,128)(2,1)S(1)}, bf16[64,2048]{1,0:T(8,128)(2,1)S(1)}, u32[]{:S(2)}, u32[]{:S(2)}) collective-permute-start(bf16[64,2048]{1,0:T(8,128)(2,1)S(1)} %get-tuple-element.15), channel_id=1, source_target_pairs={{0,4},{2,6},{4,0},{6,2},{1,5},{3,7},{5,1},{7,3},{8,12},{10,14},{12... | collective-permute-start | bytes 786440 | tf_op jit(solution)/shard_map/ppermute | solution.py:32
  81.4 23.1 %collective-permute-start.9 = (bf16[64,2048]{1,0:T(8,128)(2,1)S(1)}, bf16[64,2048]{1,0:T(8,128)(2,1)}, u32[]{:S(2)}, u32[]{:S(2)}) collective-permute-start(bf16[64,2048]{1,0:T(8,128)(2,1)S(1)} %get-tuple-element.17), channel_id=1, source_target_pairs={{0,6},{2,0},{4,2},{6,4},{1,7},{3,1},{5,3},{7,5},{8,14},{10,8},{12,... | collective-permute-start | bytes 786440 | tf_op jit(solution)/shard_map/ppermute | solution.py:32
  94.6 22.2 %all-to-all-start.3 = ((bf16[4,48,256]{2,1,0:T(8,128)(2,1)}), bf16[4,48,256]{2,1,0:T(8,128)(2,1)S(1)}, u32[]{:S(2)}, u32[]{:S(2)}) async-start(bf16[4,48,256]{2,1,0:T(8,128)(2,1)} %pad_maximum_fusion), calls=%async_computation.3 | async-start | bytes 196608 | tf_op jit(solution)/shard_map/all_to_all | solution.py:27

commit v12 on v10

--- a/solution.py
+++ b/solution.py
@@ -32,35 +32,39 @@
     return lax.ppermute(value, axis, [(source, (source - steps) % count) for source in range(count)])
 
 
-def order_kernel(place_ref, *refs):
-    chunks, slab_ref = refs[:-1], refs[-1]
-    count = chunks[0].shape[0]
+def order_kernel(*refs):
+    chunks, (slab_ref, done) = refs[:-2], refs[-2:]
+    count, chips = chunks[0].shape[0], len(chunks) // 2
+    core, chip = lax.axis_index(C), lax.axis_index(ZL)
+    copies = []
     for index, chunk in enumerate(chunks):
-        slab_ref[pl.ds(pl.multiple_of(place_ref[index] * count, count), count), :] = chunk[...]
-
-
-def in_order(places, chunks):
+        source = lax.rem(chip + index % chips, chips)
+        place = 2 * source + (core if index < chips else 1 - core)
+        rows = pl.ds(pl.multiple_of(place * count, count), count)
+        copies.append(pltpu.make_async_copy(chunk, slab_ref.at[rows, :], done.at[index]))
+        copies[-1].start()
+    for copy in copies:
+        copy.wait()
+
+
+def in_order(chunks):
     count, depth = chunks[0].shape
-    part = depth // 4
     return pl.pallas_call(
         order_kernel,
-        grid_spec=pltpu.PrefetchScalarGridSpec(
-            num_scalar_prefetch=1,
-            grid=(depth // part,),
-            in_specs=[pl.BlockSpec((count, part), lambda i, _: (0, i)) for _ in chunks],
-            out_specs=pl.BlockSpec((len(chunks) * count, part), lambda i, _: (0, i)),
-        ),
-        out_shape=jax.ShapeDtypeStruct((len(chunks) * count, depth), BF),
+        in_specs=[pl.BlockSpec(memory_space=pl.ANY) for _ in chunks],
+        out_specs=pl.BlockSpec(memory_space=pltpu.HBM),
+        out_shape=pltpu.HBM((len(chunks) * count, depth), BF),
+        scratch_shapes=[pltpu.SemaphoreType.DMA((len(chunks),))],
         compiler_params=pltpu.CompilerParams(vmem_limit_bytes=VMEM_BYTES),
         cost_estimate=pl.CostEstimate(
             flops=8 * 10**9, bytes_accessed=4 * len(chunks) * count * depth, transcendentals=0
         ),
-    )(places, *chunks)
+    )(*chunks)
 
 
 def products_kernel(
     core_ref, slab_ref, weight_ref, cotangent_ref, following_ref, filters_ref,
-    packed_ref, theirs_out, ours_out, extended_ref, grad_ref, theirs_ref, ours_ref, featured_ref,
+    packed_ref, theirs_out, ours_out, extended_ref, grad_ref, theirs_ref, featured_ref,
 ):
     step, core = pl.program_id(0), core_ref[0]
     slab_len, cols = grad_ref.shape
@@ -80,15 +84,12 @@
             there = pl.ds(pl.multiple_of((2 * index + 1 - core) * own, own), own)
             here = pl.ds(pl.multiple_of((2 * index + core) * own, own), own)
             theirs_ref[index * own : (index + 1) * own, :] = grad_ref[there, :]
-            ours_ref[index * own : (index + 1) * own, :] = grad_ref[here, :]
+            ours_out[index * own : (index + 1) * own, :] = grad_ref[here, :]
 
     weight = weight_ref[...].reshape(nxy * rows, cols)
     contract_cols = (((1,), (1,)), ((), ()))
     theirs_out[...] = lax.dot_general(
         theirs_ref[...], weight, contract_cols, preferred_element_type=F32
-    ).astype(BF)
-    ours_out[...] = lax.dot_general(
-        ours_ref[...], weight, contract_cols, preferred_element_type=F32
     ).astype(BF)
     products = lax.dot_general(
         slab_ref[...], grad_ref[...], (((0,), (0,)), ((), ())), preferred_element_type=F32
@@ -136,12 +137,11 @@
             out_specs=[
                 pl.BlockSpec((nxy, nz * rows + 16, cols), lambda i, _: (0, 0, 0)),
                 pl.BlockSpec((half, part), lambda i, _: (0, i)),
-                pl.BlockSpec((half, part), lambda i, _: (0, i)),
+                pl.BlockSpec((half, cols), lambda i, _: (0, 0)),
             ],
             scratch_shapes=[
                 pltpu.VMEM((slab_len + 8, cols), F32),
                 pltpu.VMEM((slab_len, cols), BF),
-                pltpu.VMEM((half, cols), BF),
                 pltpu.VMEM((half, cols), BF),
                 pltpu.VMEM((slab_len, cols), F32),
             ],
@@ -149,13 +149,60 @@
         out_shape=[
             jax.ShapeDtypeStruct((nxy, nz * rows + 16, cols), BF),
             jax.ShapeDtypeStruct((half, depth), BF),
-            jax.ShapeDtypeStruct((half, depth), BF),
+            jax.ShapeDtypeStruct((half, cols), BF),
         ],
         compiler_params=pltpu.CompilerParams(vmem_limit_bytes=PRODUCTS_VMEM),
         cost_estimate=pl.CostEstimate(
             flops=6 * slab_len * depth * cols, bytes_accessed=6 * slab_len * depth, transcendentals=0
         ),
     )(core.reshape(1).astype(jnp.int32), slab, gathered, cotangent, following, filters)
+
+
+def own_kernel(ours_ref, weight_ref, out_ref):
+    weight = weight_ref[...].reshape(-1, ours_ref.shape[1])
+    out_ref[...] = lax.dot_general(
+        ours_ref[...], weight, (((1,), (1,)), ((), ())), preferred_element_type=F32
+    ).astype(BF)
+
+
+def own_products(ours, gathered, nz, rows):
+    half, cols = ours.shape
+    nxy = gathered.shape[0]
+    part = nxy * rows
+    return pl.pallas_call(
+        own_kernel,
+        grid=(nz,),
+        in_specs=[
+            pl.BlockSpec((half, cols), lambda i: (0, 0)),
+            pl.BlockSpec((nxy, rows, cols), lambda i: (0, i, 0)),
+        ],
+        out_specs=pl.BlockSpec((half, part), lambda i: (0, i)),
+        out_shape=jax.ShapeDtypeStruct((half, nz * part), BF),
+        compiler_params=pltpu.CompilerParams(vmem_limit_bytes=VMEM_BYTES),
+        cost_estimate=pl.CostEstimate(flops=4 * 10**9, bytes_accessed=8 * half * part, transcendentals=0),
+    )(ours, gathered)
+
+
+def head_kernel(weight_ref, head_ref, out_ref):
+    rows = weight_ref.shape[0]
+    for index in range(out_ref.shape[0]):
+        out_ref[index, :rows, :] = weight_ref[...]
+        out_ref[index, rows:, :] = head_ref[...]
+
+
+def with_head(proj_weight, cotangent, nz):
+    rows, cols = proj_weight.shape
+    return pl.pallas_call(
+        head_kernel,
+        grid=(1,),
+        in_specs=[
+            pl.BlockSpec((rows, cols), lambda i: (0, 0)),
+            pl.BlockSpec((16, cols), lambda i: (0, 0)),
+        ],
+        out_specs=pl.BlockSpec((nz, rows + 16, cols), lambda i: (0, 0, 0)),
+        out_shape=jax.ShapeDtypeStruct((nz, rows + 16, cols), BF),
+        compiler_params=pltpu.CompilerParams(vmem_limit_bytes=60 * 1024 * 1024),
+    )(proj_weight, cotangent)
 
 
 def spread(value, axes):
@@ -179,25 +226,24 @@
     direct = [tokens] + [None] * (nzl - 1)
     for steps in (2, 1, 3):
         direct[steps] = from_ahead(tokens, ZL, steps)
-    sources = (chip + jnp.arange(nzl)) % nzl
-    places = jnp.concatenate([2 * sources + core, 2 * sources + 1 - core]).astype(jnp.int32)
 
     zh, xy = lax.axis_index(ZH), lax.axis_index((X, Y))
     head = cotangent[:8]
-    column = spread(jnp.concatenate([proj_weight, head], 0), ZH)
-    ahead = lax.dynamic_index_in_dim(column, (zh + 1) % nz, 0, keepdims=False)[rows:]
+    column = exchange(with_head(proj_weight, cotangent, nz), ZH)
+    ahead = lax.dynamic_index_in_dim(column, (zh + 1) % nz, 0, keepdims=False)[rows : rows + 8]
     column = column[:, :rows].reshape(nz * rows, cols)
     gathered = spread(jnp.concatenate([column, head, ahead], 0), (X, Y))
     heads = lax.dynamic_index_in_dim(gathered, (xy + 1) % nxy, 0, keepdims=False)[nz * rows :]
     following = jnp.where(xy == nxy - 1, heads[8:], heads[:8])
     following = jnp.where(zh * nxy + xy == ndp - 1, jnp.zeros((), BF), following).astype(F32)
     chunks = direct + [swap(value) for value in direct]
-    slab = in_order(places, chunks)
-    packed, for_other, here = local_products(
+    slab = in_order(chunks)
+    packed, for_other, ours = local_products(
         core, slab, gathered, cotangent, following, filters, nz, rows
     )
     total = jnp.sum(exchange(packed, (X, Y)).astype(F32), axis=0)
 
+    here = own_products(ours, gathered, nz, rows)
     chip_sum = (here.astype(F32) + swap(for_other).astype(F32)).astype(BF)
     chip_sum = chip_sum.reshape(nzl, own_tokens, depth)
     summed = lax.dynamic_index_in_dim(chip_sum, chip, 0, keepdims=False).astype(F32)

time: 116 us -> 115 us (level)
  Pallas kernels: 7.74 us -> 10.4 us
  local copies, waits for them, and re-layouts: 5.16 us -> 3.22 us
    pallas_call x1 -> x3, Pallas kernels: 1.19 us -> 4.03 us  [the longest x1 1.41 us: in_order(): pl.pallas_call(order_kernel, in_specs=[pl.BlockSpec(memory_space=pl.ANY)...]
    unnamed x8 -> x6, local copies, waits for them, and re-layouts: 1.33 us -> 0.02 us
  transfers between devices with their start and end apart: 15 -> 15, of which waited for: 6 -> 6; matrix products, arithmetic and copies ran while one was open for 5% -> 6% of each run, Pallas kernels for 1% -> 2%
where the time goes in v12:
time: 115 us; the launch traced here: 114 us
  starting transfers between devices  68.3 us (59%)
  waiting for transfers between devices  25.9 us (23%)
  Pallas kernels  10.4 us (9%)
  other arithmetic  4.84 us (4%)
  local copies, waits for them, and re-layouts  3.22 us (3%)
    all_to_all x4, starting transfers between devices, exchange(): return lax.all_to_all(value, axes, split_axis=0, concat_axis=0, tiled=True)  39 us
    all_to_all x4, waiting for transfers between devices, exchange(): return lax.all_to_all(value, axes, split_axis=0, concat_axis=0, tiled=True)  22.5 us
    ppermute x6, starting transfers between devices, from_ahead(): lax.ppermute(value, axis, [(source, (source - steps) % count) for source...  18.8 us
    ppermute x5, starting transfers between devices, swap(): return lax.ppermute(value, C, [(0, 1), (1, 0)])  10.6 us
    pallas_call x1, Pallas kernels, local_products(): pl.pallas_call(products_kernel, grid_spec=pltpu.PrefetchScalarGridSpec(nu...  6.35 us
  transfers between devices with their start and end apart: 15, of which 6 were waited for; matrix products, arithmetic and copies ran while one was open for 6% of the time, Pallas kernels for 2%

profile of v12, /device:TPU:8, one launch (start us, length us, event | category | flops | bytes accessed | tf_op | source)
XLA Modules:
  0.0 113.6 jit_solution(16248917503746013768)
XLA Ops:
  2.0 15.1 %all-to-all-start = ((bf16[4,48,256]{2,1,0:T(8,128)(2,1)}), bf16[4,48,256]{2,1,0:T(8,128)(2,1)S(1)}, u32[]{:S(2)}, u32[]{:S(2)}) async-start(bf16[4,48,256]{2,1,0:T(8,128)(2,1)} %shard_map.68), calls=%async_computation | async-start | bytes 196608 | tf_op jit(solution)/shard_map/all_to_all | solution.py:27
  17.1 3.8 %collective-permute-start = (bf16[64,2048]{1,0:T(8,128)(2,1)}, bf16[64,2048]{1,0:T(8,128)(2,1)S(1)}, u32[]{:S(2)}, u32[]{:S(2)}) collective-permute-start(bf16[64,2048]{1,0:T(8,128)(2,1)} %refs_0_.1), channel_id=1, source_target_pairs={{0,6},{2,0},{4,2},{6,4},{1,7},{3,1},{5,3},{7,5},{8,14},{10,8},{12,... | collective-permute-start | bytes 786440 | tf_op jit(solution)/shard_map/ppermute | solution.py:32
  20.9 2.5 %collective-permute-start.1 = (bf16[64,2048]{1,0:T(8,128)(2,1)}, bf16[64,2048]{1,0:T(8,128)(2,1)S(1)}, u32[]{:S(2)}, u32[]{:S(2)}) collective-permute-start(bf16[64,2048]{1,0:T(8,128)(2,1)} %refs_0_.1), channel_id=1, source_target_pairs={{0,4},{2,6},{4,0},{6,2},{1,5},{3,7},{5,1},{7,3},{8,12},{10,14},{12... | collective-permute-start | bytes 786440 | tf_op jit(solution)/shard_map/ppermute | solution.py:32
  23.4 2.9 %collective-permute-start.2 = (bf16[64,2048]{1,0:T(8,128)(2,1)}, bf16[64,2048]{1,0:T(8,128)(2,1)S(1)}, u32[]{:S(2)}, u32[]{:S(2)}) collective-permute-start(bf16[64,2048]{1,0:T(8,128)(2,1)} %refs_0_.1), channel_id=1, source_target_pairs={{0,2},{2,4},{4,6},{6,0},{1,3},{3,5},{5,7},{7,1},{8,10},{10,12},{12... | collective-permute-start | bytes 786440 | tf_op jit(solution)/shard_map/ppermute | solution.py:32
  27.0 4.6 %all-to-all-done = bf16[4,48,256]{2,1,0:T(8,128)(2,1)S(1)} async-done(((bf16[4,48,256]{2,1,0:T(8,128)(2,1)}), bf16[4,48,256]{2,1,0:T(8,128)(2,1)S(1)}, u32[]{:S(2)}, u32[]{:S(2)}) %all-to-all-start) | async-done | bytes 98336 | tf_op jit(solution)/shard_map/all_to_all | solution.py:27
  32.7 7.5 %all-to-all-start.1 = ((bf16[16,144,256]{2,1,0:T(8,128)(2,1)}), bf16[16,144,256]{2,1,0:T(8,128)(2,1)S(1)}, u32[]{:S(2)}, u32[]{:S(2)}) async-start(bf16[16,144,256]{2,1,0:T(8,128)(2,1)} %broadcast_in_dim.8), calls=%async_computation.1 | async-start | bytes 2359296 | tf_op jit(solution)/shard_map/all_to_all | solution.py:27
  40.3 1.9 %collective-permute-start.3 = (bf16[64,2048]{1,0:T(8,128)(2,1)S(1)}, bf16[64,2048]{1,0:T(8,128)(2,1)S(1)}, u32[]{:S(2)}, u32[]{:S(2)}) collective-permute-start(bf16[64,2048]{1,0:T(8,128)(2,1)S(1)} %copy-done.1), channel_id=1, source_target_pairs={{0,1},{1,0},{2,3},{3,2},{4,5},{5,4},{6,7},{7,6},{8,9},{9,8},{10,11... | collective-permute-start | bytes 786440 | tf_op jit(solution)/shard_map/ppermute | solution.py:213
  42.2 2.4 %collective-permute-start.4 = (bf16[64,2048]{1,0:T(8,128)(2,1)S(1)}, bf16[64,2048]{1,0:T(8,128)(2,1)S(1)}, u32[]{:S(2)}, u32[]{:S(2)}) collective-permute-start(bf16[64,2048]{1,0:T(8,128)(2,1)S(1)} %collective-permute-done.refs_1_), channel_id=1, source_target_pairs={{0,1},{1,0},{2,3},{3,2},{4,5},{5,4},{6,7},{7,6},{8,9},{9,8},{10,11... | collective-permute-start | bytes 786440 | tf_op jit(solution)/shard_map/ppermute | solution.py:213
  44.6 2.3 %collective-permute-done.1.refs_2_ = bf16[64,2048]{1,0:T(8,128)(2,1)S(1)} collective-permute-done((bf16[64,2048]{1,0:T(8,128)(2,1)}, bf16[64,2048]{1,0:T(8,128)(2,1)S(1)}, u32[]{:S(2)}, u32[]{:S(2)}) %collective-permute-start.1) | collective-permute-done | bytes 262176 | tf_op jit(solution)/shard_map/ppermute | solution.py:32
  46.9 1.9 %collective-permute-start.5 = (bf16[64,2048]{1,0:T(8,128)(2,1)S(1)}, bf16[64,2048]{1,0:T(8,128)(2,1)S(1)}, u32[]{:S(2)}, u32[]{:S(2)}) collective-permute-start(bf16[64,2048]{1,0:T(8,128)(2,1)S(1)} %collective-permute-done.1.refs_2_), channel_id=1, source_target_pairs={{0,1},{1,0},{2,3},{3,2},{4,5},{5,4},{6,7},{7,6},{8,9},{9,8},{10,11... | collective-permute-start | bytes 786440 | tf_op jit(solution)/shard_map/ppermute | solution.py:213
  48.8 2.4 %collective-permute-start.6 = (bf16[64,2048]{1,0:T(8,128)(2,1)S(1)}, bf16[64,2048]{1,0:T(8,128)(2,1)S(1)}, u32[]{:S(2)}, u32[]{:S(2)}) collective-permute-start(bf16[64,2048]{1,0:T(8,128)(2,1)S(1)} %collective-permute-done.2.refs_3_), channel_id=1, source_target_pairs={{0,1},{1,0},{2,3},{3,2},{4,5},{5,4},{6,7},{7,6},{8,9},{9,8},{10,11... | collective-permute-start | bytes 786440 | tf_op jit(solution)/shard_map/ppermute | solution.py:213
  52.4 1.4 %shard_map.67.slab_ref = bf16[512,2048]{1,0:T(8,128)(2,1)} custom-call(bf16[64,2048]{1,0:T(8,128)(2,1)S(1)} %copy-done.1, bf16[64,2048]{1,0:T(8,128)(2,1)S(1)} %collective-permute-done.refs_1_, bf16[64,2048]{1,0:T(8,128)(2,1)S(1)} %collective-permute-done.1.refs_2_, bf16[64,2048]{1,0:T(8,128)(2,1)S(1)} %collective-permute-done.2.refs_3_, ...), custom_call_target="tpu_custom_call" | custom-call | flops 8000000000 | bytes 4194304 | tf_op jit(solution)/shard_map/pallas_call | solution.py:52
  53.8 1.5 %all-to-all-done.1.weight_ref = bf16[16,144,256]{2,1,0:T(8,128)(2,1)S(1)} async-done(((bf16[16,144,256]{2,1,0:T(8,128)(2,1)}), bf16[16,144,256]{2,1,0:T(8,128)(2,1)S(1)}, u32[]{:S(2)}, u32[]{:S(2)}) %all-to-all-start.1) | async-done | bytes 1179680 | tf_op jit(solution)/shard_map/all_to_all | solution.py:27
  55.3 6.3 %shard_map.69 = (bf16[16,144,256]{2,1,0:T(8,128)(2,1)}, bf16[256,2048]{1,0:T(8,128)(2,1)S(1)}, bf16[256,256]{1,0:T(8,128)(2,1)S(1)}) custom-call(s32[1]{0:T(128)} %bitcast.core_ref, bf16[512,2048]{1,0:T(8,128)(2,1)} %shard_map.67.slab_ref, bf16[16,144,256]{2,1,0:T(8,128)(2,1)S(1)} %all-to-all-done.1.weight_ref, bf16[512,256]{1,0:T(8,128)(2,1)S(1)} %copy-done, ...), custom_call_target="tpu_custom_call" | custom-call | flops 1610612736 | bytes 6291456 | tf_op jit(solution)/shard_map/pallas_call | solution.py:125
  61.7 1.9 %collective-permute-start.7 = (bf16[256,2048]{1,0:T(8,128)(2,1)S(1)}, bf16[256,2048]{1,0:T(8,128)(2,1)}, u32[]{:S(2)}, u32[]{:S(2)}) collective-permute-start(bf16[256,2048]{1,0:T(8,128)(2,1)S(1)} %get-tuple-element.10), channel_id=1, source_target_pairs={{0,1},{1,0},{2,3},{3,2},{4,5},{5,4},{6,7},{7,6},{8,9},{9,8},{10,11... | collective-permute-start | bytes 3145736 | tf_op jit(solution)/shard_map/ppermute | solution.py:213
  63.7 6.3 %all-to-all-start.2 = ((bf16[16,144,256]{2,1,0:T(8,128)(2,1)}), bf16[16,144,256]{2,1,0:T(8,128)(2,1)S(1)}, u32[]{:S(2)}, u32[]{:S(2)}) async-start(bf16[16,144,256]{2,1,0:T(8,128)(2,1)} %get-tuple-element.8), calls=%async_computation.2 | async-start | bytes 2359296 | tf_op jit(solution)/shard_map/all_to_all | solution.py:27
  71.2 1.6 %add_convert_fusion = bf16[256,2048]{1,0:T(8,128)(2,1)S(1)} fusion(bf16[256,2048]{1,0:T(8,128)(2,1)} %collective-permute-done.7, bf16[256,2048]{1,0:T(8,128)(2,1)S(1)} %shard_map.70), kind=kLoop, calls=%fused_computation.1 | loop fusion | flops 2097152 | bytes 3145728 | tf_op jit(solution)/shard_map/convert_element_type | solution.py:247
  73.6 1.9 %collective-permute-start.10 = (bf16[64,2048]{1,0:T(8,128)(2,1)}, bf16[64,2048]{1,0:T(8,128)(2,1)S(1)}, u32[]{:S(2)}, u32[]{:S(2)}) collective-permute-start(bf16[64,2048]{1,0:T(8,128)(2,1)} %get-tuple-element.16), channel_id=1, source_target_pairs={{0,2},{2,4},{4,6},{6,0},{1,3},{3,5},{5,7},{7,1},{8,10},{10,12},{12... | collective-permute-start | bytes 786440 | tf_op jit(solution)/shard_map/ppermute | solution.py:32
  75.5 3.1 %collective-permute-start.8 = (bf16[64,2048]{1,0:T(8,128)(2,1)S(1)}, bf16[64,2048]{1,0:T(8,128)(2,1)S(1)}, u32[]{:S(2)}, u32[]{:S(2)}) collective-permute-start(bf16[64,2048]{1,0:T(8,128)(2,1)S(1)} %get-tuple-element.15), channel_id=1, source_target_pairs={{0,4},{2,6},{4,0},{6,2},{1,5},{3,7},{5,1},{7,3},{8,12},{10,14},{12... | collective-permute-start | bytes 786440 | tf_op jit(solution)/shard_map/ppermute | solution.py:32
  78.6 4.5 %collective-permute-start.9 = (bf16[64,2048]{1,0:T(8,128)(2,1)S(1)}, bf16[64,2048]{1,0:T(8,128)(2,1)}, u32[]{:S(2)}, u32[]{:S(2)}) collective-permute-start(bf16[64,2048]{1,0:T(8,128)(2,1)S(1)} %get-tuple-element.17), channel_id=1, source_target_pairs={{0,6},{2,0},{4,2},{6,4},{1,7},{3,1},{5,3},{7,5},{8,14},{10,8},{12,... | collective-permute-start | bytes 786440 | tf_op jit(solution)/shard_map/ppermute | solution.py:32
  83.2 5.0 %all-to-all-done.2 = bf16[16,144,256]{2,1,0:T(8,128)(2,1)S(1)} async-done(((bf16[16,144,256]{2,1,0:T(8,128)(2,1)}), bf16[16,144,256]{2,1,0:T(8,128)(2,1)S(1)}, u32[]{:S(2)}, u32[]{:S(2)}) %all-to-all-start.2) | async-done | bytes 1179680 | tf_op jit(solution)/shard_map/all_to_all | solution.py:27
  89.0 10.1 %all-to-all-start.3 = ((bf16[4,48,256]{2,1,0:T(8,128)(2,1)}), bf16[4,48,256]{2,1,0:T(8,128)(2,1)S(1)}, u32[]{:S(2)}, u32[]{:S(2)}) async-start(bf16[4,48,256]{2,1,0:T(8,128)(2,1)} %pad_maximum_fusion), calls=%async_computation.3 | async-start | bytes 196608 | tf_op jit(solution)/shard_map/all_to_all | solution.py:27
  99.1 1.8 %fusion.2 = bf16[64,2048]{1,0:T(8,128)(2,1)} fusion(bf16[64,2048]{1,0:T(8,128)(2,1)S(1)} %collective-permute-done.10, bf16[64,2048]{1,0:T(8,128)(2,1)} %collective-permute-done.9, bf16[64,2048]{1,0:T(8,128)(2,1)S(1)} %collective-permute-done.8, bf16[4,64,2048]{2,1,0:T(8,128)(2,1)S(1)} %bitcast.21, s32[]{:T(128)S(6)} %select_n.70), kind=kLoop, calls=%fused_computation.5 | loop fusion | flops 1048576 | bytes 1310724 | tf_op jit(solution)/shard_map/convert_element_type | solution.py:253
  100.9 11.5 %all-to-all-done.3 = bf16[4,48,256]{2,1,0:T(8,128)(2,1)S(1)} async-done(((bf16[4,48,256]{2,1,0:T(8,128)(2,1)}), bf16[4,48,256]{2,1,0:T(8,128)(2,1)S(1)}, u32[]{:S(2)}, u32[]{:S(2)}) %all-to-all-start.3) | async-done | bytes 98336 | tf_op jit(solution)/shard_map/all_to_all | solution.py:27
  (35 shorter events, 8.4 us)
Async XLA Ops:
  2.0 29.6 %all-to-all-start = ((bf16[4,48,256]{2,1,0:T(8,128)(2,1)}), bf16[4,48,256]{2,1,0:T(8,128)(2,1)S(1)}, u32[]{:S(2)}, u32[]{:S(2)}) async-start(bf16[4,48,256]{2,1,0:T(8,128)(2,1)} %shard_map.68), calls=%async_computation | async-start | bytes 196608 | tf_op jit(solution)/shard_map/all_to_all | solution.py:27
  17.1 25.1 %collective-permute-start = (bf16[64,2048]{1,0:T(8,128)(2,1)}, bf16[64,2048]{1,0:T(8,128)(2,1)S(1)}, u32[]{:S(2)}, u32[]{:S(2)}) collective-permute-start(bf16[64,2048]{1,0:T(8,128)(2,1)} %refs_0_.1), channel_id=1, source_target_pairs={{0,6},{2,0},{4,2},{6,4},{1,7},{3,1},{5,3},{7,5},{8,14},{10,8},{12,... | collective-permute-start | bytes 786440 | tf_op jit(solution)/shard_map/ppermute | solution.py:32
  20.9 26.0 %collective-permute-start.1 = (bf16[64,2048]{1,0:T(8,128)(2,1)}, bf16[64,2048]{1,0:T(8,128)(2,1)S(1)}, u32[]{:S(2)}, u32[]{:S(2)}) collective-permute-start(bf16[64,2048]{1,0:T(8,128)(2,1)} %refs_0_.1), channel_id=1, source_target_pairs={{0,4},{2,6},{4,0},{6,2},{1,5},{3,7},{5,1},{7,3},{8,12},{10,14},{12... | collective-permute-start | bytes 786440 | tf_op jit(solution)/shard_map/ppermute | solution.py:32
  23.4 25.4 %collective-permute-start.2 = (bf16[64,2048]{1,0:T(8,128)(2,1)}, bf16[64,2048]{1,0:T(8,128)(2,1)S(1)}, u32[]{:S(2)}, u32[]{:S(2)}) collective-permute-start(bf16[64,2048]{1,0:T(8,128)(2,1)} %refs_0_.1), channel_id=1, source_target_pairs={{0,2},{2,4},{4,6},{6,0},{1,3},{3,5},{5,7},{7,1},{8,10},{10,12},{12... | collective-permute-start | bytes 786440 | tf_op jit(solution)/shard_map/ppermute | solution.py:32
  32.7 7.5 %copy-start.1 = (bf16[64,2048]{1,0:T(8,128)(2,1)S(1)}, bf16[64,2048]{1,0:T(8,128)(2,1)}, u32[]{:S(2)}) copy-start(bf16[64,2048]{1,0:T(8,128)(2,1)} %refs_0_.1) | copy-start | bytes 786436
  32.7 22.6 %all-to-all-start.1 = ((bf16[16,144,256]{2,1,0:T(8,128)(2,1)}), bf16[16,144,256]{2,1,0:T(8,128)(2,1)S(1)}, u32[]{:S(2)}, u32[]{:S(2)}) async-start(bf16[16,144,256]{2,1,0:T(8,128)(2,1)} %broadcast_in_dim.8), calls=%async_computation.1 | async-start | bytes 2359296 | tf_op jit(solution)/shard_map/all_to_all | solution.py:27
  40.3 11.0 %collective-permute-start.3 = (bf16[64,2048]{1,0:T(8,128)(2,1)S(1)}, bf16[64,2048]{1,0:T(8,128)(2,1)S(1)}, u32[]{:S(2)}, u32[]{:S(2)}) collective-permute-start(bf16[64,2048]{1,0:T(8,128)(2,1)S(1)} %copy-done.1), channel_id=1, source_target_pairs={{0,1},{1,0},{2,3},{3,2},{4,5},{5,4},{6,7},{7,6},{8,9},{9,8},{10,11... | collective-permute-start | bytes 786440 | tf_op jit(solution)/shard_map/ppermute | solution.py:213
  42.2 9.1 %collective-permute-start.4 = (bf16[64,2048]{1,0:T(8,128)(2,1)S(1)}, bf16[64,2048]{1,0:T(8,128)(2,1)S(1)}, u32[]{:S(2)}, u32[]{:S(2)}) collective-permute-start(bf16[64,2048]{1,0:T(8,128)(2,1)S(1)} %collective-permute-done.refs_1_), channel_id=1, source_target_pairs={{0,1},{1,0},{2,3},{3,2},{4,5},{5,4},{6,7},{7,6},{8,9},{9,8},{10,11... | collective-permute-start | bytes 786440 | tf_op jit(solution)/shard_map/ppermute | solution.py:213
  46.9 4.4 %collective-permute-start.5 = (bf16[64,2048]{1,0:T(8,128)(2,1)S(1)}, bf16[64,2048]{1,0:T(8,128)(2,1)S(1)}, u32[]{:S(2)}, u32[]{:S(2)}) collective-permute-start(bf16[64,2048]{1,0:T(8,128)(2,1)S(1)} %collective-permute-done.1.refs_2_), channel_id=1, source_target_pairs={{0,1},{1,0},{2,3},{3,2},{4,5},{5,4},{6,7},{7,6},{8,9},{9,8},{10,11... | collective-permute-start | bytes 786440 | tf_op jit(solution)/shard_map/ppermute | solution.py:213
  48.8 3.6 %collective-permute-start.6 = (bf16[64,2048]{1,0:T(8,128)(2,1)S(1)}, bf16[64,2048]{1,0:T(8,128)(2,1)S(1)}, u32[]{:S(2)}, u32[]{:S(2)}) collective-permute-start(bf16[64,2048]{1,0:T(8,128)(2,1)S(1)} %collective-permute-done.2.refs_3_), channel_id=1, source_target_pairs={{0,1},{1,0},{2,3},{3,2},{4,5},{5,4},{6,7},{7,6},{8,9},{9,8},{10,11... | collective-permute-start | bytes 786440 | tf_op jit(solution)/shard_map/ppermute | solution.py:213
  51.3 4.1 %copy-start = (bf16[512,256]{1,0:T(8,128)(2,1)S(1)}, bf16[512,256]{1,0:T(8,128)(2,1)}, u32[]{:S(2)}) copy-start(bf16[512,256]{1,0:T(8,128)(2,1)} %cotangent_ref.1) | copy-start | bytes 786436
  51.3 4.1 %copy-start.2 = (f32[7,256]{1,0:T(8,128)S(1)}, f32[7,256]{1,0:T(8,128)}, u32[]{:S(2)}) copy-start(f32[7,256]{1,0:T(8,128)} %filters_ref.1) | copy-start | bytes 21508
  61.7 9.5 %collective-permute-start.7 = (bf16[256,2048]{1,0:T(8,128)(2,1)S(1)}, bf16[256,2048]{1,0:T(8,128)(2,1)}, u32[]{:S(2)}, u32[]{:S(2)}) collective-permute-start(bf16[256,2048]{1,0:T(8,128)(2,1)S(1)} %get-tuple-element.10), channel_id=1, source_target_pairs={{0,1},{1,0},{2,3},{3,2},{4,5},{5,4},{6,7},{7,6},{8,9},{9,8},{10,11... | collective-permute-start | bytes 3145736 | tf_op jit(solution)/shard_map/ppermute | solution.py:213
  63.7 24.5 %all-to-all-start.2 = ((bf16[16,144,256]{2,1,0:T(8,128)(2,1)}), bf16[16,144,256]{2,1,0:T(8,128)(2,1)S(1)}, u32[]{:S(2)}, u32[]{:S(2)}) async-start(bf16[16,144,256]{2,1,0:T(8,128)(2,1)} %get-tuple-element.8), calls=%async_computation.2 | async-start | bytes 2359296 | tf_op jit(solution)/shard_map/all_to_all | solution.py:27
  73.6 25.5 %collective-permute-start.10 = (bf16[64,2048]{1,0:T(8,128)(2,1)}, bf16[64,2048]{1,0:T(8,128)(2,1)S(1)}, u32[]{:S(2)}, u32[]{:S(2)}) collective-permute-start(bf16[64,2048]{1,0:T(8,128)(2,1)} %get-tuple-element.16), channel_id=1, source_target_pairs={{0,2},{2,4},{4,6},{6,0},{1,3},{3,5},{5,7},{7,1},{8,10},{10,12},{12... | collective-permute-start | bytes 786440 | tf_op jit(solution)/shard_map/ppermute | solution.py:32
  75.5 23.6 %collective-permute-start.8 = (bf16[64,2048]{1,0:T(8,128)(2,1)S(1)}, bf16[64,2048]{1,0:T(8,128)(2,1)S(1)}, u32[]{:S(2)}, u32[]{:S(2)}) collective-permute-start(bf16[64,2048]{1,0:T(8,128)(2,1)S(1)} %get-tuple-element.15), channel_id=1, source_target_pairs={{0,4},{2,6},{4,0},{6,2},{1,5},{3,7},{5,1},{7,3},{8,12},{10,14},{12... | collective-permute-start | bytes 786440 | tf_op jit(solution)/shard_map/ppermute | solution.py:32
  78.6 20.5 %collective-permute-start.9 = (bf16[64,2048]{1,0:T(8,128)(2,1)S(1)}, bf16[64,2048]{1,0:T(8,128)(2,1)}, u32[]{:S(2)}, u32[]{:S(2)}) collective-permute-start(bf16[64,2048]{1,0:T(8,128)(2,1)S(1)} %get-tuple-element.17), channel_id=1, source_target_pairs={{0,6},{2,0},{4,2},{6,4},{1,7},{3,1},{5,3},{7,5},{8,14},{10,8},{12,... | collective-permute-start | bytes 786440 | tf_op jit(solution)/shard_map/ppermute | solution.py:32
  89.0 23.4 %all-to-all-start.3 = ((bf16[4,48,256]{2,1,0:T(8,128)(2,1)}), bf16[4,48,256]{2,1,0:T(8,128)(2,1)S(1)}, u32[]{:S(2)}, u32[]{:S(2)}) async-start(bf16[4,48,256]{2,1,0:T(8,128)(2,1)} %pad_maximum_fusion), calls=%async_computation.3 | async-start | bytes 196608 | tf_op jit(solution)/shard_map/all_to_all | solution.py:27

commit v13 on v12

--- a/solution.py
+++ b/solution.py
@@ -228,8 +228,8 @@
         direct[steps] = from_ahead(tokens, ZL, steps)
 
     zh, xy = lax.axis_index(ZH), lax.axis_index((X, Y))
-    head = cotangent[:8]
     column = exchange(with_head(proj_weight, cotangent, nz), ZH)
+    head = lax.dynamic_index_in_dim(column, zh, 0, keepdims=False)[rows : rows + 8]
     ahead = lax.dynamic_index_in_dim(column, (zh + 1) % nz, 0, keepdims=False)[rows : rows + 8]
     column = column[:, :rows].reshape(nz * rows, cols)
     gathered = spread(jnp.concatenate([column, head, ahead], 0), (X, Y))

time: 115 us -> 115 us (level)
  transfers between devices with their start and end apart: 15 -> 15, of which waited for: 6 -> 6; matrix products, arithmetic and copies ran while one was open for 6% -> 5% of each run, Pallas kernels for 2% -> 2%
where the time goes in v13:
time: 115 us; the launch traced here: 114 us
  starting transfers between devices  68.3 us (59%)
  waiting for transfers between devices  26.6 us (23%)
  Pallas kernels  10.4 us (9%)
  other arithmetic  4.84 us (4%)
  local copies, waits for them, and re-layouts  2.53 us (2%)
    all_to_all x4, starting transfers between devices, exchange(): return lax.all_to_all(value, axes, split_axis=0, concat_axis=0, tiled=True)  39 us
    all_to_all x4, waiting for transfers between devices, exchange(): return lax.all_to_all(value, axes, split_axis=0, concat_axis=0, tiled=True)  23.2 us
    ppermute x6, starting transfers between devices, from_ahead(): lax.ppermute(value, axis, [(source, (source - steps) % count) for source...  18.8 us
    ppermute x5, starting transfers between devices, swap(): return lax.ppermute(value, C, [(0, 1), (1, 0)])  10.6 us
    pallas_call x1, Pallas kernels, local_products(): pl.pallas_call(products_kernel, grid_spec=pltpu.PrefetchScalarGridSpec(nu...  6.35 us
  transfers between devices with their start and end apart: 15, of which 6 were waited for; matrix products, arithmetic and copies ran while one was open for 5% of the time, Pallas kernels for 2%

profile of v13, /device:TPU:8, one launch (start us, length us, event | category | flops | bytes accessed | tf_op | source)
XLA Modules:
  0.0 113.6 jit_solution(13401335441286528969)
XLA Ops:
  2.0 15.1 %all-to-all-start = ((bf16[4,48,256]{2,1,0:T(8,128)(2,1)}), bf16[4,48,256]{2,1,0:T(8,128)(2,1)S(1)}, u32[]{:S(2)}, u32[]{:S(2)}) async-start(bf16[4,48,256]{2,1,0:T(8,128)(2,1)} %shard_map.68), calls=%async_computation | async-start | bytes 196608 | tf_op jit(solution)/shard_map/all_to_all | solution.py:27
  17.1 3.8 %collective-permute-start = (bf16[64,2048]{1,0:T(8,128)(2,1)}, bf16[64,2048]{1,0:T(8,128)(2,1)S(1)}, u32[]{:S(2)}, u32[]{:S(2)}) collective-permute-start(bf16[64,2048]{1,0:T(8,128)(2,1)} %refs_0_.1), channel_id=1, source_target_pairs={{0,6},{2,0},{4,2},{6,4},{1,7},{3,1},{5,3},{7,5},{8,14},{10,8},{12,... | collective-permute-start | bytes 786440 | tf_op jit(solution)/shard_map/ppermute | solution.py:32
  20.9 2.5 %collective-permute-start.1 = (bf16[64,2048]{1,0:T(8,128)(2,1)}, bf16[64,2048]{1,0:T(8,128)(2,1)S(1)}, u32[]{:S(2)}, u32[]{:S(2)}) collective-permute-start(bf16[64,2048]{1,0:T(8,128)(2,1)} %refs_0_.1), channel_id=1, source_target_pairs={{0,4},{2,6},{4,0},{6,2},{1,5},{3,7},{5,1},{7,3},{8,12},{10,14},{12... | collective-permute-start | bytes 786440 | tf_op jit(solution)/shard_map/ppermute | solution.py:32
  23.4 2.9 %collective-permute-start.2 = (bf16[64,2048]{1,0:T(8,128)(2,1)}, bf16[64,2048]{1,0:T(8,128)(2,1)S(1)}, u32[]{:S(2)}, u32[]{:S(2)}) collective-permute-start(bf16[64,2048]{1,0:T(8,128)(2,1)} %refs_0_.1), channel_id=1, source_target_pairs={{0,2},{2,4},{4,6},{6,0},{1,3},{3,5},{5,7},{7,1},{8,10},{10,12},{12... | collective-permute-start | bytes 786440 | tf_op jit(solution)/shard_map/ppermute | solution.py:32
  26.3 5.2 %all-to-all-done = bf16[4,48,256]{2,1,0:T(8,128)(2,1)S(1)} async-done(((bf16[4,48,256]{2,1,0:T(8,128)(2,1)}), bf16[4,48,256]{2,1,0:T(8,128)(2,1)S(1)}, u32[]{:S(2)}, u32[]{:S(2)}) %all-to-all-start) | async-done | bytes 98336 | tf_op jit(solution)/shard_map/all_to_all | solution.py:27
  32.7 7.5 %all-to-all-start.1 = ((bf16[16,144,256]{2,1,0:T(8,128)(2,1)}), bf16[16,144,256]{2,1,0:T(8,128)(2,1)S(1)}, u32[]{:S(2)}, u32[]{:S(2)}) async-start(bf16[16,144,256]{2,1,0:T(8,128)(2,1)} %broadcast_in_dim.8), calls=%async_computation.1 | async-start | bytes 2359296 | tf_op jit(solution)/shard_map/all_to_all | solution.py:27
  40.3 1.9 %collective-permute-start.3 = (bf16[64,2048]{1,0:T(8,128)(2,1)S(1)}, bf16[64,2048]{1,0:T(8,128)(2,1)S(1)}, u32[]{:S(2)}, u32[]{:S(2)}) collective-permute-start(bf16[64,2048]{1,0:T(8,128)(2,1)S(1)} %copy-done.1), channel_id=1, source_target_pairs={{0,1},{1,0},{2,3},{3,2},{4,5},{5,4},{6,7},{7,6},{8,9},{9,8},{10,11... | collective-permute-start | bytes 786440 | tf_op jit(solution)/shard_map/ppermute | solution.py:213
  42.2 2.4 %collective-permute-start.4 = (bf16[64,2048]{1,0:T(8,128)(2,1)S(1)}, bf16[64,2048]{1,0:T(8,128)(2,1)S(1)}, u32[]{:S(2)}, u32[]{:S(2)}) collective-permute-start(bf16[64,2048]{1,0:T(8,128)(2,1)S(1)} %collective-permute-done.refs_1_), channel_id=1, source_target_pairs={{0,1},{1,0},{2,3},{3,2},{4,5},{5,4},{6,7},{7,6},{8,9},{9,8},{10,11... | collective-permute-start | bytes 786440 | tf_op jit(solution)/shard_map/ppermute | solution.py:213
  44.6 2.3 %collective-permute-done.1.refs_2_ = bf16[64,2048]{1,0:T(8,128)(2,1)S(1)} collective-permute-done((bf16[64,2048]{1,0:T(8,128)(2,1)}, bf16[64,2048]{1,0:T(8,128)(2,1)S(1)}, u32[]{:S(2)}, u32[]{:S(2)}) %collective-permute-start.1) | collective-permute-done | bytes 262176 | tf_op jit(solution)/shard_map/ppermute | solution.py:32
  46.9 1.9 %collective-permute-start.5 = (bf16[64,2048]{1,0:T(8,128)(2,1)S(1)}, bf16[64,2048]{1,0:T(8,128)(2,1)S(1)}, u32[]{:S(2)}, u32[]{:S(2)}) collective-permute-start(bf16[64,2048]{1,0:T(8,128)(2,1)S(1)} %collective-permute-done.1.refs_2_), channel_id=1, source_target_pairs={{0,1},{1,0},{2,3},{3,2},{4,5},{5,4},{6,7},{7,6},{8,9},{9,8},{10,11... | collective-permute-start | bytes 786440 | tf_op jit(solution)/shard_map/ppermute | solution.py:213
  48.8 2.4 %collective-permute-start.6 = (bf16[64,2048]{1,0:T(8,128)(2,1)S(1)}, bf16[64,2048]{1,0:T(8,128)(2,1)S(1)}, u32[]{:S(2)}, u32[]{:S(2)}) collective-permute-start(bf16[64,2048]{1,0:T(8,128)(2,1)S(1)} %collective-permute-done.2.refs_3_), channel_id=1, source_target_pairs={{0,1},{1,0},{2,3},{3,2},{4,5},{5,4},{6,7},{7,6},{8,9},{9,8},{10,11... | collective-permute-start | bytes 786440 | tf_op jit(solution)/shard_map/ppermute | solution.py:213
  52.4 1.4 %shard_map.67.slab_ref = bf16[512,2048]{1,0:T(8,128)(2,1)} custom-call(bf16[64,2048]{1,0:T(8,128)(2,1)S(1)} %copy-done.1, bf16[64,2048]{1,0:T(8,128)(2,1)S(1)} %collective-permute-done.refs_1_, bf16[64,2048]{1,0:T(8,128)(2,1)S(1)} %collective-permute-done.1.refs_2_, bf16[64,2048]{1,0:T(8,128)(2,1)S(1)} %collective-permute-done.2.refs_3_, ...), custom_call_target="tpu_custom_call" | custom-call | flops 8000000000 | bytes 4194304 | tf_op jit(solution)/shard_map/pallas_call | solution.py:52
  53.8 1.5 %all-to-all-done.1.weight_ref = bf16[16,144,256]{2,1,0:T(8,128)(2,1)S(1)} async-done(((bf16[16,144,256]{2,1,0:T(8,128)(2,1)}), bf16[16,144,256]{2,1,0:T(8,128)(2,1)S(1)}, u32[]{:S(2)}, u32[]{:S(2)}) %all-to-all-start.1) | async-done | bytes 1179680 | tf_op jit(solution)/shard_map/all_to_all | solution.py:27
  55.3 6.3 %shard_map.69 = (bf16[16,144,256]{2,1,0:T(8,128)(2,1)}, bf16[256,2048]{1,0:T(8,128)(2,1)S(1)}, bf16[256,256]{1,0:T(8,128)(2,1)S(1)}) custom-call(s32[1]{0:T(128)} %bitcast.core_ref, bf16[512,2048]{1,0:T(8,128)(2,1)} %shard_map.67.slab_ref, bf16[16,144,256]{2,1,0:T(8,128)(2,1)S(1)} %all-to-all-done.1.weight_ref, bf16[512,256]{1,0:T(8,128)(2,1)S(1)} %copy-done, ...), custom_call_target="tpu_custom_call" | custom-call | flops 1610612736 | bytes 6291456 | tf_op jit(solution)/shard_map/pallas_call | solution.py:125
  61.7 1.9 %collective-permute-start.7 = (bf16[256,2048]{1,0:T(8,128)(2,1)S(1)}, bf16[256,2048]{1,0:T(8,128)(2,1)}, u32[]{:S(2)}, u32[]{:S(2)}) collective-permute-start(bf16[256,2048]{1,0:T(8,128)(2,1)S(1)} %get-tuple-element.10), channel_id=1, source_target_pairs={{0,1},{1,0},{2,3},{3,2},{4,5},{5,4},{6,7},{7,6},{8,9},{9,8},{10,11... | collective-permute-start | bytes 3145736 | tf_op jit(solution)/shard_map/ppermute | solution.py:213
  63.7 6.3 %all-to-all-start.2 = ((bf16[16,144,256]{2,1,0:T(8,128)(2,1)}), bf16[16,144,256]{2,1,0:T(8,128)(2,1)S(1)}, u32[]{:S(2)}, u32[]{:S(2)}) async-start(bf16[16,144,256]{2,1,0:T(8,128)(2,1)} %get-tuple-element.8), calls=%async_computation.2 | async-start | bytes 2359296 | tf_op jit(solution)/shard_map/all_to_all | solution.py:27
  71.2 1.6 %add_convert_fusion = bf16[256,2048]{1,0:T(8,128)(2,1)S(1)} fusion(bf16[256,2048]{1,0:T(8,128)(2,1)} %collective-permute-done.7, bf16[256,2048]{1,0:T(8,128)(2,1)S(1)} %shard_map.70), kind=kLoop, calls=%fused_computation.1 | loop fusion | flops 2097152 | bytes 3145728 | tf_op jit(solution)/shard_map/convert_element_type | solution.py:247
  73.6 1.9 %collective-permute-start.10 = (bf16[64,2048]{1,0:T(8,128)(2,1)}, bf16[64,2048]{1,0:T(8,128)(2,1)S(1)}, u32[]{:S(2)}, u32[]{:S(2)}) collective-permute-start(bf16[64,2048]{1,0:T(8,128)(2,1)} %get-tuple-element.16), channel_id=1, source_target_pairs={{0,2},{2,4},{4,6},{6,0},{1,3},{3,5},{5,7},{7,1},{8,10},{10,12},{12... | collective-permute-start | bytes 786440 | tf_op jit(solution)/shard_map/ppermute | solution.py:32
  75.5 3.1 %collective-permute-start.8 = (bf16[64,2048]{1,0:T(8,128)(2,1)S(1)}, bf16[64,2048]{1,0:T(8,128)(2,1)S(1)}, u32[]{:S(2)}, u32[]{:S(2)}) collective-permute-start(bf16[64,2048]{1,0:T(8,128)(2,1)S(1)} %get-tuple-element.15), channel_id=1, source_target_pairs={{0,4},{2,6},{4,0},{6,2},{1,5},{3,7},{5,1},{7,3},{8,12},{10,14},{12... | collective-permute-start | bytes 786440 | tf_op jit(solution)/shard_map/ppermute | solution.py:32
  78.6 4.5 %collective-permute-start.9 = (bf16[64,2048]{1,0:T(8,128)(2,1)S(1)}, bf16[64,2048]{1,0:T(8,128)(2,1)}, u32[]{:S(2)}, u32[]{:S(2)}) collective-permute-start(bf16[64,2048]{1,0:T(8,128)(2,1)S(1)} %get-tuple-element.17), channel_id=1, source_target_pairs={{0,6},{2,0},{4,2},{6,4},{1,7},{3,1},{5,3},{7,5},{8,14},{10,8},{12,... | collective-permute-start | bytes 786440 | tf_op jit(solution)/shard_map/ppermute | solution.py:32
  83.2 5.0 %all-to-all-done.2 = bf16[16,144,256]{2,1,0:T(8,128)(2,1)S(1)} async-done(((bf16[16,144,256]{2,1,0:T(8,128)(2,1)}), bf16[16,144,256]{2,1,0:T(8,128)(2,1)S(1)}, u32[]{:S(2)}, u32[]{:S(2)}) %all-to-all-start.2) | async-done | bytes 1179680 | tf_op jit(solution)/shard_map/all_to_all | solution.py:27
  89.0 10.1 %all-to-all-start.3 = ((bf16[4,48,256]{2,1,0:T(8,128)(2,1)}), bf16[4,48,256]{2,1,0:T(8,128)(2,1)S(1)}, u32[]{:S(2)}, u32[]{:S(2)}) async-start(bf16[4,48,256]{2,1,0:T(8,128)(2,1)} %pad_maximum_fusion), calls=%async_computation.3 | async-start | bytes 196608 | tf_op jit(solution)/shard_map/all_to_all | solution.py:27
  99.1 1.8 %fusion.2 = bf16[64,2048]{1,0:T(8,128)(2,1)} fusion(bf16[64,2048]{1,0:T(8,128)(2,1)S(1)} %collective-permute-done.10, bf16[64,2048]{1,0:T(8,128)(2,1)} %collective-permute-done.9, bf16[64,2048]{1,0:T(8,128)(2,1)S(1)} %collective-permute-done.8, bf16[4,64,2048]{2,1,0:T(8,128)(2,1)S(1)} %bitcast.23, s32[]{:T(128)S(6)} %select_n.74), kind=kLoop, calls=%fused_computation.5 | loop fusion | flops 1048576 | bytes 1310724 | tf_op jit(solution)/shard_map/convert_element_type | solution.py:253
  100.9 11.5 %all-to-all-done.3 = bf16[4,48,256]{2,1,0:T(8,128)(2,1)S(1)} async-done(((bf16[4,48,256]{2,1,0:T(8,128)(2,1)}), bf16[4,48,256]{2,1,0:T(8,128)(2,1)S(1)}, u32[]{:S(2)}, u32[]{:S(2)}) %all-to-all-start.3) | async-done | bytes 98336 | tf_op jit(solution)/shard_map/all_to_all | solution.py:27
  (34 shorter events, 7.7 us)
Async XLA Ops:
  2.0 29.6 %all-to-all-start = ((bf16[4,48,256]{2,1,0:T(8,128)(2,1)}), bf16[4,48,256]{2,1,0:T(8,128)(2,1)S(1)}, u32[]{:S(2)}, u32[]{:S(2)}) async-start(bf16[4,48,256]{2,1,0:T(8,128)(2,1)} %shard_map.68), calls=%async_computation | async-start | bytes 196608 | tf_op jit(solution)/shard_map/all_to_all | solution.py:27
  17.1 25.1 %collective-permute-start = (bf16[64,2048]{1,0:T(8,128)(2,1)}, bf16[64,2048]{1,0:T(8,128)(2,1)S(1)}, u32[]{:S(2)}, u32[]{:S(2)}) collective-permute-start(bf16[64,2048]{1,0:T(8,128)(2,1)} %refs_0_.1), channel_id=1, source_target_pairs={{0,6},{2,0},{4,2},{6,4},{1,7},{3,1},{5,3},{7,5},{8,14},{10,8},{12,... | collective-permute-start | bytes 786440 | tf_op jit(solution)/shard_map/ppermute | solution.py:32
  20.9 26.0 %collective-permute-start.1 = (bf16[64,2048]{1,0:T(8,128)(2,1)}, bf16[64,2048]{1,0:T(8,128)(2,1)S(1)}, u32[]{:S(2)}, u32[]{:S(2)}) collective-permute-start(bf16[64,2048]{1,0:T(8,128)(2,1)} %refs_0_.1), channel_id=1, source_target_pairs={{0,4},{2,6},{4,0},{6,2},{1,5},{3,7},{5,1},{7,3},{8,12},{10,14},{12... | collective-permute-start | bytes 786440 | tf_op jit(solution)/shard_map/ppermute | solution.py:32
  23.4 25.4 %collective-permute-start.2 = (bf16[64,2048]{1,0:T(8,128)(2,1)}, bf16[64,2048]{1,0:T(8,128)(2,1)S(1)}, u32[]{:S(2)}, u32[]{:S(2)}) collective-permute-start(bf16[64,2048]{1,0:T(8,128)(2,1)} %refs_0_.1), channel_id=1, source_target_pairs={{0,2},{2,4},{4,6},{6,0},{1,3},{3,5},{5,7},{7,1},{8,10},{10,12},{12... | collective-permute-start | bytes 786440 | tf_op jit(solution)/shard_map/ppermute | solution.py:32
  32.7 7.5 %copy-start.1 = (bf16[64,2048]{1,0:T(8,128)(2,1)S(1)}, bf16[64,2048]{1,0:T(8,128)(2,1)}, u32[]{:S(2)}) copy-start(bf16[64,2048]{1,0:T(8,128)(2,1)} %refs_0_.1) | copy-start | bytes 786436
  32.7 22.6 %all-to-all-start.1 = ((bf16[16,144,256]{2,1,0:T(8,128)(2,1)}), bf16[16,144,256]{2,1,0:T(8,128)(2,1)S(1)}, u32[]{:S(2)}, u32[]{:S(2)}) async-start(bf16[16,144,256]{2,1,0:T(8,128)(2,1)} %broadcast_in_dim.8), calls=%async_computation.1 | async-start | bytes 2359296 | tf_op jit(solution)/shard_map/all_to_all | solution.py:27
  40.3 11.0 %collective-permute-start.3 = (bf16[64,2048]{1,0:T(8,128)(2,1)S(1)}, bf16[64,2048]{1,0:T(8,128)(2,1)S(1)}, u32[]{:S(2)}, u32[]{:S(2)}) collective-permute-start(bf16[64,2048]{1,0:T(8,128)(2,1)S(1)} %copy-done.1), channel_id=1, source_target_pairs={{0,1},{1,0},{2,3},{3,2},{4,5},{5,4},{6,7},{7,6},{8,9},{9,8},{10,11... | collective-permute-start | bytes 786440 | tf_op jit(solution)/shard_map/ppermute | solution.py:213
  42.2 9.1 %collective-permute-start.4 = (bf16[64,2048]{1,0:T(8,128)(2,1)S(1)}, bf16[64,2048]{1,0:T(8,128)(2,1)S(1)}, u32[]{:S(2)}, u32[]{:S(2)}) collective-permute-start(bf16[64,2048]{1,0:T(8,128)(2,1)S(1)} %collective-permute-done.refs_1_), channel_id=1, source_target_pairs={{0,1},{1,0},{2,3},{3,2},{4,5},{5,4},{6,7},{7,6},{8,9},{9,8},{10,11... | collective-permute-start | bytes 786440 | tf_op jit(solution)/shard_map/ppermute | solution.py:213
  46.9 4.4 %collective-permute-start.5 = (bf16[64,2048]{1,0:T(8,128)(2,1)S(1)}, bf16[64,2048]{1,0:T(8,128)(2,1)S(1)}, u32[]{:S(2)}, u32[]{:S(2)}) collective-permute-start(bf16[64,2048]{1,0:T(8,128)(2,1)S(1)} %collective-permute-done.1.refs_2_), channel_id=1, source_target_pairs={{0,1},{1,0},{2,3},{3,2},{4,5},{5,4},{6,7},{7,6},{8,9},{9,8},{10,11... | collective-permute-start | bytes 786440 | tf_op jit(solution)/shard_map/ppermute | solution.py:213
  48.8 3.6 %collective-permute-start.6 = (bf16[64,2048]{1,0:T(8,128)(2,1)S(1)}, bf16[64,2048]{1,0:T(8,128)(2,1)S(1)}, u32[]{:S(2)}, u32[]{:S(2)}) collective-permute-start(bf16[64,2048]{1,0:T(8,128)(2,1)S(1)} %collective-permute-done.2.refs_3_), channel_id=1, source_target_pairs={{0,1},{1,0},{2,3},{3,2},{4,5},{5,4},{6,7},{7,6},{8,9},{9,8},{10,11... | collective-permute-start | bytes 786440 | tf_op jit(solution)/shard_map/ppermute | solution.py:213
  51.3 4.1 %copy-start = (bf16[512,256]{1,0:T(8,128)(2,1)S(1)}, bf16[512,256]{1,0:T(8,128)(2,1)}, u32[]{:S(2)}) copy-start(bf16[512,256]{1,0:T(8,128)(2,1)} %cotangent_ref.1) | copy-start | bytes 786436
  51.3 4.1 %copy-start.2 = (f32[7,256]{1,0:T(8,128)S(1)}, f32[7,256]{1,0:T(8,128)}, u32[]{:S(2)}) copy-start(f32[7,256]{1,0:T(8,128)} %filters_ref.1) | copy-start | bytes 21508
  61.7 9.5 %collective-permute-start.7 = (bf16[256,2048]{1,0:T(8,128)(2,1)S(1)}, bf16[256,2048]{1,0:T(8,128)(2,1)}, u32[]{:S(2)}, u32[]{:S(2)}) collective-permute-start(bf16[256,2048]{1,0:T(8,128)(2,1)S(1)} %get-tuple-element.10), channel_id=1, source_target_pairs={{0,1},{1,0},{2,3},{3,2},{4,5},{5,4},{6,7},{7,6},{8,9},{9,8},{10,11... | collective-permute-start | bytes 3145736 | tf_op jit(solution)/shard_map/ppermute | solution.py:213
  63.7 24.5 %all-to-all-start.2 = ((bf16[16,144,256]{2,1,0:T(8,128)(2,1)}), bf16[16,144,256]{2,1,0:T(8,128)(2,1)S(1)}, u32[]{:S(2)}, u32[]{:S(2)}) async-start(bf16[16,144,256]{2,1,0:T(8,128)(2,1)} %get-tuple-element.8), calls=%async_computation.2 | async-start | bytes 2359296 | tf_op jit(solution)/shard_map/all_to_all | solution.py:27
  73.6 25.5 %collective-permute-start.10 = (bf16[64,2048]{1,0:T(8,128)(2,1)}, bf16[64,2048]{1,0:T(8,128)(2,1)S(1)}, u32[]{:S(2)}, u32[]{:S(2)}) collective-permute-start(bf16[64,2048]{1,0:T(8,128)(2,1)} %get-tuple-element.16), channel_id=1, source_target_pairs={{0,2},{2,4},{4,6},{6,0},{1,3},{3,5},{5,7},{7,1},{8,10},{10,12},{12... | collective-permute-start | bytes 786440 | tf_op jit(solution)/shard_map/ppermute | solution.py:32
  75.5 23.6 %collective-permute-start.8 = (bf16[64,2048]{1,0:T(8,128)(2,1)S(1)}, bf16[64,2048]{1,0:T(8,128)(2,1)S(1)}, u32[]{:S(2)}, u32[]{:S(2)}) collective-permute-start(bf16[64,2048]{1,0:T(8,128)(2,1)S(1)} %get-tuple-element.15), channel_id=1, source_target_pairs={{0,4},{2,6},{4,0},{6,2},{1,5},{3,7},{5,1},{7,3},{8,12},{10,14},{12... | collective-permute-start | bytes 786440 | tf_op jit(solution)/shard_map/ppermute | solution.py:32
  78.6 20.5 %collective-permute-start.9 = (bf16[64,2048]{1,0:T(8,128)(2,1)S(1)}, bf16[64,2048]{1,0:T(8,128)(2,1)}, u32[]{:S(2)}, u32[]{:S(2)}) collective-permute-start(bf16[64,2048]{1,0:T(8,128)(2,1)S(1)} %get-tuple-element.17), channel_id=1, source_target_pairs={{0,6},{2,0},{4,2},{6,4},{1,7},{3,1},{5,3},{7,5},{8,14},{10,8},{12,... | collective-permute-start | bytes 786440 | tf_op jit(solution)/shard_map/ppermute | solution.py:32
  89.0 23.4 %all-to-all-start.3 = ((bf16[4,48,256]{2,1,0:T(8,128)(2,1)}), bf16[4,48,256]{2,1,0:T(8,128)(2,1)S(1)}, u32[]{:S(2)}, u32[]{:S(2)}) async-start(bf16[4,48,256]{2,1,0:T(8,128)(2,1)} %pad_maximum_fusion), calls=%async_computation.3 | async-start | bytes 196608 | tf_op jit(solution)/shard_map/all_to_all | solution.py:27

commit v14 on v13

--- a/solution.py
+++ b/solution.py
@@ -158,29 +158,40 @@
     )(core.reshape(1).astype(jnp.int32), slab, gathered, cotangent, following, filters)
 
 
-def own_kernel(ours_ref, weight_ref, out_ref):
+def chip_sum_kernel(ours_ref, weight_ref, other_ref, *refs):
+    outs, sum_ref = refs[:-1], refs[-1]
     weight = weight_ref[...].reshape(-1, ours_ref.shape[1])
-    out_ref[...] = lax.dot_general(
+    here = lax.dot_general(
         ours_ref[...], weight, (((1,), (1,)), ((), ())), preferred_element_type=F32
-    ).astype(BF)
-
-
-def own_products(ours, gathered, nz, rows):
+    )
+    sum_ref[...] = (here + other_ref[...].astype(F32)).astype(BF)
+    chips, chip = len(outs), lax.axis_index(ZL)
+    count = outs[0].shape[0]
+    for steps, out_ref in enumerate(outs):
+        target = lax.rem(chip + chips - steps, chips)
+        out_ref[...] = sum_ref[pl.ds(pl.multiple_of(target * count, count), count), :]
+
+
+def chip_sums(ours, gathered, from_other, nz, rows, chips):
     half, cols = ours.shape
     nxy = gathered.shape[0]
     part = nxy * rows
     return pl.pallas_call(
-        own_kernel,
+        chip_sum_kernel,
         grid=(nz,),
         in_specs=[
             pl.BlockSpec((half, cols), lambda i: (0, 0)),
             pl.BlockSpec((nxy, rows, cols), lambda i: (0, i, 0)),
+            pl.BlockSpec((half, part), lambda i: (0, i)),
         ],
-        out_specs=pl.BlockSpec((half, part), lambda i: (0, i)),
-        out_shape=jax.ShapeDtypeStruct((half, nz * part), BF),
+        out_specs=[pl.BlockSpec((half // chips, part), lambda i: (0, i)) for _ in range(chips)],
+        out_shape=[jax.ShapeDtypeStruct((half // chips, nz * part), BF) for _ in range(chips)],
+        scratch_shapes=[pltpu.VMEM((half, part), BF)],
         compiler_params=pltpu.CompilerParams(vmem_limit_bytes=VMEM_BYTES),
-        cost_estimate=pl.CostEstimate(flops=4 * 10**9, bytes_accessed=8 * half * part, transcendentals=0),
-    )(ours, gathered)
+        cost_estimate=pl.CostEstimate(
+            flops=2 * half * cols * nz * part, bytes_accessed=8 * half * nz * part, transcendentals=0
+        ),
+    )(ours, gathered, from_other)
 
 
 def head_kernel(weight_ref, head_ref, out_ref):
@@ -243,13 +254,10 @@
     )
     total = jnp.sum(exchange(packed, (X, Y)).astype(F32), axis=0)
 
-    here = own_products(ours, gathered, nz, rows)
-    chip_sum = (here.astype(F32) + swap(for_other).astype(F32)).astype(BF)
-    chip_sum = chip_sum.reshape(nzl, own_tokens, depth)
-    summed = lax.dynamic_index_in_dim(chip_sum, chip, 0, keepdims=False).astype(F32)
+    pieces = chip_sums(ours, gathered, swap(for_other), nz, rows, nzl)
+    summed = pieces[0].astype(F32)
     for steps in (2, 1, 3):
-        outgoing = lax.dynamic_index_in_dim(chip_sum, (chip - steps) % nzl, 0, keepdims=False)
-        summed = summed + from_ahead(outgoing, ZL, steps).astype(F32)
+        summed = summed + from_ahead(pieces[steps], ZL, steps).astype(F32)
     input_grad = summed.astype(BF)
 
     blocks = total[: nz * rows].astype(BF).reshape(nz, rows, cols)

time: 115 us -> 112 us (0.974)
  the two profiles are of different devices: /device:TPU:8 before, /device:TPU:96 now
where the time goes in v14:
time: 112 us; the launch traced here: 111 us
  starting transfers between devices  64.2 us (57%)
  waiting for transfers between devices  30.1 us (27%)
  Pallas kernels  10.7 us (10%)
  other arithmetic  3.57 us (3%)
  local copies, waits for them, and re-layouts  1.75 us (2%)
    all_to_all x4, starting transfers between devices, exchange(): return lax.all_to_all(value, axes, split_axis=0, concat_axis=0, tiled=True)  34.2 us
    all_to_all x4, waiting for transfers between devices, exchange(): return lax.all_to_all(value, axes, split_axis=0, concat_axis=0, tiled=True)  21.2 us
    ppermute x6, starting transfers between devices, from_ahead(): lax.ppermute(value, axis, [(source, (source - steps) % count) for source...  19.3 us
    ppermute x5, starting transfers between devices, swap(): return lax.ppermute(value, C, [(0, 1), (1, 0)])  10.6 us
    pallas_call x1, Pallas kernels, local_products(): pl.pallas_call(products_kernel, grid_spec=pltpu.PrefetchScalarGridSpec(nu...  6.35 us
    ppermute x6, waiting for transfers between devices, from_ahead(): lax.ppermute(value, axis, [(source, (source - steps) % count) for source...  5.31 us
    ppermute x5, waiting for transfers between devices, swap(): return lax.ppermute(value, C, [(0, 1), (1, 0)])  3.64 us
  transfers between devices with their start and end apart: 15, of which 8 were waited for; matrix products, arithmetic and copies ran while one was open for 4% of the time, Pallas kernels for 3%

profile of v14, /device:TPU:96, one launch (start us, length us, event | category | flops | bytes accessed | tf_op | source)
XLA Modules:
  0.0 111.2 jit_solution(6437247172539809587)
XLA Ops:
  2.0 12.4 %all-to-all-start = ((bf16[4,48,256]{2,1,0:T(8,128)(2,1)}), bf16[4,48,256]{2,1,0:T(8,128)(2,1)S(1)}, u32[]{:S(2)}, u32[]{:S(2)}) async-start(bf16[4,48,256]{2,1,0:T(8,128)(2,1)} %shard_map.68), calls=%async_computation | async-start | bytes 196608 | tf_op jit(solution)/shard_map/all_to_all | solution.py:27
  14.4 3.8 %collective-permute-start.2 = (bf16[64,2048]{1,0:T(8,128)(2,1)}, bf16[64,2048]{1,0:T(8,128)(2,1)S(1)}, u32[]{:S(2)}, u32[]{:S(2)}) collective-permute-start(bf16[64,2048]{1,0:T(8,128)(2,1)} %refs_0_.1), channel_id=1, source_target_pairs={{0,2},{2,4},{4,6},{6,0},{1,3},{3,5},{5,7},{7,1},{8,10},{10,12},{12... | collective-permute-start | bytes 786440 | tf_op jit(solution)/shard_map/ppermute | solution.py:32
  18.2 2.5 %collective-permute-start.1 = (bf16[64,2048]{1,0:T(8,128)(2,1)}, bf16[64,2048]{1,0:T(8,128)(2,1)S(1)}, u32[]{:S(2)}, u32[]{:S(2)}) collective-permute-start(bf16[64,2048]{1,0:T(8,128)(2,1)} %refs_0_.1), channel_id=1, source_target_pairs={{0,4},{2,6},{4,0},{6,2},{1,5},{3,7},{5,1},{7,3},{8,12},{10,14},{12... | collective-permute-start | bytes 786440 | tf_op jit(solution)/shard_map/ppermute | solution.py:32
  20.7 2.9 %collective-permute-start = (bf16[64,2048]{1,0:T(8,128)(2,1)}, bf16[64,2048]{1,0:T(8,128)(2,1)S(1)}, u32[]{:S(2)}, u32[]{:S(2)}) collective-permute-start(bf16[64,2048]{1,0:T(8,128)(2,1)} %refs_0_.1), channel_id=1, source_target_pairs={{0,6},{2,0},{4,2},{6,4},{1,7},{3,1},{5,3},{7,5},{8,14},{10,8},{12,... | collective-permute-start | bytes 786440 | tf_op jit(solution)/shard_map/ppermute | solution.py:32
  23.6 5.3 %all-to-all-done = bf16[4,48,256]{2,1,0:T(8,128)(2,1)S(1)} async-done(((bf16[4,48,256]{2,1,0:T(8,128)(2,1)}), bf16[4,48,256]{2,1,0:T(8,128)(2,1)S(1)}, u32[]{:S(2)}, u32[]{:S(2)}) %all-to-all-start) | async-done | bytes 98336 | tf_op jit(solution)/shard_map/all_to_all | solution.py:27
  30.0 7.2 %all-to-all-start.1 = ((bf16[16,144,256]{2,1,0:T(8,128)(2,1)}), bf16[16,144,256]{2,1,0:T(8,128)(2,1)S(1)}, u32[]{:S(2)}, u32[]{:S(2)}) async-start(bf16[16,144,256]{2,1,0:T(8,128)(2,1)} %broadcast_in_dim.8), calls=%async_computation.1 | async-start | bytes 2359296 | tf_op jit(solution)/shard_map/all_to_all | solution.py:27
  37.2 1.9 %collective-permute-start.3 = (bf16[64,2048]{1,0:T(8,128)(2,1)S(1)}, bf16[64,2048]{1,0:T(8,128)(2,1)S(1)}, u32[]{:S(2)}, u32[]{:S(2)}) collective-permute-start(bf16[64,2048]{1,0:T(8,128)(2,1)S(1)} %copy-done.1), channel_id=1, source_target_pairs={{0,1},{1,0},{2,3},{3,2},{4,5},{5,4},{6,7},{7,6},{8,9},{9,8},{10,11... | collective-permute-start | bytes 786440 | tf_op jit(solution)/shard_map/ppermute | solution.py:224
  39.2 2.4 %collective-permute-start.6 = (bf16[64,2048]{1,0:T(8,128)(2,1)S(1)}, bf16[64,2048]{1,0:T(8,128)(2,1)S(1)}, u32[]{:S(2)}, u32[]{:S(2)}) collective-permute-start(bf16[64,2048]{1,0:T(8,128)(2,1)S(1)} %collective-permute-done.2.refs_3_), channel_id=1, source_target_pairs={{0,1},{1,0},{2,3},{3,2},{4,5},{5,4},{6,7},{7,6},{8,9},{9,8},{10,11... | collective-permute-start | bytes 786440 | tf_op jit(solution)/shard_map/ppermute | solution.py:224
  41.6 2.6 %collective-permute-done.1.refs_2_ = bf16[64,2048]{1,0:T(8,128)(2,1)S(1)} collective-permute-done((bf16[64,2048]{1,0:T(8,128)(2,1)}, bf16[64,2048]{1,0:T(8,128)(2,1)S(1)}, u32[]{:S(2)}, u32[]{:S(2)}) %collective-permute-start.1) | collective-permute-done | bytes 262176 | tf_op jit(solution)/shard_map/ppermute | solution.py:32
  44.2 1.9 %collective-permute-start.5 = (bf16[64,2048]{1,0:T(8,128)(2,1)S(1)}, bf16[64,2048]{1,0:T(8,128)(2,1)S(1)}, u32[]{:S(2)}, u32[]{:S(2)}) collective-permute-start(bf16[64,2048]{1,0:T(8,128)(2,1)S(1)} %collective-permute-done.1.refs_2_), channel_id=1, source_target_pairs={{0,1},{1,0},{2,3},{3,2},{4,5},{5,4},{6,7},{7,6},{8,9},{9,8},{10,11... | collective-permute-start | bytes 786440 | tf_op jit(solution)/shard_map/ppermute | solution.py:224
  46.1 2.4 %collective-permute-start.4 = (bf16[64,2048]{1,0:T(8,128)(2,1)S(1)}, bf16[64,2048]{1,0:T(8,128)(2,1)S(1)}, u32[]{:S(2)}, u32[]{:S(2)}) collective-permute-start(bf16[64,2048]{1,0:T(8,128)(2,1)S(1)} %collective-permute-done.refs_1_), channel_id=1, source_target_pairs={{0,1},{1,0},{2,3},{3,2},{4,5},{5,4},{6,7},{7,6},{8,9},{9,8},{10,11... | collective-permute-start | bytes 786440 | tf_op jit(solution)/shard_map/ppermute | solution.py:224
  51.1 2.5 %all-to-all-done.1.weight_ref = bf16[16,144,256]{2,1,0:T(8,128)(2,1)S(1)} async-done(((bf16[16,144,256]{2,1,0:T(8,128)(2,1)}), bf16[16,144,256]{2,1,0:T(8,128)(2,1)S(1)}, u32[]{:S(2)}, u32[]{:S(2)}) %all-to-all-start.1) | async-done | bytes 1179680 | tf_op jit(solution)/shard_map/all_to_all | solution.py:27
  53.6 6.3 %shard_map.69 = (bf16[16,144,256]{2,1,0:T(8,128)(2,1)}, bf16[256,2048]{1,0:T(8,128)(2,1)S(1)}, bf16[256,256]{1,0:T(8,128)(2,1)S(1)}) custom-call(s32[1]{0:T(128)} %bitcast.core_ref, bf16[512,2048]{1,0:T(8,128)(2,1)} %shard_map.67.slab_ref, bf16[16,144,256]{2,1,0:T(8,128)(2,1)S(1)} %all-to-all-done.1.weight_ref, bf16[512,256]{1,0:T(8,128)(2,1)S(1)} %copy-done, ...), custom_call_target="tpu_custom_call" | custom-call | flops 1610612736 | bytes 6291456 | tf_op jit(solution)/shard_map/pallas_call | solution.py:125
  60.0 4.6 %all-to-all-start.2 = ((bf16[16,144,256]{2,1,0:T(8,128)(2,1)}), bf16[16,144,256]{2,1,0:T(8,128)(2,1)}, u32[]{:S(2)}, u32[]{:S(2)}) async-start(bf16[16,144,256]{2,1,0:T(8,128)(2,1)} %get-tuple-element.12), calls=%async_computation.2 | async-start | bytes 2359296 | tf_op jit(solution)/shard_map/all_to_all | solution.py:27
  64.6 2.0 %collective-permute-start.7 = (bf16[256,2048]{1,0:T(8,128)(2,1)S(1)}, bf16[256,2048]{1,0:T(8,128)(2,1)S(1)}, u32[]{:S(2)}, u32[]{:S(2)}) collective-permute-start(bf16[256,2048]{1,0:T(8,128)(2,1)S(1)} %get-tuple-element.14), channel_id=1, source_target_pairs={{0,1},{1,0},{2,3},{3,2},{4,5},{5,4},{6,7},{7,6},{8,9},{9,8},{10,11... | collective-permute-start | bytes 3145736 | tf_op jit(solution)/shard_map/ppermute | solution.py:224
  66.6 2.6 %collective-permute-done.7.other_ref = bf16[256,2048]{1,0:T(8,128)(2,1)S(1)} collective-permute-done((bf16[256,2048]{1,0:T(8,128)(2,1)S(1)}, bf16[256,2048]{1,0:T(8,128)(2,1)S(1)}, u32[]{:S(2)}, u32[]{:S(2)}) %collective-permute-start.7) | collective-permute-done | bytes 1048608 | tf_op jit(solution)/shard_map/ppermute | solution.py:224
  69.1 1.5 %shard_map.70 = (bf16[64,2048]{1,0:T(8,128)(2,1)S(1)}, bf16[64,2048]{1,0:T(8,128)(2,1)S(1)}, bf16[64,2048]{1,0:T(8,128)(2,1)S(1)}, bf16[64,2048]{1,0:T(8,128)(2,1)S(1)}) custom-call(bf16[256,256]{1,0:T(8,128)(2,1)S(1)} %get-tuple-element.13.ours_ref, bf16[16,144,256]{2,1,0:T(8,128)(2,1)S(1)} %all-to-all-done.1.weight_ref, ...), custom_call_target="tpu_custom_call" | custom-call | flops 268435456 | bytes 4194304 | tf_op jit(solution)/shard_map/pallas_call | solution.py:179
  70.7 2.5 %collective-permute-start.8 = (bf16[64,2048]{1,0:T(8,128)(2,1)S(1)}, bf16[64,2048]{1,0:T(8,128)(2,1)S(1)}, u32[]{:S(2)}, u32[]{:S(2)}) collective-permute-start(bf16[64,2048]{1,0:T(8,128)(2,1)S(1)} %get-tuple-element.16), channel_id=1, source_target_pairs={{0,4},{2,6},{4,0},{6,2},{1,5},{3,7},{5,1},{7,3},{8,12},{10,14},{12... | collective-permute-start | bytes 786440 | tf_op jit(solution)/shard_map/ppermute | solution.py:32
  73.2 3.6 %collective-permute-start.9 = (bf16[64,2048]{1,0:T(8,128)(2,1)S(1)}, bf16[64,2048]{1,0:T(8,128)(2,1)S(1)}, u32[]{:S(2)}, u32[]{:S(2)}) collective-permute-start(bf16[64,2048]{1,0:T(8,128)(2,1)S(1)} %get-tuple-element.17), channel_id=1, source_target_pairs={{0,6},{2,0},{4,2},{6,4},{1,7},{3,1},{5,3},{7,5},{8,14},{10,8},{12,... | collective-permute-start | bytes 786440 | tf_op jit(solution)/shard_map/ppermute | solution.py:32
  76.8 4.0 %collective-permute-start.10 = (bf16[64,2048]{1,0:T(8,128)(2,1)S(1)}, bf16[64,2048]{1,0:T(8,128)(2,1)S(1)}, u32[]{:S(2)}, u32[]{:S(2)}) collective-permute-start(bf16[64,2048]{1,0:T(8,128)(2,1)S(1)} %get-tuple-element.18), channel_id=1, source_target_pairs={{0,2},{2,4},{4,6},{6,0},{1,3},{3,5},{5,7},{7,1},{8,10},{10,12},{12... | collective-permute-start | bytes 786440 | tf_op jit(solution)/shard_map/ppermute | solution.py:32
  80.8 3.6 %all-to-all-done.2 = bf16[16,144,256]{2,1,0:T(8,128)(2,1)} async-done(((bf16[16,144,256]{2,1,0:T(8,128)(2,1)}), bf16[16,144,256]{2,1,0:T(8,128)(2,1)}, u32[]{:S(2)}, u32[]{:S(2)}) %all-to-all-start.2) | async-done | bytes 1179680 | tf_op jit(solution)/shard_map/all_to_all | solution.py:27
  86.6 10.1 %all-to-all-start.3 = ((bf16[4,48,256]{2,1,0:T(8,128)(2,1)}), bf16[4,48,256]{2,1,0:T(8,128)(2,1)S(1)}, u32[]{:S(2)}, u32[]{:S(2)}) async-start(bf16[4,48,256]{2,1,0:T(8,128)(2,1)} %pad_maximum_fusion), calls=%async_computation.3 | async-start | bytes 196608 | tf_op jit(solution)/shard_map/all_to_all | solution.py:27
  96.7 2.7 %collective-permute-done.10 = bf16[64,2048]{1,0:T(8,128)(2,1)S(1)} collective-permute-done((bf16[64,2048]{1,0:T(8,128)(2,1)S(1)}, bf16[64,2048]{1,0:T(8,128)(2,1)S(1)}, u32[]{:S(2)}, u32[]{:S(2)}) %collective-permute-start.10) | collective-permute-done | bytes 262176 | tf_op jit(solution)/shard_map/ppermute | solution.py:32
  100.2 9.7 %all-to-all-done.3 = bf16[4,48,256]{2,1,0:T(8,128)(2,1)S(1)} async-done(((bf16[4,48,256]{2,1,0:T(8,128)(2,1)}), bf16[4,48,256]{2,1,0:T(8,128)(2,1)S(1)}, u32[]{:S(2)}, u32[]{:S(2)}) %all-to-all-start.3) | async-done | bytes 98336 | tf_op jit(solution)/shard_map/all_to_all | solution.py:27
  (32 shorter events, 9.2 us)
Async XLA Ops:
  2.0 26.9 %all-to-all-start = ((bf16[4,48,256]{2,1,0:T(8,128)(2,1)}), bf16[4,48,256]{2,1,0:T(8,128)(2,1)S(1)}, u32[]{:S(2)}, u32[]{:S(2)}) async-start(bf16[4,48,256]{2,1,0:T(8,128)(2,1)} %shard_map.68), calls=%async_computation | async-start | bytes 196608 | tf_op jit(solution)/shard_map/all_to_all | solution.py:27
  14.4 24.8 %collective-permute-start.2 = (bf16[64,2048]{1,0:T(8,128)(2,1)}, bf16[64,2048]{1,0:T(8,128)(2,1)S(1)}, u32[]{:S(2)}, u32[]{:S(2)}) collective-permute-start(bf16[64,2048]{1,0:T(8,128)(2,1)} %refs_0_.1), channel_id=1, source_target_pairs={{0,2},{2,4},{4,6},{6,0},{1,3},{3,5},{5,7},{7,1},{8,10},{10,12},{12... | collective-permute-start | bytes 786440 | tf_op jit(solution)/shard_map/ppermute | solution.py:32
  18.2 26.0 %collective-permute-start.1 = (bf16[64,2048]{1,0:T(8,128)(2,1)}, bf16[64,2048]{1,0:T(8,128)(2,1)S(1)}, u32[]{:S(2)}, u32[]{:S(2)}) collective-permute-start(bf16[64,2048]{1,0:T(8,128)(2,1)} %refs_0_.1), channel_id=1, source_target_pairs={{0,4},{2,6},{4,0},{6,2},{1,5},{3,7},{5,1},{7,3},{8,12},{10,14},{12... | collective-permute-start | bytes 786440 | tf_op jit(solution)/shard_map/ppermute | solution.py:32
  20.7 25.4 %collective-permute-start = (bf16[64,2048]{1,0:T(8,128)(2,1)}, bf16[64,2048]{1,0:T(8,128)(2,1)S(1)}, u32[]{:S(2)}, u32[]{:S(2)}) collective-permute-start(bf16[64,2048]{1,0:T(8,128)(2,1)} %refs_0_.1), channel_id=1, source_target_pairs={{0,6},{2,0},{4,2},{6,4},{1,7},{3,1},{5,3},{7,5},{8,14},{10,8},{12,... | collective-permute-start | bytes 786440 | tf_op jit(solution)/shard_map/ppermute | solution.py:32
  30.0 7.2 %copy-start.1 = (bf16[64,2048]{1,0:T(8,128)(2,1)S(1)}, bf16[64,2048]{1,0:T(8,128)(2,1)}, u32[]{:S(2)}) copy-start(bf16[64,2048]{1,0:T(8,128)(2,1)} %refs_0_.1) | copy-start | bytes 786436
  30.0 23.6 %all-to-all-start.1 = ((bf16[16,144,256]{2,1,0:T(8,128)(2,1)}), bf16[16,144,256]{2,1,0:T(8,128)(2,1)S(1)}, u32[]{:S(2)}, u32[]{:S(2)}) async-start(bf16[16,144,256]{2,1,0:T(8,128)(2,1)} %broadcast_in_dim.8), calls=%async_computation.1 | async-start | bytes 2359296 | tf_op jit(solution)/shard_map/all_to_all | solution.py:27
  37.2 11.4 %collective-permute-start.3 = (bf16[64,2048]{1,0:T(8,128)(2,1)S(1)}, bf16[64,2048]{1,0:T(8,128)(2,1)S(1)}, u32[]{:S(2)}, u32[]{:S(2)}) collective-permute-start(bf16[64,2048]{1,0:T(8,128)(2,1)S(1)} %copy-done.1), channel_id=1, source_target_pairs={{0,1},{1,0},{2,3},{3,2},{4,5},{5,4},{6,7},{7,6},{8,9},{9,8},{10,11... | collective-permute-start | bytes 786440 | tf_op jit(solution)/shard_map/ppermute | solution.py:224
  39.2 9.4 %collective-permute-start.6 = (bf16[64,2048]{1,0:T(8,128)(2,1)S(1)}, bf16[64,2048]{1,0:T(8,128)(2,1)S(1)}, u32[]{:S(2)}, u32[]{:S(2)}) collective-permute-start(bf16[64,2048]{1,0:T(8,128)(2,1)S(1)} %collective-permute-done.2.refs_3_), channel_id=1, source_target_pairs={{0,1},{1,0},{2,3},{3,2},{4,5},{5,4},{6,7},{7,6},{8,9},{9,8},{10,11... | collective-permute-start | bytes 786440 | tf_op jit(solution)/shard_map/ppermute | solution.py:224
  44.2 4.4 %collective-permute-start.5 = (bf16[64,2048]{1,0:T(8,128)(2,1)S(1)}, bf16[64,2048]{1,0:T(8,128)(2,1)S(1)}, u32[]{:S(2)}, u32[]{:S(2)}) collective-permute-start(bf16[64,2048]{1,0:T(8,128)(2,1)S(1)} %collective-permute-done.1.refs_2_), channel_id=1, source_target_pairs={{0,1},{1,0},{2,3},{3,2},{4,5},{5,4},{6,7},{7,6},{8,9},{9,8},{10,11... | collective-permute-start | bytes 786440 | tf_op jit(solution)/shard_map/ppermute | solution.py:224
  46.1 3.6 %collective-permute-start.4 = (bf16[64,2048]{1,0:T(8,128)(2,1)S(1)}, bf16[64,2048]{1,0:T(8,128)(2,1)S(1)}, u32[]{:S(2)}, u32[]{:S(2)}) collective-permute-start(bf16[64,2048]{1,0:T(8,128)(2,1)S(1)} %collective-permute-done.refs_1_), channel_id=1, source_target_pairs={{0,1},{1,0},{2,3},{3,2},{4,5},{5,4},{6,7},{7,6},{8,9},{9,8},{10,11... | collective-permute-start | bytes 786440 | tf_op jit(solution)/shard_map/ppermute | solution.py:224
  48.5 5.1 %copy-start = (bf16[512,256]{1,0:T(8,128)(2,1)S(1)}, bf16[512,256]{1,0:T(8,128)(2,1)}, u32[]{:S(2)}) copy-start(bf16[512,256]{1,0:T(8,128)(2,1)} %cotangent_ref.1) | copy-start | bytes 786436
  48.6 5.0 %copy-start.2 = (f32[7,256]{1,0:T(8,128)S(1)}, f32[7,256]{1,0:T(8,128)}, u32[]{:S(2)}) copy-start(f32[7,256]{1,0:T(8,128)} %filters_ref.1) | copy-start | bytes 21508
  60.0 24.5 %all-to-all-start.2 = ((bf16[16,144,256]{2,1,0:T(8,128)(2,1)}), bf16[16,144,256]{2,1,0:T(8,128)(2,1)}, u32[]{:S(2)}, u32[]{:S(2)}) async-start(bf16[16,144,256]{2,1,0:T(8,128)(2,1)} %get-tuple-element.12), calls=%async_computation.2 | async-start | bytes 2359296 | tf_op jit(solution)/shard_map/all_to_all | solution.py:27
  64.6 4.6 %collective-permute-start.7 = (bf16[256,2048]{1,0:T(8,128)(2,1)S(1)}, bf16[256,2048]{1,0:T(8,128)(2,1)S(1)}, u32[]{:S(2)}, u32[]{:S(2)}) collective-permute-start(bf16[256,2048]{1,0:T(8,128)(2,1)S(1)} %get-tuple-element.14), channel_id=1, source_target_pairs={{0,1},{1,0},{2,3},{3,2},{4,5},{5,4},{6,7},{7,6},{8,9},{9,8},{10,11... | collective-permute-start | bytes 3145736 | tf_op jit(solution)/shard_map/ppermute | solution.py:224
  70.7 26.0 %collective-permute-start.8 = (bf16[64,2048]{1,0:T(8,128)(2,1)S(1)}, bf16[64,2048]{1,0:T(8,128)(2,1)S(1)}, u32[]{:S(2)}, u32[]{:S(2)}) collective-permute-start(bf16[64,2048]{1,0:T(8,128)(2,1)S(1)} %get-tuple-element.16), channel_id=1, source_target_pairs={{0,4},{2,6},{4,0},{6,2},{1,5},{3,7},{5,1},{7,3},{8,12},{10,14},{12... | collective-permute-start | bytes 786440 | tf_op jit(solution)/shard_map/ppermute | solution.py:32
  73.2 23.5 %collective-permute-start.9 = (bf16[64,2048]{1,0:T(8,128)(2,1)S(1)}, bf16[64,2048]{1,0:T(8,128)(2,1)S(1)}, u32[]{:S(2)}, u32[]{:S(2)}) collective-permute-start(bf16[64,2048]{1,0:T(8,128)(2,1)S(1)} %get-tuple-element.17), channel_id=1, source_target_pairs={{0,6},{2,0},{4,2},{6,4},{1,7},{3,1},{5,3},{7,5},{8,14},{10,8},{12,... | collective-permute-start | bytes 786440 | tf_op jit(solution)/shard_map/ppermute | solution.py:32
  76.8 22.6 %collective-permute-start.10 = (bf16[64,2048]{1,0:T(8,128)(2,1)S(1)}, bf16[64,2048]{1,0:T(8,128)(2,1)S(1)}, u32[]{:S(2)}, u32[]{:S(2)}) collective-permute-start(bf16[64,2048]{1,0:T(8,128)(2,1)S(1)} %get-tuple-element.18), channel_id=1, source_target_pairs={{0,2},{2,4},{4,6},{6,0},{1,3},{3,5},{5,7},{7,1},{8,10},{10,12},{12... | collective-permute-start | bytes 786440 | tf_op jit(solution)/shard_map/ppermute | solution.py:32
  86.6 23.3 %all-to-all-start.3 = ((bf16[4,48,256]{2,1,0:T(8,128)(2,1)}), bf16[4,48,256]{2,1,0:T(8,128)(2,1)S(1)}, u32[]{:S(2)}, u32[]{:S(2)}) async-start(bf16[4,48,256]{2,1,0:T(8,128)(2,1)} %pad_maximum_fusion), calls=%async_computation.3 | async-start | bytes 196608 | tf_op jit(solution)/shard_map/all_to_all | solution.py:27

commit v15 on v14

--- a/solution.py
+++ b/solution.py
@@ -6,6 +6,7 @@
 from jax.sharding import Mesh, PartitionSpec as P
 
 TAPS = 7
+ORDER = (0, 2, 1, 3)
 VMEM_BYTES = 12 * 1024 * 1024
 PRODUCTS_VMEM = 49 * 1024 * 1024
 BF = jnp.bfloat16
@@ -38,7 +39,7 @@
     core, chip = lax.axis_index(C), lax.axis_index(ZL)
     copies = []
     for index, chunk in enumerate(chunks):
-        source = lax.rem(chip + index % chips, chips)
+        source = lax.rem(chip + ORDER[index % chips], chips)
         place = 2 * source + (core if index < chips else 1 - core)
         rows = pl.ds(pl.multiple_of(place * count, count), count)
         copies.append(pltpu.make_async_copy(chunk, slab_ref.at[rows, :], done.at[index]))
@@ -247,6 +248,7 @@
     heads = lax.dynamic_index_in_dim(gathered, (xy + 1) % nxy, 0, keepdims=False)[nz * rows :]
     following = jnp.where(xy == nxy - 1, heads[8:], heads[:8])
     following = jnp.where(zh * nxy + xy == ndp - 1, jnp.zeros((), BF), following).astype(F32)
+    direct = [direct[steps] for steps in ORDER]
     chunks = direct + [swap(value) for value in direct]
     slab = in_order(chunks)
     packed, for_other, ours = local_products(

time: 112 us -> 112 us (level)
  the two profiles are of different devices: /device:TPU:96 before, /device:TPU:8 now
where the time goes in v15:
time: 112 us; the launch traced here: 111 us
  starting transfers between devices  65.3 us (58%)
  waiting for transfers between devices  28.7 us (26%)
  Pallas kernels  10.7 us (10%)
  other arithmetic  3.57 us (3%)
  local copies, waits for them, and re-layouts  1.75 us (2%)
    all_to_all x4, starting transfers between devices, exchange(): return lax.all_to_all(value, axes, split_axis=0, concat_axis=0, tiled=True)  37.1 us
    all_to_all x4, waiting for transfers between devices, exchange(): return lax.all_to_all(value, axes, split_axis=0, concat_axis=0, tiled=True)  21.2 us
    ppermute x6, starting transfers between devices, from_ahead(): lax.ppermute(value, axis, [(source, (source - steps) % count) for source...  18.1 us
    ppermute x5, starting transfers between devices, swap(): return lax.ppermute(value, C, [(0, 1), (1, 0)])  10.1 us
    pallas_call x1, Pallas kernels, local_products(): pl.pallas_call(products_kernel, grid_spec=pltpu.PrefetchScalarGridSpec(nu...  6.35 us
    ppermute x5, waiting for transfers between devices, swap(): return lax.ppermute(value, C, [(0, 1), (1, 0)])  4.05 us
    ppermute x6, waiting for transfers between devices, from_ahead(): lax.ppermute(value, axis, [(source, (source - steps) % count) for source...  3.48 us
  transfers between devices with their start and end apart: 15, of which 8 were waited for; matrix products, arithmetic and copies ran while one was open for 4% of the time, Pallas kernels for 3%

profile of v15, /device:TPU:8, one launch (start us, length us, event | category | flops | bytes accessed | tf_op | source)
XLA Modules:
  0.0 110.9 jit_solution(16884514946919058747)
XLA Ops:
  2.0 15.1 %all-to-all-start = ((bf16[4,48,256]{2,1,0:T(8,128)(2,1)}), bf16[4,48,256]{2,1,0:T(8,128)(2,1)S(1)}, u32[]{:S(2)}, u32[]{:S(2)}) async-start(bf16[4,48,256]{2,1,0:T(8,128)(2,1)} %shard_map.68), calls=%async_computation | async-start | bytes 196608 | tf_op jit(solution)/shard_map/all_to_all | solution.py:28
  17.1 2.9 %collective-permute-start.2 = (bf16[64,2048]{1,0:T(8,128)(2,1)}, bf16[64,2048]{1,0:T(8,128)(2,1)S(1)}, u32[]{:S(2)}, u32[]{:S(2)}) collective-permute-start(bf16[64,2048]{1,0:T(8,128)(2,1)} %refs_0_.1), channel_id=1, source_target_pairs={{0,2},{2,4},{4,6},{6,0},{1,3},{3,5},{5,7},{7,1},{8,10},{10,12},{12... | collective-permute-start | bytes 786440 | tf_op jit(solution)/shard_map/ppermute | solution.py:33
  20.0 4.7 %collective-permute-start.1 = (bf16[64,2048]{1,0:T(8,128)(2,1)}, bf16[64,2048]{1,0:T(8,128)(2,1)S(1)}, u32[]{:S(2)}, u32[]{:S(2)}) collective-permute-start(bf16[64,2048]{1,0:T(8,128)(2,1)} %refs_0_.1), channel_id=1, source_target_pairs={{0,6},{2,0},{4,2},{6,4},{1,7},{3,1},{5,3},{7,5},{8,14},{10,8},{12,... | collective-permute-start | bytes 786440 | tf_op jit(solution)/shard_map/ppermute | solution.py:33
  24.7 1.9 %collective-permute-start = (bf16[64,2048]{1,0:T(8,128)(2,1)}, bf16[64,2048]{1,0:T(8,128)(2,1)S(1)}, u32[]{:S(2)}, u32[]{:S(2)}) collective-permute-start(bf16[64,2048]{1,0:T(8,128)(2,1)} %refs_0_.1), channel_id=1, source_target_pairs={{0,4},{2,6},{4,0},{6,2},{1,5},{3,7},{5,1},{7,3},{8,12},{10,14},{12... | collective-permute-start | bytes 786440 | tf_op jit(solution)/shard_map/ppermute | solution.py:33
  26.7 5.0 %all-to-all-done = bf16[4,48,256]{2,1,0:T(8,128)(2,1)S(1)} async-done(((bf16[4,48,256]{2,1,0:T(8,128)(2,1)}), bf16[4,48,256]{2,1,0:T(8,128)(2,1)S(1)}, u32[]{:S(2)}, u32[]{:S(2)}) %all-to-all-start) | async-done | bytes 98336 | tf_op jit(solution)/shard_map/all_to_all | solution.py:28
  32.8 7.5 %all-to-all-start.1 = ((bf16[16,144,256]{2,1,0:T(8,128)(2,1)}), bf16[16,144,256]{2,1,0:T(8,128)(2,1)S(1)}, u32[]{:S(2)}, u32[]{:S(2)}) async-start(bf16[16,144,256]{2,1,0:T(8,128)(2,1)} %broadcast_in_dim.8), calls=%async_computation.1 | async-start | bytes 2359296 | tf_op jit(solution)/shard_map/all_to_all | solution.py:28
  40.4 1.9 %collective-permute-start.3 = (bf16[64,2048]{1,0:T(8,128)(2,1)S(1)}, bf16[64,2048]{1,0:T(8,128)(2,1)S(1)}, u32[]{:S(2)}, u32[]{:S(2)}) collective-permute-start(bf16[64,2048]{1,0:T(8,128)(2,1)S(1)} %copy-done.1), channel_id=1, source_target_pairs={{0,1},{1,0},{2,3},{3,2},{4,5},{5,4},{6,7},{7,6},{8,9},{9,8},{10,11... | collective-permute-start | bytes 786440 | tf_op jit(solution)/shard_map/ppermute | solution.py:225
  42.3 2.4 %collective-permute-start.6 = (bf16[64,2048]{1,0:T(8,128)(2,1)S(1)}, bf16[64,2048]{1,0:T(8,128)(2,1)S(1)}, u32[]{:S(2)}, u32[]{:S(2)}) collective-permute-start(bf16[64,2048]{1,0:T(8,128)(2,1)S(1)} %collective-permute-done.2.refs_3_), channel_id=1, source_target_pairs={{0,1},{1,0},{2,3},{3,2},{4,5},{5,4},{6,7},{7,6},{8,9},{9,8},{10,11... | collective-permute-start | bytes 786440 | tf_op jit(solution)/shard_map/ppermute | solution.py:225
  44.7 1.9 %collective-permute-start.5 = (bf16[64,2048]{1,0:T(8,128)(2,1)S(1)}, bf16[64,2048]{1,0:T(8,128)(2,1)S(1)}, u32[]{:S(2)}, u32[]{:S(2)}) collective-permute-start(bf16[64,2048]{1,0:T(8,128)(2,1)S(1)} %collective-permute-done.1.refs_2_), channel_id=1, source_target_pairs={{0,1},{1,0},{2,3},{3,2},{4,5},{5,4},{6,7},{7,6},{8,9},{9,8},{10,11... | collective-permute-start | bytes 786440 | tf_op jit(solution)/shard_map/ppermute | solution.py:225
  46.6 1.7 %collective-permute-done.refs_1_ = bf16[64,2048]{1,0:T(8,128)(2,1)S(1)} collective-permute-done((bf16[64,2048]{1,0:T(8,128)(2,1)}, bf16[64,2048]{1,0:T(8,128)(2,1)S(1)}, u32[]{:S(2)}, u32[]{:S(2)}) %collective-permute-start) | collective-permute-done | bytes 262176 | tf_op jit(solution)/shard_map/ppermute | solution.py:33
  48.3 1.9 %collective-permute-start.4 = (bf16[64,2048]{1,0:T(8,128)(2,1)S(1)}, bf16[64,2048]{1,0:T(8,128)(2,1)S(1)}, u32[]{:S(2)}, u32[]{:S(2)}) collective-permute-start(bf16[64,2048]{1,0:T(8,128)(2,1)S(1)} %collective-permute-done.refs_1_), channel_id=1, source_target_pairs={{0,1},{1,0},{2,3},{3,2},{4,5},{5,4},{6,7},{7,6},{8,9},{9,8},{10,11... | collective-permute-start | bytes 786440 | tf_op jit(solution)/shard_map/ppermute | solution.py:225
  53.2 2.3 %all-to-all-done.1.weight_ref = bf16[16,144,256]{2,1,0:T(8,128)(2,1)S(1)} async-done(((bf16[16,144,256]{2,1,0:T(8,128)(2,1)}), bf16[16,144,256]{2,1,0:T(8,128)(2,1)S(1)}, u32[]{:S(2)}, u32[]{:S(2)}) %all-to-all-start.1) | async-done | bytes 1179680 | tf_op jit(solution)/shard_map/all_to_all | solution.py:28
  55.5 6.3 %shard_map.69 = (bf16[16,144,256]{2,1,0:T(8,128)(2,1)}, bf16[256,2048]{1,0:T(8,128)(2,1)S(1)}, bf16[256,256]{1,0:T(8,128)(2,1)S(1)}) custom-call(s32[1]{0:T(128)} %bitcast.core_ref, bf16[512,2048]{1,0:T(8,128)(2,1)} %shard_map.67.slab_ref, bf16[16,144,256]{2,1,0:T(8,128)(2,1)S(1)} %all-to-all-done.1.weight_ref, bf16[512,256]{1,0:T(8,128)(2,1)S(1)} %copy-done, ...), custom_call_target="tpu_custom_call" | custom-call | flops 1610612736 | bytes 6291456 | tf_op jit(solution)/shard_map/pallas_call | solution.py:126
  61.8 5.5 %all-to-all-start.2 = ((bf16[16,144,256]{2,1,0:T(8,128)(2,1)}), bf16[16,144,256]{2,1,0:T(8,128)(2,1)}, u32[]{:S(2)}, u32[]{:S(2)}) async-start(bf16[16,144,256]{2,1,0:T(8,128)(2,1)} %get-tuple-element.12), calls=%async_computation.2 | async-start | bytes 2359296 | tf_op jit(solution)/shard_map/all_to_all | solution.py:28
  67.3 1.9 %collective-permute-start.7 = (bf16[256,2048]{1,0:T(8,128)(2,1)S(1)}, bf16[256,2048]{1,0:T(8,128)(2,1)S(1)}, u32[]{:S(2)}, u32[]{:S(2)}) collective-permute-start(bf16[256,2048]{1,0:T(8,128)(2,1)S(1)} %get-tuple-element.14), channel_id=1, source_target_pairs={{0,1},{1,0},{2,3},{3,2},{4,5},{5,4},{6,7},{7,6},{8,9},{9,8},{10,11... | collective-permute-start | bytes 3145736 | tf_op jit(solution)/shard_map/ppermute | solution.py:225
  69.2 2.6 %collective-permute-done.7.other_ref = bf16[256,2048]{1,0:T(8,128)(2,1)S(1)} collective-permute-done((bf16[256,2048]{1,0:T(8,128)(2,1)S(1)}, bf16[256,2048]{1,0:T(8,128)(2,1)S(1)}, u32[]{:S(2)}, u32[]{:S(2)}) %collective-permute-start.7) | collective-permute-done | bytes 1048608 | tf_op jit(solution)/shard_map/ppermute | solution.py:225
  71.8 1.5 %shard_map.70 = (bf16[64,2048]{1,0:T(8,128)(2,1)S(1)}, bf16[64,2048]{1,0:T(8,128)(2,1)S(1)}, bf16[64,2048]{1,0:T(8,128)(2,1)S(1)}, bf16[64,2048]{1,0:T(8,128)(2,1)S(1)}) custom-call(bf16[256,256]{1,0:T(8,128)(2,1)S(1)} %get-tuple-element.13.ours_ref, bf16[16,144,256]{2,1,0:T(8,128)(2,1)S(1)} %all-to-all-done.1.weight_ref, ...), custom_call_target="tpu_custom_call" | custom-call | flops 268435456 | bytes 4194304 | tf_op jit(solution)/shard_map/pallas_call | solution.py:180
  73.4 2.7 %collective-permute-start.8 = (bf16[64,2048]{1,0:T(8,128)(2,1)S(1)}, bf16[64,2048]{1,0:T(8,128)(2,1)S(1)}, u32[]{:S(2)}, u32[]{:S(2)}) collective-permute-start(bf16[64,2048]{1,0:T(8,128)(2,1)S(1)} %get-tuple-element.16), channel_id=1, source_target_pairs={{0,4},{2,6},{4,0},{6,2},{1,5},{3,7},{5,1},{7,3},{8,12},{10,14},{12... | collective-permute-start | bytes 786440 | tf_op jit(solution)/shard_map/ppermute | solution.py:33
  76.1 3.8 %collective-permute-start.9 = (bf16[64,2048]{1,0:T(8,128)(2,1)S(1)}, bf16[64,2048]{1,0:T(8,128)(2,1)S(1)}, u32[]{:S(2)}, u32[]{:S(2)}) collective-permute-start(bf16[64,2048]{1,0:T(8,128)(2,1)S(1)} %get-tuple-element.17), channel_id=1, source_target_pairs={{0,6},{2,0},{4,2},{6,4},{1,7},{3,1},{5,3},{7,5},{8,14},{10,8},{12,... | collective-permute-start | bytes 786440 | tf_op jit(solution)/shard_map/ppermute | solution.py:33
  79.9 2.0 %collective-permute-start.10 = (bf16[64,2048]{1,0:T(8,128)(2,1)S(1)}, bf16[64,2048]{1,0:T(8,128)(2,1)S(1)}, u32[]{:S(2)}, u32[]{:S(2)}) collective-permute-start(bf16[64,2048]{1,0:T(8,128)(2,1)S(1)} %get-tuple-element.18), channel_id=1, source_target_pairs={{0,2},{2,4},{4,6},{6,0},{1,3},{3,5},{5,7},{7,1},{8,10},{10,12},{12... | collective-permute-start | bytes 786440 | tf_op jit(solution)/shard_map/ppermute | solution.py:33
  81.9 3.3 %all-to-all-done.2 = bf16[16,144,256]{2,1,0:T(8,128)(2,1)} async-done(((bf16[16,144,256]{2,1,0:T(8,128)(2,1)}), bf16[16,144,256]{2,1,0:T(8,128)(2,1)}, u32[]{:S(2)}, u32[]{:S(2)}) %all-to-all-start.2) | async-done | bytes 1179680 | tf_op jit(solution)/shard_map/all_to_all | solution.py:28
  87.4 9.0 %all-to-all-start.3 = ((bf16[4,48,256]{2,1,0:T(8,128)(2,1)}), bf16[4,48,256]{2,1,0:T(8,128)(2,1)S(1)}, u32[]{:S(2)}, u32[]{:S(2)}) async-start(bf16[4,48,256]{2,1,0:T(8,128)(2,1)} %pad_maximum_fusion), calls=%async_computation.3 | async-start | bytes 196608 | tf_op jit(solution)/shard_map/all_to_all | solution.py:28
  96.4 1.8 %collective-permute-done.9 = bf16[64,2048]{1,0:T(8,128)(2,1)S(1)} collective-permute-done((bf16[64,2048]{1,0:T(8,128)(2,1)S(1)}, bf16[64,2048]{1,0:T(8,128)(2,1)S(1)}, u32[]{:S(2)}, u32[]{:S(2)}) %collective-permute-start.9) | collective-permute-done | bytes 262176 | tf_op jit(solution)/shard_map/ppermute | solution.py:33
  99.1 10.6 %all-to-all-done.3 = bf16[4,48,256]{2,1,0:T(8,128)(2,1)S(1)} async-done(((bf16[4,48,256]{2,1,0:T(8,128)(2,1)}), bf16[4,48,256]{2,1,0:T(8,128)(2,1)S(1)}, u32[]{:S(2)}, u32[]{:S(2)}) %all-to-all-start.3) | async-done | bytes 98336 | tf_op jit(solution)/shard_map/all_to_all | solution.py:28
  (32 shorter events, 9.5 us)
Async XLA Ops:
  2.0 29.7 %all-to-all-start = ((bf16[4,48,256]{2,1,0:T(8,128)(2,1)}), bf16[4,48,256]{2,1,0:T(8,128)(2,1)S(1)}, u32[]{:S(2)}, u32[]{:S(2)}) async-start(bf16[4,48,256]{2,1,0:T(8,128)(2,1)} %shard_map.68), calls=%async_computation | async-start | bytes 196608 | tf_op jit(solution)/shard_map/all_to_all | solution.py:28
  17.1 25.2 %collective-permute-start.2 = (bf16[64,2048]{1,0:T(8,128)(2,1)}, bf16[64,2048]{1,0:T(8,128)(2,1)S(1)}, u32[]{:S(2)}, u32[]{:S(2)}) collective-permute-start(bf16[64,2048]{1,0:T(8,128)(2,1)} %refs_0_.1), channel_id=1, source_target_pairs={{0,2},{2,4},{4,6},{6,0},{1,3},{3,5},{5,7},{7,1},{8,10},{10,12},{12... | collective-permute-start | bytes 786440 | tf_op jit(solution)/shard_map/ppermute | solution.py:33
  20.0 24.7 %collective-permute-start.1 = (bf16[64,2048]{1,0:T(8,128)(2,1)}, bf16[64,2048]{1,0:T(8,128)(2,1)S(1)}, u32[]{:S(2)}, u32[]{:S(2)}) collective-permute-start(bf16[64,2048]{1,0:T(8,128)(2,1)} %refs_0_.1), channel_id=1, source_target_pairs={{0,6},{2,0},{4,2},{6,4},{1,7},{3,1},{5,3},{7,5},{8,14},{10,8},{12,... | collective-permute-start | bytes 786440 | tf_op jit(solution)/shard_map/ppermute | solution.py:33
  24.7 23.6 %collective-permute-start = (bf16[64,2048]{1,0:T(8,128)(2,1)}, bf16[64,2048]{1,0:T(8,128)(2,1)S(1)}, u32[]{:S(2)}, u32[]{:S(2)}) collective-permute-start(bf16[64,2048]{1,0:T(8,128)(2,1)} %refs_0_.1), channel_id=1, source_target_pairs={{0,4},{2,6},{4,0},{6,2},{1,5},{3,7},{5,1},{7,3},{8,12},{10,14},{12... | collective-permute-start | bytes 786440 | tf_op jit(solution)/shard_map/ppermute | solution.py:33
  32.8 7.5 %copy-start.1 = (bf16[64,2048]{1,0:T(8,128)(2,1)S(1)}, bf16[64,2048]{1,0:T(8,128)(2,1)}, u32[]{:S(2)}) copy-start(bf16[64,2048]{1,0:T(8,128)(2,1)} %refs_0_.1) | copy-start | bytes 786436
  32.8 22.6 %all-to-all-start.1 = ((bf16[16,144,256]{2,1,0:T(8,128)(2,1)}), bf16[16,144,256]{2,1,0:T(8,128)(2,1)S(1)}, u32[]{:S(2)}, u32[]{:S(2)}) async-start(bf16[16,144,256]{2,1,0:T(8,128)(2,1)} %broadcast_in_dim.8), calls=%async_computation.1 | async-start | bytes 2359296 | tf_op jit(solution)/shard_map/all_to_all | solution.py:28
  40.4 9.9 %collective-permute-start.3 = (bf16[64,2048]{1,0:T(8,128)(2,1)S(1)}, bf16[64,2048]{1,0:T(8,128)(2,1)S(1)}, u32[]{:S(2)}, u32[]{:S(2)}) collective-permute-start(bf16[64,2048]{1,0:T(8,128)(2,1)S(1)} %copy-done.1), channel_id=1, source_target_pairs={{0,1},{1,0},{2,3},{3,2},{4,5},{5,4},{6,7},{7,6},{8,9},{9,8},{10,11... | collective-permute-start | bytes 786440 | tf_op jit(solution)/shard_map/ppermute | solution.py:225
  42.3 8.0 %collective-permute-start.6 = (bf16[64,2048]{1,0:T(8,128)(2,1)S(1)}, bf16[64,2048]{1,0:T(8,128)(2,1)S(1)}, u32[]{:S(2)}, u32[]{:S(2)}) collective-permute-start(bf16[64,2048]{1,0:T(8,128)(2,1)S(1)} %collective-permute-done.2.refs_3_), channel_id=1, source_target_pairs={{0,1},{1,0},{2,3},{3,2},{4,5},{5,4},{6,7},{7,6},{8,9},{9,8},{10,11... | collective-permute-start | bytes 786440 | tf_op jit(solution)/shard_map/ppermute | solution.py:225
  44.7 5.6 %collective-permute-start.5 = (bf16[64,2048]{1,0:T(8,128)(2,1)S(1)}, bf16[64,2048]{1,0:T(8,128)(2,1)S(1)}, u32[]{:S(2)}, u32[]{:S(2)}) collective-permute-start(bf16[64,2048]{1,0:T(8,128)(2,1)S(1)} %collective-permute-done.1.refs_2_), channel_id=1, source_target_pairs={{0,1},{1,0},{2,3},{3,2},{4,5},{5,4},{6,7},{7,6},{8,9},{9,8},{10,11... | collective-permute-start | bytes 786440 | tf_op jit(solution)/shard_map/ppermute | solution.py:225
  48.3 3.4 %collective-permute-start.4 = (bf16[64,2048]{1,0:T(8,128)(2,1)S(1)}, bf16[64,2048]{1,0:T(8,128)(2,1)S(1)}, u32[]{:S(2)}, u32[]{:S(2)}) collective-permute-start(bf16[64,2048]{1,0:T(8,128)(2,1)S(1)} %collective-permute-done.refs_1_), channel_id=1, source_target_pairs={{0,1},{1,0},{2,3},{3,2},{4,5},{5,4},{6,7},{7,6},{8,9},{9,8},{10,11... | collective-permute-start | bytes 786440 | tf_op jit(solution)/shard_map/ppermute | solution.py:225
  50.3 5.2 %copy-start = (bf16[512,256]{1,0:T(8,128)(2,1)S(1)}, bf16[512,256]{1,0:T(8,128)(2,1)}, u32[]{:S(2)}) copy-start(bf16[512,256]{1,0:T(8,128)(2,1)} %cotangent_ref.1) | copy-start | bytes 786436
  50.3 5.2 %copy-start.2 = (f32[7,256]{1,0:T(8,128)S(1)}, f32[7,256]{1,0:T(8,128)}, u32[]{:S(2)}) copy-start(f32[7,256]{1,0:T(8,128)} %filters_ref.1) | copy-start | bytes 21508
  61.8 23.5 %all-to-all-start.2 = ((bf16[16,144,256]{2,1,0:T(8,128)(2,1)}), bf16[16,144,256]{2,1,0:T(8,128)(2,1)}, u32[]{:S(2)}, u32[]{:S(2)}) async-start(bf16[16,144,256]{2,1,0:T(8,128)(2,1)} %get-tuple-element.12), calls=%async_computation.2 | async-start | bytes 2359296 | tf_op jit(solution)/shard_map/all_to_all | solution.py:28
  67.3 4.5 %collective-permute-start.7 = (bf16[256,2048]{1,0:T(8,128)(2,1)S(1)}, bf16[256,2048]{1,0:T(8,128)(2,1)S(1)}, u32[]{:S(2)}, u32[]{:S(2)}) collective-permute-start(bf16[256,2048]{1,0:T(8,128)(2,1)S(1)} %get-tuple-element.14), channel_id=1, source_target_pairs={{0,1},{1,0},{2,3},{3,2},{4,5},{5,4},{6,7},{7,6},{8,9},{9,8},{10,11... | collective-permute-start | bytes 3145736 | tf_op jit(solution)/shard_map/ppermute | solution.py:225
  73.4 23.1 %collective-permute-start.8 = (bf16[64,2048]{1,0:T(8,128)(2,1)S(1)}, bf16[64,2048]{1,0:T(8,128)(2,1)S(1)}, u32[]{:S(2)}, u32[]{:S(2)}) collective-permute-start(bf16[64,2048]{1,0:T(8,128)(2,1)S(1)} %get-tuple-element.16), channel_id=1, source_target_pairs={{0,4},{2,6},{4,0},{6,2},{1,5},{3,7},{5,1},{7,3},{8,12},{10,14},{12... | collective-permute-start | bytes 786440 | tf_op jit(solution)/shard_map/ppermute | solution.py:33
  76.1 22.2 %collective-permute-start.9 = (bf16[64,2048]{1,0:T(8,128)(2,1)S(1)}, bf16[64,2048]{1,0:T(8,128)(2,1)S(1)}, u32[]{:S(2)}, u32[]{:S(2)}) collective-permute-start(bf16[64,2048]{1,0:T(8,128)(2,1)S(1)} %get-tuple-element.17), channel_id=1, source_target_pairs={{0,6},{2,0},{4,2},{6,4},{1,7},{3,1},{5,3},{7,5},{8,14},{10,8},{12,... | collective-permute-start | bytes 786440 | tf_op jit(solution)/shard_map/ppermute | solution.py:33
  79.9 18.3 %collective-permute-start.10 = (bf16[64,2048]{1,0:T(8,128)(2,1)S(1)}, bf16[64,2048]{1,0:T(8,128)(2,1)S(1)}, u32[]{:S(2)}, u32[]{:S(2)}) collective-permute-start(bf16[64,2048]{1,0:T(8,128)(2,1)S(1)} %get-tuple-element.18), channel_id=1, source_target_pairs={{0,2},{2,4},{4,6},{6,0},{1,3},{3,5},{5,7},{7,1},{8,10},{10,12},{12... | collective-permute-start | bytes 786440 | tf_op jit(solution)/shard_map/ppermute | solution.py:33
  87.4 22.2 %all-to-all-start.3 = ((bf16[4,48,256]{2,1,0:T(8,128)(2,1)}), bf16[4,48,256]{2,1,0:T(8,128)(2,1)S(1)}, u32[]{:S(2)}, u32[]{:S(2)}) async-start(bf16[4,48,256]{2,1,0:T(8,128)(2,1)} %pad_maximum_fusion), calls=%async_computation.3 | async-start | bytes 196608 | tf_op jit(solution)/shard_map/all_to_all | solution.py:28

commit v16 on v15

--- a/solution.py
+++ b/solution.py
@@ -58,7 +58,7 @@
         scratch_shapes=[pltpu.SemaphoreType.DMA((len(chunks),))],
         compiler_params=pltpu.CompilerParams(vmem_limit_bytes=VMEM_BYTES),
         cost_estimate=pl.CostEstimate(
-            flops=8 * 10**9, bytes_accessed=4 * len(chunks) * count * depth, transcendentals=0
+            flops=6 * 10**9, bytes_accessed=4 * len(chunks) * count * depth, transcendentals=0
         ),
     )(*chunks)
 

time: 112 us -> 124 us (1.11)
  waiting for transfers between devices: 28.7 us -> 45.3 us
  starting transfers between devices: 65.3 us -> 60.5 us
    ppermute x6, waiting for transfers between devices: 3.48 us -> 18.6 us  [from_ahead(): lax.ppermute(value, axis, [(source, (source - steps) % count) for source...]
    all_to_all x4, starting transfers between devices: 37.1 us -> 33.1 us  [exchange(): return lax.all_to_all(value, axes, split_axis=0, concat_axis=0, tiled=True)]
    all_to_all x4, waiting for transfers between devices: 21.2 us -> 22.7 us  [exchange(): return lax.all_to_all(value, axes, split_axis=0, concat_axis=0, tiled=True)]
  transfers between devices with their start and end apart: 15 -> 15, of which waited for: 8 -> 8; matrix products, arithmetic and copies ran while one was open for 4% -> 2% of each run, Pallas kernels for 3% -> 2%
where the time goes in v16:
time: 124 us; the launch traced here: 123 us
  starting transfers between devices  60.5 us (49%)
  waiting for transfers between devices  45.3 us (37%)
  Pallas kernels  10.7 us (9%)
  other arithmetic  3.58 us (3%)
  local copies, waits for them, and re-layouts  1.75 us (1%)
    all_to_all x4, starting transfers between devices, exchange(): return lax.all_to_all(value, axes, split_axis=0, concat_axis=0, tiled=True)  33.1 us
    all_to_all x4, waiting for transfers between devices, exchange(): return lax.all_to_all(value, axes, split_axis=0, concat_axis=0, tiled=True)  22.7 us
    ppermute x6, waiting for transfers between devices, from_ahead(): lax.ppermute(value, axis, [(source, (source - steps) % count) for source...  18.6 us
    ppermute x6, starting transfers between devices, from_ahead(): lax.ppermute(value, axis, [(source, (source - steps) % count) for source...  17.3 us
    ppermute x5, starting transfers between devices, swap(): return lax.ppermute(value, C, [(0, 1), (1, 0)])  10.1 us
    pallas_call x1, Pallas kernels, local_products(): pl.pallas_call(products_kernel, grid_spec=pltpu.PrefetchScalarGridSpec(nu...  6.35 us
    ppermute x5, waiting for transfers between devices, swap(): return lax.ppermute(value, C, [(0, 1), (1, 0)])  4.05 us
  transfers between devices with their start and end apart: 15, of which 8 were waited for; matrix products, arithmetic and copies ran while one was open for 2% of the time, Pallas kernels for 2%

profile of v16, /device:TPU:8, one launch (start us, length us, event | category | flops | bytes accessed | tf_op | source)
XLA Modules:
  0.0 122.7 jit_solution(17464049848764841351)
XLA Ops:
  2.0 15.1 %all-to-all-start = ((bf16[4,48,256]{2,1,0:T(8,128)(2,1)}), bf16[4,48,256]{2,1,0:T(8,128)(2,1)S(1)}, u32[]{:S(2)}, u32[]{:S(2)}) async-start(bf16[4,48,256]{2,1,0:T(8,128)(2,1)} %shard_map.68), calls=%async_computation | async-start | bytes 196608 | tf_op jit(solution)/shard_map/all_to_all | solution.py:28
  17.1 14.4 %all-to-all-done = bf16[4,48,256]{2,1,0:T(8,128)(2,1)S(1)} async-done(((bf16[4,48,256]{2,1,0:T(8,128)(2,1)}), bf16[4,48,256]{2,1,0:T(8,128)(2,1)S(1)}, u32[]{:S(2)}, u32[]{:S(2)}) %all-to-all-start) | async-done | bytes 98336 | tf_op jit(solution)/shard_map/all_to_all | solution.py:28
  32.6 7.5 %all-to-all-start.1 = ((bf16[16,144,256]{2,1,0:T(8,128)(2,1)}), bf16[16,144,256]{2,1,0:T(8,128)(2,1)S(1)}, u32[]{:S(2)}, u32[]{:S(2)}) async-start(bf16[16,144,256]{2,1,0:T(8,128)(2,1)} %broadcast_in_dim.8), calls=%async_computation.1 | async-start | bytes 2359296 | tf_op jit(solution)/shard_map/all_to_all | solution.py:28
  40.2 2.2 %collective-permute-start.2 = (bf16[64,2048]{1,0:T(8,128)(2,1)S(1)}, bf16[64,2048]{1,0:T(8,128)(2,1)S(1)}, u32[]{:S(2)}, u32[]{:S(2)}) collective-permute-start(bf16[64,2048]{1,0:T(8,128)(2,1)S(1)} %copy-done.1), channel_id=1, source_target_pairs={{0,2},{2,4},{4,6},{6,0},{1,3},{3,5},{5,7},{7,1},{8,10},{10,12},{12... | collective-permute-start | bytes 786440 | tf_op jit(solution)/shard_map/ppermute | solution.py:33
  42.3 5.5 %collective-permute-start.1 = (bf16[64,2048]{1,0:T(8,128)(2,1)S(1)}, bf16[64,2048]{1,0:T(8,128)(2,1)S(1)}, u32[]{:S(2)}, u32[]{:S(2)}) collective-permute-start(bf16[64,2048]{1,0:T(8,128)(2,1)S(1)} %copy-done.1), channel_id=1, source_target_pairs={{0,6},{2,0},{4,2},{6,4},{1,7},{3,1},{5,3},{7,5},{8,14},{10,8},{12,... | collective-permute-start | bytes 786440 | tf_op jit(solution)/shard_map/ppermute | solution.py:33
  47.8 1.9 %collective-permute-start = (bf16[64,2048]{1,0:T(8,128)(2,1)S(1)}, bf16[64,2048]{1,0:T(8,128)(2,1)S(1)}, u32[]{:S(2)}, u32[]{:S(2)}) collective-permute-start(bf16[64,2048]{1,0:T(8,128)(2,1)S(1)} %copy-done.1), channel_id=1, source_target_pairs={{0,4},{2,6},{4,0},{6,2},{1,5},{3,7},{5,1},{7,3},{8,12},{10,14},{12... | collective-permute-start | bytes 786440 | tf_op jit(solution)/shard_map/ppermute | solution.py:33
  49.7 1.9 %collective-permute-start.3 = (bf16[64,2048]{1,0:T(8,128)(2,1)S(1)}, bf16[64,2048]{1,0:T(8,128)(2,1)S(1)}, u32[]{:S(2)}, u32[]{:S(2)}) collective-permute-start(bf16[64,2048]{1,0:T(8,128)(2,1)S(1)} %copy-done.1), channel_id=1, source_target_pairs={{0,1},{1,0},{2,3},{3,2},{4,5},{5,4},{6,7},{7,6},{8,9},{9,8},{10,11... | collective-permute-start | bytes 786440 | tf_op jit(solution)/shard_map/ppermute | solution.py:225
  51.7 1.5 %collective-permute-done.2.refs_3_ = bf16[64,2048]{1,0:T(8,128)(2,1)S(1)} collective-permute-done((bf16[64,2048]{1,0:T(8,128)(2,1)S(1)}, bf16[64,2048]{1,0:T(8,128)(2,1)S(1)}, u32[]{:S(2)}, u32[]{:S(2)}) %collective-permute-start.2) | collective-permute-done | bytes 262176 | tf_op jit(solution)/shard_map/ppermute | solution.py:33
  53.2 1.9 %collective-permute-start.6 = (bf16[64,2048]{1,0:T(8,128)(2,1)S(1)}, bf16[64,2048]{1,0:T(8,128)(2,1)S(1)}, u32[]{:S(2)}, u32[]{:S(2)}) collective-permute-start(bf16[64,2048]{1,0:T(8,128)(2,1)S(1)} %collective-permute-done.2.refs_3_), channel_id=1, source_target_pairs={{0,1},{1,0},{2,3},{3,2},{4,5},{5,4},{6,7},{7,6},{8,9},{9,8},{10,11... | collective-permute-start | bytes 786440 | tf_op jit(solution)/shard_map/ppermute | solution.py:225
  55.1 2.4 %collective-permute-start.5 = (bf16[64,2048]{1,0:T(8,128)(2,1)S(1)}, bf16[64,2048]{1,0:T(8,128)(2,1)S(1)}, u32[]{:S(2)}, u32[]{:S(2)}) collective-permute-start(bf16[64,2048]{1,0:T(8,128)(2,1)S(1)} %collective-permute-done.1.refs_2_), channel_id=1, source_target_pairs={{0,1},{1,0},{2,3},{3,2},{4,5},{5,4},{6,7},{7,6},{8,9},{9,8},{10,11... | collective-permute-start | bytes 786440 | tf_op jit(solution)/shard_map/ppermute | solution.py:225
  57.5 8.6 %collective-permute-done.refs_1_ = bf16[64,2048]{1,0:T(8,128)(2,1)S(1)} collective-permute-done((bf16[64,2048]{1,0:T(8,128)(2,1)S(1)}, bf16[64,2048]{1,0:T(8,128)(2,1)S(1)}, u32[]{:S(2)}, u32[]{:S(2)}) %collective-permute-start) | collective-permute-done | bytes 262176 | tf_op jit(solution)/shard_map/ppermute | solution.py:33
  66.1 1.9 %collective-permute-start.4 = (bf16[64,2048]{1,0:T(8,128)(2,1)S(1)}, bf16[64,2048]{1,0:T(8,128)(2,1)S(1)}, u32[]{:S(2)}, u32[]{:S(2)}) collective-permute-start(bf16[64,2048]{1,0:T(8,128)(2,1)S(1)} %collective-permute-done.refs_1_), channel_id=1, source_target_pairs={{0,1},{1,0},{2,3},{3,2},{4,5},{5,4},{6,7},{7,6},{8,9},{9,8},{10,11... | collective-permute-start | bytes 786440 | tf_op jit(solution)/shard_map/ppermute | solution.py:225
  71.0 6.3 %shard_map.69 = (bf16[16,144,256]{2,1,0:T(8,128)(2,1)}, bf16[256,2048]{1,0:T(8,128)(2,1)S(1)}, bf16[256,256]{1,0:T(8,128)(2,1)S(1)}) custom-call(s32[1]{0:T(128)} %bitcast.core_ref, bf16[512,2048]{1,0:T(8,128)(2,1)} %shard_map.67.slab_ref, bf16[16,144,256]{2,1,0:T(8,128)(2,1)S(1)} %all-to-all-done.1.weight_ref, bf16[512,256]{1,0:T(8,128)(2,1)S(1)} %copy-done, ...), custom_call_target="tpu_custom_call" | custom-call | flops 1610612736 | bytes 6291456 | tf_op jit(solution)/shard_map/pallas_call | solution.py:126
  77.3 7.2 %all-to-all-start.2 = ((bf16[16,144,256]{2,1,0:T(8,128)(2,1)}), bf16[16,144,256]{2,1,0:T(8,128)(2,1)}, u32[]{:S(2)}, u32[]{:S(2)}) async-start(bf16[16,144,256]{2,1,0:T(8,128)(2,1)} %get-tuple-element.12), calls=%async_computation.2 | async-start | bytes 2359296 | tf_op jit(solution)/shard_map/all_to_all | solution.py:28
  84.5 1.9 %collective-permute-start.7 = (bf16[256,2048]{1,0:T(8,128)(2,1)S(1)}, bf16[256,2048]{1,0:T(8,128)(2,1)S(1)}, u32[]{:S(2)}, u32[]{:S(2)}) collective-permute-start(bf16[256,2048]{1,0:T(8,128)(2,1)S(1)} %get-tuple-element.14), channel_id=1, source_target_pairs={{0,1},{1,0},{2,3},{3,2},{4,5},{5,4},{6,7},{7,6},{8,9},{9,8},{10,11... | collective-permute-start | bytes 3145736 | tf_op jit(solution)/shard_map/ppermute | solution.py:225
  86.5 2.6 %collective-permute-done.7.other_ref = bf16[256,2048]{1,0:T(8,128)(2,1)S(1)} collective-permute-done((bf16[256,2048]{1,0:T(8,128)(2,1)S(1)}, bf16[256,2048]{1,0:T(8,128)(2,1)S(1)}, u32[]{:S(2)}, u32[]{:S(2)}) %collective-permute-start.7) | collective-permute-done | bytes 1048608 | tf_op jit(solution)/shard_map/ppermute | solution.py:225
  89.1 1.5 %shard_map.70 = (bf16[64,2048]{1,0:T(8,128)(2,1)S(1)}, bf16[64,2048]{1,0:T(8,128)(2,1)S(1)}, bf16[64,2048]{1,0:T(8,128)(2,1)S(1)}, bf16[64,2048]{1,0:T(8,128)(2,1)S(1)}) custom-call(bf16[256,256]{1,0:T(8,128)(2,1)S(1)} %get-tuple-element.13.ours_ref, bf16[16,144,256]{2,1,0:T(8,128)(2,1)S(1)} %all-to-all-done.1.weight_ref, ...), custom_call_target="tpu_custom_call" | custom-call | flops 268435456 | bytes 4194304 | tf_op jit(solution)/shard_map/pallas_call | solution.py:180
  90.6 1.9 %collective-permute-start.8 = (bf16[64,2048]{1,0:T(8,128)(2,1)S(1)}, bf16[64,2048]{1,0:T(8,128)(2,1)S(1)}, u32[]{:S(2)}, u32[]{:S(2)}) collective-permute-start(bf16[64,2048]{1,0:T(8,128)(2,1)S(1)} %get-tuple-element.16), channel_id=1, source_target_pairs={{0,4},{2,6},{4,0},{6,2},{1,5},{3,7},{5,1},{7,3},{8,12},{10,14},{12... | collective-permute-start | bytes 786440 | tf_op jit(solution)/shard_map/ppermute | solution.py:33
  92.6 2.8 %collective-permute-start.9 = (bf16[64,2048]{1,0:T(8,128)(2,1)S(1)}, bf16[64,2048]{1,0:T(8,128)(2,1)S(1)}, u32[]{:S(2)}, u32[]{:S(2)}) collective-permute-start(bf16[64,2048]{1,0:T(8,128)(2,1)S(1)} %get-tuple-element.17), channel_id=1, source_target_pairs={{0,6},{2,0},{4,2},{6,4},{1,7},{3,1},{5,3},{7,5},{8,14},{10,8},{12,... | collective-permute-start | bytes 786440 | tf_op jit(solution)/shard_map/ppermute | solution.py:33
  95.3 3.1 %collective-permute-start.10 = (bf16[64,2048]{1,0:T(8,128)(2,1)S(1)}, bf16[64,2048]{1,0:T(8,128)(2,1)S(1)}, u32[]{:S(2)}, u32[]{:S(2)}) collective-permute-start(bf16[64,2048]{1,0:T(8,128)(2,1)S(1)} %get-tuple-element.18), channel_id=1, source_target_pairs={{0,2},{2,4},{4,6},{6,0},{1,3},{3,5},{5,7},{7,1},{8,10},{10,12},{12... | collective-permute-start | bytes 786440 | tf_op jit(solution)/shard_map/ppermute | solution.py:33
  98.4 4.5 %all-to-all-done.2 = bf16[16,144,256]{2,1,0:T(8,128)(2,1)} async-done(((bf16[16,144,256]{2,1,0:T(8,128)(2,1)}), bf16[16,144,256]{2,1,0:T(8,128)(2,1)}, u32[]{:S(2)}, u32[]{:S(2)}) %all-to-all-start.2) | async-done | bytes 1179680 | tf_op jit(solution)/shard_map/all_to_all | solution.py:28
  105.0 3.3 %all-to-all-start.3 = ((bf16[4,48,256]{2,1,0:T(8,128)(2,1)}), bf16[4,48,256]{2,1,0:T(8,128)(2,1)S(1)}, u32[]{:S(2)}, u32[]{:S(2)}) async-start(bf16[4,48,256]{2,1,0:T(8,128)(2,1)} %pad_maximum_fusion), calls=%async_computation.3 | async-start | bytes 196608 | tf_op jit(solution)/shard_map/all_to_all | solution.py:28
  108.4 8.5 %collective-permute-done.9 = bf16[64,2048]{1,0:T(8,128)(2,1)S(1)} collective-permute-done((bf16[64,2048]{1,0:T(8,128)(2,1)S(1)}, bf16[64,2048]{1,0:T(8,128)(2,1)S(1)}, u32[]{:S(2)}, u32[]{:S(2)}) %collective-permute-start.9) | collective-permute-done | bytes 262176 | tf_op jit(solution)/shard_map/ppermute | solution.py:33
  117.7 3.8 %all-to-all-done.3 = bf16[4,48,256]{2,1,0:T(8,128)(2,1)S(1)} async-done(((bf16[4,48,256]{2,1,0:T(8,128)(2,1)}), bf16[4,48,256]{2,1,0:T(8,128)(2,1)S(1)}, u32[]{:S(2)}, u32[]{:S(2)}) %all-to-all-start.3) | async-done | bytes 98336 | tf_op jit(solution)/shard_map/all_to_all | solution.py:28
  (32 shorter events, 9.5 us)
Async XLA Ops:
  2.0 29.5 %all-to-all-start = ((bf16[4,48,256]{2,1,0:T(8,128)(2,1)}), bf16[4,48,256]{2,1,0:T(8,128)(2,1)S(1)}, u32[]{:S(2)}, u32[]{:S(2)}) async-start(bf16[4,48,256]{2,1,0:T(8,128)(2,1)} %shard_map.68), calls=%async_computation | async-start | bytes 196608 | tf_op jit(solution)/shard_map/all_to_all | solution.py:28
  32.6 7.5 %copy-start.1 = (bf16[64,2048]{1,0:T(8,128)(2,1)S(1)}, bf16[64,2048]{1,0:T(8,128)(2,1)}, u32[]{:S(2)}) copy-start(bf16[64,2048]{1,0:T(8,128)(2,1)} %refs_0_.1) | copy-start | bytes 786436
  32.6 38.3 %all-to-all-start.1 = ((bf16[16,144,256]{2,1,0:T(8,128)(2,1)}), bf16[16,144,256]{2,1,0:T(8,128)(2,1)S(1)}, u32[]{:S(2)}, u32[]{:S(2)}) async-start(bf16[16,144,256]{2,1,0:T(8,128)(2,1)} %broadcast_in_dim.8), calls=%async_computation.1 | async-start | bytes 2359296 | tf_op jit(solution)/shard_map/all_to_all | solution.py:28
  40.2 13.0 %collective-permute-start.2 = (bf16[64,2048]{1,0:T(8,128)(2,1)S(1)}, bf16[64,2048]{1,0:T(8,128)(2,1)S(1)}, u32[]{:S(2)}, u32[]{:S(2)}) collective-permute-start(bf16[64,2048]{1,0:T(8,128)(2,1)S(1)} %copy-done.1), channel_id=1, source_target_pairs={{0,2},{2,4},{4,6},{6,0},{1,3},{3,5},{5,7},{7,1},{8,10},{10,12},{12... | collective-permute-start | bytes 786440 | tf_op jit(solution)/shard_map/ppermute | solution.py:33
  42.3 12.8 %collective-permute-start.1 = (bf16[64,2048]{1,0:T(8,128)(2,1)S(1)}, bf16[64,2048]{1,0:T(8,128)(2,1)S(1)}, u32[]{:S(2)}, u32[]{:S(2)}) collective-permute-start(bf16[64,2048]{1,0:T(8,128)(2,1)S(1)} %copy-done.1), channel_id=1, source_target_pairs={{0,6},{2,0},{4,2},{6,4},{1,7},{3,1},{5,3},{7,5},{8,14},{10,8},{12,... | collective-permute-start | bytes 786440 | tf_op jit(solution)/shard_map/ppermute | solution.py:33
  47.8 18.3 %collective-permute-start = (bf16[64,2048]{1,0:T(8,128)(2,1)S(1)}, bf16[64,2048]{1,0:T(8,128)(2,1)S(1)}, u32[]{:S(2)}, u32[]{:S(2)}) collective-permute-start(bf16[64,2048]{1,0:T(8,128)(2,1)S(1)} %copy-done.1), channel_id=1, source_target_pairs={{0,4},{2,6},{4,0},{6,2},{1,5},{3,7},{5,1},{7,3},{8,12},{10,14},{12... | collective-permute-start | bytes 786440 | tf_op jit(solution)/shard_map/ppermute | solution.py:33
  49.7 18.3 %collective-permute-start.3 = (bf16[64,2048]{1,0:T(8,128)(2,1)S(1)}, bf16[64,2048]{1,0:T(8,128)(2,1)S(1)}, u32[]{:S(2)}, u32[]{:S(2)}) collective-permute-start(bf16[64,2048]{1,0:T(8,128)(2,1)S(1)} %copy-done.1), channel_id=1, source_target_pairs={{0,1},{1,0},{2,3},{3,2},{4,5},{5,4},{6,7},{7,6},{8,9},{9,8},{10,11... | collective-permute-start | bytes 786440 | tf_op jit(solution)/shard_map/ppermute | solution.py:225
  53.2 14.9 %collective-permute-start.6 = (bf16[64,2048]{1,0:T(8,128)(2,1)S(1)}, bf16[64,2048]{1,0:T(8,128)(2,1)S(1)}, u32[]{:S(2)}, u32[]{:S(2)}) collective-permute-start(bf16[64,2048]{1,0:T(8,128)(2,1)S(1)} %collective-permute-done.2.refs_3_), channel_id=1, source_target_pairs={{0,1},{1,0},{2,3},{3,2},{4,5},{5,4},{6,7},{7,6},{8,9},{9,8},{10,11... | collective-permute-start | bytes 786440 | tf_op jit(solution)/shard_map/ppermute | solution.py:225
  55.1 13.0 %collective-permute-start.5 = (bf16[64,2048]{1,0:T(8,128)(2,1)S(1)}, bf16[64,2048]{1,0:T(8,128)(2,1)S(1)}, u32[]{:S(2)}, u32[]{:S(2)}) collective-permute-start(bf16[64,2048]{1,0:T(8,128)(2,1)S(1)} %collective-permute-done.1.refs_2_), channel_id=1, source_target_pairs={{0,1},{1,0},{2,3},{3,2},{4,5},{5,4},{6,7},{7,6},{8,9},{9,8},{10,11... | collective-permute-start | bytes 786440 | tf_op jit(solution)/shard_map/ppermute | solution.py:225
  66.1 3.4 %collective-permute-start.4 = (bf16[64,2048]{1,0:T(8,128)(2,1)S(1)}, bf16[64,2048]{1,0:T(8,128)(2,1)S(1)}, u32[]{:S(2)}, u32[]{:S(2)}) collective-permute-start(bf16[64,2048]{1,0:T(8,128)(2,1)S(1)} %collective-permute-done.refs_1_), channel_id=1, source_target_pairs={{0,1},{1,0},{2,3},{3,2},{4,5},{5,4},{6,7},{7,6},{8,9},{9,8},{10,11... | collective-permute-start | bytes 786440 | tf_op jit(solution)/shard_map/ppermute | solution.py:225
  68.0 2.9 %copy-start = (bf16[512,256]{1,0:T(8,128)(2,1)S(1)}, bf16[512,256]{1,0:T(8,128)(2,1)}, u32[]{:S(2)}) copy-start(bf16[512,256]{1,0:T(8,128)(2,1)} %cotangent_ref.1) | copy-start | bytes 786436
  68.0 2.9 %copy-start.2 = (f32[7,256]{1,0:T(8,128)S(1)}, f32[7,256]{1,0:T(8,128)}, u32[]{:S(2)}) copy-start(f32[7,256]{1,0:T(8,128)} %filters_ref.1) | copy-start | bytes 21508
  77.3 25.6 %all-to-all-start.2 = ((bf16[16,144,256]{2,1,0:T(8,128)(2,1)}), bf16[16,144,256]{2,1,0:T(8,128)(2,1)}, u32[]{:S(2)}, u32[]{:S(2)}) async-start(bf16[16,144,256]{2,1,0:T(8,128)(2,1)} %get-tuple-element.12), calls=%async_computation.2 | async-start | bytes 2359296 | tf_op jit(solution)/shard_map/all_to_all | solution.py:28
  84.5 4.5 %collective-permute-start.7 = (bf16[256,2048]{1,0:T(8,128)(2,1)S(1)}, bf16[256,2048]{1,0:T(8,128)(2,1)S(1)}, u32[]{:S(2)}, u32[]{:S(2)}) collective-permute-start(bf16[256,2048]{1,0:T(8,128)(2,1)S(1)} %get-tuple-element.14), channel_id=1, source_target_pairs={{0,1},{1,0},{2,3},{3,2},{4,5},{5,4},{6,7},{7,6},{8,9},{9,8},{10,11... | collective-permute-start | bytes 3145736 | tf_op jit(solution)/shard_map/ppermute | solution.py:225
  90.6 17.7 %collective-permute-start.8 = (bf16[64,2048]{1,0:T(8,128)(2,1)S(1)}, bf16[64,2048]{1,0:T(8,128)(2,1)S(1)}, u32[]{:S(2)}, u32[]{:S(2)}) collective-permute-start(bf16[64,2048]{1,0:T(8,128)(2,1)S(1)} %get-tuple-element.16), channel_id=1, source_target_pairs={{0,4},{2,6},{4,0},{6,2},{1,5},{3,7},{5,1},{7,3},{8,12},{10,14},{12... | collective-permute-start | bytes 786440 | tf_op jit(solution)/shard_map/ppermute | solution.py:33
  92.6 24.3 %collective-permute-start.9 = (bf16[64,2048]{1,0:T(8,128)(2,1)S(1)}, bf16[64,2048]{1,0:T(8,128)(2,1)S(1)}, u32[]{:S(2)}, u32[]{:S(2)}) collective-permute-start(bf16[64,2048]{1,0:T(8,128)(2,1)S(1)} %get-tuple-element.17), channel_id=1, source_target_pairs={{0,6},{2,0},{4,2},{6,4},{1,7},{3,1},{5,3},{7,5},{8,14},{10,8},{12,... | collective-permute-start | bytes 786440 | tf_op jit(solution)/shard_map/ppermute | solution.py:33
  95.3 21.5 %collective-permute-start.10 = (bf16[64,2048]{1,0:T(8,128)(2,1)S(1)}, bf16[64,2048]{1,0:T(8,128)(2,1)S(1)}, u32[]{:S(2)}, u32[]{:S(2)}) collective-permute-start(bf16[64,2048]{1,0:T(8,128)(2,1)S(1)} %get-tuple-element.18), channel_id=1, source_target_pairs={{0,2},{2,4},{4,6},{6,0},{1,3},{3,5},{5,7},{7,1},{8,10},{10,12},{12... | collective-permute-start | bytes 786440 | tf_op jit(solution)/shard_map/ppermute | solution.py:33
  105.0 16.5 %all-to-all-start.3 = ((bf16[4,48,256]{2,1,0:T(8,128)(2,1)}), bf16[4,48,256]{2,1,0:T(8,128)(2,1)S(1)}, u32[]{:S(2)}, u32[]{:S(2)}) async-start(bf16[4,48,256]{2,1,0:T(8,128)(2,1)} %pad_maximum_fusion), calls=%async_computation.3 | async-start | bytes 196608 | tf_op jit(solution)/shard_map/all_to_all | solution.py:28
